TPU v7x, 32 devices: a whole 2x2x4 slice. The times are simulated.
32 devices in a mesh: dp: 8 (over y, x, core), ctx: 4 (over z).
Axes of the slice: x: 2, y: 2, z: 4, core: 2. Of those that a mesh axis runs over, the one named last changes fastest.
Arguments:
- hidden_in: bfloat16 [8, 1536, 1024], P('dp', 'ctx'), may hold values from -6 to 6
- cotangent: bfloat16 [8, 1536, 1024], P('dp', 'ctx'), may hold values from -6 to 6
- context_len: int32 [8], P('dp'), may hold values from 576 to 1152, as said below
- block_device: int32 [8], P('dp'), may hold values from 0 to 3
- timestep: int32 [8], P('dp'), may hold values from 0 to 511, as said below
- query_weight: bfloat16 [1024, 1024], P('ctx'), may hold values from -0.1875 to 0.1875
- key_weight: bfloat16 [1024, 1024], P('ctx'), may hold values from -0.1875 to 0.1875
- value_weight: bfloat16 [1024, 1024], P('ctx'), may hold values from -0.1875 to 0.1875
- output_weight: bfloat16 [1024, 1024], P('ctx'), may hold values from -1.5 to 1.5
- inner_weight: bfloat16 [1024, 4096], P('ctx'), may hold values from -0.1875 to 0.1875
- outer_weight: bfloat16 [4096, 1024], P('ctx'), may hold values from -0.09375 to 0.09375
- query_bias: bfloat16 [1024], replicated, may hold values from -1.5 to 1.5
- value_bias: bfloat16 [1024], replicated, may hold values from -1.5 to 1.5
- output_bias: bfloat16 [1024], replicated, may hold values from -1.5 to 1.5
- inner_bias: bfloat16 [4096], replicated, may hold values from -1.5 to 1.5
- outer_bias: bfloat16 [1024], replicated, may hold values from -1.5 to 1.5
- attn_gain: bfloat16 [1024], replicated, may hold values from 0.5 to 1.5
- attn_shift: bfloat16 [1024], replicated, may hold values from -1.5 to 1.5
- ffn_gain: bfloat16 [1024], replicated, may hold values from 0.5 to 1.5
- ffn_shift: bfloat16 [1024], replicated, may hold values from -1.5 to 1.5
- time_table: bfloat16 [512, 1024], replicated, may hold values from -3 to 3
Outputs:
- hidden_out: bfloat16 [8, 1536, 1024], P('dp', 'ctx')
- grad_hidden: float32 [8, 1536, 1024], P('dp', 'ctx')
- query_weight_grad: float32 [1024, 1024], P('ctx')
- key_weight_grad: float32 [1024, 1024], P('ctx')
- value_weight_grad: float32 [1024, 1024], P('ctx')
- output_weight_grad: float32 [1024, 1024], P('ctx')
- inner_weight_grad: float32 [1024, 4096], P('ctx')
- outer_weight_grad: float32 [4096, 1024], P('ctx')
- query_bias_grad: float32 [1024], P('ctx')
- value_bias_grad: float32 [1024], P('ctx')
- output_bias_grad: float32 [1024], P('ctx')
- inner_bias_grad: float32 [4096], P('ctx')
- outer_bias_grad: float32 [1024], P('ctx')
- attn_gain_grad: float32 [1024], P('ctx')
- attn_shift_grad: float32 [1024], P('ctx')
- ffn_gain_grad: float32 [1024], P('ctx')
- ffn_shift_grad: float32 [1024], P('ctx')
- time_table_grad: float32 [512, 1024], P('ctx')
Inputs may be any that keep to these rules, and one draw needn't show every extreme that they name: `context_len`: at least half of 1152; some row has exactly 1152. `timestep`: mostly in the upper half, a few near zero.
All inputs are finite; a program needn't handle non-finite values.
Results may differ from a plain program's by a relative error of at most 0.014.
Values may be sent and summed in bfloat16 or wider, within the bound.
No kernel may reach another device: no remote copies, remote signals or barrier semaphores. Data moves between devices by JAX's collectives and lax.ppermute only.
A program may use at most 192 MiB of HBM per device.

v0:
```python
import math

import jax
import jax.numpy as jnp
from jax import lax
from jax.sharding import PartitionSpec as P

HEADS = 16
HD = 64
BLOCK = 25


EPSILON = 1e-05


def layer_norm(values, gain, shift):
    center = values - jnp.mean(values, -1, keepdims=True)
    spread = jnp.mean(center * center, -1, keepdims=True)
    return center * lax.rsqrt(spread + EPSILON) * gain + shift


def left_dot(left, right):
    return lax.dot_general(
        left, right, (((0,), (0,)), ((), ())), preferred_element_type=jnp.float32
    )


def right_dot(left, right):
    return lax.dot_general(
        left, right, (((1,), (1,)), ((), ())), preferred_element_type=jnp.float32
    )


def part_counts(context_len, block_device, count_ctx):
    device = jnp.arange(count_ctx, dtype=jnp.int32)[None, :]
    base = (context_len // (count_ctx - 1))[:, None]
    extra = (context_len % (count_ctx - 1))[:, None]
    order = device - (device > block_device[:, None]).astype(jnp.int32)
    count = base + (order < extra).astype(jnp.int32)
    return jnp.where(device == block_device[:, None], BLOCK, count)


def head_slice(array, head):
    return lax.dynamic_slice_in_dim(array, head * HD, HD, 2)


def head_scores(query, keys, keymask, head):
    scale = 1.0 / math.sqrt(HD)
    scores = (
        jnp.einsum(
            "rqe,rke->rqk",
            head_slice(query, head),
            head_slice(keys, head),
            preferred_element_type=jnp.float32,
        )
        * scale
    )
    return jnp.where(keymask[:, None, :], scores, -1e30)


def forward_head(query, keys, values, keymask, head):
    scores = head_scores(query, keys, keymask, head)
    highest = jnp.max(scores, -1, keepdims=True)
    expo = jnp.exp(scores - highest)
    total = jnp.sum(expo, -1, keepdims=True)
    probs = (expo / total).astype(jnp.bfloat16)
    mixed = jnp.einsum(
        "rqk,rke->rqe", probs, head_slice(values, head), preferred_element_type=jnp.float32
    )
    return (mixed.astype(jnp.bfloat16), (highest + jnp.log(total))[..., 0])


def score_grads(query, keys, values, grad_attn, keymask, head, logsum):
    scale = 1.0 / math.sqrt(HD)
    scores = head_scores(query, keys, keymask, head)
    probs = jnp.exp(scores - logsum[..., None])
    grad_head = head_slice(grad_attn, head)
    grad_probs = jnp.einsum(
        "rqe,rke->rqk", grad_head, head_slice(values, head), preferred_element_type=jnp.float32
    )
    center = jnp.sum(grad_probs * probs, -1, keepdims=True)
    grad_scores = (probs * (grad_probs - center)).astype(jnp.bfloat16)
    grad_query = (
        jnp.einsum(
            "rqk,rke->rqe", grad_scores, head_slice(keys, head), preferred_element_type=jnp.float32
        )
        * scale
    )
    return (probs, grad_head, grad_scores, grad_query, center[..., 0])


def backward_head(query, keys, values, grad_attn, keymask, head, logsum):
    scale = 1.0 / math.sqrt(HD)
    probs, grad_head, grad_scores, grad_query, center = score_grads(
        query, keys, values, grad_attn, keymask, head, logsum
    )
    grad_keys = (
        jnp.einsum(
            "rqk,rqe->rke", grad_scores, head_slice(query, head), preferred_element_type=jnp.float32
        )
        * scale
    )
    grad_values = jnp.einsum(
        "rqk,rqe->rke", probs.astype(jnp.bfloat16), grad_head, preferred_element_type=jnp.float32
    )
    return (grad_query, grad_keys, grad_values)


def per_device(
    hidden_in,
    cotangent,
    context_len,
    block_device,
    timestep,
    query_weight,
    key_weight,
    value_weight,
    output_weight,
    inner_weight,
    outer_weight,
    query_bias,
    value_bias,
    output_bias,
    inner_bias,
    outer_bias,
    attn_gain,
    attn_shift,
    ffn_gain,
    ffn_shift,
    time_table,
):
    count_ctx = lax.axis_size("ctx")
    place = lax.axis_index("ctx")
    rows, slots, width = hidden_in.shape
    tokens = rows * slots
    query_full, key_full, value_full, output_full, inner_full, outer_full = (
        lax.all_gather(query_weight, "ctx", axis=0, tiled=True),
        lax.all_gather(key_weight, "ctx", axis=0, tiled=True),
        lax.all_gather(value_weight, "ctx", axis=0, tiled=True),
        lax.all_gather(output_weight, "ctx", axis=0, tiled=True),
        lax.all_gather(inner_weight, "ctx", axis=0, tiled=True),
        lax.all_gather(outer_weight, "ctx", axis=0, tiled=True),
    )
    counts = part_counts(context_len, block_device, count_ctx)
    slot = jnp.arange(slots, dtype=jnp.int32)
    keymask = (slot[None, None, :] < counts[:, :, None]).reshape(rows, count_ctx * slots)
    device = jnp.arange(count_ctx, dtype=jnp.int32)
    owned = jnp.sum(jnp.where(device[None, :] == place, counts, 0), 1)
    own_mask = slot[None, :] < owned[:, None]
    valid = own_mask.astype(jnp.float32).reshape(tokens, 1)
    block = ((block_device == place)[:, None] & (slot[None, :] < BLOCK)).astype(jnp.float32)
    levels = jnp.arange(time_table.shape[0], dtype=jnp.int32)
    onehot = levels[None, :] == timestep[:, None]
    embed = jnp.dot(onehot.astype(jnp.bfloat16), time_table, preferred_element_type=jnp.float32)
    start = (hidden_in.astype(jnp.float32) + block[..., None] * embed[:, None, :]).reshape(
        tokens, width
    )
    start_low = start.astype(jnp.bfloat16)
    query = (
        (
            jnp.dot(start_low, query_full, preferred_element_type=jnp.float32)
            + query_bias.astype(jnp.float32)
        )
        .astype(jnp.bfloat16)
        .reshape(rows, slots, width)
    )
    keys = jnp.dot(start_low, key_full, preferred_element_type=jnp.float32).astype(jnp.bfloat16)
    keys = keys.reshape(rows, slots, width)
    values = (
        (
            jnp.dot(start_low, value_full, preferred_element_type=jnp.float32)
            + value_bias.astype(jnp.float32)
        )
        .astype(jnp.bfloat16)
        .reshape(rows, slots, width)
    )
    keys_all, values_all = (
        lax.all_gather(keys, "ctx", axis=1, tiled=True),
        lax.all_gather(values, "ctx", axis=1, tiled=True),
    )
    head_ids = jnp.arange(HEADS, dtype=jnp.int32)
    mixed, logsums = lax.map(
        lambda head: forward_head(query, keys_all, values_all, keymask, head), head_ids
    )
    attn = mixed.transpose(1, 2, 0, 3).reshape(tokens, width)
    first = (
        jnp.dot(attn, output_full, preferred_element_type=jnp.float32)
        + output_bias.astype(jnp.float32)
        + start
    )
    normed, norm_pull = jax.vjp(
        layer_norm, first, attn_gain.astype(jnp.float32), attn_shift.astype(jnp.float32)
    )
    normed_low = normed.astype(jnp.bfloat16)
    inner = jnp.dot(normed_low, inner_full, preferred_element_type=jnp.float32) + inner_bias.astype(
        jnp.float32
    )
    active, gelu_pull = jax.vjp(jax.nn.gelu, inner)
    active_low = active.astype(jnp.bfloat16)
    second = (
        jnp.dot(active_low, outer_full, preferred_element_type=jnp.float32)
        + outer_bias.astype(jnp.float32)
        + normed
    )
    result, final_pull = jax.vjp(
        layer_norm, second, ffn_gain.astype(jnp.float32), ffn_shift.astype(jnp.float32)
    )
    hidden_out = (result * valid).astype(jnp.bfloat16).reshape(rows, slots, width)
    incoming = cotangent.astype(jnp.float32).reshape(tokens, width) * valid
    grad_second, ffn_gain_grad, ffn_shift_grad = final_pull(incoming)
    outer_bias_grad = jnp.sum(grad_second, 0)
    second_low = grad_second.astype(jnp.bfloat16)
    outer_weight_grad = left_dot(active_low, second_low)
    grad_active = right_dot(second_low, outer_full)
    (grad_inner,) = gelu_pull(grad_active)
    inner_low = grad_inner.astype(jnp.bfloat16)
    inner_bias_grad = jnp.sum(inner_low.astype(jnp.float32), 0)
    inner_weight_grad = left_dot(normed_low, inner_low)
    grad_normed = right_dot(inner_low, inner_full) + grad_second
    grad_first, attn_gain_grad, attn_shift_grad = norm_pull(grad_normed)
    output_bias_grad = jnp.sum(grad_first, 0)
    first_low = grad_first.astype(jnp.bfloat16)
    output_weight_grad = left_dot(attn, first_low)
    grad_attn = right_dot(first_low, output_full).astype(jnp.bfloat16).reshape(rows, slots, width)
    keys_back, values_back = (
        lax.all_gather(keys, "ctx", axis=1, tiled=True),
        lax.all_gather(values, "ctx", axis=1, tiled=True),
    )
    grad_query, grad_keys, grad_values = lax.map(
        lambda item: backward_head(
            query, keys_back, values_back, grad_attn, keymask, item[0], item[1]
        ),
        (head_ids, logsums),
    )
    keys_whole = grad_keys.transpose(1, 2, 0, 3).reshape(rows, count_ctx * slots, width)
    values_whole = grad_values.transpose(1, 2, 0, 3).reshape(rows, count_ctx * slots, width)
    keys_owned, values_owned = (
        lax.psum_scatter(keys_whole, "ctx", scatter_dimension=1, tiled=True),
        lax.psum_scatter(values_whole, "ctx", scatter_dimension=1, tiled=True),
    )
    query_low = grad_query.transpose(1, 2, 0, 3).reshape(tokens, width).astype(jnp.bfloat16)
    keys_low = keys_owned.reshape(tokens, width).astype(jnp.bfloat16)
    values_low = values_owned.reshape(tokens, width).astype(jnp.bfloat16)
    query_weight_grad = left_dot(start_low, query_low)
    key_weight_grad = left_dot(start_low, keys_low)
    value_weight_grad = left_dot(start_low, values_low)
    query_bias_grad = jnp.sum(query_low.astype(jnp.float32), 0)
    value_bias_grad = jnp.sum(values_low.astype(jnp.float32), 0)
    grad_start = (
        right_dot(query_low, query_full)
        + right_dot(keys_low, key_full)
        + right_dot(values_low, value_full)
        + grad_first
    )
    grad_hidden = grad_start.reshape(rows, slots, width)
    block_sums = jnp.sum(grad_hidden * block[..., None], 1)
    time_table_grad = lax.dot_general(
        onehot.astype(jnp.float32),
        block_sums,
        (((0,), (0,)), ((), ())),
        precision=lax.Precision.HIGHEST,
        preferred_element_type=jnp.float32,
    )
    grads = (
        query_weight_grad,
        key_weight_grad,
        value_weight_grad,
        output_weight_grad,
        inner_weight_grad,
        outer_weight_grad,
        query_bias_grad,
        value_bias_grad,
        output_bias_grad,
        inner_bias_grad,
        outer_bias_grad,
        attn_gain_grad,
        attn_shift_grad,
        ffn_gain_grad,
        ffn_shift_grad,
        time_table_grad,
    )
    partial_shares = (
        lax.psum_scatter(grads[0], "ctx", scatter_dimension=0, tiled=True),
        lax.psum_scatter(grads[1], "ctx", scatter_dimension=0, tiled=True),
        lax.psum_scatter(grads[2], "ctx", scatter_dimension=0, tiled=True),
        lax.psum_scatter(grads[3], "ctx", scatter_dimension=0, tiled=True),
        lax.psum_scatter(grads[4], "ctx", scatter_dimension=0, tiled=True),
        lax.psum_scatter(grads[5], "ctx", scatter_dimension=0, tiled=True),
        lax.psum_scatter(grads[6], "ctx", scatter_dimension=0, tiled=True),
        lax.psum_scatter(grads[7], "ctx", scatter_dimension=0, tiled=True),
        lax.psum_scatter(grads[8], "ctx", scatter_dimension=0, tiled=True),
        lax.psum_scatter(grads[9], "ctx", scatter_dimension=0, tiled=True),
        lax.psum_scatter(grads[10], "ctx", scatter_dimension=0, tiled=True),
        lax.psum_scatter(grads[11], "ctx", scatter_dimension=0, tiled=True),
        lax.psum_scatter(grads[12], "ctx", scatter_dimension=0, tiled=True),
        lax.psum_scatter(grads[13], "ctx", scatter_dimension=0, tiled=True),
        lax.psum_scatter(grads[14], "ctx", scatter_dimension=0, tiled=True),
        lax.psum_scatter(grads[15], "ctx", scatter_dimension=0, tiled=True),
    )
    shares = lax.psum(
        (
            partial_shares[0],
            partial_shares[1],
            partial_shares[2],
            partial_shares[3],
            partial_shares[4],
            partial_shares[5],
            partial_shares[6],
            partial_shares[7],
            partial_shares[8],
            partial_shares[9],
            partial_shares[10],
            partial_shares[11],
            partial_shares[12],
            partial_shares[13],
            partial_shares[14],
            partial_shares[15],
        ),
        "dp",
    )
    return (hidden_out, grad_hidden) + tuple(shares)


def solution(mesh):
    placed = (
        P("dp", "ctx", None),
        P("dp", "ctx", None),
        P("dp"),
        P("dp"),
        P("dp"),
        P("ctx", None),
        P("ctx", None),
        P("ctx", None),
        P("ctx", None),
        P("ctx", None),
        P("ctx", None),
        P(),
        P(),
        P(),
        P(),
        P(),
        P(),
        P(),
        P(),
        P(),
        P(),
    )
    return jax.shard_map(
        per_device,
        mesh=mesh,
        in_specs=placed,
        out_specs=(
            P("dp", "ctx", None),
            P("dp", "ctx", None),
            P("ctx", None),
            P("ctx", None),
            P("ctx", None),
            P("ctx", None),
            P("ctx", None),
            P("ctx", None),
            P("ctx"),
            P("ctx"),
            P("ctx"),
            P("ctx"),
            P("ctx"),
            P("ctx"),
            P("ctx"),
            P("ctx"),
            P("ctx"),
            P("ctx", None),
        ),
        check_vma=False,
    )
```

profile of v0, /device:TPU:0, one launch (start us, length us, event | category | flops | bytes accessed | tf_op | source)
XLA Modules:
  0.0 2201.0 jit_solution(12669285281446793789)
XLA Ops:
  11.1 47.2 %all-gather.13.cloned.1.call-done = bf16[1024,1024]{1,0:T(8,128)(2,1)} async-done(((bf16[256,1024]{1,0:T(8,128)(2,1)}), bf16[1024,1024]{1,0:T(8,128)(2,1)}) %all-gather.13.cloned.1.call-update) | async-done | bytes 2097168 | tf_op jit(solution)/shard_map/all_gather | solution.py:138
  58.3 3.5 convolution_convert_fusion.1
  61.9 42.6 %all-gather.15.cloned.1.call-done = bf16[1024,1024]{1,0:T(8,128)(2,1)} async-done(((bf16[256,1024]{1,0:T(8,128)(2,1)}), bf16[1024,1024]{1,0:T(8,128)(2,1)}) %all-gather.15.cloned.1.call-update) | async-done | bytes 2097168 | tf_op jit(solution)/shard_map/all_gather | solution.py:139
  104.5 3.5 add_convert_fusion
  113.0 37.8 %all-gather.11.cloned.1.call-done = bf16[1024,1024]{1,0:T(8,128)(2,1)} async-done(((bf16[256,1024]{1,0:T(8,128)(2,1)}), bf16[1024,1024]{1,0:T(8,128)(2,1)}) %all-gather.11.cloned.1.call-update) | async-done | bytes 2097168 | tf_op jit(solution)/shard_map/all_gather | solution.py:137
  150.8 2.6 fusion.63
  153.4 61.6 %all-gather.23.cloned.1.call-done = bf16[1536,1024]{1,0:T(8,128)(2,1)} async-done(((bf16[384,1024]{1,0:T(8,128)(2,1)}), bf16[1536,1024]{1,0:T(8,128)(2,1)}) %all-gather.23.cloned.1.call-update) | async-done | bytes 3145744 | tf_op jit(solution)/shard_map/all_gather | solution.py:178
  215.0 64.2 %all-gather.25.cloned.1.call-done = bf16[1536,1024]{1,0:T(8,128)(2,1)} async-done(((bf16[384,1024]{1,0:T(8,128)(2,1)}), bf16[1536,1024]{1,0:T(8,128)(2,1)}) %all-gather.25.cloned.1.call-update) | async-done | bytes 3145744 | tf_op jit(solution)/shard_map/all_gather | solution.py:179
  279.2 84.7 %while.28 = (s32[]{:T(128)}, bf16[16,1,384,64]{2,3,1,0:T(8,128)(2,1)S(1)}, f32[16,1,384]{2,1,0:T(1,128)S(1)}, s32[16]{0:T(128)S(1)}, bf16[1,384,1024]{2,1,0:T(8,...) while((s32[]{:T(128)}, ...), condition=%wide.region_3.4_spmd.clone, body=%wide.region_0.3_spmd.clone.sunk | while | flops 155739264 | bytes 8036563 | solution.py:182
  364.8 2.7 fusion.101
  367.8 107.3 %all-gather.19.cloned.1.call-done = bf16[1024,4096]{1,0:T(8,128)(2,1)} async-done(((bf16[256,4096]{1,0:T(8,128)(2,1)}), bf16[1024,4096]{1,0:T(8,128)(2,1)}) %all-gather.19.cloned.1.call-update) | async-done | bytes 8388624 | tf_op jit(solution)/shard_map/all_gather | solution.py:141
  475.2 8.9 convolution_add_fusion
  484.0 140.6 %all-gather.21.cloned.1.call-done = bf16[4096,1024]{1,0:T(8,128)(2,1)} async-done(((bf16[1024,1024]{1,0:T(8,128)(2,1)}), bf16[4096,1024]{1,0:T(8,128)(2,1)}) %all-gather.21.cloned.1.call-update) | async-done | bytes 8388624 | tf_op jit(solution)/shard_map/all_gather | solution.py:142
  624.6 9.4 fusion.102
  638.2 10.3 convert_reduce_fusion
  648.6 3.9 multiply_reduce_fusion.2
  656.1 184.8 %while.29 = (s32[]{:T(128)}, bf16[16,1,384,64]{2,3,1,0:T(8,128)(2,1)}, f32[16,1,1536,64]{2,3,1,0:T(8,128)}, f32[16,1,1536,64]{2,3,1,0:T(8,128)}, s32[16]{0:T(128...) while((s32[]{:T(128)}, ...), condition=%wide.region_15.16_spmd.clone, body=%wide.region_13.15_spmd.clone.sunk | while | flops 382919808 | bytes 20168444 | solution.py:229
  661.2 2.3 fusion.158
  665.6 2.1 fusion.160
  672.8 2.3 fusion.158
  684.3 2.3 fusion.158
  695.8 2.3 fusion.158
  698.1 2.1 fusion.159
  707.4 2.3 fusion.158
  718.9 2.3 fusion.158
  723.3 2.1 fusion.160
  730.5 2.3 fusion.158
  742.0 2.3 fusion.158
  746.4 2.1 fusion.160
  753.6 2.3 fusion.158
  765.2 2.3 fusion.158
  776.7 2.3 fusion.158
  788.2 2.3 fusion.158
  792.6 2.1 fusion.160
  799.8 2.3 fusion.158
  802.1 2.1 fusion.159
  811.3 2.3 fusion.158
  822.9 2.3 fusion.158
  825.2 2.1 fusion.159
  834.4 2.3 fusion.158
  838.8 2.1 fusion.160
  841.5 5.1 fusion.93
  846.9 4.8 fusion.90
  852.9 3.8 fusion.104
  856.7 93.4 %reduce-scatter.10.cloned.1.call-done = f32[1,384,1024]{1,2,0:T(8,128)} async-done(((f32[1,1536,1024]{1,2,0:T(8,128)}), f32[1,384,1024]{1,2,0:T(8,128)}) %reduce-scatter.10.cloned.1.call-update) | async-done | bytes 1572880 | tf_op jit(solution)/shard_map/reduce_scatter | solution.py:238
  950.0 4.2 fusion.73
  954.3 109.2 %reduce-scatter.12.cloned.1.call-done = f32[1,384,1024]{1,2,0:T(8,128)} async-done(((f32[1,1536,1024]{1,2,0:T(8,128)}), f32[1,384,1024]{1,2,0:T(8,128)}) %reduce-scatter.12.cloned.1.call-update) | async-done | bytes 1572880 | tf_op jit(solution)/shard_map/reduce_scatter | solution.py:239
  1063.5 5.9 multiply_reduce_fusion.1
  1071.0 4.9 fusion.71
  1075.9 4.8 fusion.68
  1080.8 10.2 fusion.95
  1092.4 11.6 fusion.88
  1104.1 39.6 %reduce-scatter.14.cloned.1.call-done = f32[256,1024]{1,0:T(8,128)} async-done(((f32[1024,1024]{1,0:T(8,128)}), f32[256,1024]{1,0:T(8,128)}) %reduce-scatter.14.cloned.1.call-update) | async-done | bytes 1048592 | tf_op jit(solution)/shard_map/reduce_scatter | solution.py:283
  1143.7 79.5 %reduce-scatter.20.cloned.1.call-done = f32[256,1024]{1,0:T(8,128)} async-done(((f32[1024,1024]{1,0:T(8,128)}), f32[256,1024]{1,0:T(8,128)}) %reduce-scatter.20.cloned.1.call-update) | async-done | bytes 1048592 | tf_op jit(solution)/shard_map/reduce_scatter | solution.py:286
  1223.2 46.7 %reduce-scatter.26.cloned.1.call-done = f32[128,1024]{1,0:T(8,128)} async-done(((f32[512,1024]{1,0:T(8,128)}), f32[128,1024]{1,0:T(8,128)}) %reduce-scatter.26.cloned.1.call-update) | async-done | bytes 524304 | tf_op jit(solution)/shard_map/reduce_scatter | solution.py:298
  1269.9 78.9 %reduce-scatter.16.cloned.1.call-done = f32[256,1024]{1,0:T(8,128)} async-done(((f32[1024,1024]{1,0:T(8,128)}), f32[256,1024]{1,0:T(8,128)}) %reduce-scatter.16.cloned.1.call-update) | async-done | bytes 1048592 | tf_op jit(solution)/shard_map/reduce_scatter | solution.py:284
  1348.9 79.4 %reduce-scatter.18.cloned.1.call-done = f32[256,1024]{1,0:T(8,128)} async-done(((f32[1024,1024]{1,0:T(8,128)}), f32[256,1024]{1,0:T(8,128)}) %reduce-scatter.18.cloned.1.call-update) | async-done | bytes 1048592 | tf_op jit(solution)/shard_map/reduce_scatter | solution.py:285
  1428.3 283.2 %reduce-scatter.22.cloned.1.call-done = f32[256,4096]{1,0:T(8,128)} async-done(((f32[1024,4096]{1,0:T(8,128)}), f32[256,4096]{1,0:T(8,128)}) %reduce-scatter.22.cloned.1.call-update) | async-done | bytes 4194320 | tf_op jit(solution)/shard_map/reduce_scatter | solution.py:287
  1711.5 283.3 %reduce-scatter.24.cloned.1.call-done = f32[1024,1024]{1,0:T(8,128)} async-done(((f32[4096,1024]{1,0:T(8,128)}), f32[1024,1024]{1,0:T(8,128)}) %reduce-scatter.24.cloned.1.call-update) | async-done | bytes 4194320 | tf_op jit(solution)/shard_map/reduce_scatter | solution.py:288
  2000.3 18.9 all-reduce.11
  2019.9 23.8 %all-reduce.9 = (f32[256]{0:T(256)}, f32[256]{0:T(256)}, f32[256]{0:T(256)}, f32[1024]{0:T(1024)}, f32[256]{0:T(256)}, /*index=5*/f32[256]{0:T(256)}, f32[256]{0:T(256)}, f32[256]{0:T(256)}, f32[256]{0:T(256)}) all-reduce(f32[256]{0:T(256)S(1)} %dynamic-slice.1, f32[256]{0:T(256)S(1)} %dynamic-slice.3, ...), channel_id=1, replica_groups=mesh['dp'=8,'ctx'=4] {'dp'}, use_global_device_ids=true, to_apply=%region_32.33 | all-reduce | flops 3072 | bytes 24576 | tf_op jit(solution)/shard_map/psum | solution.py:300
  2043.6 138.1 %all-reduce.14.cloned.1.call-done = (f32[256,1024]{1,0:T(8,128)}, f32[256,1024]{1,0:T(8,128)}, f32[256,1024]{1,0:T(8,128)}, f32[256,1024]{1,0:T(8,128)}, f32[256...) async-done(((f32[256,1024]{1,0:T(8,128)}, f32[256,1024]{1,0:T(8,128)}, f32[256,1024]{1,0:T(8,128)}, f32[256,1024]{1,0:T(8,128)}, f32[256,4096]{1,0:T(8,128)}, ...) | async-done | bytes 13107216 | tf_op jit(solution)/shard_map/psum | solution.py:300
  2181.8 2.5 copy.75
  2187.3 2.1 copy.79
  (425 shorter events, 227.1 us)
Async XLA Ops:
  7.2 3.6 copy-start
  7.2 51.1 %copy-start.2 = (bf16[1,384,1024]{2,1,0:T(8,128)(2,1)S(1)}, bf16[1,384,1024]{2,1,0:T(8,128)(2,1)}, u32[]{:S(2)}) copy-start(bf16[1,384,1024]{2,1,0:T(8,128)(2,1)} %param.25) | copy-start | bytes 2359300
  7.2 51.1 %all-gather.13.cloned.1.call-start = ((), (), s32[]{:S(2)}) async-start(), calls=%async_computation.10 | async-start | bytes 2621440 | tf_op jit(solution)/shard_map/all_gather | solution.py:138
  8.0 96.6 %all-gather.15.cloned.1.call-start = ((), (), s32[]{:S(2)}) async-start(), calls=%async_computation.11 | async-start | bytes 2621440 | tf_op jit(solution)/shard_map/all_gather | solution.py:139
  8.7 142.1 %all-gather.11.cloned.1.call-start = ((), (), s32[]{:S(2)}) async-start(), calls=%async_computation.9 | async-start | bytes 2621440 | tf_op jit(solution)/shard_map/all_gather | solution.py:137
  9.4 205.6 %all-gather.23.cloned.1.call-start = ((), (), s32[]{:S(2)}) async-start(), calls=%async_computation.24 | async-start | bytes 3932160 | tf_op jit(solution)/shard_map/all_gather | solution.py:178
  58.3 3.6 copy-start.21
  61.8 217.3 %all-gather.25.cloned.1.call-start = ((), (), s32[]{:S(2)}) async-start(), calls=%async_computation.25 | async-start | bytes 3932160 | tf_op jit(solution)/shard_map/all_gather | solution.py:179
  108.1 255.9 %all-gather.17.cloned.1.call-start = ((), (), s32[]{:S(2)}) async-start(), calls=%async_computation.12 | async-start | bytes 2621440 | tf_op jit(solution)/shard_map/all_gather | solution.py:140
  108.7 366.5 %all-gather.19.cloned.1.call-start = ((), (), s32[]{:S(2)}) async-start(), calls=%async_computation.13 | async-start | bytes 10485760 | tf_op jit(solution)/shard_map/all_gather | solution.py:141
  109.4 2.1 copy-start.22
  109.4 2.1 copy-start.23
  109.4 2.2 copy-start.24
  109.4 2.2 copy-start.25
  109.4 2.2 copy-start.26
  109.5 2.2 copy-start.20
  109.5 3.5 copy-start.27
  109.5 3.5 copy-start.28
  109.5 515.1 %all-gather.21.cloned.1.call-start = ((), (), s32[]{:S(2)}) async-start(), calls=%async_computation.14 | async-start | bytes 10485760 | tf_op jit(solution)/shard_map/all_gather | solution.py:142
  110.2 839.8 %reduce-scatter.10.cloned.1.call-start = ((), (), s32[]{:S(2)}) async-start(), calls=%async_computation.15 | async-start | bytes 7864320 | tf_op jit(solution)/shard_map/reduce_scatter | solution.py:238
  363.9 0.9 copy-start.15
  634.0 1.1 copy-start.13
  635.1 3.1 copy-start.8
  635.9 12.7 slice-start
  637.6 11.0 copy-start.6
  638.2 10.4 slice-start.1
  648.5 4.0 copy-start.11
  652.5 1.7 copy-start.14
  653.1 3.0 copy-start.3
  840.9 222.6 %reduce-scatter.12.cloned.1.call-start = ((), (), s32[]{:S(2)}) async-start(), calls=%async_computation.16 | async-start | bytes 7864320 | tf_op jit(solution)/shard_map/reduce_scatter | solution.py:239
  841.5 302.2 %reduce-scatter.14.cloned.1.call-start = ((), (), s32[]{:S(2)}) async-start(), calls=%async_computation.17 | async-start | bytes 5242880 | tf_op jit(solution)/shard_map/reduce_scatter | solution.py:283
  846.7 376.5 %reduce-scatter.20.cloned.1.call-start = ((), (), s32[]{:S(2)}) async-start(), calls=%async_computation.20 | async-start | bytes 5242880 | tf_op jit(solution)/shard_map/reduce_scatter | solution.py:286
  851.8 1.1 copy-start.12
  851.8 418.1 %reduce-scatter.26.cloned.1.call-start = ((), (), s32[]{:S(2)}) async-start(), calls=%async_computation.23 | async-start | bytes 2621440 | tf_op jit(solution)/shard_map/reduce_scatter | solution.py:298
  1070.9 277.9 %reduce-scatter.16.cloned.1.call-start = ((), (), s32[]{:S(2)}) async-start(), calls=%async_computation.18 | async-start | bytes 5242880 | tf_op jit(solution)/shard_map/reduce_scatter | solution.py:284
  1075.9 352.4 %reduce-scatter.18.cloned.1.call-start = ((), (), s32[]{:S(2)}) async-start(), calls=%async_computation.19 | async-start | bytes 5242880 | tf_op jit(solution)/shard_map/reduce_scatter | solution.py:285
  1080.7 630.7 %reduce-scatter.22.cloned.1.call-start = ((), (), s32[]{:S(2)}) async-start(), calls=%async_computation.21 | async-start | bytes 20971520 | tf_op jit(solution)/shard_map/reduce_scatter | solution.py:287
  1091.0 1.4 copy-start.7
  1091.0 903.7 %reduce-scatter.24.cloned.1.call-start = ((), (), s32[]{:S(2)}) async-start(), calls=%async_computation.22 | async-start | bytes 20971520 | tf_op jit(solution)/shard_map/reduce_scatter | solution.py:288
  1104.0 1077.8 %all-reduce.14.cloned.1.call-start = ((), (), s32[]{:S(2)}) async-start(), calls=%async_computation.26 | async-start | bytes 26214400 | tf_op jit(solution)/shard_map/psum | solution.py:300
  1994.7 0.7 copy-start.29
  1994.7 4.0 copy-start.4
  1998.7 1.4 copy-start.5
  2181.8 2.5 copy-start.18
  2181.8 3.4 copy-start.17
  2181.8 4.4 copy-start.16
  2184.3 3.1 copy-start.10
  2187.3 3.7 copy-start.9
  2191.0 2.0 copy-start.19
  2191.0 2.8 copy-start.1
Sparse Core Ops, SparseCore 0:
  9.6 48.6 all-gather.12
  59.9 44.6 all-gather.14
  106.1 44.6 all-gather.10
  152.8 62.1 all-gather.22
  217.0 62.1 all-gather.24
  280.6 44.3 all-gather.16
  326.6 148.5 all-gather.18
  476.7 147.8 all-gather.20
  841.0 108.9 reduce-scatter.9
  952.2 111.2 reduce-scatter.11
  1066.3 77.2 reduce-scatter.13
  1145.9 77.2 reduce-scatter.19
  1225.5 44.3 reduce-scatter.25
  1272.8 76.0 reduce-scatter.15
  1351.0 77.2 reduce-scatter.17
  1430.6 280.7 reduce-scatter.21
  1713.7 281.0 reduce-scatter.23
  2000.2 181.5 all-reduce.13
where the time goes:
time: 2210 us; the launch traced here: 2200 us
  waiting for transfers between devices  1740 us (79%)
  matrix products  316 us (14%)
  blocking collectives  42.7 us (2%)
  local copies, waits for them, and re-layouts  40.5 us (2%)
  other arithmetic  22.9 us (1%)
    reduce_scatter x1, waiting for transfers between devices, per_device(): lax.psum_scatter(grads[5], 'ctx', scatter_dimension=0, tiled=True)  283 us
    reduce_scatter x1, waiting for transfers between devices, per_device(): lax.psum_scatter(grads[4], 'ctx', scatter_dimension=0, tiled=True)  283 us
    all_gather x1, waiting for transfers between devices, per_device(): lax.all_gather(outer_weight, 'ctx', axis=0, tiled=True)  141 us
    psum x1, waiting for transfers between devices, per_device(): lax.psum((partial_shares[0], partial_shares[1], partial_shares[2], partia...  138 us
    reduce_scatter x1, waiting for transfers between devices, per_device(): lax.psum_scatter(values_whole, 'ctx', scatter_dimension=1, tiled=True)  109 us
    all_gather x1, waiting for transfers between devices, per_device(): lax.all_gather(inner_weight, 'ctx', axis=0, tiled=True)  107 us
    reduce_scatter x1, waiting for transfers between devices, per_device(): lax.psum_scatter(keys_whole, 'ctx', scatter_dimension=1, tiled=True)  93.4 us
    reduce_scatter x1, waiting for transfers between devices, per_device(): lax.psum_scatter(grads[3], 'ctx', scatter_dimension=0, tiled=True)  79.5 us
  transfers between devices with their start and end apart: 18, of which 17 were waited for; matrix products, arithmetic and copies ran while one was open for 7% of the time, Pallas kernels for 0%

commit v1 on v0

v1 whole, which is shorter than its diff:
```python
import functools
import math

import jax
import jax.numpy as jnp
from jax import lax
from jax.experimental import pallas as pl
from jax.experimental.pallas import tpu as pltpu
from jax.sharding import PartitionSpec as P

HEADS = 16
HD = 64
BLOCK = 25
EPSILON = 1e-05
GROUP = 8
TAIL = 128
PAIR = 2 * HD
LOG2E = 1.4426950408889634
LOW = jnp.bfloat16
WIDE = jnp.float32
VMEM = pl.BlockSpec(memory_space=pltpu.VMEM)
SMEM = pl.BlockSpec(memory_space=pltpu.SMEM)
ANY = pl.BlockSpec(memory_space=pl.ANY)


def params(mib=48):
    return pltpu.CompilerParams(vmem_limit_bytes=mib << 20)


def layer_norm(values, gain, shift):
    center = values - jnp.mean(values, -1, keepdims=True)
    spread = jnp.mean(center * center, -1, keepdims=True)
    return center * lax.rsqrt(spread + EPSILON) * gain + shift


def dot(left, right, dims, out=WIDE):
    return lax.dot_general(left, right, (dims, ((), ())), preferred_element_type=out)


def left_dot(left, right, out=WIDE):
    return dot(left, right, ((0,), (0,)), out)


def right_dot(left, right):
    return dot(left, right, ((1,), (1,)))


def swap(value, mask):
    size = lax.axis_size("dp")
    return lax.ppermute(value, "dp", [(i, i ^ mask) for i in range(size)])


def turn(value, k):
    size = lax.axis_size("ctx")
    return lax.ppermute(value, "ctx", [(i, (i + k) % size) for i in range(size)])


def take(value, index, axis=0):
    return lax.dynamic_index_in_dim(value, index, axis, keepdims=False)


def add(left, right):
    return (left.astype(WIDE) + right.astype(WIDE)).astype(LOW)


def plane_gather(one, two):
    one, two = {0: one}, {0: two}
    one[2], two[4] = swap(one[0], 2), swap(two[0], 4)
    one[4], two[2] = swap(one[0], 4), swap(two[0], 2)
    one[6], two[6] = swap(one[2], 4), swap(two[4], 2)
    for mask in (0, 2, 4, 6):
        one[mask + 1], two[mask + 1] = swap(one[mask], 1), swap(two[mask], 1)
    return [one[m] for m in range(GROUP)], [two[m] for m in range(GROUP)]


def plane_reduce(grad, d):
    core, x, y = d & 1, (d >> 1) & 1, (d >> 2) & 1
    grad = add(take(grad, core, 3), swap(take(grad, 1 - core, 3), 1))
    one, two = grad[:, :, :, 0], grad[:, :, :, 1]
    got_one, got_two = swap(take(one, 1 - x, 2), 2), swap(take(two, 1 - y, 1), 4)
    one, two = add(take(one, x, 2), got_one), add(take(two, y, 1), got_two)
    got_one, got_two = swap(take(one, 1 - y, 1), 4), swap(take(two, 1 - x, 1), 2)
    return add(take(one, y, 1), got_one), add(take(two, x, 1), got_two)


def place_weight(shard, masks, halves, ids_ref, own_ref, *refs):
    pieces, out_ref, sems = refs[:-2], refs[-2], refs[-1]
    n = out_ref.shape[0] // shard
    part = shard // GROUP
    rows = part // halves
    copies = [
        pltpu.make_async_copy(
            own_ref, out_ref.at[pl.ds(pl.multiple_of(ids_ref[0] * shard, 16), shard)], sems.at[0]
        )
    ]
    for m in range(masks):
        start = (ids_ref[1] ^ m) * part
        for h in range(halves):
            piece = pieces[m * halves + h]
            for k in range(1, n):
                home = lax.rem(ids_ref[0] + n - k, n) * shard
                where = pl.multiple_of(home + start + h * rows, rows)
                copies.append(
                    pltpu.make_async_copy(
                        piece.at[k - 1], out_ref.at[pl.ds(where, rows)], sems.at[len(copies)]
                    )
                )
    for copy in copies:
        copy.start()
    for copy in copies:
        copy.wait()


def whole_weight(ids, own, pieces, halves, n):
    rows, cols = own.shape
    body = functools.partial(place_weight, rows, GROUP, halves)
    return pl.pallas_call(
        body,
        out_shape=jax.ShapeDtypeStruct((n * rows, cols), own.dtype),
        in_specs=[SMEM] + [ANY] * (1 + len(pieces)),
        out_specs=VMEM,
        scratch_shapes=[pltpu.SemaphoreType.DMA((1 + len(pieces) * (n - 1),))],
        compiler_params=params(),
        cost_estimate=pl.CostEstimate(
            flops=0, bytes_accessed=n * rows * cols * 4, transcendentals=0
        ),
    )(ids, own, *pieces)


def gather_weight(ids, own, d, n):
    part = own.shape[0] // GROUP
    piece = lax.dynamic_slice_in_dim(own, d * part, part, 0)
    got = jnp.stack([turn(piece, k) for k in range(1, n)])
    one, two = plane_gather(got[:, : part // 2], got[:, part // 2 :])
    pieces = [item for pair in zip(one, two) for item in pair]
    return whole_weight(ids, own, pieces, 2, n)


def gather_columns(ids, own, d, place, n):
    part = own.shape[0] // GROUP
    cols = own.shape[1] // n
    blocks = own.reshape(own.shape[0], 3, n, cols // 3)
    piece = lax.dynamic_slice_in_dim(blocks, d * part, part, 0)
    pick = lambda v, g: take(v, g % n, 2).reshape(v.shape[0], cols)
    got = jnp.stack([turn(pick(piece, place + k), k) for k in range(1, n)])
    pieces = [got] + [swap(got, m) for m in range(1, GROUP)]
    return whole_weight(ids, pick(blocks, place), pieces, 1, n)


def place_grad(ids_ref, *refs):
    pieces, out_ref = refs[:-1], refs[-1]
    rows = pieces[0].shape[0]
    for i, piece in enumerate(pieces):
        where = ((ids_ref[1] ^ (i // 2)) * 2 + i % 2) * rows
        out_ref[pl.ds(pl.multiple_of(where, rows), rows), :] = piece[...].astype(WIDE)


def share_grad(ids, grad, d, place, n):
    rows, cols = grad.shape
    part = rows // (n * GROUP * 2)
    one, two = plane_reduce(grad.reshape(n, 2, 2, 2, 2, part, cols), d)
    both = jnp.stack([one, two], 1)
    return finish_grad(ids, both, place, n)


def finish_grad(ids, both, place, n):
    got = [turn(take(both, (place + k) % n), k) for k in range(1, n)]
    total = take(both, place).astype(WIDE)
    for item in got:
        total = total + item.astype(WIDE)
    return spread_grad(ids, total)


def spread_grad(ids, total):
    total = total.astype(LOW)
    mask = GROUP
    while mask < lax.axis_size("dp"):
        total = add(total, swap(total, mask))
        mask *= 2
    one, two = plane_gather(total[0], total[1])
    pieces = [item for pair in zip(one, two) for item in pair]
    part, cols = total.shape[1:]
    return pl.pallas_call(
        place_grad,
        out_shape=jax.ShapeDtypeStruct((2 * GROUP * part, cols), WIDE),
        in_specs=[SMEM] + [VMEM] * len(pieces),
        out_specs=VMEM,
        compiler_params=params(),
    )(ids, *pieces)


def attend(full, bias_ref, q_ref, k_ref, v_ref, out_ref, lse_ref):
    tile = pl.program_id(0)
    slots = out_ref.shape[0]
    first = lax.broadcasted_iota(jnp.int32, (1, PAIR), 1) < HD

    def work(rows):
        query = q_ref[:rows, :]
        keys, values = k_ref[...], v_ref[...]
        outs = []
        for h in range(2):
            mine = first if h == 0 else jnp.logical_not(first)
            scores = right_dot(jnp.where(mine, query, 0), keys)
            scores = scores * (LOG2E / math.sqrt(HD)) + bias_ref[...]
            high = jnp.max(scores, -1, keepdims=True)
            expo = jnp.exp2(scores - high)
            total = jnp.sum(expo, -1, keepdims=True)
            probs = (expo * (1.0 / total)).astype(LOW)
            outs.append(dot(probs, values, ((1,), (0,))))
            lse = jnp.broadcast_to(high + jnp.log2(total), (rows, 128))
            lse_ref[h : h + 1, :rows] = lse.T[:1, :]
        out_ref[:rows, :] = jnp.where(first, outs[0], outs[1]).astype(LOW)

    @pl.when(tile < full)
    def _():
        work(slots)

    @pl.when(tile == full)
    def _():
        work(TAIL)
        out_ref[TAIL:, :] = jnp.zeros((slots - TAIL, PAIR), LOW)
        lse_ref[:, TAIL:] = jnp.zeros((8, slots - TAIL), WIDE)


def attention(qkv, bias, pair, pairs, n, slots):
    span = qkv.shape[0]
    whole = lambda col: pl.BlockSpec((span, PAIR), lambda t: (0, col))
    return pl.pallas_call(
        functools.partial(attend, n - 1),
        grid=(n,),
        out_shape=(
            jax.ShapeDtypeStruct((n * slots, PAIR), LOW),
            jax.ShapeDtypeStruct((8, n * slots), WIDE),
        ),
        in_specs=[
            pl.BlockSpec((1, span), lambda t: (0, 0)),
            pl.BlockSpec((slots, PAIR), lambda t: (t, pair)),
            whole(pairs + pair),
            whole(2 * pairs + pair),
        ],
        out_specs=(
            pl.BlockSpec((slots, PAIR), lambda t: (t, 0)),
            pl.BlockSpec((8, slots), lambda t: (0, t)),
        ),
        compiler_params=params(),
        cost_estimate=pl.CostEstimate(
            flops=8 * span * span * PAIR, bytes_accessed=span * PAIR * 10, transcendentals=0
        ),
    )(bias, qkv, qkv, qkv)


def attend_back(full, bias_ref, q_ref, k_ref, v_ref, do_ref, lse_ref, out_ref, dk_ref, dv_ref):
    tile = pl.program_id(0)
    slots = q_ref.shape[0]
    span = k_ref.shape[0]
    first = lax.broadcasted_iota(jnp.int32, (1, PAIR), 1) < HD
    scale = 1.0 / math.sqrt(HD)

    @pl.when(tile == 0)
    def _():
        dk_ref[...] = jnp.zeros_like(dk_ref)
        dv_ref[...] = jnp.zeros_like(dv_ref)
        out_ref[span:, :] = jnp.zeros((out_ref.shape[0] - span, 3 * PAIR), LOW)

    def work(rows):
        keys, values = k_ref[...], v_ref[...]
        outs = []
        for h in range(2):
            mine = first if h == 0 else jnp.logical_not(first)
            query = jnp.where(mine, q_ref[:rows, :], 0)
            grad = jnp.where(mine, do_ref[:rows, :], 0)
            scores = right_dot(keys, query) * (LOG2E * scale)
            bias = jnp.concatenate([bias_ref[...]] * (rows // 128), 1)
            probs = jnp.exp2(scores + bias - lse_ref[h : h + 1, :rows])
            grad_probs = right_dot(values, grad)
            center = jnp.sum(grad_probs * probs, 0, keepdims=True)
            grad_scores = (probs * (grad_probs - center)).astype(LOW)
            dk_ref[...] += dot(grad_scores, query, ((1,), (0,)))
            dv_ref[...] += dot(probs.astype(LOW), grad, ((1,), (0,)))
            outs.append(left_dot(grad_scores, keys))
        start = pl.multiple_of(tile * slots, slots)
        out_ref[pl.ds(start, rows), :PAIR] = (jnp.where(first, outs[0], outs[1]) * scale).astype(LOW)

    @pl.when(tile < full)
    def _():
        work(slots)

    @pl.when(tile == full)
    def _():
        work(TAIL)
        out_ref[:span, PAIR : 2 * PAIR] = (dk_ref[...] * scale).astype(LOW)
        out_ref[:span, 2 * PAIR :] = dv_ref[...].astype(LOW)


def attention_back(qkv, bias, grad, lse, pair, pairs, n, slots):
    span = qkv.shape[0]
    whole = lambda col: pl.BlockSpec((span, PAIR), lambda t: (0, col))
    return pl.pallas_call(
        functools.partial(attend_back, n - 1),
        grid=(n,),
        out_shape=jax.ShapeDtypeStruct((n * slots, 3 * PAIR), LOW),
        in_specs=[
            pl.BlockSpec((span, 128), lambda t: (0, 0)),
            pl.BlockSpec((slots, PAIR), lambda t: (t, pair)),
            whole(pairs + pair),
            whole(2 * pairs + pair),
            pl.BlockSpec((slots, PAIR), lambda t: (t, pair)),
            pl.BlockSpec((8, slots), lambda t: (0, t)),
        ],
        out_specs=pl.BlockSpec((n * slots, 3 * PAIR), lambda t: (0, 0)),
        scratch_shapes=[pltpu.VMEM((span, PAIR), WIDE), pltpu.VMEM((span, PAIR), WIDE)],
        compiler_params=params(),
        cost_estimate=pl.CostEstimate(
            flops=20 * span * span * PAIR, bytes_accessed=span * PAIR * 20, transcendentals=0
        ),
    )(bias, qkv, qkv, qkv, grad, lse)


def per_device(
    hidden_in,
    cotangent,
    context_len,
    block_device,
    timestep,
    query_weight,
    key_weight,
    value_weight,
    output_weight,
    inner_weight,
    outer_weight,
    query_bias,
    value_bias,
    output_bias,
    inner_bias,
    outer_bias,
    attn_gain,
    attn_shift,
    ffn_gain,
    ffn_shift,
    time_table,
):
    n = lax.axis_size("ctx")
    place = lax.axis_index("ctx")
    dp_index = lax.axis_index("dp")
    d = dp_index % GROUP
    ids = jnp.stack([place, d]).astype(jnp.int32)
    rows, slots, width = hidden_in.shape
    own_cols = width // n
    pairs = own_cols // PAIR
    span = (n - 1) * slots + TAIL
    holder = block_device[0]
    context = context_len[0]

    order = [j + (j >= holder).astype(jnp.int32) for j in range(n - 1)] + [holder]
    steps = [(place - g + n) % n for g in order]
    position = lambda g: jnp.where(g == holder, n - 1, g - (g > holder).astype(jnp.int32))
    counts = [context // (n - 1) + (j < context % (n - 1)).astype(jnp.int32) for j in range(n - 1)]
    counts = jnp.stack(counts + [jnp.int32(BLOCK)])
    slot = jnp.arange(slots, dtype=jnp.int32)
    live = (slot[None, :] < counts[:, None]).reshape(n * slots)[:span]
    bias = jnp.where(live, 0.0, -1e30).astype(WIDE)
    bias_row, bias_col = bias[None, :], jnp.broadcast_to(bias[:, None], (span, 128))
    owned = take(counts, position(place))
    valid = (slot < owned).astype(WIDE)[:, None]
    block = ((holder == place) & (slot < BLOCK)).astype(WIDE)[:, None]
    embed = lax.dynamic_slice_in_dim(time_table, timestep[0], 1, 0).astype(WIDE)
    start = hidden_in[0].astype(WIDE) + block * embed
    start_low = start.astype(LOW)

    qkv_weight = jnp.concatenate([query_weight, key_weight, value_weight], 1)
    qkv_own = gather_columns(ids, qkv_weight, d, place, n)
    parts = jnp.stack([start_low] + [turn(start_low, k) for k in range(1, n)])
    compact = jnp.concatenate([take(parts, k) for k in steps])
    output_full = gather_weight(ids, output_weight, d, n)
    inner_full = gather_weight(ids, inner_weight, d, n)
    outer_full = gather_weight(ids, outer_weight, d, n)
    qkv_full = gather_weight(ids, qkv_weight, d, n)

    own_bias = lambda v: lax.dynamic_slice_in_dim(v, place * own_cols, own_cols, 0).astype(WIDE)
    qkv_bias = jnp.concatenate(
        [own_bias(query_bias), jnp.zeros((own_cols,), WIDE), own_bias(value_bias)]
    )
    qkv = (jnp.dot(compact[:span], qkv_own, preferred_element_type=WIDE) + qkv_bias).astype(LOW)

    to_group = lambda v, g: lax.dynamic_slice_in_dim(v, position(g % n) * slots, slots, 0)

    def by_group(parts):
        turned = jnp.stack([parts[-k % n] for k in range(n)] * 2)
        return lax.dynamic_slice_in_dim(turned, (n - place) % n, n, 0)

    mixed, lses = [], []
    for pair in range(pairs):
        out, lse = attention(qkv, bias_row, pair, pairs, n, slots)
        lses.append(lse)
        mixed.append(
            by_group([to_group(out, place)] + [turn(to_group(out, place + k), k) for k in range(1, n)])
        )
    attn = jnp.stack(mixed).transpose(2, 1, 0, 3).reshape(slots, width)

    first = (
        jnp.dot(attn, output_full, preferred_element_type=WIDE) + output_bias.astype(WIDE) + start
    )
    normed, norm_pull = jax.vjp(layer_norm, first, attn_gain.astype(WIDE), attn_shift.astype(WIDE))
    normed_low = normed.astype(LOW)
    inner = jnp.dot(normed_low, inner_full, preferred_element_type=WIDE) + inner_bias.astype(WIDE)
    active, gelu_pull = jax.vjp(jax.nn.gelu, inner)
    active_low = active.astype(LOW)
    second = (
        jnp.dot(active_low, outer_full, preferred_element_type=WIDE)
        + outer_bias.astype(WIDE)
        + normed
    )
    result, final_pull = jax.vjp(layer_norm, second, ffn_gain.astype(WIDE), ffn_shift.astype(WIDE))
    hidden_out = (result * valid).astype(LOW)[None]
    incoming = cotangent[0].astype(WIDE) * valid
    grad_second, ffn_gain_grad, ffn_shift_grad = final_pull(incoming)
    outer_bias_grad = jnp.sum(grad_second, 0)
    second_low = grad_second.astype(LOW)
    outer_weight_grad = share_grad(ids, left_dot(active_low, second_low, LOW), d, place, n)
    (grad_inner,) = gelu_pull(right_dot(second_low, outer_full))
    inner_low = grad_inner.astype(LOW)
    inner_bias_grad = jnp.sum(inner_low.astype(WIDE), 0)
    inner_weight_grad = share_grad(ids, left_dot(normed_low, inner_low, LOW), d, place, n)
    grad_normed = right_dot(inner_low, inner_full) + grad_second
    grad_first, attn_gain_grad, attn_shift_grad = norm_pull(grad_normed)
    output_bias_grad = jnp.sum(grad_first, 0)
    first_low = grad_first.astype(LOW)
    output_weight_grad = share_grad(ids, left_dot(attn, first_low, LOW), d, place, n)
    grad_attn = right_dot(first_low, output_full).astype(LOW)

    columns = lambda v, g: lax.dynamic_slice_in_dim(v, (g % n) * own_cols, own_cols, 1)
    parts = jnp.stack(
        [columns(grad_attn, place)]
        + [turn(columns(grad_attn, place + k), k) for k in range(1, n)]
    )
    grad_mixed = jnp.concatenate([take(parts, k) for k in steps])
    backs, received = [], []
    for pair in range(pairs):
        back = attention_back(qkv, bias_col, grad_mixed, lses[pair], pair, pairs, n, slots)
        backs.append(back)
        received.append(
            by_group([to_group(back, place)] + [turn(to_group(back, place + k), k) for k in range(1, n)])
        )
    grad_qkv = jnp.stack(received).reshape(pairs, n, slots, 3, PAIR)
    grad_qkv = grad_qkv.transpose(2, 3, 1, 0, 4).reshape(slots, 3 * width)
    grad_start = right_dot(grad_qkv, qkv_full) + grad_first
    grad_hidden = grad_start[None]

    back = jnp.stack(backs).reshape(pairs, n * slots, 3, PAIR)
    back = back.transpose(1, 2, 0, 3).reshape(n * slots, 3 * own_cols)
    bias_sums = jnp.sum(back.astype(WIDE), 0)
    own_grad = left_dot(compact, back, LOW)
    part = width // (n * GROUP * 2)
    one, two = plane_reduce(own_grad.reshape(n, 2, 2, 2, 2, part, 3 * own_cols), d)
    both = jnp.stack([one, two], 1)
    got = [take(both, place)] + [turn(take(both, (place + k) % n), k) for k in range(1, n)]
    got = by_group(got).reshape(n, 2, part, 3, own_cols)
    got = got.transpose(1, 2, 3, 0, 4).reshape(2, part, 3 * width)
    qkv_grad = spread_grad(ids, got)
    weight_grads = [qkv_grad[:, i * width : (i + 1) * width] for i in range(3)]

    small = [
        output_bias_grad,
        inner_bias_grad,
        outer_bias_grad,
        attn_gain_grad,
        attn_shift_grad,
        ffn_gain_grad,
        ffn_shift_grad,
    ]
    packed = jnp.concatenate([v.reshape(n, -1) for v in small], 1)
    total = take(packed, place)
    for k in range(1, n):
        total = total + turn(take(packed, (place + k) % n), k)
    total = jnp.concatenate([total, bias_sums])
    mask = 1
    while mask < lax.axis_size("dp"):
        total = total + swap(total, mask)
        mask *= 2
    sums, at = [], 0
    for v in small:
        sums.append(total[at : at + v.shape[0] // n])
        at += v.shape[0] // n
    query_sum, value_sum = total[at : at + own_cols], total[at + 2 * own_cols : at + 3 * own_cols]

    block_sums = lax.psum(jnp.sum(grad_start * block, 0), "ctx")
    all_sums = lax.all_gather(block_sums, "dp")
    all_steps = lax.all_gather(timestep, "dp", tiled=True)
    levels = jnp.arange(time_table.shape[0] // n, dtype=jnp.int32) + place * (
        time_table.shape[0] // n
    )
    onehot = (all_steps[:, None] == levels[None, :]).astype(WIDE)
    time_table_grad = lax.dot_general(
        onehot,
        all_sums,
        (((0,), (0,)), ((), ())),
        precision=lax.Precision.HIGHEST,
        preferred_element_type=WIDE,
    )
    return (
        hidden_out,
        grad_hidden,
        *weight_grads,
        output_weight_grad,
        inner_weight_grad,
        outer_weight_grad,
        query_sum,
        value_sum,
        *sums,
        time_table_grad,
    )


def solution(mesh):
    row, shard, same = P("dp", "ctx", None), P("ctx", None), P()
    return jax.shard_map(
        per_device,
        mesh=mesh,
        in_specs=(row, row, P("dp"), P("dp"), P("dp")) + (shard,) * 6 + (same,) * 10,
        out_specs=(row, row) + (shard,) * 6 + (P("ctx"),) * 9 + (shard,),
        check_vma=False,
    )
```

time: 2210 us -> 864 us (0.39)
  waiting for transfers between devices: 1740 us -> 331 us
  matrix products: 316 us -> 72.5 us
  starting transfers between devices: 1.71 us -> 168 us
  Pallas kernels: 0 us -> 89.7 us
  local copies, waits for them, and re-layouts: 40.5 us -> 123 us
    reduce_scatter x9 -> x0, waiting for transfers between devices: 1090 us -> none  [the longest x1 283 us: per_device(): lax.psum_scatter(grads[5], 'ctx', scatter_dimension=0, tiled=True)]
    all_gather x8 -> x0, waiting for transfers between devices: 501 us -> none  [the longest x1 141 us: per_device(): lax.all_gather(outer_weight, 'ctx', axis=0, tiled=True)]
    ppermute x0 -> x190, waiting for transfers between devices: none -> 331 us  [the longest x48 186 us: turn(): lax.ppermute(value, 'ctx', [(i, (i + k) % size) for i in range(size)])]
    dot_general x131 -> x13, matrix products: 316 us -> 72.5 us  [the longest x8 47.4 us: dot(): lax.dot_general(left, right, (dims, ((), ())), preferred_element_type=out)]
    ppermute x0 -> x190, starting transfers between devices: none -> 168 us  [the longest x142 98.2 us: swap(): return lax.ppermute(value, 'dp', [(i, i ^ mask) for i in range(size)])]
    psum x1 -> x0, waiting for transfers between devices: 138 us -> none  [per_device(): lax.psum((partial_shares[0], partial_shares[1], partial_shares[2], partia...]
    pallas_call x0 -> x13, Pallas kernels: none -> 89.7 us  [the longest x5 38 us: whole_weight(): pl.pallas_call(body, out_shape=jax.ShapeDtypeStruct((n * rows, cols), own...]
    unnamed x81 -> x341, local copies, waits for them, and re-layouts: 20.5 us -> 48.2 us
  transfers between devices with their start and end apart: 18 -> 190, of which waited for: 17 -> 55; matrix products, arithmetic and copies ran while one was open for 7% -> 18% of each run, Pallas kernels for 0% -> 9%
where the time goes in v1:
time: 864 us; the launch traced here: 855 us
  waiting for transfers between devices  331 us (38%)
  starting transfers between devices  168 us (19%)
  local copies, waits for them, and re-layouts  123 us (14%)
  Pallas kernels  89.7 us (10%)
  matrix products  72.5 us (8%)
  other arithmetic  39.1 us (5%)
  blocking collectives  25.3 us (3%)
    ppermute x48, waiting for transfers between devices, turn(): lax.ppermute(value, 'ctx', [(i, (i + k) % size) for i in range(size)])  186 us
    ppermute x142, waiting for transfers between devices, swap(): return lax.ppermute(value, 'dp', [(i, i ^ mask) for i in range(size)])  146 us
    ppermute x142, starting transfers between devices, swap(): return lax.ppermute(value, 'dp', [(i, i ^ mask) for i in range(size)])  98.2 us
    ppermute x48, starting transfers between devices, turn(): lax.ppermute(value, 'ctx', [(i, (i + k) % size) for i in range(size)])  69.8 us
    unnamed x341, local copies, waits for them, and re-layouts  48.2 us
    dot_general x8, matrix products, dot(): lax.dot_general(left, right, (dims, ((), ())), preferred_element_type=out)  47.4 us
    pallas_call x5, Pallas kernels, whole_weight(): pl.pallas_call(body, out_shape=jax.ShapeDtypeStruct((n * rows, cols), own...  38 us
    pallas_call x2, Pallas kernels, attention_back(): pl.pallas_call(functools.partial(attend_back, n - 1), grid=(n,), out_shap...  26.6 us
  transfers between devices with their start and end apart: 190, of which 55 were waited for; matrix products, arithmetic and copies ran while one was open for 18% of the time, Pallas kernels for 9%

profile of v1, /device:TPU:0, one launch (start us, length us, event | category | flops | bytes accessed | tf_op | source)
XLA Modules:
  0.0 854.6 jit_solution(17087140005419015918)
XLA Ops:
  1.6 5.0 collective-permute-start.21
  14.2 2.9 collective-permute-start.5
  31.4 3.8 collective-permute-start.81
  44.2 8.0 all-reduce
  63.0 2.9 collective-permute-start.38
  66.0 4.1 collective-permute-done.9.refs_4_
  79.7 3.3 collective-permute-start.55
  83.5 7.1 collective-permute-done.37
  91.3 4.6 collective-permute-start.2
  103.8 80.3 %collective-permute-done.54 = bf16[128,1024]{1,0:T(8,128)(2,1)S(1)} collective-permute-done((bf16[128,1024]{1,0:T(8,128)(2,1)S(1)}, bf16[128,1024]{1,0:T(8,128)(2,1)S(1)}, u32[]{:S(2)}, u32[]{:S(2)}) %collective-permute-start.54) | collective-permute-done | bytes 262176 | tf_op jit(solution)/shard_map/ppermute | solution.py:55
  185.7 3.0 collective-permute-done.32.refs_12_
  191.7 3.7 shard_map.343
  201.1 8.5 shard_map.342
  209.7 8.5 shard_map.341
  220.4 4.7 copy.133
  227.0 7.1 collective-permute-done.17
  234.8 6.0 collective-permute-done.18
  257.0 5.7 collective-permute-done.14
  266.1 3.2 collective-permute-done.15
  271.9 3.3 collective-permute-done.41.refs_4_
  275.4 6.9 collective-permute-done.42.refs_5_
  298.0 2.9 collective-permute-done.49.refs_12_
  311.1 8.5 shard_map.348
  319.7 8.9 %shard_map.344 = bf16[1024,4096]{1,0:T(8,128)(2,1)} custom-call(s32[2]{0:T(128)S(1)} %pad_add_fusion.1.ids_ref, bf16[256,4096]{1,0:T(8,128)(2,1)} %own_ref.4, bf16[3,16,4096]{2,1,0:T(8,128)(2,1)S(1)} %copy-done, bf16[3,16,4096]{2,1,0:T(8,128)(2,1)S(1)} %get-tuple-element.87.refs_1_, bf16[3,16,4096]{2,1,0:T(8,128)(2,1)S(1)} %copy-done.15, ...), custom_call_target="tpu_custom_call" | custom-call | bytes 16777216 | tf_op jit(solution)/shard_map/pallas_call | solution.py:117
  329.9 8.9 %convolution_add_fusion = f32[384,4096]{1,0:T(8,128)} fusion(bf16[1024,4096]{1,0:T(8,128)(2,1)} %shard_map.344, f32[4096]{0:T(1024)S(1)} %copy-done.126, f32[384,1024]{1,0:T(8,128)S(1)} %get-tuple-element.127, f32[1024]{0:T(1024)S(1)} %copy-done.132, f32[1024]{0:T(1024)S(1)} %copy-done.127, f32[384]{0:T(512)S(1)} %fusion.106, ...), kind=kOutput, calls=%fused_computation.15 | convolution fusion | flops 3224764416 | bytes 16280576 | tf_op jit(solution)/shard_map/dot_general | solution.py:405
  339.6 14.2 %shard_map.345 = bf16[4096,1024]{1,0:T(8,128)(2,1)} custom-call(s32[2]{0:T(128)S(1)} %pad_add_fusion.1.ids_ref, bf16[1024,1024]{1,0:T(8,128)(2,1)} %own_ref.5, bf16[3,64,1024]{2,1,0:T(8,128)(2,1)S(1)} %get-tuple-element.90.refs_0_, bf16[3,64,1024]{2,1,0:T(8,128)(2,1)S(1)} %get-tuple-element.89.refs_1_, bf16[3,64,1024]{2,1,0:T(8,128)(2,1)S(1)} %copy-done.7, ...), custom_call_target="tpu_custom_call" | custom-call | bytes 16777216 | tf_op jit(solution)/shard_map/pallas_call | solution.py:117
  353.8 9.4 %fusion.129 = (f32[384]{0:T(512)S(1)}, f32[384,1024]{1,0:T(8,128)S(1)}) fusion(f32[1024]{0:T(1024)S(1)} %copy-done.132, f32[1024]{0:T(1024)S(1)} %copy-done.127, f32[384]{0:T(512)S(1)} %fusion.106, f32[384,1024]{1,0:T(8,128)S(1)} %get-tuple-element.127, f32[384]{0:T(512)S(1)} %broadcast_multiply_fusion.1, f32[1024]{0:T(1024)S(1)} %copy-done.133, ...), kind=kOutput, calls=%fused_computation.372 | convolution fusion | flops 3238133248 | bytes 17842688 | tf_op jit(solution)/shard_map/dot_general | solution.py:409
  366.8 10.6 %convert_reduce_fusion = (f32[4096]{0:T(1024)S(1)}, bf16[384,4096]{1,0:T(8,128)(2,1)S(1)}) fusion(f32[384,4096]{1,0:T(8,128)} %convolution_add_fusion, bf16[4096,1024]{1,0:T(8,128)(2,1)} %shard_map.345, f32[384,1024]{1,0:T(8,128)S(1)} %get-tuple-element.42, f32[384]{0:T(512)S(1)} %negate_multiply_fusion.1), kind=kOutput, calls=%fused_computation.13 | convolution fusion | flops 3256610816 | bytes 19416576 | tf_op jit(solution)/shard_map/dot_general | solution.py:37
  377.4 3.9 multiply_reduce_fusion.1
  381.3 7.3 fusion.111
  388.7 11.1 %fusion.109 = bf16[4096,1024]{1,0:T(8,128)(2,1)} fusion(f32[384,1024]{1,0:T(8,128)S(1)} %get-tuple-element.42, f32[384]{0:T(512)S(1)} %negate_multiply_fusion.1, f32[384,4096]{1,0:T(8,128)} %convolution_add_fusion), kind=kOutput, calls=%fused_computation.354 | convolution fusion | flops 3236167680 | bytes 16254464 | tf_op jit(solution)/shard_map/dot_general | solution.py:37
  402.6 2.8 collective-permute-start.72
  406.8 8.1 constant_dynamic-slice_fusion.7
  414.9 4.4 constant_dynamic-slice_fusion.5
  434.6 6.8 collective-permute-done.70
  444.3 13.5 %shard_map.347 = bf16[1536,384]{1,0:T(8,128)(2,1)S(1)} custom-call(f32[1280,128]{1,0:T(8,128)S(1)} %broadcast_in_dim.31.bias_ref, bf16[1280,768]{1,0:T(8,128)(2,1)S(1)} %copy-done.91, bf16[1280,768]{1,0:T(8,128)(2,1)S(1)} %copy-done.91, bf16[1280,768]{1,0:T(8,128)(2,1)S(1)} %copy-done.91, bf16[1536,256]{1,0:T(8,128)(2,1)S(1)} %pad_maximum_fusion.5.do_ref, ...), custom_call_target="tpu_custom_call" | custom-call | flops 4194304000 | bytes 3276800 | tf_op jit(solution)/shard_map/pallas_call | solution.py:298
  463.7 13.1 %shard_map.346 = bf16[1536,384]{1,0:T(8,128)(2,1)S(1)} custom-call(f32[1280,128]{1,0:T(8,128)S(1)} %copy-done.3, bf16[1280,768]{1,0:T(8,128)(2,1)S(1)} %copy-done.92, bf16[1280,768]{1,0:T(8,128)(2,1)S(1)} %copy-done.92, bf16[1280,768]{1,0:T(8,128)(2,1)S(1)} %copy-done.92, bf16[1536,256]{1,0:T(8,128)(2,1)S(1)} %pad_maximum_fusion.5.do_ref, ...), custom_call_target="tpu_custom_call" | custom-call | flops 4194304000 | bytes 3276800 | tf_op jit(solution)/shard_map/pallas_call | solution.py:298
  479.3 3.0 maximum_bitcast_fusion.1
  483.6 7.0 copy.136
  490.6 6.4 reshape.395
  497.2 5.4 fusion.10
  513.1 18.5 %collective-permute-done.77 = bf16[384,384]{1,0:T(8,128)(2,1)S(1)} collective-permute-done((bf16[384,384]{1,0:T(8,128)(2,1)S(1)}, bf16[384,384]{1,0:T(8,128)(2,1)S(1)}, u32[]{:S(2)}, u32[]{:S(2)}) %collective-permute-start.77) | collective-permute-done | bytes 294944 | tf_op jit(solution)/shard_map/ppermute | solution.py:55
  531.8 7.7 collective-permute-done.73
  539.5 12.7 %collective-permute-start.75 = (bf16[384,384]{1,0:T(8,128)(2,1)S(1)}, bf16[384,384]{1,0:T(8,128)(2,1)S(1)}, u32[]{:S(2)}, u32[]{:S(2)}) collective-permute-start(bf16[384,384]{1,0:T(8,128)(2,1)S(1)} %copy-done.115), channel_id=1, source_target_pairs={{0,1},{1,2},{2,3},{3,0},{4,5},{5,6},{6,7},{7,4},{8,9},{9,10},{10,1... | collective-permute-start | bytes 884744 | tf_op jit(solution)/shard_map/ppermute | solution.py:55
  553.0 3.1 collective-permute-done.74
  574.3 7.0 collective-permute-done.98
  582.8 3.2 collective-permute-done.100
  601.3 3.1 collective-permute-done.124
  605.9 5.0 fusion.1
  613.1 4.3 fusion
  619.9 17.7 %collective-permute-done.141 = bf16[4,2,16,4096]{3,2,0,1:T(8,128)(2,1)S(1)} collective-permute-done((bf16[4,2,16,4096]{3,2,0,1:T(8,128)(2,1)S(1)}, bf16[4,2,16,4096]{3,2,0,1:T(8,128)(2,1)S(1)}, u32[]{:S(2)}, u32[]{:S(2)}) %collective-permute-start.141) | collective-permute-done | bytes 1048608 | tf_op jit(solution)/shard_map/ppermute | solution.py:50
  639.6 20.1 %collective-permute-done.163 = bf16[4,2,64,1024]{3,2,0,1:T(8,128)(2,1)S(1)} collective-permute-done((bf16[4,2,64,1024]{3,2,0,1:T(8,128)(2,1)S(1)}, bf16[4,2,64,1024]{3,2,0,1:T(8,128)(2,1)S(1)}, u32[]{:S(2)}, u32[]{:S(2)}) %collective-permute-start.163) | collective-permute-done | bytes 1048608 | tf_op jit(solution)/shard_map/ppermute | solution.py:50
  663.7 20.7 %collective-permute-done.165 = bf16[4,2,64,1024]{3,2,0,1:T(8,128)(2,1)S(1)} collective-permute-done((bf16[4,2,64,1024]{3,2,0,1:T(8,128)(2,1)S(1)}, bf16[4,2,64,1024]{3,2,0,1:T(8,128)(2,1)S(1)}, u32[]{:S(2)}, u32[]{:S(2)}) %collective-permute-start.165) | collective-permute-done | bytes 1048608 | tf_op jit(solution)/shard_map/ppermute | solution.py:50
  686.7 10.4 %collective-permute-done.142 = bf16[4,16,4096]{2,1,0:T(8,128)(2,1)S(1)} collective-permute-done((bf16[4,16,4096]{2,1,0:T(8,128)(2,1)S(1)}, bf16[4,16,4096]{2,1,0:T(8,128)(2,1)S(1)}, u32[]{:S(2)}, u32[]{:S(2)}) %collective-permute-start.142) | collective-permute-done | bytes 524320 | tf_op jit(solution)/shard_map/ppermute | solution.py:50
  698.7 10.2 %collective-permute-done.144 = bf16[4,16,4096]{2,1,0:T(8,128)(2,1)S(1)} collective-permute-done((bf16[4,16,4096]{2,1,0:T(8,128)(2,1)S(1)}, bf16[4,16,4096]{2,1,0:T(8,128)(2,1)S(1)}, u32[]{:S(2)}, u32[]{:S(2)}) %collective-permute-start.144) | collective-permute-done | bytes 524320 | tf_op jit(solution)/shard_map/ppermute | solution.py:50
  714.4 8.4 collective-permute-done.110.refs_8_
  737.3 13.4 %collective-permute-done.146 = bf16[2,16,4096]{2,1,0:T(8,128)(2,1)S(1)} collective-permute-done((bf16[2,16,4096]{2,1,0:T(8,128)(2,1)S(1)}, bf16[2,16,4096]{2,1,0:T(8,128)(2,1)S(1)}, u32[]{:S(2)}, u32[]{:S(2)}) %collective-permute-start.146) | collective-permute-done | bytes 262176 | tf_op jit(solution)/shard_map/ppermute | solution.py:55
  759.1 4.1 collective-permute-done.169
  763.2 16.3 %collective-permute-done.168 = bf16[2,64,1024]{2,1,0:T(8,128)(2,1)S(1)} collective-permute-done((bf16[2,64,1024]{2,1,0:T(8,128)(2,1)S(1)}, bf16[2,64,1024]{2,1,0:T(8,128)(2,1)S(1)}, u32[]{:S(2)}, u32[]{:S(2)}) %collective-permute-start.168) | collective-permute-done | bytes 262176 | tf_op jit(solution)/shard_map/ppermute | solution.py:55
  803.5 6.8 multiply_reduce_fusion
  810.3 8.3 psum.7
  818.7 8.9 %all-gather = f32[8,1,1024]{2,1,0:T(1,128)S(1)} all-gather(f32[1,1,1024]{2,1,0:T(1,128)S(1)} %bitcast.442), channel_id=1, replica_groups=mesh['dp'=8,'ctx'=4] {'dp'}, dimensions={0}, use_global_device_ids=true | all-gather | bytes 36864 | tf_op jit(solution)/shard_map/all_gather | solution.py:487
  848.5 2.8 shard_map.351
  851.4 2.8 shard_map.352
  (863 shorter events, 294.2 us)
Async XLA Ops:
  1.6 29.8 %collective-permute-start.21 = (bf16[32,1024]{1,0:T(8,128)(2,1)S(1)}, bf16[32,1024]{1,0:T(8,128)(2,1)S(1)}, u32[]{:S(2)}, u32[]{:S(2)}) collective-permute-start(bf16[32,1024]{1,0:T(8,128)(2,1)S(1)} %constant_dynamic-slice_fusion.27), channel_id=1, source_target_pairs={{0,3},{1,0},{2,1},{3,2},{4,7},{5,4},{6,5},{7,6},{8,11},{9,8},{10,9... | collective-permute-start | bytes 196616 | tf_op jit(solution)/shard_map/ppermute | solution.py:55
  6.6 24.8 %collective-permute-start.20 = (bf16[32,1024]{1,0:T(8,128)(2,1)S(1)}, bf16[32,1024]{1,0:T(8,128)(2,1)S(1)}, u32[]{:S(2)}, u32[]{:S(2)}) collective-permute-start(bf16[32,1024]{1,0:T(8,128)(2,1)S(1)} %constant_dynamic-slice_fusion.27), channel_id=1, source_target_pairs={{0,2},{1,3},{2,0},{3,1},{4,6},{5,7},{6,4},{7,5},{8,10},{9,11},{10,... | collective-permute-start | bytes 196616 | tf_op jit(solution)/shard_map/ppermute | solution.py:55
  6.6 28.6 %collective-permute-start.19 = (bf16[32,1024]{1,0:T(8,128)(2,1)S(1)}, bf16[32,1024]{1,0:T(8,128)(2,1)S(1)}, u32[]{:S(2)}, u32[]{:S(2)}) collective-permute-start(bf16[32,1024]{1,0:T(8,128)(2,1)S(1)} %constant_dynamic-slice_fusion.27), channel_id=1, source_target_pairs={{0,1},{1,2},{2,3},{3,0},{4,5},{5,6},{6,7},{7,4},{8,9},{9,10},{10,1... | collective-permute-start | bytes 196616 | tf_op jit(solution)/shard_map/ppermute | solution.py:55
  14.2 21.2 %collective-permute-start.5 = (bf16[32,768]{1,0:T(8,128)(2,1)S(1)}, bf16[32,768]{1,0:T(8,128)(2,1)S(1)}, u32[]{:S(2)}, u32[]{:S(2)}) collective-permute-start(bf16[32,768]{1,0:T(8,128)(2,1)S(1)} %bitcast.439), channel_id=1, source_target_pairs={{0,3},{1,0},{2,1},{3,2},{4,7},{5,4},{6,5},{7,6},{8,11},{9,8},{10,9... | collective-permute-start | bytes 147464 | tf_op jit(solution)/shard_map/ppermute | solution.py:55
  17.0 19.8 %collective-permute-start.4 = (bf16[32,768]{1,0:T(8,128)(2,1)S(1)}, bf16[32,768]{1,0:T(8,128)(2,1)S(1)}, u32[]{:S(2)}, u32[]{:S(2)}) collective-permute-start(bf16[32,768]{1,0:T(8,128)(2,1)S(1)} %bitcast.438), channel_id=1, source_target_pairs={{0,2},{1,3},{2,0},{3,1},{4,6},{5,7},{6,4},{7,5},{8,10},{9,11},{10,... | collective-permute-start | bytes 147464 | tf_op jit(solution)/shard_map/ppermute | solution.py:55
  31.4 26.2 %collective-permute-start.81 = (bf16[32,3072]{1,0:T(8,128)(2,1)}, bf16[32,3072]{1,0:T(8,128)(2,1)S(1)}, u32[]{:S(2)}, u32[]{:S(2)}) collective-permute-start(bf16[32,3072]{1,0:T(8,128)(2,1)} %constant_dynamic-slice_fusion.13), channel_id=1, source_target_pairs={{0,3},{1,0},{2,1},{3,2},{4,7},{5,4},{6,5},{7,6},{8,11},{9,8},{10,9... | collective-permute-start | bytes 589832 | tf_op jit(solution)/shard_map/ppermute | solution.py:55
  39.6 20.2 %collective-permute-start.80 = (bf16[32,3072]{1,0:T(8,128)(2,1)}, bf16[32,3072]{1,0:T(8,128)(2,1)S(1)}, u32[]{:S(2)}, u32[]{:S(2)}) collective-permute-start(bf16[32,3072]{1,0:T(8,128)(2,1)} %constant_dynamic-slice_fusion.13), channel_id=1, source_target_pairs={{0,2},{1,3},{2,0},{3,1},{4,6},{5,7},{6,4},{7,5},{8,10},{9,11},{10,... | collective-permute-start | bytes 589832 | tf_op jit(solution)/shard_map/ppermute | solution.py:55
  41.5 19.0 %collective-permute-start.79 = (bf16[32,3072]{1,0:T(8,128)(2,1)}, bf16[32,3072]{1,0:T(8,128)(2,1)}, u32[]{:S(2)}, u32[]{:S(2)}) collective-permute-start(bf16[32,3072]{1,0:T(8,128)(2,1)} %constant_dynamic-slice_fusion.13), channel_id=1, source_target_pairs={{0,1},{1,2},{2,3},{3,0},{4,5},{5,6},{6,7},{7,4},{8,9},{9,10},{10,1... | collective-permute-start | bytes 589832 | tf_op jit(solution)/shard_map/ppermute | solution.py:55
  63.0 20.0 %collective-permute-start.38 = (bf16[32,4096]{1,0:T(8,128)(2,1)S(1)}, bf16[32,4096]{1,0:T(8,128)(2,1)S(1)}, u32[]{:S(2)}, u32[]{:S(2)}) collective-permute-start(bf16[32,4096]{1,0:T(8,128)(2,1)S(1)} %constant_dynamic-slice_fusion.26), channel_id=1, source_target_pairs={{0,3},{1,0},{2,1},{3,2},{4,7},{5,4},{6,5},{7,6},{8,11},{9,8},{10,9... | collective-permute-start | bytes 786440 | tf_op jit(solution)/shard_map/ppermute | solution.py:55
  70.0 20.6 %collective-permute-start.37 = (bf16[32,4096]{1,0:T(8,128)(2,1)S(1)}, bf16[32,4096]{1,0:T(8,128)(2,1)S(1)}, u32[]{:S(2)}, u32[]{:S(2)}) collective-permute-start(bf16[32,4096]{1,0:T(8,128)(2,1)S(1)} %constant_dynamic-slice_fusion.26), channel_id=1, source_target_pairs={{0,2},{1,3},{2,0},{3,1},{4,6},{5,7},{6,4},{7,5},{8,10},{9,11},{10,... | collective-permute-start | bytes 786440 | tf_op jit(solution)/shard_map/ppermute | solution.py:55
  73.4 17.2 %collective-permute-start.36 = (bf16[32,4096]{1,0:T(8,128)(2,1)S(1)}, bf16[32,4096]{1,0:T(8,128)(2,1)S(1)}, u32[]{:S(2)}, u32[]{:S(2)}) collective-permute-start(bf16[32,4096]{1,0:T(8,128)(2,1)S(1)} %constant_dynamic-slice_fusion.26), channel_id=1, source_target_pairs={{0,1},{1,2},{2,3},{3,0},{4,5},{5,6},{6,7},{7,4},{8,9},{9,10},{10,1... | collective-permute-start | bytes 786440 | tf_op jit(solution)/shard_map/ppermute | solution.py:55
  79.7 20.7 %collective-permute-start.55 = (bf16[128,1024]{1,0:T(8,128)(2,1)S(1)}, bf16[128,1024]{1,0:T(8,128)(2,1)S(1)}, u32[]{:S(2)}, u32[]{:S(2)}) collective-permute-start(bf16[128,1024]{1,0:T(8,128)(2,1)S(1)} %constant_dynamic-slice_fusion.25), channel_id=1, source_target_pairs={{0,3},{1,0},{2,1},{3,2},{4,7},{5,4},{6,5},{7,6},{8,11},{9,8},{10,9... | collective-permute-start | bytes 786440 | tf_op jit(solution)/shard_map/ppermute | solution.py:55
  91.3 104.1 %collective-permute-start.2 = (bf16[384,1024]{1,0:T(8,128)(2,1)}, bf16[384,1024]{1,0:T(8,128)(2,1)S(1)}, u32[]{:S(2)}, u32[]{:S(2)}) collective-permute-start(bf16[384,1024]{1,0:T(8,128)(2,1)} %fusion.27), channel_id=1, source_target_pairs={{0,3},{1,0},{2,1},{3,2},{4,7},{5,4},{6,5},{7,6},{8,11},{9,8},{10,9... | collective-permute-start | bytes 2359304 | tf_op jit(solution)/shard_map/ppermute | solution.py:55
  95.9 99.6 %collective-permute-start.1 = (bf16[384,1024]{1,0:T(8,128)(2,1)}, bf16[384,1024]{1,0:T(8,128)(2,1)S(1)}, u32[]{:S(2)}, u32[]{:S(2)}) collective-permute-start(bf16[384,1024]{1,0:T(8,128)(2,1)} %fusion.27), channel_id=1, source_target_pairs={{0,2},{1,3},{2,0},{3,1},{4,6},{5,7},{6,4},{7,5},{8,10},{9,11},{10,... | collective-permute-start | bytes 2359304 | tf_op jit(solution)/shard_map/ppermute | solution.py:55
  98.4 97.7 %collective-permute-start = (bf16[384,1024]{1,0:T(8,128)(2,1)}, bf16[384,1024]{1,0:T(8,128)(2,1)S(1)}, u32[]{:S(2)}, u32[]{:S(2)}) collective-permute-start(bf16[384,1024]{1,0:T(8,128)(2,1)} %fusion.27), channel_id=1, source_target_pairs={{0,1},{1,2},{2,3},{3,0},{4,5},{5,6},{6,7},{7,4},{8,9},{9,10},{10,1... | collective-permute-start | bytes 2359304 | tf_op jit(solution)/shard_map/ppermute | solution.py:55
  100.4 83.8 %collective-permute-start.54 = (bf16[128,1024]{1,0:T(8,128)(2,1)S(1)}, bf16[128,1024]{1,0:T(8,128)(2,1)S(1)}, u32[]{:S(2)}, u32[]{:S(2)}) collective-permute-start(bf16[128,1024]{1,0:T(8,128)(2,1)S(1)} %constant_dynamic-slice_fusion.25), channel_id=1, source_target_pairs={{0,2},{1,3},{2,0},{3,1},{4,6},{5,7},{6,4},{7,5},{8,10},{9,11},{10,... | collective-permute-start | bytes 786440 | tf_op jit(solution)/shard_map/ppermute | solution.py:55
  100.4 83.7 %collective-permute-start.53 = (bf16[128,1024]{1,0:T(8,128)(2,1)S(1)}, bf16[128,1024]{1,0:T(8,128)(2,1)S(1)}, u32[]{:S(2)}, u32[]{:S(2)}) collective-permute-start(bf16[128,1024]{1,0:T(8,128)(2,1)S(1)} %constant_dynamic-slice_fusion.25), channel_id=1, source_target_pairs={{0,1},{1,2},{2,3},{3,0},{4,5},{5,6},{6,7},{7,4},{8,9},{9,10},{10,1... | collective-permute-start | bytes 786440 | tf_op jit(solution)/shard_map/ppermute | solution.py:55
  190.1 54.8 %collective-permute-start.82 = (bf16[3,16,3072]{2,1,0:T(8,128)(2,1)}, bf16[3,16,3072]{2,1,0:T(8,128)(2,1)}, u32[]{:S(2)}, u32[]{:S(2)}) collective-permute-start(bf16[3,16,3072]{2,1,0:T(8,128)(2,1)} %get-tuple-element.92.refs_0_), channel_id=1, source_target_pairs={{0,4},{4,0},{8,12},{12,8},{16,20},{20,16},{24,28},{28,24},{1,5},{5... | collective-permute-start | bytes 884744 | tf_op jit(solution)/shard_map/ppermute | solution.py:50
  190.2 56.3 %collective-permute-start.84 = (bf16[3,16,3072]{2,1,0:T(8,128)(2,1)}, bf16[3,16,3072]{2,1,0:T(8,128)(2,1)}, u32[]{:S(2)}, u32[]{:S(2)}) collective-permute-start(bf16[3,16,3072]{2,1,0:T(8,128)(2,1)} %get-tuple-element.92.refs_0_), channel_id=1, source_target_pairs={{0,8},{4,12},{8,0},{12,4},{16,24},{20,28},{24,16},{28,20},{1,9},{5... | collective-permute-start | bytes 884744 | tf_op jit(solution)/shard_map/ppermute | solution.py:50
  195.4 49.7 %collective-permute-start.83 = (bf16[3,16,3072]{2,1,0:T(8,128)(2,1)}, bf16[3,16,3072]{2,1,0:T(8,128)(2,1)}, u32[]{:S(2)}, u32[]{:S(2)}) collective-permute-start(bf16[3,16,3072]{2,1,0:T(8,128)(2,1)} %get-tuple-element.91.refs_1_), channel_id=1, source_target_pairs={{0,4},{4,0},{8,12},{12,8},{16,20},{20,16},{24,28},{28,24},{1,5},{5... | collective-permute-start | bytes 884744 | tf_op jit(solution)/shard_map/ppermute | solution.py:50
  195.5 51.6 %collective-permute-start.85 = (bf16[3,16,3072]{2,1,0:T(8,128)(2,1)}, bf16[3,16,3072]{2,1,0:T(8,128)(2,1)}, u32[]{:S(2)}, u32[]{:S(2)}) collective-permute-start(bf16[3,16,3072]{2,1,0:T(8,128)(2,1)} %get-tuple-element.91.refs_1_), channel_id=1, source_target_pairs={{0,8},{4,12},{8,0},{12,4},{16,24},{20,28},{24,16},{28,20},{1,9},{5... | collective-permute-start | bytes 884744 | tf_op jit(solution)/shard_map/ppermute | solution.py:50
  264.3 18.0 %collective-permute-start.42 = (bf16[3,16,4096]{2,1,0:T(8,128)(2,1)S(1)}, bf16[3,16,4096]{2,1,0:T(8,128)(2,1)}, u32[]{:S(2)}, u32[]{:S(2)}) collective-permute-start(bf16[3,16,4096]{2,1,0:T(8,128)(2,1)S(1)} %get-tuple-element.87.refs_1_), channel_id=1, source_target_pairs={{0,8},{4,12},{8,0},{12,4},{16,24},{20,28},{24,16},{28,20},{1,9},{5... | collective-permute-start | bytes 1179656 | tf_op jit(solution)/shard_map/ppermute | solution.py:50
  264.9 17.4 %collective-permute-start.45 = (bf16[3,16,4096]{2,1,0:T(8,128)(2,1)}, bf16[3,16,4096]{2,1,0:T(8,128)(2,1)}, u32[]{:S(2)}, u32[]{:S(2)}) collective-permute-start(bf16[3,16,4096]{2,1,0:T(8,128)(2,1)} %get-tuple-element.88.refs_0_), channel_id=1, source_target_pairs={{0,16},{4,20},{8,24},{12,28},{16,0},{20,4},{24,8},{28,12},{1,17},{... | collective-permute-start | bytes 1179656 | tf_op jit(solution)/shard_map/ppermute | solution.py:50
  306.5 22.2 %collective-permute-start.59 = (bf16[3,64,1024]{2,1,0:T(8,128)(2,1)S(1)}, bf16[3,64,1024]{2,1,0:T(8,128)(2,1)S(1)}, u32[]{:S(2)}, u32[]{:S(2)}) collective-permute-start(bf16[3,64,1024]{2,1,0:T(8,128)(2,1)S(1)} %get-tuple-element.89.refs_1_), channel_id=1, source_target_pairs={{0,8},{4,12},{8,0},{12,4},{16,24},{20,28},{24,16},{28,20},{1,9},{5... | collective-permute-start | bytes 1179656 | tf_op jit(solution)/shard_map/ppermute | solution.py:50
  307.1 21.6 %collective-permute-start.62 = (bf16[3,64,1024]{2,1,0:T(8,128)(2,1)S(1)}, bf16[3,64,1024]{2,1,0:T(8,128)(2,1)S(1)}, u32[]{:S(2)}, u32[]{:S(2)}) collective-permute-start(bf16[3,64,1024]{2,1,0:T(8,128)(2,1)S(1)} %get-tuple-element.90.refs_0_), channel_id=1, source_target_pairs={{0,16},{4,20},{8,24},{12,28},{16,0},{20,4},{24,8},{28,12},{1,17},{... | collective-permute-start | bytes 1179656 | tf_op jit(solution)/shard_map/ppermute | solution.py:50
  308.7 20.5 %collective-permute-start.60 = (bf16[3,64,1024]{2,1,0:T(8,128)(2,1)S(1)}, bf16[3,64,1024]{2,1,0:T(8,128)(2,1)S(1)}, u32[]{:S(2)}, u32[]{:S(2)}) collective-permute-start(bf16[3,64,1024]{2,1,0:T(8,128)(2,1)S(1)} %copy-done.11), channel_id=1, source_target_pairs={{0,4},{4,0},{8,12},{12,8},{16,20},{20,16},{24,28},{28,24},{1,5},{5... | collective-permute-start | bytes 1179656 | tf_op jit(solution)/shard_map/ppermute | solution.py:50
  308.7 20.6 %collective-permute-start.66 = (bf16[3,64,1024]{2,1,0:T(8,128)(2,1)S(1)}, bf16[3,64,1024]{2,1,0:T(8,128)(2,1)S(1)}, u32[]{:S(2)}, u32[]{:S(2)}) collective-permute-start(bf16[3,64,1024]{2,1,0:T(8,128)(2,1)S(1)} %copy-done.11), channel_id=1, source_target_pairs={{0,16},{4,20},{8,24},{12,28},{16,0},{20,4},{24,8},{28,12},{1,17},{... | collective-permute-start | bytes 1179656 | tf_op jit(solution)/shard_map/ppermute | solution.py:50
  309.2 20.5 %collective-permute-start.67 = (bf16[3,64,1024]{2,1,0:T(8,128)(2,1)S(1)}, bf16[3,64,1024]{2,1,0:T(8,128)(2,1)S(1)}, u32[]{:S(2)}, u32[]{:S(2)}) collective-permute-start(bf16[3,64,1024]{2,1,0:T(8,128)(2,1)S(1)} %copy-done.13), channel_id=1, source_target_pairs={{0,8},{4,12},{8,0},{12,4},{16,24},{20,28},{24,16},{28,20},{1,9},{5... | collective-permute-start | bytes 1179656 | tf_op jit(solution)/shard_map/ppermute | solution.py:50
  402.6 31.8 %collective-permute-start.72 = (bf16[384,256]{1,0:T(8,128)(2,1)}, bf16[384,256]{1,0:T(8,128)(2,1)}, u32[]{:S(2)}, u32[]{:S(2)}) collective-permute-start(bf16[384,256]{1,0:T(8,128)(2,1)} %get-tuple-element.84), channel_id=1, source_target_pairs={{0,3},{1,0},{2,1},{3,2},{4,7},{5,4},{6,5},{7,6},{8,11},{9,8},{10,9... | collective-permute-start | bytes 589832 | tf_op jit(solution)/shard_map/ppermute | solution.py:55
  405.4 29.2 %collective-permute-start.71 = (bf16[384,256]{1,0:T(8,128)(2,1)}, bf16[384,256]{1,0:T(8,128)(2,1)}, u32[]{:S(2)}, u32[]{:S(2)}) collective-permute-start(bf16[384,256]{1,0:T(8,128)(2,1)} %get-tuple-element.85), channel_id=1, source_target_pairs={{0,2},{1,3},{2,0},{3,1},{4,6},{5,7},{6,4},{7,5},{8,10},{9,11},{10,... | collective-permute-start | bytes 589832 | tf_op jit(solution)/shard_map/ppermute | solution.py:55
  433.9 133.3 %collective-permute-start.118 = (bf16[4,2,2,2,16,1024]{5,4,0,2,3,1:T(8,128)(2,1)}, bf16[4,2,2,2,16,1024]{5,4,0,2,3,1:T(8,128)(2,1)}, u32[]{:S(2)}, u32[]{:S(2)}) collective-permute-start(bf16[4,2,2,2,16,1024]{5,4,0,2,3,1:T(8,128)(2,1)} %bitcast.376), channel_id=1, source_target_pairs={{0,4},{4,0},{8,12},{12,8},{16,20},{20,16},{24,28},{28,24},{1,5},{5... | collective-permute-start | bytes 3145736 | tf_op jit(solution)/shard_map/ppermute | solution.py:50
  433.9 172.0 %collective-permute-start.140 = (bf16[4,2,2,2,16,4096]{5,4,0,2,3,1:T(8,128)(2,1)}, bf16[4,2,2,2,16,4096]{5,4,0,2,3,1:T(8,128)(2,1)}, u32[]{:S(2)}, u32[]{:S(2)}) collective-permute-start(bf16[4,2,2,2,16,4096]{5,4,0,2,3,1:T(8,128)(2,1)} %bitcast.375), channel_id=1, source_target_pairs={{0,4},{4,0},{8,12},{12,8},{16,20},{20,16},{24,28},{28,24},{1,5},{5... | collective-permute-start | bytes 12582920 | tf_op jit(solution)/shard_map/ppermute | solution.py:50
  434.4 178.6 %collective-permute-start.162 = (bf16[4,2,2,2,64,1024]{5,4,0,2,3,1:T(8,128)(2,1)}, bf16[4,2,2,2,64,1024]{5,4,0,2,3,1:T(8,128)(2,1)}, u32[]{:S(2)}, u32[]{:S(2)}) collective-permute-start(bf16[4,2,2,2,64,1024]{5,4,0,2,3,1:T(8,128)(2,1)} %bitcast.374), channel_id=1, source_target_pairs={{0,4},{4,0},{8,12},{12,8},{16,20},{20,16},{24,28},{28,24},{1,5},{5... | collective-permute-start | bytes 12582920 | tf_op jit(solution)/shard_map/ppermute | solution.py:50
  483.2 28.2 %collective-permute-start.76 = (bf16[384,384]{1,0:T(8,128)(2,1)}, bf16[384,384]{1,0:T(8,128)(2,1)S(1)}, u32[]{:S(2)}, u32[]{:S(2)}) collective-permute-start(bf16[384,384]{1,0:T(8,128)(2,1)} %get-tuple-element.68), channel_id=1, source_target_pairs={{0,3},{1,0},{2,1},{3,2},{4,7},{5,4},{6,5},{7,6},{8,11},{9,8},{10,9... | collective-permute-start | bytes 884744 | tf_op jit(solution)/shard_map/ppermute | solution.py:55
  510.2 21.4 %collective-permute-start.77 = (bf16[384,384]{1,0:T(8,128)(2,1)S(1)}, bf16[384,384]{1,0:T(8,128)(2,1)S(1)}, u32[]{:S(2)}, u32[]{:S(2)}) collective-permute-start(bf16[384,384]{1,0:T(8,128)(2,1)S(1)} %copy-done.119), channel_id=1, source_target_pairs={{0,2},{1,3},{2,0},{3,1},{4,6},{5,7},{6,4},{7,5},{8,10},{9,11},{10,... | collective-permute-start | bytes 884744 | tf_op jit(solution)/shard_map/ppermute | solution.py:55
  511.4 20.2 %collective-permute-start.78 = (bf16[384,384]{1,0:T(8,128)(2,1)S(1)}, bf16[384,384]{1,0:T(8,128)(2,1)S(1)}, u32[]{:S(2)}, u32[]{:S(2)}) collective-permute-start(bf16[384,384]{1,0:T(8,128)(2,1)S(1)} %copy-done.118), channel_id=1, source_target_pairs={{0,1},{1,2},{2,3},{3,0},{4,5},{5,6},{6,7},{7,4},{8,9},{9,10},{10,1... | collective-permute-start | bytes 884744 | tf_op jit(solution)/shard_map/ppermute | solution.py:55
  531.6 24.5 %collective-permute-start.74 = (bf16[384,384]{1,0:T(8,128)(2,1)S(1)}, bf16[384,384]{1,0:T(8,128)(2,1)S(1)}, u32[]{:S(2)}, u32[]{:S(2)}) collective-permute-start(bf16[384,384]{1,0:T(8,128)(2,1)S(1)} %copy-done.116), channel_id=1, source_target_pairs={{0,2},{1,3},{2,0},{3,1},{4,6},{5,7},{6,4},{7,5},{8,10},{9,11},{10,... | collective-permute-start | bytes 884744 | tf_op jit(solution)/shard_map/ppermute | solution.py:55
  539.5 17.4 %collective-permute-start.75 = (bf16[384,384]{1,0:T(8,128)(2,1)S(1)}, bf16[384,384]{1,0:T(8,128)(2,1)S(1)}, u32[]{:S(2)}, u32[]{:S(2)}) collective-permute-start(bf16[384,384]{1,0:T(8,128)(2,1)S(1)} %copy-done.115), channel_id=1, source_target_pairs={{0,1},{1,2},{2,3},{3,0},{4,5},{5,6},{6,7},{7,4},{8,9},{9,10},{10,1... | collective-permute-start | bytes 884744 | tf_op jit(solution)/shard_map/ppermute | solution.py:55
  569.0 17.1 %collective-permute-start.119 = (bf16[4,2,16,1024]{3,2,0,1:T(8,128)(2,1)S(1)}, bf16[4,2,16,1024]{3,2,0,1:T(8,128)(2,1)S(1)}, u32[]{:S(2)}, u32[]{:S(2)}) collective-permute-start(bf16[4,2,16,1024]{3,2,0,1:T(8,128)(2,1)S(1)} %dynamic-slice_bitcast_fusion.16), channel_id=1, source_target_pairs={{0,8},{4,12},{8,0},{12,4},{16,24},{20,28},{24,16},{28,20},{1,9},{5... | collective-permute-start | bytes 786440 | tf_op jit(solution)/shard_map/ppermute | solution.py:50
  601.3 109.4 %collective-permute-start.104 = (bf16[16,3072]{1,0:T(8,128)(2,1)S(1)}, bf16[16,3072]{1,0:T(8,128)(2,1)S(1)}, u32[]{:S(2)}, u32[]{:S(2)}) collective-permute-start(bf16[16,3072]{1,0:T(8,128)(2,1)S(1)} %squeeze.249.refs_0_), channel_id=1, source_target_pairs={{0,4},{4,0},{8,12},{12,8},{16,20},{20,16},{24,28},{28,24},{1,5},{5... | collective-permute-start | bytes 294920 | tf_op jit(solution)/shard_map/ppermute | solution.py:50
  604.4 108.5 %collective-permute-start.106 = (bf16[16,3072]{1,0:T(8,128)(2,1)S(1)}, bf16[16,3072]{1,0:T(8,128)(2,1)S(1)}, u32[]{:S(2)}, u32[]{:S(2)}) collective-permute-start(bf16[16,3072]{1,0:T(8,128)(2,1)S(1)} %squeeze.249.refs_0_), channel_id=1, source_target_pairs={{0,8},{4,12},{8,0},{12,4},{16,24},{20,28},{24,16},{28,20},{1,9},{5... | collective-permute-start | bytes 294920 | tf_op jit(solution)/shard_map/ppermute | solution.py:50
  605.9 105.2 %collective-permute-start.105 = (bf16[16,3072]{1,0:T(8,128)(2,1)S(1)}, bf16[16,3072]{1,0:T(8,128)(2,1)S(1)}, u32[]{:S(2)}, u32[]{:S(2)}) collective-permute-start(bf16[16,3072]{1,0:T(8,128)(2,1)S(1)} %squeeze.250.refs_1_), channel_id=1, source_target_pairs={{0,4},{4,0},{8,12},{12,8},{16,20},{20,16},{24,28},{28,24},{1,5},{5... | collective-permute-start | bytes 294920 | tf_op jit(solution)/shard_map/ppermute | solution.py:50
  611.6 26.0 %collective-permute-start.141 = (bf16[4,2,16,4096]{3,2,0,1:T(8,128)(2,1)S(1)}, bf16[4,2,16,4096]{3,2,0,1:T(8,128)(2,1)S(1)}, u32[]{:S(2)}, u32[]{:S(2)}) collective-permute-start(bf16[4,2,16,4096]{3,2,0,1:T(8,128)(2,1)S(1)} %dynamic-slice_bitcast_fusion.3), channel_id=1, source_target_pairs={{0,8},{4,12},{8,0},{12,4},{16,24},{20,28},{24,16},{28,20},{1,9},{5... | collective-permute-start | bytes 3145736 | tf_op jit(solution)/shard_map/ppermute | solution.py:50
  618.2 41.5 %collective-permute-start.163 = (bf16[4,2,64,1024]{3,2,0,1:T(8,128)(2,1)S(1)}, bf16[4,2,64,1024]{3,2,0,1:T(8,128)(2,1)S(1)}, u32[]{:S(2)}, u32[]{:S(2)}) collective-permute-start(bf16[4,2,64,1024]{3,2,0,1:T(8,128)(2,1)S(1)} %dynamic-slice_bitcast_fusion.1), channel_id=1, source_target_pairs={{0,8},{4,12},{8,0},{12,4},{16,24},{20,28},{24,16},{28,20},{1,9},{5... | collective-permute-start | bytes 3145736 | tf_op jit(solution)/shard_map/ppermute | solution.py:50
  637.6 24.4 %collective-permute-start.143 = (bf16[4,2,16,4096]{3,2,0,1:T(8,128)(2,1)S(1)}, bf16[4,2,16,4096]{3,2,0,1:T(8,128)(2,1)S(1)}, u32[]{:S(2)}, u32[]{:S(2)}) collective-permute-start(bf16[4,2,16,4096]{3,2,0,1:T(8,128)(2,1)S(1)} %dynamic-slice_bitcast_fusion.2), channel_id=1, source_target_pairs={{0,16},{4,20},{8,24},{12,28},{16,0},{20,4},{24,8},{28,12},{1,17},{... | collective-permute-start | bytes 3145736 | tf_op jit(solution)/shard_map/ppermute | solution.py:50
  659.7 24.8 %collective-permute-start.165 = (bf16[4,2,64,1024]{3,2,0,1:T(8,128)(2,1)S(1)}, bf16[4,2,64,1024]{3,2,0,1:T(8,128)(2,1)S(1)}, u32[]{:S(2)}, u32[]{:S(2)}) collective-permute-start(bf16[4,2,64,1024]{3,2,0,1:T(8,128)(2,1)S(1)} %dynamic-slice_bitcast_fusion), channel_id=1, source_target_pairs={{0,16},{4,20},{8,24},{12,28},{16,0},{20,4},{24,8},{28,12},{1,17},{... | collective-permute-start | bytes 3145736 | tf_op jit(solution)/shard_map/ppermute | solution.py:50
  662.0 52.4 %collective-permute-start.107 = (bf16[16,3072]{1,0:T(8,128)(2,1)S(1)}, bf16[16,3072]{1,0:T(8,128)(2,1)S(1)}, u32[]{:S(2)}, u32[]{:S(2)}) collective-permute-start(bf16[16,3072]{1,0:T(8,128)(2,1)S(1)} %squeeze.250.refs_1_), channel_id=1, source_target_pairs={{0,8},{4,12},{8,0},{12,4},{16,24},{20,28},{24,16},{28,20},{1,9},{5... | collective-permute-start | bytes 294920 | tf_op jit(solution)/shard_map/ppermute | solution.py:50
  728.2 22.5 %collective-permute-start.146 = (bf16[2,16,4096]{2,1,0:T(8,128)(2,1)S(1)}, bf16[2,16,4096]{2,1,0:T(8,128)(2,1)S(1)}, u32[]{:S(2)}, u32[]{:S(2)}) collective-permute-start(bf16[2,16,4096]{2,1,0:T(8,128)(2,1)S(1)} %get-tuple-element.73), channel_id=1, source_target_pairs={{0,2},{1,3},{2,0},{3,1},{4,6},{5,7},{6,4},{7,5},{8,10},{9,11},{10,... | collective-permute-start | bytes 786440 | tf_op jit(solution)/shard_map/ppermute | solution.py:55
  728.2 23.2 %collective-permute-start.145 = (bf16[2,16,4096]{2,1,0:T(8,128)(2,1)S(1)}, bf16[2,16,4096]{2,1,0:T(8,128)(2,1)S(1)}, u32[]{:S(2)}, u32[]{:S(2)}) collective-permute-start(bf16[2,16,4096]{2,1,0:T(8,128)(2,1)S(1)} %get-tuple-element.72), channel_id=1, source_target_pairs={{0,1},{1,2},{2,3},{3,0},{4,5},{5,6},{6,7},{7,4},{8,9},{9,10},{10,1... | collective-permute-start | bytes 786440 | tf_op jit(solution)/shard_map/ppermute | solution.py:55
  732.6 18.9 %collective-permute-start.127 = (bf16[16,1024]{1,0:T(8,128)(2,1)S(1)}, bf16[16,1024]{1,0:T(8,128)(2,1)S(1)}, u32[]{:S(2)}, u32[]{:S(2)}) collective-permute-start(bf16[16,1024]{1,0:T(8,128)(2,1)S(1)} %get-tuple-element.116.refs_1_), channel_id=1, source_target_pairs={{0,4},{4,0},{8,12},{12,8},{16,20},{20,16},{24,28},{28,24},{1,5},{5... | collective-permute-start | bytes 98312 | tf_op jit(solution)/shard_map/ppermute | solution.py:50
  735.0 20.6 %collective-permute-start.129 = (bf16[16,1024]{1,0:T(8,128)(2,1)S(1)}, bf16[16,1024]{1,0:T(8,128)(2,1)S(1)}, u32[]{:S(2)}, u32[]{:S(2)}) collective-permute-start(bf16[16,1024]{1,0:T(8,128)(2,1)S(1)} %get-tuple-element.116.refs_1_), channel_id=1, source_target_pairs={{0,8},{4,12},{8,0},{12,4},{16,24},{20,28},{24,16},{28,20},{1,9},{5... | collective-permute-start | bytes 98312 | tf_op jit(solution)/shard_map/ppermute | solution.py:50
  736.9 18.7 %collective-permute-start.132 = (bf16[16,1024]{1,0:T(8,128)(2,1)S(1)}, bf16[16,1024]{1,0:T(8,128)(2,1)S(1)}, u32[]{:S(2)}, u32[]{:S(2)}) collective-permute-start(bf16[16,1024]{1,0:T(8,128)(2,1)S(1)} %get-tuple-element.117.refs_0_), channel_id=1, source_target_pairs={{0,16},{4,20},{8,24},{12,28},{16,0},{20,4},{24,8},{28,12},{1,17},{... | collective-permute-start | bytes 98312 | tf_op jit(solution)/shard_map/ppermute | solution.py:50
  755.6 23.9 %collective-permute-start.168 = (bf16[2,64,1024]{2,1,0:T(8,128)(2,1)S(1)}, bf16[2,64,1024]{2,1,0:T(8,128)(2,1)S(1)}, u32[]{:S(2)}, u32[]{:S(2)}) collective-permute-start(bf16[2,64,1024]{2,1,0:T(8,128)(2,1)S(1)} %get-tuple-element.70), channel_id=1, source_target_pairs={{0,2},{1,3},{2,0},{3,1},{4,6},{5,7},{6,4},{7,5},{8,10},{9,11},{10,... | collective-permute-start | bytes 786440 | tf_op jit(solution)/shard_map/ppermute | solution.py:55
  756.3 23.2 %collective-permute-start.167 = (bf16[2,64,1024]{2,1,0:T(8,128)(2,1)S(1)}, bf16[2,64,1024]{2,1,0:T(8,128)(2,1)S(1)}, u32[]{:S(2)}, u32[]{:S(2)}) collective-permute-start(bf16[2,64,1024]{2,1,0:T(8,128)(2,1)S(1)} %get-tuple-element.69), channel_id=1, source_target_pairs={{0,1},{1,2},{2,3},{3,0},{4,5},{5,6},{6,7},{7,4},{8,9},{9,10},{10,1... | collective-permute-start | bytes 786440 | tf_op jit(solution)/shard_map/ppermute | solution.py:55
  758.5 23.4 %collective-permute-start.135 = (bf16[16,1024]{1,0:T(8,128)(2,1)S(1)}, bf16[16,1024]{1,0:T(8,128)(2,1)S(1)}, u32[]{:S(2)}, u32[]{:S(2)}) collective-permute-start(bf16[16,1024]{1,0:T(8,128)(2,1)S(1)} %collective-permute-done.133.refs_9_), channel_id=1, source_target_pairs={{0,4},{4,0},{8,12},{12,8},{16,20},{20,16},{24,28},{28,24},{1,5},{5... | collective-permute-start | bytes 98312 | tf_op jit(solution)/shard_map/ppermute | solution.py:50
  758.6 21.6 %collective-permute-start.131 = (bf16[16,1024]{1,0:T(8,128)(2,1)S(1)}, bf16[16,1024]{1,0:T(8,128)(2,1)S(1)}, u32[]{:S(2)}, u32[]{:S(2)}) collective-permute-start(bf16[16,1024]{1,0:T(8,128)(2,1)S(1)} %collective-permute-done.129.refs_5_), channel_id=1, source_target_pairs={{0,4},{4,0},{8,12},{12,8},{16,20},{20,16},{24,28},{28,24},{1,5},{5... | collective-permute-start | bytes 98312 | tf_op jit(solution)/shard_map/ppermute | solution.py:50
  763.2 17.7 %collective-permute-start.134 = (bf16[16,1024]{1,0:T(8,128)(2,1)S(1)}, bf16[16,1024]{1,0:T(8,128)(2,1)S(1)}, u32[]{:S(2)}, u32[]{:S(2)}) collective-permute-start(bf16[16,1024]{1,0:T(8,128)(2,1)S(1)} %collective-permute-done.132.refs_8_), channel_id=1, source_target_pairs={{0,4},{4,0},{8,12},{12,8},{16,20},{20,16},{24,28},{28,24},{1,5},{5... | collective-permute-start | bytes 98312 | tf_op jit(solution)/shard_map/ppermute | solution.py:50
  799.9 30.2 %collective-permute-start.158 = (bf16[16,4096]{1,0:T(8,128)(2,1)S(1)}, bf16[16,4096]{1,0:T(8,128)(2,1)S(1)}, u32[]{:S(2)}, u32[]{:S(2)}) collective-permute-start(bf16[16,4096]{1,0:T(8,128)(2,1)S(1)} %collective-permute-done.150.refs_4_), channel_id=1, source_target_pairs={{0,16},{4,20},{8,24},{12,28},{16,0},{20,4},{24,8},{28,12},{1,17},{... | collective-permute-start | bytes 393224 | tf_op jit(solution)/shard_map/ppermute | solution.py:50
  801.2 28.0 %collective-permute-start.157 = (bf16[16,4096]{1,0:T(8,128)(2,1)S(1)}, bf16[16,4096]{1,0:T(8,128)(2,1)S(1)}, u32[]{:S(2)}, u32[]{:S(2)}) collective-permute-start(bf16[16,4096]{1,0:T(8,128)(2,1)S(1)} %collective-permute-done.155.refs_9_), channel_id=1, source_target_pairs={{0,4},{4,0},{8,12},{12,8},{16,20},{20,16},{24,28},{28,24},{1,5},{5... | collective-permute-start | bytes 393224 | tf_op jit(solution)/shard_map/ppermute | solution.py:50
  801.6 28.5 %collective-permute-start.159 = (bf16[16,4096]{1,0:T(8,128)(2,1)S(1)}, bf16[16,4096]{1,0:T(8,128)(2,1)S(1)}, u32[]{:S(2)}, u32[]{:S(2)}) collective-permute-start(bf16[16,4096]{1,0:T(8,128)(2,1)S(1)} %collective-permute-done.155.refs_9_), channel_id=1, source_target_pairs={{0,8},{4,12},{8,0},{12,4},{16,24},{20,28},{24,16},{28,20},{1,9},{5... | collective-permute-start | bytes 393224 | tf_op jit(solution)/shard_map/ppermute | solution.py:50
  803.0 24.7 %collective-permute-start.153 = (bf16[16,4096]{1,0:T(8,128)(2,1)S(1)}, bf16[16,4096]{1,0:T(8,128)(2,1)S(1)}, u32[]{:S(2)}, u32[]{:S(2)}) collective-permute-start(bf16[16,4096]{1,0:T(8,128)(2,1)S(1)} %collective-permute-done.151.refs_5_), channel_id=1, source_target_pairs={{0,4},{4,0},{8,12},{12,8},{16,20},{20,16},{24,28},{28,24},{1,5},{5... | collective-permute-start | bytes 393224 | tf_op jit(solution)/shard_map/ppermute | solution.py:50
  803.0 25.0 %collective-permute-start.156 = (bf16[16,4096]{1,0:T(8,128)(2,1)S(1)}, bf16[16,4096]{1,0:T(8,128)(2,1)S(1)}, u32[]{:S(2)}, u32[]{:S(2)}) collective-permute-start(bf16[16,4096]{1,0:T(8,128)(2,1)S(1)} %collective-permute-done.154.refs_8_), channel_id=1, source_target_pairs={{0,4},{4,0},{8,12},{12,8},{16,20},{20,16},{24,28},{28,24},{1,5},{5... | collective-permute-start | bytes 393224 | tf_op jit(solution)/shard_map/ppermute | solution.py:50
  827.7 17.9 %collective-permute-start.174 = (bf16[64,1024]{1,0:T(8,128)(2,1)S(1)}, bf16[64,1024]{1,0:T(8,128)(2,1)S(1)}, u32[]{:S(2)}, u32[]{:S(2)}) collective-permute-start(bf16[64,1024]{1,0:T(8,128)(2,1)S(1)} %collective-permute-done.172.refs_4_), channel_id=1, source_target_pairs={{0,4},{4,0},{8,12},{12,8},{16,20},{20,16},{24,28},{28,24},{1,5},{5... | collective-permute-start | bytes 393224 | tf_op jit(solution)/shard_map/ppermute | solution.py:50
  828.0 17.6 %collective-permute-start.180 = (bf16[64,1024]{1,0:T(8,128)(2,1)S(1)}, bf16[64,1024]{1,0:T(8,128)(2,1)S(1)}, u32[]{:S(2)}, u32[]{:S(2)}) collective-permute-start(bf16[64,1024]{1,0:T(8,128)(2,1)S(1)} %collective-permute-done.172.refs_4_), channel_id=1, source_target_pairs={{0,16},{4,20},{8,24},{12,28},{16,0},{20,4},{24,8},{28,12},{1,17},{... | collective-permute-start | bytes 393224 | tf_op jit(solution)/shard_map/ppermute | solution.py:50
  (272 other events, 3598.6 us)

commit v2 on v1

v2 whole, which is shorter than its diff:
```python
import functools
import math

import jax
import jax.numpy as jnp
from jax import lax
from jax.experimental import pallas as pl
from jax.experimental.pallas import tpu as pltpu
from jax.sharding import PartitionSpec as P

HEADS = 16
HD = 64
BLOCK = 25
EPSILON = 1e-05
GROUP = 8
TAIL = 128
PAIR = 2 * HD
STEP = 512
LOG2E = 1.4426950408889634
LOW = jnp.bfloat16
WIDE = jnp.float32
VMEM = pl.BlockSpec(memory_space=pltpu.VMEM)
SMEM = pl.BlockSpec(memory_space=pltpu.SMEM)
ANY = pl.BlockSpec(memory_space=pl.ANY)
PLACE, INDEX, CORE, X, Y, OWNED, HERE, LISTS = range(8)


def params(mib=56):
    return pltpu.CompilerParams(vmem_limit_bytes=mib << 20)


def cost(flops, nbytes):
    return pl.CostEstimate(flops=int(flops), bytes_accessed=int(nbytes), transcendentals=0)


def shape(*dims, dtype=LOW):
    return jax.ShapeDtypeStruct(dims, dtype)


def dot(left, right, dims=((1,), (0,))):
    return lax.dot_general(left, right, (dims, ((), ())), preferred_element_type=WIDE)


def left_dot(left, right):
    return dot(left, right, ((0,), (0,)))


def right_dot(left, right):
    return dot(left, right, ((1,), (1,)))


def part_of(start, size):
    return pl.ds(pl.multiple_of(start, size), size)


def swap(value, mask):
    size = lax.axis_size("dp")
    return lax.ppermute(value, "dp", [(i, i ^ mask) for i in range(size)])


def turn(value, k):
    size = lax.axis_size("ctx")
    return lax.ppermute(value, "ctx", [(i, (i + k) % size) for i in range(size)])


def after(value, *others):
    return lax.optimization_barrier((value, *others))[0]


def plane_gather(one, two):
    one, two = {0: one}, {0: two}
    one[2], two[4] = swap(one[0], 2), swap(two[0], 4)
    one[4], two[2] = swap(one[0], 4), swap(two[0], 2)
    one[6], two[6] = swap(one[2], 4), swap(two[4], 2)
    for mask in (0, 2, 4, 6):
        one[mask + 1], two[mask + 1] = swap(one[mask], 1), swap(two[mask], 1)
    return [item[m] for m in range(GROUP) for item in (one, two)]


def loads(ids, own, pieces, sems, held, rows, row, col):
    n, _, cols = held.shape
    copies = []
    at = 0
    for ref, width in own:
        copies.append(
            pltpu.make_async_copy(ref, held.at[0, :, pl.ds(at, width)], sems.at[len(copies)])
        )
        at += width
    for i, piece in enumerate(pieces):
        where = ((ids[INDEX] ^ (i // 2)) * 2 + i % 2) * rows
        copies.append(
            pltpu.make_async_copy(
                piece.at[:, pl.ds(row, rows), pl.ds(col, cols)],
                held.at[pl.ds(1, n - 1), part_of(where, rows), :],
                sems.at[len(copies)],
            )
        )
    return copies


def begin(copies):
    for copy in copies:
        copy.start()


def finish(copies):
    for copy in copies:
        copy.wait()


def shard_of(ids, k, n):
    return lax.rem(ids[PLACE] + n - k, n)


def project(n, ids, *refs):
    parts, (wq, wk, wv), refs = refs[:n], refs[n : n + 3], refs[n + 3 :]
    pieces, (bias, compact, out, held, sems) = refs[: 2 * GROUP], refs[2 * GROUP :]
    slots, width = parts[0].shape
    cols = width // n
    rows = pieces[0].shape[1]
    copies = []
    for j, own in enumerate((wq, wk, wv)):
        copies.append(
            pltpu.make_async_copy(
                own.at[:, part_of(ids[PLACE] * cols, cols)],
                held.at[0, :, pl.ds(j * cols, cols)],
                sems.at[len(copies)],
            )
        )
        for i, piece in enumerate(pieces):
            where = ((ids[INDEX] ^ (i // 2)) * 2 + i % 2) * rows
            copies.append(
                pltpu.make_async_copy(
                    piece.at[:, :, part_of(j * width + ids[PLACE] * cols, cols)],
                    held.at[pl.ds(1, n - 1), part_of(where, rows), pl.ds(j * cols, cols)],
                    sems.at[len(copies)],
                )
            )
    begin(copies)
    for k in range(n):
        compact[part_of(ids[LISTS + k] * slots, slots), :] = parts[k][...]
    finish(copies)

    def block(i, _):
        row = part_of(i * 256, 256)
        total = bias[...]
        for k in range(n):
            column = part_of(shard_of(ids, k, n) * cols, cols)
            total = total + dot(compact[row, column], held[k])
        out[row, :] = total.astype(LOW)
        return 0

    lax.fori_loop(0, out.shape[0] // 256, block, 0)


def attend(n, ids, bias_ref, q_ref, k_ref, v_ref, *refs):
    outs, lse_ref = refs[:n], refs[n]
    tile = pl.program_id(0)
    slots = q_ref.shape[0]
    first = lax.broadcasted_iota(jnp.int32, (1, PAIR), 1) < HD

    def work(rows):
        query = q_ref[:rows, :]
        keys, values = k_ref[...], v_ref[...]
        mixed = []
        for h in range(2):
            mine = first if h == 0 else jnp.logical_not(first)
            scores = right_dot(jnp.where(mine, query, 0), keys)
            scores = scores * (LOG2E / math.sqrt(HD)) + bias_ref[...]
            high = jnp.max(scores, -1, keepdims=True)
            expo = jnp.exp2(scores - high)
            total = jnp.sum(expo, -1, keepdims=True)
            probs = (expo * (1.0 / total)).astype(LOW)
            mixed.append(dot(probs, values))
            lse = jnp.broadcast_to(high + jnp.log2(total), (rows, 128))
            lse_ref[h : h + 1, :rows] = lse.T[:1, :]
        result = jnp.where(first, mixed[0], mixed[1]).astype(LOW)
        for k, out_ref in enumerate(outs):

            @pl.when(ids[LISTS + n + tile] == k)
            def _():
                out_ref[:rows, :] = result
                if rows < slots:
                    out_ref[rows:, :] = jnp.zeros((slots - rows, PAIR), LOW)

    @pl.when(tile < n - 1)
    def _():
        work(slots)

    @pl.when(tile == n - 1)
    def _():
        work(TAIL)
        lse_ref[:, TAIL:] = jnp.zeros((8, slots - TAIL), WIDE)


def attention(ids, qkv, bias, pair, pairs, n, slots):
    span = qkv.shape[0]
    whole = lambda col: pl.BlockSpec((span, PAIR), lambda t, ids: (0, col))
    return pl.pallas_call(
        functools.partial(attend, n),
        grid_spec=pltpu.PrefetchScalarGridSpec(
            num_scalar_prefetch=1,
            grid=(n,),
            in_specs=[
                pl.BlockSpec((1, span), lambda t, ids: (0, 0)),
                pl.BlockSpec((slots, PAIR), lambda t, ids: (t, pair)),
                whole(pairs + pair),
                whole(2 * pairs + pair),
            ],
            out_specs=[pl.BlockSpec((slots, PAIR), lambda t, ids: (0, 0))] * n
            + [pl.BlockSpec((8, slots), lambda t, ids: (0, t))],
        ),
        out_shape=[shape(slots, PAIR)] * n + [shape(8, n * slots, dtype=WIDE)],
        compiler_params=params(),
        cost_estimate=cost(8 * span * span * PAIR, span * PAIR * 10),
    )(ids, bias, qkv, qkv, qkv)


def attend_back(n, ids, bias_ref, q_ref, k_ref, v_ref, *refs):
    grads, (lse_ref,), outs = refs[:n], refs[n : n + 1], refs[n + 1 : 2 * n + 1]
    do_ref, dk_ref, dv_ref = refs[2 * n + 1 :]
    tile = pl.program_id(0)
    slots = q_ref.shape[0]
    span = k_ref.shape[0]
    first = lax.broadcasted_iota(jnp.int32, (1, PAIR), 1) < HD
    scale = 1.0 / math.sqrt(HD)

    @pl.when(tile == 0)
    def _():
        dk_ref[...] = jnp.zeros_like(dk_ref)
        dv_ref[...] = jnp.zeros_like(dv_ref)
        for k in range(n):
            do_ref[part_of(ids[LISTS + k] * slots, slots), :] = grads[k][...]

    def work(rows):
        keys, values = k_ref[...], v_ref[...]
        here = pl.ds(pl.multiple_of(tile * slots, slots), rows)
        parts = []
        for h in range(2):
            mine = first if h == 0 else jnp.logical_not(first)
            query = jnp.where(mine, q_ref[:rows, :], 0)
            grad = jnp.where(mine, do_ref[here, :], 0)
            scores = right_dot(keys, query) * (LOG2E * scale)
            bias = jnp.concatenate([bias_ref[...]] * (rows // 128), 1)
            probs = jnp.exp2(scores + bias - lse_ref[h : h + 1, :rows])
            grad_probs = right_dot(values, grad)
            center = jnp.sum(grad_probs * probs, 0, keepdims=True)
            grad_scores = (probs * (grad_probs - center)).astype(LOW)
            dk_ref[:span, :] += dot(grad_scores, query)
            dv_ref[:span, :] += dot(probs.astype(LOW), grad)
            parts.append(left_dot(grad_scores, keys))
        result = (jnp.where(first, parts[0], parts[1]) * scale).astype(LOW)
        for k, out_ref in enumerate(outs):

            @pl.when(ids[LISTS + n + tile] == k)
            def _():
                out_ref[:rows, :PAIR] = result
                if rows < slots:
                    out_ref[rows:, :PAIR] = jnp.zeros((slots - rows, PAIR), LOW)

    @pl.when(tile < n - 1)
    def _():
        work(slots)

    @pl.when(tile == n - 1)
    def _():
        work(TAIL)
        for k, out_ref in enumerate(outs):
            here = part_of(ids[LISTS + 2 * n + k] * slots, slots)
            out_ref[:, PAIR : 2 * PAIR] = (dk_ref[here, :] * scale).astype(LOW)
            out_ref[:, 2 * PAIR :] = dv_ref[here, :].astype(LOW)


def attention_back(ids, qkv, bias, grads, lse, pair, pairs, n, slots):
    span = qkv.shape[0]
    whole = lambda col: pl.BlockSpec((span, PAIR), lambda t, ids: (0, col))
    return pl.pallas_call(
        functools.partial(attend_back, n),
        grid_spec=pltpu.PrefetchScalarGridSpec(
            num_scalar_prefetch=1,
            grid=(n,),
            in_specs=[
                pl.BlockSpec((span, 128), lambda t, ids: (0, 0)),
                pl.BlockSpec((slots, PAIR), lambda t, ids: (t, pair)),
                whole(pairs + pair),
                whole(2 * pairs + pair),
            ]
            + [pl.BlockSpec((slots, PAIR), lambda t, ids: (0, pair))] * n
            + [pl.BlockSpec((8, slots), lambda t, ids: (0, t))],
            out_specs=[pl.BlockSpec((slots, 3 * PAIR), lambda t, ids: (0, 0))] * n,
            scratch_shapes=[
                pltpu.VMEM((n * slots, PAIR), LOW),
                pltpu.VMEM((n * slots, PAIR), WIDE),
                pltpu.VMEM((n * slots, PAIR), WIDE),
            ],
        ),
        out_shape=[shape(slots, 3 * PAIR)] * n,
        compiler_params=params(),
        cost_estimate=cost(20 * span * span * PAIR, span * PAIR * 20),
    )(ids, bias, qkv, qkv, qkv, *grads, lse)


def normal(values):
    center = values - jnp.mean(values, -1, keepdims=True)
    scale = lax.rsqrt(jnp.mean(center * center, -1, keepdims=True) + EPSILON)
    return center * scale, scale


def normal_back(grad, unit, scale):
    inner = jnp.mean(grad * unit, -1, keepdims=True)
    return (grad - jnp.mean(grad, -1, keepdims=True) - unit * inner) * scale


def wide(ref):
    return ref[...].astype(WIDE)


def forward(n, pairs, ids, *refs):
    parts, refs = refs[: n * pairs], refs[n * pairs :]
    start, cotangent, wo_own, wi_own, wu_own = refs[:5]
    bo, bi, bu, gain1, shift1, gain2, shift2 = refs[5:12]
    refs = refs[12:]
    side, tall, refs = refs[: 2 * GROUP], refs[2 * GROUP : 4 * GROUP], refs[4 * GROUP :]
    attn, first, normed_low, active, slope, out, grad_second, second_low, sums = refs[:9]
    wo, wi, wu, normed, second, sem_o, sem_i, sem_u = refs[9:]
    slots, width = start.shape
    cols = width // n
    hidden = active.shape[1]
    deep = hidden // n
    row_o, row_u = cols // (2 * GROUP), deep // (2 * GROUP)
    get_o = loads(ids, [(wo_own, width)], tall, sem_o, wo, row_o, 0, 0)
    get_i = loads(ids, [(wi_own, hidden)], side, sem_i, wi, row_o, 0, 3 * width)
    get_u = loads(ids, [(wu_own, width)], tall, sem_u, wu, row_u, row_o, 0)
    begin(get_o)
    begin(get_i)
    begin(get_u)
    for k in range(n):
        mine = jnp.concatenate([parts[p * n + k][...] for p in range(pairs)], 1)
        attn[:, part_of(shard_of(ids, k, n) * cols, cols)] = mine
    finish(get_o)

    def mix(j, _):
        column = part_of(j * STEP, STEP)
        total = start[:, column] + wide(bo.at[:, column])
        for k in range(n):
            left = attn[:, part_of(shard_of(ids, k, n) * cols, cols)]
            total = total + dot(left, wo[k, :, column])
        first[:, column] = total
        return 0

    lax.fori_loop(0, width // STEP, mix, 0)

    def norm(i, _):
        row = part_of(i * 128, 128)
        unit, _ = normal(first[row, :])
        value = unit * wide(gain1) + wide(shift1)
        normed[row, :] = value
        normed_low[row, :] = value.astype(LOW)
        return 0

    lax.fori_loop(0, slots // 128, norm, 0)
    finish(get_i)

    def expand(j, _):
        column = part_of(j * STEP, STEP)
        x = jnp.broadcast_to(wide(bi.at[:, column]), (slots, STEP))
        for k in range(n):
            left = normed_low[:, part_of(shard_of(ids, k, n) * cols, cols)]
            x = x + dot(left, wi[k, :, column])
        factor = math.sqrt(2 / math.pi)
        square = x * x
        t = jnp.tanh(factor * x * (1.0 + 0.044715 * square))
        half = 0.5 * (1.0 + t)
        active[:, column] = (x * half).astype(LOW)
        slope[:, column] = half + (0.5 * factor) * x * (1.0 - t * t) * (1.0 + 0.134145 * square)
        return 0

    lax.fori_loop(0, hidden // STEP, expand, 0)
    finish(get_u)

    def contract(j, _):
        column = part_of(j * STEP, STEP)
        total = normed[:, column] + wide(bu.at[:, column])
        for k in range(n):
            left = active[:, part_of(shard_of(ids, k, n) * deep, deep)]
            total = total + dot(left, wu[k, :, column])
        second[:, column] = total
        return 0

    lax.fori_loop(0, width // STEP, contract, 0)
    sums[...] = jnp.zeros_like(sums)

    def last(i, _):
        row = part_of(i * 128, 128)
        live = lax.broadcasted_iota(jnp.int32, (128, 1), 0) + i * 128 < ids[OWNED]
        live = live.astype(WIDE)
        unit, scale = normal(second[row, :])
        out[row, :] = ((unit * wide(gain2) + wide(shift2)) * live).astype(LOW)
        grad = cotangent[row, :].astype(WIDE) * live
        result = normal_back(grad * wide(gain2), unit, scale)
        grad_second[row, :] = result
        second_low[row, :] = result.astype(LOW)
        for j, item in enumerate((grad * unit, grad, result)):
            sums[j : j + 1, :] += jnp.sum(item, 0, keepdims=True)
        return 0

    lax.fori_loop(0, slots // 128, last, 0)


def backward(n, ids, *refs):
    second_low, grad_second, slope, first, gain1, sums = refs[:6]
    wo_own, wi_own, wu_own = refs[6:9]
    refs = refs[9:]
    side, tall, refs = refs[: 2 * GROUP], refs[2 * GROUP : 4 * GROUP], refs[4 * GROUP :]
    inner_low, grad_first, first_low = refs[:3]
    outs, small = refs[3 : 3 + n], refs[3 + n]
    wo, wi, wu, grad_normed, bias_sum, more, sem_o, sem_i, sem_u = refs[4 + n :]
    slots, width = first.shape
    cols = width // n
    hidden = slope.shape[1]
    deep = hidden // n
    row_o, row_u = cols // (2 * GROUP), deep // (2 * GROUP)
    get_o = loads(ids, [(wo_own, width)], tall, sem_o, wo, row_o, 0, 0)
    get_i = loads(ids, [(wi_own, hidden)], side, sem_i, wi, row_o, 0, 3 * width)
    get_u = loads(ids, [(wu_own, width)], tall, sem_u, wu, row_u, row_o, 0)
    begin(get_u)
    begin(get_i)
    begin(get_o)
    finish(get_u)

    def expand(j, _):
        for k in range(n):
            column = part_of(shard_of(ids, k, n) * deep + j * STEP, STEP)
            grad = right_dot(second_low[...], wu[k, part_of(j * STEP, STEP), :])
            value = (grad * slope[:, column]).astype(LOW)
            inner_low[:, column] = value
            bias_sum[:, column] = jnp.sum(value.astype(WIDE), 0, keepdims=True)
        return 0

    lax.fori_loop(0, deep // STEP, expand, 0)
    finish(get_i)
    for k in range(n):
        column = part_of(shard_of(ids, k, n) * cols, cols)
        grad_normed[:, column] = right_dot(inner_low[...], wi[k]) + grad_second[:, column]
    more[...] = jnp.zeros_like(more)

    def norm(i, _):
        row = part_of(i * 128, 128)
        unit, scale = normal(first[row, :])
        grad = grad_normed[row, :]
        result = normal_back(grad * wide(gain1), unit, scale)
        grad_first[row, :] = result
        first_low[row, :] = result.astype(LOW)
        for j, item in enumerate((result, grad * unit, grad)):
            more[j : j + 1, :] += jnp.sum(item, 0, keepdims=True)
        return 0

    lax.fori_loop(0, slots // 128, norm, 0)
    finish(get_o)
    for k in range(n):
        outs[k][...] = right_dot(first_low[...], wo[k]).astype(LOW)
    small[...] = jnp.zeros_like(small)
    for z in range(n):
        far = lax.rem(z + n - ids[PLACE], n)
        here = pl.ds(z * cols, cols)
        rows = [more[0:1, here]]
        rows += [bias_sum[:, pl.ds(z * deep + j * cols, cols)] for j in range(deep // cols)]
        rows += [sums[2:3, here], more[1:2, here], more[2:3, here], sums[0:1, here], sums[1:2, here]]
        for j, item in enumerate(rows):
            small[far, j : j + 1, :] = item


def finish_hidden(n, pairs, ids, *refs):
    parts, refs = refs[: n * pairs], refs[n * pairs :]
    grad_first, wq, wk, wv = refs[:4]
    side, (out, total, held, acts, sems) = refs[4 : 4 + 2 * GROUP], refs[4 + 2 * GROUP :]
    slots, width = out.shape
    cols = width // n
    copies = loads(
        ids, [(wq, width), (wk, width), (wv, width)], side, sems, held, cols // (2 * GROUP), 0, 0
    )
    begin(copies)
    for k in range(n):
        for p in range(pairs):
            for j in range(3):
                column = j * width + shard_of(ids, k, n) * cols + p * PAIR
                acts[:, part_of(column, PAIR)] = parts[p * n + k][:, j * PAIR : (j + 1) * PAIR]
    finish(copies)
    for k in range(n):
        column = part_of(shard_of(ids, k, n) * cols, cols)
        out[:, column] = right_dot(acts[...], held[k]) + grad_first[:, column]
    block = lax.broadcasted_iota(jnp.int32, (32, 1), 0) < ids[HERE]
    total[...] = jnp.sum(jnp.where(block, out[:32, :], 0.0), 0, keepdims=True)


def outer_product(spec, keep, ids, *refs):
    lefts, rights = [], []
    for count, _ in spec:
        lefts.append(refs[:count])
        rights.append(refs[count : 2 * count])
        refs = refs[2 * count :]
    at = 0
    for (count, cols), left, right in zip(spec, lefts, rights):
        step = min(cols, 1024)
        for col in range(0, cols, step):
            total = left_dot(left[0][...], right[0][:, col : col + step])
            for i in range(1, count):
                total = total + left_dot(left[i][...], right[i][:, col : col + step])
            here = slice(at + col, at + col + step)
            if not keep:
                refs[0][0, :, here] = total.astype(LOW)
                continue
            got, outs = refs[0], refs[1:]
            total = (total + got[0, :, here].astype(WIDE)).astype(LOW)
            split_halves(ids, total, [out.at[0, :, here] for out in outs], (X, Y))
        at += cols


def split_halves(ids, total, outs, bits):
    rows = total.shape[0] // 4
    parts = [total[i * rows : (i + 1) * rows] for i in range(4)]
    for half, bit in enumerate(bits):
        high = ids[bit] == 1
        low_part, high_part = parts[2 * half], parts[2 * half + 1]
        outs[2 * half][...] = jnp.where(high, low_part, high_part)
        outs[2 * half + 1][...] = jnp.where(high, high_part, low_part)


def gradient(ids, spec, n, got=None):
    rows = spec[0][0][0][0].shape[1] // (2 * n)
    keep = got is not None
    in_specs, args, total, flops = [], [], 0, 0
    for pairs, cols in spec:
        for left, _ in pairs:
            block = lambda z, ids: (0, 2 * z + (ids[CORE] if keep else 1 - ids[CORE]))
            in_specs.append(pl.BlockSpec((left.shape[0], rows), block))
            args.append(left)
        for _, right in pairs:
            in_specs.append(pl.BlockSpec(right.shape, lambda z, ids: (0, 0)))
            args.append(right)
            flops += 2 * n * rows * right.shape[0] * cols
        total += cols
    if keep:
        in_specs.append(pl.BlockSpec((1, rows, total), lambda z, ids: (z, 0, 0)))
        args.append(got)
    out_rows, count = (rows // 4, 4) if keep else (rows, 1)
    return pl.pallas_call(
        functools.partial(outer_product, [(len(pairs), cols) for pairs, cols in spec], keep),
        grid_spec=pltpu.PrefetchScalarGridSpec(
            num_scalar_prefetch=1,
            grid=(n,),
            in_specs=in_specs,
            out_specs=[pl.BlockSpec((1, out_rows, total), lambda z, ids: (z, 0, 0))] * count,
        ),
        out_shape=[shape(n, out_rows, total)] * count,
        compiler_params=params(),
        cost_estimate=cost(flops, flops / 500),
    )(ids, *args)


def fold_two(ids, keep_one, got_one, keep_two, got_two, *outs):
    rows = keep_one.shape[1] // 2
    for z in range(keep_one.shape[0]):
        one = (keep_one[z].astype(WIDE) + got_one[z].astype(WIDE)).astype(LOW)
        two = (keep_two[z].astype(WIDE) + got_two[z].astype(WIDE)).astype(LOW)
        for total, bit, (send, keep) in ((one, Y, outs[:2]), (two, X, outs[2:])):
            high = ids[bit] == 1
            send[z] = jnp.where(high, total[:rows], total[rows:])
            keep[z] = jnp.where(high, total[rows:], total[:rows])


def fold_three(ids, keep_one, got_one, keep_two, got_two, *outs):
    n = len(outs)
    for k, out in enumerate(outs):
        z = lax.rem(ids[PLACE] + k, n)
        out[0] = (keep_one[z].astype(WIDE) + got_one[z].astype(WIDE)).astype(LOW)
        out[1] = (keep_two[z].astype(WIDE) + got_two[z].astype(WIDE)).astype(LOW)


def fold_four(*refs):
    refs, outs = refs[:-2], refs[-2:]
    for h, out in enumerate(outs):
        total = refs[0][h].astype(WIDE)
        for ref in refs[1:]:
            total = total + ref[h].astype(WIDE)
        out[...] = total.astype(LOW)


def fold_heads(ids, *refs):
    refs, outs = refs[:-2], refs[-2:]
    n, cols = len(refs), refs[0].shape[2]
    for h, out in enumerate(outs):
        for k, ref in enumerate(refs):
            out[:, part_of(shard_of(ids, k, n) * cols, cols)] = ref[h]


def small_call(body, ids, args, outs):
    nbytes = sum(v.size * 2 for v in args)
    return pl.pallas_call(
        body,
        in_specs=([SMEM] if ids is not None else []) + [VMEM] * len(args),
        out_specs=[VMEM] * len(outs),
        out_shape=outs,
        compiler_params=params(),
        cost_estimate=cost(0, 2 * nbytes),
    )(*([ids] if ids is not None else []), *args)


def reduce_first(ids, spec, n):
    (send,) = gradient(ids, spec, n)
    return swap(send, 1)


def reduce_second(ids, spec, n, got):
    send_one, keep_one, send_two, keep_two = gradient(ids, spec, n, got)
    return keep_one, swap(send_one, 2), keep_two, swap(send_two, 4)


def reduce_third(ids, n, held):
    rows, cols = held[0].shape[1:]
    outs = [shape(n, rows // 2, cols)] * 4
    send_one, keep_one, send_two, keep_two = small_call(fold_two, ids, held, outs)
    return keep_one, swap(send_one, 4), keep_two, swap(send_two, 2)


def reduce_fourth(ids, n, held):
    rows, cols = held[0].shape[1:]
    outs = small_call(fold_three, ids, held, [shape(2, rows, cols)] * n)
    return [outs[0]] + [turn(outs[k], k) for k in range(1, n)]


def reduce_fifth(ids, held, heads=False):
    rows, cols = held[0].shape[1:]
    if heads:
        one, two = small_call(fold_heads, ids, held, [shape(rows, len(held) * cols)] * 2)
    else:
        one, two = small_call(fold_four, None, held, [shape(rows, cols)] * 2)
    mask = GROUP
    while mask < lax.axis_size("dp"):
        one, two = [(v.astype(WIDE) + swap(v, mask).astype(WIDE)).astype(LOW) for v in (one, two)]
        mask *= 2
    return plane_gather(one, two)


def place_grad(plan, ids, *refs):
    pieces, outs = refs[: 2 * GROUP], refs[2 * GROUP :]
    rows = pieces[0].shape[0]
    for i, piece in enumerate(pieces):
        home = ids[INDEX] ^ (i // 2)
        core, x, y = home & 1, (home >> 1) & 1, (home >> 2) & 1
        block = core * 8 + (x * 2 + y if i % 2 == 0 else 4 + y * 2 + x)
        row = part_of(block * rows, rows)
        for out, moves in zip(outs, plan):
            for source, target, size in moves:
                out[row, target : target + size] = piece[:, source : source + size].astype(WIDE)


def reduce_last(ids, pieces, plan, widths):
    rows = pieces[0].shape[0] * 2 * GROUP
    return small_call(
        functools.partial(place_grad, plan),
        ids,
        pieces,
        [shape(rows, width, dtype=WIDE) for width in widths],
    )


def per_device(
    hidden_in,
    cotangent,
    context_len,
    block_device,
    timestep,
    query_weight,
    key_weight,
    value_weight,
    output_weight,
    inner_weight,
    outer_weight,
    query_bias,
    value_bias,
    output_bias,
    inner_bias,
    outer_bias,
    attn_gain,
    attn_shift,
    ffn_gain,
    ffn_shift,
    time_table,
):
    n = lax.axis_size("ctx")
    place = lax.axis_index("ctx")
    d = lax.axis_index("dp") % GROUP
    _, slots, width = hidden_in.shape
    hidden = inner_weight.shape[1]
    cols = width // n
    deep = hidden // n
    pairs = cols // PAIR
    span = (n - 1) * slots + TAIL
    holder = block_device[0]
    context = context_len[0]

    order = [j + (j >= holder).astype(jnp.int32) for j in range(n - 1)] + [holder]
    position = lambda g: jnp.where(g == holder, n - 1, g - (g > holder).astype(jnp.int32))
    counts = [context // (n - 1) + (j < context % (n - 1)).astype(jnp.int32) for j in range(n - 1)]
    counts = jnp.stack(counts + [jnp.int32(BLOCK)])
    slot = jnp.arange(slots, dtype=jnp.int32)
    live = (slot[None, :] < counts[:, None]).reshape(n * slots)[:span]
    bias = jnp.where(live, 0.0, -1e30).astype(WIDE)
    bias_row, bias_col = bias[None, :], jnp.broadcast_to(bias[:, None], (span, 128))
    owned = lax.dynamic_index_in_dim(counts, position(place), keepdims=False)
    here = jnp.where(holder == place, BLOCK, 0)
    ids = [place, d, d & 1, (d >> 1) & 1, (d >> 2) & 1, owned, here]
    ids += [position((place - k + n) % n) for k in range(n)]
    ids += [(g - place + n) % n for g in order]
    ids += [position((place + k) % n) for k in range(n)]
    ids = jnp.stack([jnp.asarray(v, jnp.int32) for v in ids])
    embed = lax.dynamic_slice_in_dim(time_table, timestep[0], 1, 0).astype(WIDE)
    block = ((holder == place) & (slot < BLOCK)).astype(WIDE)[:, None]
    start = hidden_in[0].astype(WIDE) + block * embed
    start_low = start.astype(LOW)

    def piece(weight):
        part = weight.shape[0] // GROUP
        return lax.dynamic_slice_in_dim(weight, d * part, part, 0).reshape(2, part // 2, -1)

    side_piece = jnp.concatenate(
        [piece(w) for w in (query_weight, key_weight, value_weight, inner_weight)], 2
    )
    tall_piece = jnp.concatenate([piece(output_weight), piece(outer_weight)], 1)
    side = jnp.stack([turn(side_piece, k) for k in range(1, n)])
    tall_piece = after(tall_piece, side)
    tall = jnp.stack([turn(tall_piece, k) for k in range(1, n)])
    sent = after(start_low, tall)
    parts = [start_low] + [turn(sent, k) for k in range(1, n)]
    side = plane_gather(side[:, 0], side[:, 1])
    tall = plane_gather(tall[:, 0], tall[:, 1])
    own_bias = lambda v: lax.dynamic_slice_in_dim(v, place * cols, cols, 0).astype(WIDE)
    qkv_bias = jnp.concatenate([own_bias(query_bias), jnp.zeros((cols,), WIDE), own_bias(value_bias)])
    _, qkv = pl.pallas_call(
        functools.partial(project, n),
        in_specs=[SMEM] + [VMEM] * n + [ANY] * (3 + 2 * GROUP) + [VMEM],
        out_specs=[VMEM, VMEM],
        out_shape=[shape(n * slots, width), shape(span, 3 * cols)],
        scratch_shapes=[
            pltpu.VMEM((n, cols, 3 * cols), LOW),
            pltpu.SemaphoreType.DMA((3 + 6 * GROUP,)),
        ],
        compiler_params=params(),
        cost_estimate=cost(6 * span * width * cols, 4 * span * width),
    )(ids, *parts, query_weight, key_weight, value_weight, *side, qkv_bias[None])

    mixed, lses = [], []
    for pair in range(pairs):
        *outs, lse = attention(ids, qkv, bias_row, pair, pairs, n, slots)
        lses.append(lse)
        mixed += [outs[0]] + [turn(outs[k], k) for k in range(1, n)]

    row = lambda v: v[None, :]
    weights = [
        pltpu.VMEM((n, cols, width), LOW),
        pltpu.VMEM((n, cols, hidden), LOW),
        pltpu.VMEM((n, deep, width), LOW),
    ]
    sems = [pltpu.SemaphoreType.DMA((1 + 2 * GROUP,))] * 3
    flops = 2 * slots * width * (width + 2 * hidden)
    attn, first, normed_low, active, slope, out, grad_second, second_low, sums = pl.pallas_call(
        functools.partial(forward, n, pairs),
        in_specs=[SMEM] + [VMEM] * (n * pairs + 2) + [ANY] * 3 + [VMEM] * 7 + [ANY] * (4 * GROUP),
        out_specs=[VMEM] * 9,
        out_shape=[
            shape(slots, width),
            shape(slots, width, dtype=WIDE),
            shape(slots, width),
            shape(slots, hidden),
            shape(slots, hidden, dtype=WIDE),
            shape(slots, width),
            shape(slots, width, dtype=WIDE),
            shape(slots, width),
            shape(8, width, dtype=WIDE),
        ],
        scratch_shapes=weights
        + [pltpu.VMEM((slots, width), WIDE), pltpu.VMEM((slots, width), WIDE)]
        + sems,
        compiler_params=params(),
        cost_estimate=cost(flops, flops / 300),
    )(
        ids,
        *mixed,
        start,
        cotangent[0],
        output_weight,
        inner_weight,
        outer_weight,
        row(output_bias),
        row(inner_bias),
        row(outer_bias),
        row(attn_gain),
        row(attn_shift),
        row(ffn_gain),
        row(ffn_shift),
        *side,
        *tall,
    )
    outer_spec = [([(active, second_low)], width)]
    outer_held = reduce_first(ids, outer_spec, n)

    inner_low, grad_first, first_low, *rest = pl.pallas_call(
        functools.partial(backward, n),
        in_specs=[SMEM] + [VMEM] * 6 + [ANY] * (3 + 4 * GROUP),
        out_specs=[VMEM] * (4 + n),
        out_shape=[
            shape(slots, hidden),
            shape(slots, width, dtype=WIDE),
            shape(slots, width),
        ]
        + [shape(slots, cols)] * n
        + [shape(n, 16, cols, dtype=WIDE)],
        scratch_shapes=weights
        + [
            pltpu.VMEM((slots, width), WIDE),
            pltpu.VMEM((1, hidden), WIDE),
            pltpu.VMEM((8, width), WIDE),
        ]
        + sems,
        compiler_params=params(),
        cost_estimate=cost(flops, flops / 300),
    )(
        ids,
        second_low,
        grad_second,
        slope,
        first,
        row(attn_gain),
        sums,
        output_weight,
        inner_weight,
        outer_weight,
        *side,
        *tall,
    )
    grad_parts, small = rest[:n], rest[n]
    grad_mixed = [grad_parts[0]] + [turn(grad_parts[n - k], k) for k in range(1, n)]
    inner_spec = [([(normed_low, inner_low)], hidden), ([(attn, first_low)], width)]
    inner_held = reduce_first(ids, inner_spec, n)
    outer_held = reduce_second(ids, outer_spec, n, outer_held)
    inner_held = reduce_second(ids, inner_spec, n, inner_held)
    outer_held = reduce_third(ids, n, outer_held)

    backs, received = [], []
    for pair in range(pairs):
        back = attention_back(ids, qkv, bias_col, grad_mixed, lses[pair], pair, pairs, n, slots)
        backs.append(back)
        received += [back[0]] + [turn(back[k], k) for k in range(1, n)]
        if pair == 0:
            outer_held = reduce_fourth(ids, n, outer_held)
            inner_held = reduce_third(ids, n, inner_held)
    qkv_spec = [([(parts[-k % n], back[k]) for k in range(n)], 3 * PAIR) for back in backs]
    qkv_held = reduce_first(ids, qkv_spec, n)
    qkv_held = reduce_second(ids, qkv_spec, n, qkv_held)
    inner_held = reduce_fourth(ids, n, inner_held)
    outer_pieces = reduce_fifth(ids, outer_held)
    qkv_held = reduce_third(ids, n, qkv_held)
    qkv_held = reduce_fourth(ids, n, qkv_held)
    inner_pieces = reduce_fifth(ids, inner_held)
    qkv_pieces = reduce_fifth(ids, qkv_held, heads=True)
    (outer_grad,) = reduce_last(ids, outer_pieces, [[(0, 0, width)]], [width])
    inner_grad, output_grad = reduce_last(
        ids, inner_pieces, [[(0, 0, hidden)], [(hidden, 0, width)]], [hidden, width]
    )
    plan = [
        [
            (g * 3 * cols + p * 3 * PAIR + j * PAIR, g * cols + p * PAIR, PAIR)
            for g in range(n)
            for p in range(pairs)
        ]
        for j in range(3)
    ]
    weight_grads = reduce_last(ids, qkv_pieces, plan, [width] * 3)

    grad_hidden, block_sum = pl.pallas_call(
        functools.partial(finish_hidden, n, pairs),
        in_specs=[SMEM] + [VMEM] * (n * pairs + 1) + [ANY] * (3 + 2 * GROUP),
        out_specs=[VMEM] * 2,
        out_shape=[shape(slots, width, dtype=WIDE), shape(1, width, dtype=WIDE)],
        scratch_shapes=[
            pltpu.VMEM((n, cols, 3 * width), LOW),
            pltpu.VMEM((slots, 3 * width), LOW),
            pltpu.SemaphoreType.DMA((3 + 2 * GROUP,)),
        ],
        compiler_params=params(),
        cost_estimate=cost(6 * slots * width * width, 8 * width * width),
    )(ids, *received, grad_first, query_weight, key_weight, value_weight, *side)

    def everywhere(value):
        mask = 1
        while mask < lax.axis_size("dp"):
            value = value + swap(value, mask)
            mask *= 2
        return value

    total = small[0]
    for k in range(1, n):
        total = total + turn(small[k], k)
    total = everywhere(total)
    per = deep // cols
    sums = [total[0], total[1 : 1 + per].reshape(deep)] + [total[1 + per + i] for i in range(5)]
    bias_sums = jnp.stack([sum(jnp.sum(v.astype(WIDE), 0) for v in back) for back in backs])
    bias_sums = everywhere(bias_sums)
    query_sum = bias_sums[:, :PAIR].reshape(cols)
    value_sum = bias_sums[:, 2 * PAIR :].reshape(cols)

    vector, level = block_sum, timestep.astype(WIDE)[:, None]
    vector = vector + sum(turn(block_sum, k) for k in range(1, n))
    mask = 1
    while mask < lax.axis_size("dp"):
        vector = jnp.concatenate([vector, swap(vector, mask)])
        level = jnp.concatenate([level, swap(level, mask)])
        mask *= 2
    share = time_table.shape[0] // n
    levels = (jnp.arange(share, dtype=jnp.int32) + place * share).astype(WIDE)
    onehot = (level == levels[None, :]).astype(WIDE)
    time_table_grad = lax.dot_general(
        onehot,
        vector,
        (((0,), (0,)), ((), ())),
        precision=lax.Precision.HIGHEST,
        preferred_element_type=WIDE,
    )
    return (
        out[None],
        grad_hidden[None],
        *weight_grads,
        output_grad,
        inner_grad,
        outer_grad,
        query_sum,
        value_sum,
        *sums,
        time_table_grad,
    )


def solution(mesh):
    row, shard, same = P("dp", "ctx", None), P("ctx", None), P()
    return jax.shard_map(
        per_device,
        mesh=mesh,
        in_specs=(row, row, P("dp"), P("dp"), P("dp")) + (shard,) * 6 + (same,) * 10,
        out_specs=(row, row) + (shard,) * 6 + (P("ctx"),) * 9 + (shard,),
        check_vma=False,
    )
```

time: 864 us -> 676 us (0.78)
  Pallas kernels: 89.7 us -> 205 us
  local copies, waits for them, and re-layouts: 123 us -> 24 us
  waiting for transfers between devices: 331 us -> 248 us
  matrix products: 72.5 us -> 1.28 us
  other arithmetic: 39.1 us -> 7.9 us
  blocking collectives: 25.3 us -> 0 us
    pallas_call x13 -> x26, Pallas kernels: 89.7 us -> 205 us  [the longest x6 45.7 us: gradient(): pl.pallas_call(functools.partial(outer_product, [(len(pairs), cols) for p...]
    dot_general x13 -> x1, matrix products: 72.5 us -> 1.28 us  [per_device(): lax.dot_general(onehot, vector, (((0,), (0,)), ((), ())), precision=lax.P...]
    ppermute x142 -> x97, waiting for transfers between devices: 146 us -> 81 us  [swap(): return lax.ppermute(value, 'dp', [(i, i ^ mask) for i in range(size)])]
    ppermute x48 -> x39, starting transfers between devices: 69.8 us -> 108 us  [turn(): lax.ppermute(value, 'ctx', [(i, (i + k) % size) for i in range(size)])]
    unnamed x341 -> x298, local copies, waits for them, and re-layouts: 48.2 us -> 10.7 us
    ppermute x142 -> x97, starting transfers between devices: 98.2 us -> 63.5 us  [swap(): return lax.ppermute(value, 'dp', [(i, i ^ mask) for i in range(size)])]
    dynamic_slice x25 -> x5, local copies, waits for them, and re-layouts: 36.3 us -> 4.3 us  [the longest x4 3.72 us: piece(): lax.dynamic_slice_in_dim(weight, d * part, part, 0)]
    convert_element_type x26 -> x2, other arithmetic: 20.8 us -> 0.78 us  [the longest x1 0.77 us: per_device(): lax.dynamic_slice_in_dim(v, place * cols, cols, 0).astype(WIDE)]
  transfers between devices with their start and end apart: 190 -> 136, of which waited for: 55 -> 42; matrix products, arithmetic and copies ran while one was open for 18% -> 3% of each run, Pallas kernels for 9% -> 22%
where the time goes in v2:
time: 676 us; the launch traced here: 663 us
  waiting for transfers between devices  248 us (37%)
  Pallas kernels  205 us (30%)
  starting transfers between devices  172 us (25%)
  local copies, waits for them, and re-layouts  24 us (4%)
  other arithmetic  7.9 us (1%)
    ppermute x39, waiting for transfers between devices, turn(): lax.ppermute(value, 'ctx', [(i, (i + k) % size) for i in range(size)])  167 us
    ppermute x39, starting transfers between devices, turn(): lax.ppermute(value, 'ctx', [(i, (i + k) % size) for i in range(size)])  108 us
    ppermute x97, waiting for transfers between devices, swap(): return lax.ppermute(value, 'dp', [(i, i ^ mask) for i in range(size)])  81 us
    ppermute x97, starting transfers between devices, swap(): return lax.ppermute(value, 'dp', [(i, i ^ mask) for i in range(size)])  63.5 us
    pallas_call x6, Pallas kernels, gradient(): pl.pallas_call(functools.partial(outer_product, [(len(pairs), cols) for p...  45.7 us
    pallas_call x2, Pallas kernels, attention_back(): pl.pallas_call(functools.partial(attend_back, n), grid_spec=pltpu.Prefetc...  41.2 us
    pallas_call x12, Pallas kernels, small_call(): pl.pallas_call(body, in_specs=([SMEM] if ids is not None else []) + [VMEM...  35.2 us
    pallas_call x1, Pallas kernels, per_device(): pl.pallas_call(functools.partial(forward, n, pairs), in_specs=[SMEM] + [V...  24.4 us
  transfers between devices with their start and end apart: 136, of which 42 were waited for; matrix products, arithmetic and copies ran while one was open for 3% of the time, Pallas kernels for 22%

profile of v2, /device:TPU:0, one launch (start us, length us, event | category | flops | bytes accessed | tf_op | source)
XLA Modules:
  0.0 662.7 jit_solution(15739408679085925861)
XLA Ops:
  3.5 3.1 collective-permute-start
  6.5 2.6 collective-permute-start.1
  11.5 8.6 %collective-permute-done = bf16[2,16,7168]{2,1,0:T(8,128)(2,1)S(1)} collective-permute-done((bf16[2,16,7168]{2,1,0:T(8,128)(2,1)S(1)}, bf16[2,16,7168]{2,1,0:T(8,128)(2,1)S(1)}, u32[]{:S(2)}, u32[]{:S(2)}) %collective-permute-start) | collective-permute-done | bytes 458784 | tf_op jit(solution)/shard_map/ppermute | solution.py:63
  20.1 18.8 %collective-permute-done.1 = bf16[2,16,7168]{2,1,0:T(8,128)(2,1)S(1)} collective-permute-done((bf16[2,16,7168]{2,1,0:T(8,128)(2,1)S(1)}, bf16[2,16,7168]{2,1,0:T(8,128)(2,1)S(1)}, u32[]{:S(2)}, u32[]{:S(2)}) %collective-permute-start.1) | collective-permute-done | bytes 458784 | tf_op jit(solution)/shard_map/ppermute | solution.py:63
  39.0 10.3 %collective-permute-start.3 = (bf16[2,80,1024]{2,1,0:T(8,128)(2,1)S(1)}, bf16[2,80,1024]{2,1,0:T(8,128)(2,1)S(1)}, u32[]{:S(2)}, u32[]{:S(2)}) collective-permute-start(bf16[2,80,1024]{2,1,0:T(8,128)(2,1)S(1)} %pad_maximum_fusion.3), channel_id=1, source_target_pairs={{0,1},{1,2},{2,3},{3,0},{4,5},{5,6},{6,7},{7,4},{8,9},{9,10},{10,1... | collective-permute-start | bytes 983048 | tf_op jit(solution)/shard_map/ppermute | solution.py:63
  55.0 4.2 collective-permute-done.3
  60.7 10.8 %collective-permute-done.4 = bf16[2,80,1024]{2,1,0:T(8,128)(2,1)S(1)} collective-permute-done((bf16[2,80,1024]{2,1,0:T(8,128)(2,1)S(1)}, bf16[2,80,1024]{2,1,0:T(8,128)(2,1)S(1)}, u32[]{:S(2)}, u32[]{:S(2)}) %collective-permute-start.4) | collective-permute-done | bytes 327712 | tf_op jit(solution)/shard_map/ppermute | solution.py:63
  78.7 4.0 collective-permute-done.12.refs_12_.refs_25_.refs_14_.refs_17_
  84.9 4.9 collective-permute-done.15.refs_15_.refs_28_.refs_17_.refs_20_
  94.5 6.6 collective-permute-start.6
  101.1 3.4 collective-permute-start.7
  104.4 5.7 collective-permute-start.8
  113.2 9.2 %collective-permute-done.6.refs_1_.refs_3_.refs_11_ = bf16[384,1024]{1,0:T(8,128)(2,1)S(1)} collective-permute-done((bf16[384,1024]{1,0:T(8,128)(2,1)S(1)}, bf16[384,1024]{1,0:T(8,128)(2,1)S(1)}, u32[]{:S(2)}, u32[]{:S(2)}) %collective-permute-start.6) | collective-permute-done | bytes 786464 | tf_op jit(solution)/shard_map/ppermute | solution.py:63
  122.9 32.9 %collective-permute-done.7.refs_2_.refs_10_ = bf16[384,1024]{1,0:T(8,128)(2,1)S(1)} collective-permute-done((bf16[384,1024]{1,0:T(8,128)(2,1)S(1)}, bf16[384,1024]{1,0:T(8,128)(2,1)S(1)}, u32[]{:S(2)}, u32[]{:S(2)}) %collective-permute-start.7) | collective-permute-done | bytes 786464 | tf_op jit(solution)/shard_map/ppermute | solution.py:63
  156.7 12.8 %collective-permute-done.40.refs_49_.refs_38_ = bf16[3,80,1024]{2,1,0:T(8,128)(2,1)S(1)} collective-permute-done((bf16[3,80,1024]{2,1,0:T(8,128)(2,1)S(1)}, bf16[3,80,1024]{2,1,0:T(8,128)(2,1)S(1)}, u32[]{:S(2)}, u32[]{:S(2)}) %collective-permute-start.40) | collective-permute-done | bytes 491552 | tf_op jit(solution)/shard_map/ppermute | solution.py:58
  177.7 8.5 %shard_map.340 = (bf16[1536,1024]{1,0:T(8,128)(2,1)}, bf16[1280,768]{1,0:T(8,128)(2,1)}) custom-call(s32[19]{0:T(128)} %stack.112.ids, bf16[384,1024]{1,0:T(8,128)(2,1)} %copy-done, bf16[384,1024]{1,0:T(8,128)(2,1)} %copy-done.1, bf16[384,1024]{1,0:T(8,128)(2,1)} %copy-done.2, bf16[384,1024]{1,0:T(8,128)(2,1)} %copy-done.3, bf16[256,1024]{1,0:T(8,128)(2,1)} %refs_9_.1, ...), custom_call_target="tpu_custom_call" | custom-call | flops 2013265920 | bytes 5242880 | tf_op jit(solution)/shard_map/pallas_call | solution.py:740
  186.3 10.9 %shard_map.342 = (bf16[384,128]{1,0:T(8,128)(2,1)}, bf16[384,128]{1,0:T(8,128)(2,1)}, bf16[384,128]{1,0:T(8,128)(2,1)}, bf16[384,128]{1,0:T(8,128)(2,1)}, f32[8,1536]{1,0:T(8,128)}) custom-call(s32[19]{0:T(128)} %stack.112.ids, f32[1,1280]{1,0:T(1,128)} %broadcast_in_dim.60.bias_ref, bf16[1280,768]{1,0:T(8,128)(2,1)} %get-tuple-element.107.q_ref.k_ref.v_ref, ...), custom_call_target="tpu_custom_call" | custom-call | flops 1677721600 | bytes 1638400 | tf_op jit(solution)/shard_map/pallas_call | solution.py:199
  197.3 17.2 %collective-permute-start.26 = (bf16[384,128]{1,0:T(8,128)(2,1)}, bf16[384,128]{1,0:T(8,128)(2,1)S(1)}, u32[]{:S(2)}, u32[]{:S(2)}) collective-permute-start(bf16[384,128]{1,0:T(8,128)(2,1)} %get-tuple-element.113), channel_id=1, source_target_pairs={{0,1},{1,2},{2,3},{3,0},{4,5},{5,6},{6,7},{7,4},{8,9},{9,10},{10,1... | collective-permute-start | bytes 294920 | tf_op jit(solution)/shard_map/ppermute | solution.py:63
  214.4 10.9 %shard_map.341 = (bf16[384,128]{1,0:T(8,128)(2,1)}, bf16[384,128]{1,0:T(8,128)(2,1)}, bf16[384,128]{1,0:T(8,128)(2,1)}, bf16[384,128]{1,0:T(8,128)(2,1)}, f32[8,1536]{1,0:T(8,128)}) custom-call(s32[19]{0:T(128)} %stack.112.ids, f32[1,1280]{1,0:T(1,128)} %broadcast_in_dim.60.bias_ref, bf16[1280,768]{1,0:T(8,128)(2,1)} %get-tuple-element.107.q_ref.k_ref.v_ref, ...), custom_call_target="tpu_custom_call" | custom-call | flops 1677721600 | bytes 1638400 | tf_op jit(solution)/shard_map/pallas_call | solution.py:199
  227.9 2.6 collective-permute-start.24
  236.3 4.9 collective-permute-done.24.refs_2_
  241.9 24.4 %shard_map.343 = (bf16[384,1024]{1,0:T(8,128)(2,1)}, f32[384,1024]{1,0:T(8,128)}, bf16[384,1024]{1,0:T(8,128)(2,1)}, bf16[384,4096]{1,0:T(8,128)(2,1)}, f32[384,...) custom-call(s32[19]{0:T(128)} %stack.112.ids, ...), custom_call_target="tpu_custom_call" | custom-call | flops 7247757312 | bytes 24159192 | tf_op jit(solution)/shard_map/pallas_call | solution.py:767
  266.3 19.1 %shard_map.344 = (bf16[384,4096]{1,0:T(8,128)(2,1)}, f32[384,1024]{1,0:T(8,128)}, bf16[384,1024]{1,0:T(8,128)(2,1)}, bf16[384,256]{1,0:T(8,128)(2,1)}, bf16[384,...) custom-call(s32[19]{0:T(128)} %stack.112.ids, ...), custom_call_target="tpu_custom_call" | custom-call | flops 7247757312 | bytes 24159192 | tf_op jit(solution)/shard_map/pallas_call | solution.py:808
  285.5 8.1 %shard_map.354 = bf16[4,128,5120]{2,1,0:T(8,128)(2,1)} custom-call(s32[19]{0:T(128)} %stack.112.ids, bf16[384,1024]{1,0:T(8,128)(2,1)} %get-tuple-element.155.refs_0_, bf16[384,4096]{1,0:T(8,128)(2,1)} %get-tuple-element.156.refs_1_, bf16[384,1024]{1,0:T(8,128)(2,1)} %get-tuple-element.157.refs_2_, bf16[384,1024]{1,0:T(8,128)(2,1)} %get-tuple-element.158.refs_3_), custom_call_target="tpu_custom_call" | custom-call | flops 2013265920 | bytes 4026531 | tf_op jit(solution)/shard_map/pallas_call | solution.py:547
  293.6 6.7 %shard_map.360 = bf16[4,512,1024]{2,1,0:T(8,128)(2,1)} custom-call(s32[19]{0:T(128)} %stack.112.ids, bf16[384,4096]{1,0:T(8,128)(2,1)} %get-tuple-element.175.refs_0_, bf16[384,1024]{1,0:T(8,128)(2,1)} %get-tuple-element.117.refs_0_.refs_1_), custom_call_target="tpu_custom_call" | custom-call | flops 1610612736 | bytes 3221225 | tf_op jit(solution)/shard_map/pallas_call | solution.py:547
  300.8 2.6 collective-permute-start.121
  310.6 2.8 collective-permute-start.44
  315.1 4.2 collective-permute-done.43.refs_1_
  319.8 7.0 %collective-permute-done.44.refs_2_ = bf16[384,256]{1,0:T(8,128)(2,1)S(1)} collective-permute-done((bf16[384,256]{1,0:T(8,128)(2,1)S(1)}, bf16[384,256]{1,0:T(8,128)(2,1)S(1)}, u32[]{:S(2)}, u32[]{:S(2)}) %collective-permute-start.44) | collective-permute-done | bytes 196640 | tf_op jit(solution)/shard_map/ppermute | solution.py:63
  328.4 24.9 %shard_map.346 = (bf16[384,384]{1,0:T(8,128)(2,1)}, bf16[384,384]{1,0:T(8,128)(2,1)}, bf16[384,384]{1,0:T(8,128)(2,1)}, bf16[384,384]{1,0:T(8,128)(2,1)}) custom-call(s32[19]{0:T(128)} %stack.112.ids, f32[1280,128]{1,0:T(8,128)} %broadcast_in_dim.71.bias_ref, bf16[1280,768]{1,0:T(8,128)(2,1)} %get-tuple-element.107.q_ref.k_ref.v_ref, ...), custom_call_target="tpu_custom_call" | custom-call | flops 4194304000 | bytes 3276800 | tf_op jit(solution)/shard_map/pallas_call | solution.py:277
  353.3 16.2 %shard_map.345 = (bf16[384,384]{1,0:T(8,128)(2,1)}, bf16[384,384]{1,0:T(8,128)(2,1)}, bf16[384,384]{1,0:T(8,128)(2,1)}, bf16[384,384]{1,0:T(8,128)(2,1)}) custom-call(s32[19]{0:T(128)} %stack.112.ids, f32[1280,128]{1,0:T(8,128)} %broadcast_in_dim.71.bias_ref, bf16[1280,768]{1,0:T(8,128)(2,1)} %get-tuple-element.107.q_ref.k_ref.v_ref, ...), custom_call_target="tpu_custom_call" | custom-call | flops 4194304000 | bytes 3276800 | tf_op jit(solution)/shard_map/pallas_call | solution.py:277
  369.6 7.3 %shard_map.348 = bf16[4,128,768]{2,1,0:T(8,128)(2,1)} custom-call(s32[19]{0:T(128)} %stack.112.ids, bf16[384,1024]{1,0:T(8,128)(2,1)} %copy-done, bf16[384,1024]{1,0:T(8,128)(2,1)} %copy-done.3, bf16[384,1024]{1,0:T(8,128)(2,1)} %copy-done.2, bf16[384,1024]{1,0:T(8,128)(2,1)} %copy-done.1, bf16[384,384]{1,0:T(8,128)(2,1)} %get-tuple-element.127.refs_0_.refs_4_, ...), custom_call_target="tpu_custom_call" | custom-call | flops 1207959552 | bytes 2415919 | tf_op jit(solution)/shard_map/pallas_call | solution.py:547
  383.9 3.8 collective-permute-start.49
  389.9 7.5 %collective-permute-done.49.refs_5_ = bf16[384,384]{1,0:T(8,128)(2,1)S(1)} collective-permute-done((bf16[384,384]{1,0:T(8,128)(2,1)S(1)}, bf16[384,384]{1,0:T(8,128)(2,1)S(1)}, u32[]{:S(2)}, u32[]{:S(2)}) %collective-permute-start.49) | collective-permute-done | bytes 294944 | tf_op jit(solution)/shard_map/ppermute | solution.py:63
  398.4 9.8 %collective-permute-done.50.refs_6_ = bf16[384,384]{1,0:T(8,128)(2,1)S(1)} collective-permute-done((bf16[384,384]{1,0:T(8,128)(2,1)S(1)}, bf16[384,384]{1,0:T(8,128)(2,1)S(1)}, u32[]{:S(2)}, u32[]{:S(2)}) %collective-permute-start.50) | collective-permute-done | bytes 294944 | tf_op jit(solution)/shard_map/ppermute | solution.py:63
  408.2 5.3 collective-permute-start.46
  413.6 3.4 collective-permute-start.47
  417.1 7.3 %shard_map.349 = (bf16[4,32,768]{2,1,0:T(8,128)(2,1)}, bf16[4,32,768]{2,1,0:T(8,128)(2,1)}, bf16[4,32,768]{2,1,0:T(8,128)(2,1)}, bf16[4,32,768]{2,1,0:T(8,128)(2,1)}) custom-call(s32[19]{0:T(128)} %stack.112.ids, bf16[384,1024]{1,0:T(8,128)(2,1)} %copy-done, bf16[384,1024]{1,0:T(8,128)(2,1)} %copy-done.3, bf16[384,1024]{1,0:T(8,128)(2,1)} %copy-done.2, ...), custom_call_target="tpu_custom_call" | custom-call | flops 1207959552 | bytes 2415919 | tf_op jit(solution)/shard_map/pallas_call | solution.py:547
  424.4 7.3 %shard_map.361 = (bf16[4,128,1024]{2,1,0:T(8,128)(2,1)}, bf16[4,128,1024]{2,1,0:T(8,128)(2,1)}, bf16[4,128,1024]{2,1,0:T(8,128)(2,1)}, bf16[4,128,1024]{2,1,0:T(8,128)(2,1)}) custom-call(s32[19]{0:T(128)} %stack.112.ids, bf16[384,4096]{1,0:T(8,128)(2,1)} %get-tuple-element.175.refs_0_, bf16[384,1024]{1,0:T(8,128)(2,1)} %get-tuple-element.117.refs_0_.refs_1_, ...), custom_call_target="tpu_custom_call" | custom-call | flops 1610612736 | bytes 3221225 | tf_op jit(solution)/shard_map/pallas_call | solution.py:547
  438.0 8.9 %shard_map.347 = (f32[384,1024]{1,0:T(8,128)}, f32[1,1024]{1,0:T(1,128)}) custom-call(s32[19]{0:T(128)} %stack.112.ids, bf16[384,384]{1,0:T(8,128)(2,1)} %get-tuple-element.127.refs_0_.refs_4_, bf16[384,384]{1,0:T(8,128)(2,1)} %copy-done.51, bf16[384,384]{1,0:T(8,128)(2,1)} %copy-done.52, bf16[384,384]{1,0:T(8,128)(2,1)} %copy-done.53, ...), custom_call_target="tpu_custom_call" | custom-call | flops 2415919104 | bytes 8388608 | tf_op jit(solution)/shard_map/pallas_call | solution.py:881
  446.9 4.8 collective-permute-start.130
  457.4 9.1 %shard_map.355 = (bf16[4,32,5120]{2,1,0:T(8,128)(2,1)}, bf16[4,32,5120]{2,1,0:T(8,128)(2,1)}, bf16[4,32,5120]{2,1,0:T(8,128)(2,1)}, bf16[4,32,5120]{2,1,0:T(8,128)(2,1)}) custom-call(s32[19]{0:T(128)} %stack.112.ids, bf16[384,1024]{1,0:T(8,128)(2,1)} %get-tuple-element.155.refs_0_, bf16[384,4096]{1,0:T(8,128)(2,1)} %get-tuple-element.156.refs_1_, ...), custom_call_target="tpu_custom_call" | custom-call | flops 2013265920 | bytes 4026531 | tf_op jit(solution)/shard_map/pallas_call | solution.py:547
  468.2 2.9 collective-permute-start.132
  474.5 23.2 %collective-permute-done.55.got_one = bf16[4,16,768]{2,1,0:T(8,128)(2,1)S(1)} collective-permute-done((bf16[4,16,768]{2,1,0:T(8,128)(2,1)}, bf16[4,16,768]{2,1,0:T(8,128)(2,1)S(1)}, u32[]{:S(2)}, u32[]{:S(2)}) %collective-permute-start.55) | collective-permute-done | bytes 98336 | tf_op jit(solution)/shard_map/ppermute | solution.py:58
  498.9 3.6 collective-permute-done.56.got_two
  506.9 4.1 collective-permute-done.57.refs_1_
  511.0 5.5 collective-permute-done.58.refs_2_
  517.6 3.2 collective-permute-done.59.refs_3_
  527.8 3.9 shard_map.362
  535.4 7.5 %collective-permute-done.63.refs_5_ = bf16[16,3072]{1,0:T(8,128)(2,1)S(1)} collective-permute-done((bf16[16,3072]{1,0:T(8,128)(2,1)S(1)}, bf16[16,3072]{1,0:T(8,128)(2,1)S(1)}, u32[]{:S(2)}, u32[]{:S(2)}) %collective-permute-start.63) | collective-permute-done | bytes 98336 | tf_op jit(solution)/shard_map/ppermute | solution.py:58
  544.0 3.6 collective-permute-done.66.refs_8_
  553.2 4.5 shard_map.356
  559.9 2.6 shard_map.363
  563.0 3.3 collective-permute-start.102
  566.8 7.2 %collective-permute-done.101.refs_1_ = bf16[2,64,1024]{2,1,0:T(8,128)(2,1)S(1)} collective-permute-done((bf16[2,64,1024]{2,1,0:T(8,128)(2,1)}, bf16[2,64,1024]{2,1,0:T(8,128)(2,1)S(1)}, u32[]{:S(2)}, u32[]{:S(2)}) %collective-permute-start.101) | collective-permute-done | bytes 262176 | tf_op jit(solution)/shard_map/ppermute | solution.py:63
  574.0 9.4 %collective-permute-done.102.refs_2_ = bf16[2,64,1024]{2,1,0:T(8,128)(2,1)S(1)} collective-permute-done((bf16[2,64,1024]{2,1,0:T(8,128)(2,1)}, bf16[2,64,1024]{2,1,0:T(8,128)(2,1)S(1)}, u32[]{:S(2)}, u32[]{:S(2)}) %collective-permute-start.102) | collective-permute-done | bytes 262176 | tf_op jit(solution)/shard_map/ppermute | solution.py:63
  594.3 3.0 shard_map.357
  597.3 5.6 collective-permute-start.79
  611.7 13.2 %collective-permute-done.80.refs_2_ = bf16[2,16,5120]{2,1,0:T(8,128)(2,1)S(1)} collective-permute-done((bf16[2,16,5120]{2,1,0:T(8,128)(2,1)}, bf16[2,16,5120]{2,1,0:T(8,128)(2,1)S(1)}, u32[]{:S(2)}, u32[]{:S(2)}) %collective-permute-start.80) | collective-permute-done | bytes 327712 | tf_op jit(solution)/shard_map/ppermute | solution.py:63
  633.0 6.2 collective-permute-done.84.refs_4_
  642.7 3.2 collective-permute-done.92.refs_12_
  648.8 3.3 shard_map.353
  652.3 3.9 shard_map.365
  657.8 4.5 shard_map.359
  (595 shorter events, 147.0 us)
Async XLA Ops:
  3.5 16.6 %collective-permute-start = (bf16[2,16,7168]{2,1,0:T(8,128)(2,1)S(1)}, bf16[2,16,7168]{2,1,0:T(8,128)(2,1)S(1)}, u32[]{:S(2)}, u32[]{:S(2)}) collective-permute-start(bf16[2,16,7168]{2,1,0:T(8,128)(2,1)S(1)} %pad_maximum_fusion.2), channel_id=1, source_target_pairs={{0,1},{1,2},{2,3},{3,0},{4,5},{5,6},{6,7},{7,4},{8,9},{9,10},{10,1... | collective-permute-start | bytes 1376264 | tf_op jit(solution)/shard_map/ppermute | solution.py:63
  6.5 32.3 %collective-permute-start.1 = (bf16[2,16,7168]{2,1,0:T(8,128)(2,1)S(1)}, bf16[2,16,7168]{2,1,0:T(8,128)(2,1)S(1)}, u32[]{:S(2)}, u32[]{:S(2)}) collective-permute-start(bf16[2,16,7168]{2,1,0:T(8,128)(2,1)S(1)} %pad_maximum_fusion.2), channel_id=1, source_target_pairs={{0,2},{1,3},{2,0},{3,1},{4,6},{5,7},{6,4},{7,5},{8,10},{9,11},{10,... | collective-permute-start | bytes 1376264 | tf_op jit(solution)/shard_map/ppermute | solution.py:63
  9.1 29.8 %collective-permute-start.2 = (bf16[2,16,7168]{2,1,0:T(8,128)(2,1)S(1)}, bf16[2,16,7168]{2,1,0:T(8,128)(2,1)S(1)}, u32[]{:S(2)}, u32[]{:S(2)}) collective-permute-start(bf16[2,16,7168]{2,1,0:T(8,128)(2,1)S(1)} %pad_maximum_fusion.2), channel_id=1, source_target_pairs={{0,3},{1,0},{2,1},{3,2},{4,7},{5,4},{6,5},{7,6},{8,11},{9,8},{10,9... | collective-permute-start | bytes 1376264 | tf_op jit(solution)/shard_map/ppermute | solution.py:63
  39.0 20.1 %collective-permute-start.3 = (bf16[2,80,1024]{2,1,0:T(8,128)(2,1)S(1)}, bf16[2,80,1024]{2,1,0:T(8,128)(2,1)S(1)}, u32[]{:S(2)}, u32[]{:S(2)}) collective-permute-start(bf16[2,80,1024]{2,1,0:T(8,128)(2,1)S(1)} %pad_maximum_fusion.3), channel_id=1, source_target_pairs={{0,1},{1,2},{2,3},{3,0},{4,5},{5,6},{6,7},{7,4},{8,9},{9,10},{10,1... | collective-permute-start | bytes 983048 | tf_op jit(solution)/shard_map/ppermute | solution.py:63
  49.5 26.9 %collective-permute-start.11 = (bf16[3,16,7168]{2,1,0:T(8,128)(2,1)S(1)}, bf16[3,16,7168]{2,1,0:T(8,128)(2,1)S(1)}, u32[]{:S(2)}, u32[]{:S(2)}) collective-permute-start(bf16[3,16,7168]{2,1,0:T(8,128)(2,1)S(1)} %get-tuple-element.193.refs_7_.refs_20_.refs_9_.refs_12_), channel_id=1, source_target_pairs={{0,8},{4,12},{8,0},{12,4},{16,24},{20,28},{24,16},{28,20},{1,9},{5... | collective-permute-start | bytes 2064392 | tf_op jit(solution)/shard_map/ppermute | solution.py:58
  51.1 20.4 %collective-permute-start.4 = (bf16[2,80,1024]{2,1,0:T(8,128)(2,1)S(1)}, bf16[2,80,1024]{2,1,0:T(8,128)(2,1)S(1)}, u32[]{:S(2)}, u32[]{:S(2)}) collective-permute-start(bf16[2,80,1024]{2,1,0:T(8,128)(2,1)S(1)} %pad_maximum_fusion.3), channel_id=1, source_target_pairs={{0,2},{1,3},{2,0},{3,1},{4,6},{5,7},{6,4},{7,5},{8,10},{9,11},{10,... | collective-permute-start | bytes 983048 | tf_op jit(solution)/shard_map/ppermute | solution.py:63
  52.7 20.3 %collective-permute-start.5 = (bf16[2,80,1024]{2,1,0:T(8,128)(2,1)S(1)}, bf16[2,80,1024]{2,1,0:T(8,128)(2,1)S(1)}, u32[]{:S(2)}, u32[]{:S(2)}) collective-permute-start(bf16[2,80,1024]{2,1,0:T(8,128)(2,1)S(1)} %pad_maximum_fusion.3), channel_id=1, source_target_pairs={{0,3},{1,0},{2,1},{3,2},{4,7},{5,4},{6,5},{7,6},{8,11},{9,8},{10,9... | collective-permute-start | bytes 983048 | tf_op jit(solution)/shard_map/ppermute | solution.py:63
  53.5 23.6 %collective-permute-start.16 = (bf16[3,16,7168]{2,1,0:T(8,128)(2,1)S(1)}, bf16[3,16,7168]{2,1,0:T(8,128)(2,1)S(1)}, u32[]{:S(2)}, u32[]{:S(2)}) collective-permute-start(bf16[3,16,7168]{2,1,0:T(8,128)(2,1)S(1)} %get-tuple-element.192.refs_8_.refs_21_.refs_10_.refs_13_), channel_id=1, source_target_pairs={{0,16},{4,20},{8,24},{12,28},{16,0},{20,4},{24,8},{28,12},{1,17},{... | collective-permute-start | bytes 2064392 | tf_op jit(solution)/shard_map/ppermute | solution.py:58
  59.2 23.5 %collective-permute-start.12 = (bf16[3,16,7168]{2,1,0:T(8,128)(2,1)S(1)}, bf16[3,16,7168]{2,1,0:T(8,128)(2,1)S(1)}, u32[]{:S(2)}, u32[]{:S(2)}) collective-permute-start(bf16[3,16,7168]{2,1,0:T(8,128)(2,1)S(1)} %get-tuple-element.192.refs_8_.refs_21_.refs_10_.refs_13_), channel_id=1, source_target_pairs={{0,8},{4,12},{8,0},{12,4},{16,24},{20,28},{24,16},{28,20},{1,9},{5... | collective-permute-start | bytes 2064392 | tf_op jit(solution)/shard_map/ppermute | solution.py:58
  71.4 18.4 %collective-permute-start.15 = (bf16[3,16,7168]{2,1,0:T(8,128)(2,1)S(1)}, bf16[3,16,7168]{2,1,0:T(8,128)(2,1)}, u32[]{:S(2)}, u32[]{:S(2)}) collective-permute-start(bf16[3,16,7168]{2,1,0:T(8,128)(2,1)S(1)} %get-tuple-element.193.refs_7_.refs_20_.refs_9_.refs_12_), channel_id=1, source_target_pairs={{0,16},{4,20},{8,24},{12,28},{16,0},{20,4},{24,8},{28,12},{1,17},{... | collective-permute-start | bytes 2064392 | tf_op jit(solution)/shard_map/ppermute | solution.py:58
  73.7 17.7 %collective-permute-start.10 = (bf16[3,16,7168]{2,1,0:T(8,128)(2,1)S(1)}, bf16[3,16,7168]{2,1,0:T(8,128)(2,1)}, u32[]{:S(2)}, u32[]{:S(2)}) collective-permute-start(bf16[3,16,7168]{2,1,0:T(8,128)(2,1)S(1)} %get-tuple-element.192.refs_8_.refs_21_.refs_10_.refs_13_), channel_id=1, source_target_pairs={{0,4},{4,0},{8,12},{12,8},{16,20},{20,16},{24,28},{28,24},{1,5},{5... | collective-permute-start | bytes 2064392 | tf_op jit(solution)/shard_map/ppermute | solution.py:58
  76.4 18.0 %collective-permute-start.9 = (bf16[3,16,7168]{2,1,0:T(8,128)(2,1)S(1)}, bf16[3,16,7168]{2,1,0:T(8,128)(2,1)S(1)}, u32[]{:S(2)}, u32[]{:S(2)}) collective-permute-start(bf16[3,16,7168]{2,1,0:T(8,128)(2,1)S(1)} %get-tuple-element.193.refs_7_.refs_20_.refs_9_.refs_12_), channel_id=1, source_target_pairs={{0,4},{4,0},{8,12},{12,8},{16,20},{20,16},{24,28},{28,24},{1,5},{5... | collective-permute-start | bytes 2064392 | tf_op jit(solution)/shard_map/ppermute | solution.py:58
  77.1 17.4 %collective-permute-start.31 = (bf16[3,80,1024]{2,1,0:T(8,128)(2,1)S(1)}, bf16[3,80,1024]{2,1,0:T(8,128)(2,1)}, u32[]{:S(2)}, u32[]{:S(2)}) collective-permute-start(bf16[3,80,1024]{2,1,0:T(8,128)(2,1)S(1)} %get-tuple-element.195.refs_36_.refs_25_), channel_id=1, source_target_pairs={{0,8},{4,12},{8,0},{12,4},{16,24},{20,28},{24,16},{28,20},{1,9},{5... | collective-permute-start | bytes 1474568 | tf_op jit(solution)/shard_map/ppermute | solution.py:58
  82.7 18.4 %collective-permute-start.36 = (bf16[3,80,1024]{2,1,0:T(8,128)(2,1)S(1)}, bf16[3,80,1024]{2,1,0:T(8,128)(2,1)S(1)}, u32[]{:S(2)}, u32[]{:S(2)}) collective-permute-start(bf16[3,80,1024]{2,1,0:T(8,128)(2,1)S(1)} %get-tuple-element.194.refs_37_.refs_26_), channel_id=1, source_target_pairs={{0,16},{4,20},{8,24},{12,28},{16,0},{20,4},{24,8},{28,12},{1,17},{... | collective-permute-start | bytes 1474568 | tf_op jit(solution)/shard_map/ppermute | solution.py:58
  89.9 14.6 %collective-permute-start.32 = (bf16[3,80,1024]{2,1,0:T(8,128)(2,1)S(1)}, bf16[3,80,1024]{2,1,0:T(8,128)(2,1)S(1)}, u32[]{:S(2)}, u32[]{:S(2)}) collective-permute-start(bf16[3,80,1024]{2,1,0:T(8,128)(2,1)S(1)} %get-tuple-element.194.refs_37_.refs_26_), channel_id=1, source_target_pairs={{0,8},{4,12},{8,0},{12,4},{16,24},{20,28},{24,16},{28,20},{1,9},{5... | collective-permute-start | bytes 1474568 | tf_op jit(solution)/shard_map/ppermute | solution.py:58
  91.4 18.8 %collective-permute-start.35 = (bf16[3,80,1024]{2,1,0:T(8,128)(2,1)S(1)}, bf16[3,80,1024]{2,1,0:T(8,128)(2,1)S(1)}, u32[]{:S(2)}, u32[]{:S(2)}) collective-permute-start(bf16[3,80,1024]{2,1,0:T(8,128)(2,1)S(1)} %get-tuple-element.195.refs_36_.refs_25_), channel_id=1, source_target_pairs={{0,16},{4,20},{8,24},{12,28},{16,0},{20,4},{24,8},{28,12},{1,17},{... | collective-permute-start | bytes 1474568 | tf_op jit(solution)/shard_map/ppermute | solution.py:58
  94.4 15.8 %collective-permute-start.29 = (bf16[3,80,1024]{2,1,0:T(8,128)(2,1)S(1)}, bf16[3,80,1024]{2,1,0:T(8,128)(2,1)S(1)}, u32[]{:S(2)}, u32[]{:S(2)}) collective-permute-start(bf16[3,80,1024]{2,1,0:T(8,128)(2,1)S(1)} %get-tuple-element.195.refs_36_.refs_25_), channel_id=1, source_target_pairs={{0,4},{4,0},{8,12},{12,8},{16,20},{20,16},{24,28},{28,24},{1,5},{5... | collective-permute-start | bytes 1474568 | tf_op jit(solution)/shard_map/ppermute | solution.py:58
  94.5 27.9 %collective-permute-start.6 = (bf16[384,1024]{1,0:T(8,128)(2,1)S(1)}, bf16[384,1024]{1,0:T(8,128)(2,1)S(1)}, u32[]{:S(2)}, u32[]{:S(2)}) collective-permute-start(bf16[384,1024]{1,0:T(8,128)(2,1)S(1)} %get-tuple-element.106.refs_0_.refs_8_), channel_id=1, source_target_pairs={{0,1},{1,2},{2,3},{3,0},{4,5},{5,6},{6,7},{7,4},{8,9},{9,10},{10,1... | collective-permute-start | bytes 2359304 | tf_op jit(solution)/shard_map/ppermute | solution.py:63
  101.1 54.7 %collective-permute-start.7 = (bf16[384,1024]{1,0:T(8,128)(2,1)S(1)}, bf16[384,1024]{1,0:T(8,128)(2,1)S(1)}, u32[]{:S(2)}, u32[]{:S(2)}) collective-permute-start(bf16[384,1024]{1,0:T(8,128)(2,1)S(1)} %get-tuple-element.106.refs_0_.refs_8_), channel_id=1, source_target_pairs={{0,2},{1,3},{2,0},{3,1},{4,6},{5,7},{6,4},{7,5},{8,10},{9,11},{10,... | collective-permute-start | bytes 2359304 | tf_op jit(solution)/shard_map/ppermute | solution.py:63
  104.4 51.4 %collective-permute-start.8 = (bf16[384,1024]{1,0:T(8,128)(2,1)S(1)}, bf16[384,1024]{1,0:T(8,128)(2,1)S(1)}, u32[]{:S(2)}, u32[]{:S(2)}) collective-permute-start(bf16[384,1024]{1,0:T(8,128)(2,1)S(1)} %get-tuple-element.106.refs_0_.refs_8_), channel_id=1, source_target_pairs={{0,3},{1,0},{2,1},{3,2},{4,7},{5,4},{6,5},{7,6},{8,11},{9,8},{10,9... | collective-permute-start | bytes 2359304 | tf_op jit(solution)/shard_map/ppermute | solution.py:63
  110.2 46.2 %collective-permute-start.39 = (bf16[3,80,1024]{2,1,0:T(8,128)(2,1)}, bf16[3,80,1024]{2,1,0:T(8,128)(2,1)S(1)}, u32[]{:S(2)}, u32[]{:S(2)}) collective-permute-start(bf16[3,80,1024]{2,1,0:T(8,128)(2,1)} %collective-permute-done.31.refs_40_.refs_29_), channel_id=1, source_target_pairs={{0,16},{4,20},{8,24},{12,28},{16,0},{20,4},{24,8},{28,12},{1,17},{... | collective-permute-start | bytes 1474568 | tf_op jit(solution)/shard_map/ppermute | solution.py:58
  112.1 58.8 %collective-permute-start.19 = (bf16[3,16,7168]{2,1,0:T(8,128)(2,1)}, bf16[3,16,7168]{2,1,0:T(8,128)(2,1)}, u32[]{:S(2)}, u32[]{:S(2)}) collective-permute-start(bf16[3,16,7168]{2,1,0:T(8,128)(2,1)} %copy-done.6), channel_id=1, source_target_pairs={{0,16},{4,20},{8,24},{12,28},{16,0},{20,4},{24,8},{28,12},{1,17},{... | collective-permute-start | bytes 2064392 | tf_op jit(solution)/shard_map/ppermute | solution.py:58
  122.4 48.5 %collective-permute-start.20 = (bf16[3,16,7168]{2,1,0:T(8,128)(2,1)}, bf16[3,16,7168]{2,1,0:T(8,128)(2,1)}, u32[]{:S(2)}, u32[]{:S(2)}) collective-permute-start(bf16[3,16,7168]{2,1,0:T(8,128)(2,1)} %copy-done.7), channel_id=1, source_target_pairs={{0,8},{4,12},{8,0},{12,4},{16,24},{20,28},{24,16},{28,20},{1,9},{5... | collective-permute-start | bytes 2064392 | tf_op jit(solution)/shard_map/ppermute | solution.py:58
  155.8 15.5 %collective-permute-start.13 = (bf16[3,16,7168]{2,1,0:T(8,128)(2,1)}, bf16[3,16,7168]{2,1,0:T(8,128)(2,1)}, u32[]{:S(2)}, u32[]{:S(2)}) collective-permute-start(bf16[3,16,7168]{2,1,0:T(8,128)(2,1)} %copy-done.6), channel_id=1, source_target_pairs={{0,4},{4,0},{8,12},{12,8},{16,20},{20,16},{24,28},{28,24},{1,5},{5... | collective-permute-start | bytes 2064392 | tf_op jit(solution)/shard_map/ppermute | solution.py:58
  174.3 22.9 %collective-permute-start.34 = (bf16[3,80,1024]{2,1,0:T(8,128)(2,1)}, bf16[3,80,1024]{2,1,0:T(8,128)(2,1)}, u32[]{:S(2)}, u32[]{:S(2)}) collective-permute-start(bf16[3,80,1024]{2,1,0:T(8,128)(2,1)} %copy-done.32), channel_id=1, source_target_pairs={{0,4},{4,0},{8,12},{12,8},{16,20},{20,16},{24,28},{28,24},{1,5},{5... | collective-permute-start | bytes 1474568 | tf_op jit(solution)/shard_map/ppermute | solution.py:58
  176.7 48.8 %collective-permute-start.38 = (bf16[3,80,1024]{2,1,0:T(8,128)(2,1)}, bf16[3,80,1024]{2,1,0:T(8,128)(2,1)S(1)}, u32[]{:S(2)}, u32[]{:S(2)}) collective-permute-start(bf16[3,80,1024]{2,1,0:T(8,128)(2,1)} %copy-done.31), channel_id=1, source_target_pairs={{0,4},{4,0},{8,12},{12,8},{16,20},{20,16},{24,28},{28,24},{1,5},{5... | collective-permute-start | bytes 1474568 | tf_op jit(solution)/shard_map/ppermute | solution.py:58
  176.8 48.6 %collective-permute-start.37 = (bf16[3,80,1024]{2,1,0:T(8,128)(2,1)}, bf16[3,80,1024]{2,1,0:T(8,128)(2,1)S(1)}, u32[]{:S(2)}, u32[]{:S(2)}) collective-permute-start(bf16[3,80,1024]{2,1,0:T(8,128)(2,1)} %copy-done.33), channel_id=1, source_target_pairs={{0,4},{4,0},{8,12},{12,8},{16,20},{20,16},{24,28},{28,24},{1,5},{5... | collective-permute-start | bytes 1474568 | tf_op jit(solution)/shard_map/ppermute | solution.py:58
  177.2 50.6 %collective-permute-start.41 = (bf16[3,80,1024]{2,1,0:T(8,128)(2,1)}, bf16[3,80,1024]{2,1,0:T(8,128)(2,1)S(1)}, u32[]{:S(2)}, u32[]{:S(2)}) collective-permute-start(bf16[3,80,1024]{2,1,0:T(8,128)(2,1)} %copy-done.36), channel_id=1, source_target_pairs={{0,4},{4,0},{8,12},{12,8},{16,20},{20,16},{24,28},{28,24},{1,5},{5... | collective-permute-start | bytes 1474568 | tf_op jit(solution)/shard_map/ppermute | solution.py:58
  177.3 50.6 %collective-permute-start.42 = (bf16[3,80,1024]{2,1,0:T(8,128)(2,1)}, bf16[3,80,1024]{2,1,0:T(8,128)(2,1)S(1)}, u32[]{:S(2)}, u32[]{:S(2)}) collective-permute-start(bf16[3,80,1024]{2,1,0:T(8,128)(2,1)} %copy-done.37), channel_id=1, source_target_pairs={{0,4},{4,0},{8,12},{12,8},{16,20},{20,16},{24,28},{28,24},{1,5},{5... | collective-permute-start | bytes 1474568 | tf_op jit(solution)/shard_map/ppermute | solution.py:58
  197.3 33.2 %collective-permute-start.26 = (bf16[384,128]{1,0:T(8,128)(2,1)}, bf16[384,128]{1,0:T(8,128)(2,1)S(1)}, u32[]{:S(2)}, u32[]{:S(2)}) collective-permute-start(bf16[384,128]{1,0:T(8,128)(2,1)} %get-tuple-element.113), channel_id=1, source_target_pairs={{0,1},{1,2},{2,3},{3,0},{4,5},{5,6},{6,7},{7,4},{8,9},{9,10},{10,1... | collective-permute-start | bytes 294920 | tf_op jit(solution)/shard_map/ppermute | solution.py:63
  293.6 161.4 %collective-permute-start.74 = (bf16[4,128,5120]{2,1,0:T(8,128)(2,1)}, bf16[4,128,5120]{2,1,0:T(8,128)(2,1)S(1)}, u32[]{:S(2)}, u32[]{:S(2)}) collective-permute-start(bf16[4,128,5120]{2,1,0:T(8,128)(2,1)} %shard_map.354), channel_id=1, source_target_pairs={{0,4},{4,0},{8,12},{12,8},{16,20},{20,16},{24,28},{28,24},{1,5},{5... | collective-permute-start | bytes 15728648 | tf_op jit(solution)/shard_map/ppermute | solution.py:58
  300.3 116.6 %collective-permute-start.96 = (bf16[4,512,1024]{2,1,0:T(8,128)(2,1)}, bf16[4,512,1024]{2,1,0:T(8,128)(2,1)}, u32[]{:S(2)}, u32[]{:S(2)}) collective-permute-start(bf16[4,512,1024]{2,1,0:T(8,128)(2,1)} %shard_map.360), channel_id=1, source_target_pairs={{0,4},{4,0},{8,12},{12,8},{16,20},{20,16},{24,28},{28,24},{1,5},{5... | collective-permute-start | bytes 12582920 | tf_op jit(solution)/shard_map/ppermute | solution.py:58
  310.6 16.2 %collective-permute-start.44 = (bf16[384,256]{1,0:T(8,128)(2,1)S(1)}, bf16[384,256]{1,0:T(8,128)(2,1)S(1)}, u32[]{:S(2)}, u32[]{:S(2)}) collective-permute-start(bf16[384,256]{1,0:T(8,128)(2,1)S(1)} %copy-done.135), channel_id=1, source_target_pairs={{0,2},{1,3},{2,0},{3,1},{4,6},{5,7},{6,4},{7,5},{8,10},{9,11},{10,... | collective-permute-start | bytes 589832 | tf_op jit(solution)/shard_map/ppermute | solution.py:63
  313.4 13.9 %collective-permute-start.45 = (bf16[384,256]{1,0:T(8,128)(2,1)S(1)}, bf16[384,256]{1,0:T(8,128)(2,1)S(1)}, u32[]{:S(2)}, u32[]{:S(2)}) collective-permute-start(bf16[384,256]{1,0:T(8,128)(2,1)S(1)} %copy-done.134), channel_id=1, source_target_pairs={{0,3},{1,0},{2,1},{3,2},{4,7},{5,4},{6,5},{7,6},{8,11},{9,8},{10,9... | collective-permute-start | bytes 589832 | tf_op jit(solution)/shard_map/ppermute | solution.py:63
  319.3 58.9 %collective-permute-start.128 = (f32[2,1]{0,1:T(1,128)S(1)}, f32[2,1]{0,1:T(1,128)S(1)}, u32[]{:S(2)}, u32[]{:S(2)}) collective-permute-start(f32[2,1]{0,1:T(1,128)S(1)} %pad_maximum_fusion.8), channel_id=1, source_target_pairs={{0,8},{4,12},{8,0},{12,4},{16,24},{20,28},{24,16},{28,20},{1,9},{5... | collective-permute-start | bytes 32 | tf_op jit(solution)/shard_map/ppermute | solution.py:58
  326.8 52.1 %collective-permute-start.125 = (f32[16,256]{1,0:T(8,128)S(1)}, f32[16,256]{1,0:T(8,128)S(1)}, u32[]{:S(2)}, u32[]{:S(2)}) collective-permute-start(f32[16,256]{1,0:T(8,128)S(1)} %add.275), channel_id=1, source_target_pairs={{0,8},{4,12},{8,0},{12,4},{16,24},{20,28},{24,16},{28,20},{1,9},{5... | collective-permute-start | bytes 49160 | tf_op jit(solution)/shard_map/ppermute | solution.py:58
  376.9 36.7 %collective-permute-start.52 = (bf16[4,128,768]{2,1,0:T(8,128)(2,1)}, bf16[4,128,768]{2,1,0:T(8,128)(2,1)S(1)}, u32[]{:S(2)}, u32[]{:S(2)}) collective-permute-start(bf16[4,128,768]{2,1,0:T(8,128)(2,1)} %shard_map.348), channel_id=1, source_target_pairs={{0,4},{4,0},{8,12},{12,8},{16,20},{20,16},{24,28},{28,24},{1,5},{5... | collective-permute-start | bytes 2359304 | tf_op jit(solution)/shard_map/ppermute | solution.py:58
  387.7 20.5 %collective-permute-start.50 = (bf16[384,384]{1,0:T(8,128)(2,1)S(1)}, bf16[384,384]{1,0:T(8,128)(2,1)S(1)}, u32[]{:S(2)}, u32[]{:S(2)}) collective-permute-start(bf16[384,384]{1,0:T(8,128)(2,1)S(1)} %copy-done.18), channel_id=1, source_target_pairs={{0,2},{1,3},{2,0},{3,1},{4,6},{5,7},{6,4},{7,5},{8,10},{9,11},{10,... | collective-permute-start | bytes 884744 | tf_op jit(solution)/shard_map/ppermute | solution.py:63
  397.3 34.3 %collective-permute-start.51 = (bf16[384,384]{1,0:T(8,128)(2,1)S(1)}, bf16[384,384]{1,0:T(8,128)(2,1)S(1)}, u32[]{:S(2)}, u32[]{:S(2)}) collective-permute-start(bf16[384,384]{1,0:T(8,128)(2,1)S(1)} %copy-done.16), channel_id=1, source_target_pairs={{0,3},{1,0},{2,1},{3,2},{4,7},{5,4},{6,5},{7,6},{8,11},{9,8},{10,9... | collective-permute-start | bytes 884744 | tf_op jit(solution)/shard_map/ppermute | solution.py:63
  408.2 24.9 %collective-permute-start.46 = (bf16[384,384]{1,0:T(8,128)(2,1)S(1)}, bf16[384,384]{1,0:T(8,128)(2,1)S(1)}, u32[]{:S(2)}, u32[]{:S(2)}) collective-permute-start(bf16[384,384]{1,0:T(8,128)(2,1)S(1)} %copy-done.15), channel_id=1, source_target_pairs={{0,1},{1,2},{2,3},{3,0},{4,5},{5,6},{6,7},{7,4},{8,9},{9,10},{10,1... | collective-permute-start | bytes 884744 | tf_op jit(solution)/shard_map/ppermute | solution.py:63
  413.6 21.5 %collective-permute-start.47 = (bf16[384,384]{1,0:T(8,128)(2,1)S(1)}, bf16[384,384]{1,0:T(8,128)(2,1)S(1)}, u32[]{:S(2)}, u32[]{:S(2)}) collective-permute-start(bf16[384,384]{1,0:T(8,128)(2,1)S(1)} %copy-done.14), channel_id=1, source_target_pairs={{0,2},{1,3},{2,0},{3,1},{4,6},{5,7},{6,4},{7,5},{8,10},{9,11},{10,... | collective-permute-start | bytes 884744 | tf_op jit(solution)/shard_map/ppermute | solution.py:63
  417.0 19.2 %collective-permute-start.48 = (bf16[384,384]{1,0:T(8,128)(2,1)S(1)}, bf16[384,384]{1,0:T(8,128)(2,1)S(1)}, u32[]{:S(2)}, u32[]{:S(2)}) collective-permute-start(bf16[384,384]{1,0:T(8,128)(2,1)S(1)} %copy-done.13), channel_id=1, source_target_pairs={{0,3},{1,0},{2,1},{3,2},{4,7},{5,4},{6,5},{7,6},{8,11},{9,8},{10,9... | collective-permute-start | bytes 884744 | tf_op jit(solution)/shard_map/ppermute | solution.py:63
  431.6 15.3 %collective-permute-start.120 = (f32[2,384]{1,0:T(2,128)S(1)}, f32[2,384]{1,0:T(2,128)S(1)}, u32[]{:S(2)}, u32[]{:S(2)}) collective-permute-start(f32[2,384]{1,0:T(2,128)S(1)} %fusion.19), channel_id=1, source_target_pairs={{0,16},{4,20},{8,24},{12,28},{16,0},{20,4},{24,8},{28,12},{1,17},{... | collective-permute-start | bytes 9224 | tf_op jit(solution)/shard_map/ppermute | solution.py:58
  433.2 34.2 %collective-permute-start.53 = (bf16[4,32,768]{2,1,0:T(8,128)(2,1)}, bf16[4,32,768]{2,1,0:T(8,128)(2,1)S(1)}, u32[]{:S(2)}, u32[]{:S(2)}) collective-permute-start(bf16[4,32,768]{2,1,0:T(8,128)(2,1)} %get-tuple-element.139), channel_id=1, source_target_pairs={{0,8},{4,12},{8,0},{12,4},{16,24},{20,28},{24,16},{28,20},{1,9},{5... | collective-permute-start | bytes 589832 | tf_op jit(solution)/shard_map/ppermute | solution.py:58
  435.1 90.6 %collective-permute-start.97 = (bf16[4,128,1024]{2,1,0:T(8,128)(2,1)}, bf16[4,128,1024]{2,1,0:T(8,128)(2,1)S(1)}, u32[]{:S(2)}, u32[]{:S(2)}) collective-permute-start(bf16[4,128,1024]{2,1,0:T(8,128)(2,1)} %get-tuple-element.177), channel_id=1, source_target_pairs={{0,8},{4,12},{8,0},{12,4},{16,24},{20,28},{24,16},{28,20},{1,9},{5... | collective-permute-start | bytes 3145736 | tf_op jit(solution)/shard_map/ppermute | solution.py:58
  436.9 89.6 %collective-permute-start.98 = (bf16[4,128,1024]{2,1,0:T(8,128)(2,1)}, bf16[4,128,1024]{2,1,0:T(8,128)(2,1)S(1)}, u32[]{:S(2)}, u32[]{:S(2)}) collective-permute-start(bf16[4,128,1024]{2,1,0:T(8,128)(2,1)} %get-tuple-element.179), channel_id=1, source_target_pairs={{0,16},{4,20},{8,24},{12,28},{16,0},{20,4},{24,8},{28,12},{1,17},{... | collective-permute-start | bytes 3145736 | tf_op jit(solution)/shard_map/ppermute | solution.py:58
  466.5 84.7 %collective-permute-start.75 = (bf16[4,32,5120]{2,1,0:T(8,128)(2,1)}, bf16[4,32,5120]{2,1,0:T(8,128)(2,1)S(1)}, u32[]{:S(2)}, u32[]{:S(2)}) collective-permute-start(bf16[4,32,5120]{2,1,0:T(8,128)(2,1)} %get-tuple-element.160), channel_id=1, source_target_pairs={{0,8},{4,12},{8,0},{12,4},{16,24},{20,28},{24,16},{28,20},{1,9},{5... | collective-permute-start | bytes 3932168 | tf_op jit(solution)/shard_map/ppermute | solution.py:58
  467.4 84.7 %collective-permute-start.76 = (bf16[4,32,5120]{2,1,0:T(8,128)(2,1)}, bf16[4,32,5120]{2,1,0:T(8,128)(2,1)S(1)}, u32[]{:S(2)}, u32[]{:S(2)}) collective-permute-start(bf16[4,32,5120]{2,1,0:T(8,128)(2,1)} %get-tuple-element.162), channel_id=1, source_target_pairs={{0,16},{4,20},{8,24},{12,28},{16,0},{20,4},{24,8},{28,12},{1,17},{... | collective-permute-start | bytes 3932168 | tf_op jit(solution)/shard_map/ppermute | solution.py:58
  473.2 24.5 %collective-permute-start.55 = (bf16[4,16,768]{2,1,0:T(8,128)(2,1)}, bf16[4,16,768]{2,1,0:T(8,128)(2,1)S(1)}, u32[]{:S(2)}, u32[]{:S(2)}) collective-permute-start(bf16[4,16,768]{2,1,0:T(8,128)(2,1)} %get-tuple-element.143), channel_id=1, source_target_pairs={{0,16},{4,20},{8,24},{12,28},{16,0},{20,4},{24,8},{28,12},{1,17},{... | collective-permute-start | bytes 294920 | tf_op jit(solution)/shard_map/ppermute | solution.py:58
  532.3 25.4 %collective-permute-start.100 = (bf16[4,64,1024]{2,1,0:T(8,128)(2,1)}, bf16[4,64,1024]{2,1,0:T(8,128)(2,1)S(1)}, u32[]{:S(2)}, u32[]{:S(2)}) collective-permute-start(bf16[4,64,1024]{2,1,0:T(8,128)(2,1)} %get-tuple-element.183), channel_id=1, source_target_pairs={{0,8},{4,12},{8,0},{12,4},{16,24},{20,28},{24,16},{28,20},{1,9},{5... | collective-permute-start | bytes 1572872 | tf_op jit(solution)/shard_map/ppermute | solution.py:58
  533.2 25.7 %collective-permute-start.99 = (bf16[4,64,1024]{2,1,0:T(8,128)(2,1)}, bf16[4,64,1024]{2,1,0:T(8,128)(2,1)S(1)}, u32[]{:S(2)}, u32[]{:S(2)}) collective-permute-start(bf16[4,64,1024]{2,1,0:T(8,128)(2,1)} %get-tuple-element.181), channel_id=1, source_target_pairs={{0,16},{4,20},{8,24},{12,28},{16,0},{20,4},{24,8},{28,12},{1,17},{... | collective-permute-start | bytes 1572872 | tf_op jit(solution)/shard_map/ppermute | solution.py:58
  552.1 14.3 %collective-permute-start.64 = (bf16[16,3072]{1,0:T(8,128)(2,1)S(1)}, bf16[16,3072]{1,0:T(8,128)(2,1)}, u32[]{:S(2)}, u32[]{:S(2)}) collective-permute-start(bf16[16,3072]{1,0:T(8,128)(2,1)S(1)} %collective-permute-done.62.refs_4_), channel_id=1, source_target_pairs={{0,4},{4,0},{8,12},{12,8},{16,20},{20,16},{24,28},{28,24},{1,5},{5... | collective-permute-start | bytes 294920 | tf_op jit(solution)/shard_map/ppermute | solution.py:58
  557.7 35.5 %collective-permute-start.77 = (bf16[4,16,5120]{2,1,0:T(8,128)(2,1)}, bf16[4,16,5120]{2,1,0:T(8,128)(2,1)S(1)}, u32[]{:S(2)}, u32[]{:S(2)}) collective-permute-start(bf16[4,16,5120]{2,1,0:T(8,128)(2,1)} %get-tuple-element.164), channel_id=1, source_target_pairs={{0,16},{4,20},{8,24},{12,28},{16,0},{20,4},{24,8},{28,12},{1,17},{... | collective-permute-start | bytes 1966088 | tf_op jit(solution)/shard_map/ppermute | solution.py:58
  559.0 34.2 %collective-permute-start.78 = (bf16[4,16,5120]{2,1,0:T(8,128)(2,1)}, bf16[4,16,5120]{2,1,0:T(8,128)(2,1)S(1)}, u32[]{:S(2)}, u32[]{:S(2)}) collective-permute-start(bf16[4,16,5120]{2,1,0:T(8,128)(2,1)} %get-tuple-element.166), channel_id=1, source_target_pairs={{0,8},{4,12},{8,0},{12,4},{16,24},{20,28},{24,16},{28,20},{1,9},{5... | collective-permute-start | bytes 1966088 | tf_op jit(solution)/shard_map/ppermute | solution.py:58
  563.0 20.4 %collective-permute-start.102 = (bf16[2,64,1024]{2,1,0:T(8,128)(2,1)}, bf16[2,64,1024]{2,1,0:T(8,128)(2,1)S(1)}, u32[]{:S(2)}, u32[]{:S(2)}) collective-permute-start(bf16[2,64,1024]{2,1,0:T(8,128)(2,1)} %get-tuple-element.186), channel_id=1, source_target_pairs={{0,2},{1,3},{2,0},{3,1},{4,6},{5,7},{6,4},{7,5},{8,10},{9,11},{10,... | collective-permute-start | bytes 786440 | tf_op jit(solution)/shard_map/ppermute | solution.py:63
  566.4 17.0 %collective-permute-start.103 = (bf16[2,64,1024]{2,1,0:T(8,128)(2,1)}, bf16[2,64,1024]{2,1,0:T(8,128)(2,1)S(1)}, u32[]{:S(2)}, u32[]{:S(2)}) collective-permute-start(bf16[2,64,1024]{2,1,0:T(8,128)(2,1)} %get-tuple-element.187), channel_id=1, source_target_pairs={{0,3},{1,0},{2,1},{3,2},{4,7},{5,4},{6,5},{7,6},{8,11},{9,8},{10,9... | collective-permute-start | bytes 786440 | tf_op jit(solution)/shard_map/ppermute | solution.py:63
  597.3 14.0 %collective-permute-start.79 = (bf16[2,16,5120]{2,1,0:T(8,128)(2,1)}, bf16[2,16,5120]{2,1,0:T(8,128)(2,1)S(1)}, u32[]{:S(2)}, u32[]{:S(2)}) collective-permute-start(bf16[2,16,5120]{2,1,0:T(8,128)(2,1)} %get-tuple-element.168), channel_id=1, source_target_pairs={{0,1},{1,2},{2,3},{3,0},{4,5},{5,6},{6,7},{7,4},{8,9},{9,10},{10,1... | collective-permute-start | bytes 983048 | tf_op jit(solution)/shard_map/ppermute | solution.py:63
  603.0 21.9 %collective-permute-start.80 = (bf16[2,16,5120]{2,1,0:T(8,128)(2,1)}, bf16[2,16,5120]{2,1,0:T(8,128)(2,1)S(1)}, u32[]{:S(2)}, u32[]{:S(2)}) collective-permute-start(bf16[2,16,5120]{2,1,0:T(8,128)(2,1)} %get-tuple-element.169), channel_id=1, source_target_pairs={{0,2},{1,3},{2,0},{3,1},{4,6},{5,7},{6,4},{7,5},{8,10},{9,11},{10,... | collective-permute-start | bytes 983048 | tf_op jit(solution)/shard_map/ppermute | solution.py:63
  603.0 21.8 %collective-permute-start.81 = (bf16[2,16,5120]{2,1,0:T(8,128)(2,1)}, bf16[2,16,5120]{2,1,0:T(8,128)(2,1)S(1)}, u32[]{:S(2)}, u32[]{:S(2)}) collective-permute-start(bf16[2,16,5120]{2,1,0:T(8,128)(2,1)} %get-tuple-element.170), channel_id=1, source_target_pairs={{0,3},{1,0},{2,1},{3,2},{4,7},{5,4},{6,5},{7,6},{8,11},{9,8},{10,9... | collective-permute-start | bytes 983048 | tf_op jit(solution)/shard_map/ppermute | solution.py:63
  610.6 17.5 %collective-permute-start.108 = (bf16[64,1024]{1,0:T(8,128)(2,1)S(1)}, bf16[64,1024]{1,0:T(8,128)(2,1)S(1)}, u32[]{:S(2)}, u32[]{:S(2)}) collective-permute-start(bf16[64,1024]{1,0:T(8,128)(2,1)S(1)} %collective-permute-done.106.refs_4_), channel_id=1, source_target_pairs={{0,4},{4,0},{8,12},{12,8},{16,20},{20,16},{24,28},{28,24},{1,5},{5... | collective-permute-start | bytes 393224 | tf_op jit(solution)/shard_map/ppermute | solution.py:58
  611.1 19.1 %collective-permute-start.113 = (bf16[64,1024]{1,0:T(8,128)(2,1)S(1)}, bf16[64,1024]{1,0:T(8,128)(2,1)S(1)}, u32[]{:S(2)}, u32[]{:S(2)}) collective-permute-start(bf16[64,1024]{1,0:T(8,128)(2,1)S(1)} %collective-permute-done.111.refs_9_), channel_id=1, source_target_pairs={{0,4},{4,0},{8,12},{12,8},{16,20},{20,16},{24,28},{28,24},{1,5},{5... | collective-permute-start | bytes 393224 | tf_op jit(solution)/shard_map/ppermute | solution.py:58
  611.3 16.9 %collective-permute-start.109 = (bf16[64,1024]{1,0:T(8,128)(2,1)S(1)}, bf16[64,1024]{1,0:T(8,128)(2,1)S(1)}, u32[]{:S(2)}, u32[]{:S(2)}) collective-permute-start(bf16[64,1024]{1,0:T(8,128)(2,1)S(1)} %collective-permute-done.107.refs_5_), channel_id=1, source_target_pairs={{0,4},{4,0},{8,12},{12,8},{16,20},{20,16},{24,28},{28,24},{1,5},{5... | collective-permute-start | bytes 393224 | tf_op jit(solution)/shard_map/ppermute | solution.py:58
  642.1 14.1 %collective-permute-start.91 = (bf16[16,5120]{1,0:T(8,128)(2,1)S(1)}, bf16[16,5120]{1,0:T(8,128)(2,1)S(1)}, u32[]{:S(2)}, u32[]{:S(2)}) collective-permute-start(bf16[16,5120]{1,0:T(8,128)(2,1)S(1)} %collective-permute-done.89.refs_9_), channel_id=1, source_target_pairs={{0,4},{4,0},{8,12},{12,8},{16,20},{20,16},{24,28},{28,24},{1,5},{5... | collective-permute-start | bytes 491528 | tf_op jit(solution)/shard_map/ppermute | solution.py:58
  642.2 14.0 %collective-permute-start.87 = (bf16[16,5120]{1,0:T(8,128)(2,1)S(1)}, bf16[16,5120]{1,0:T(8,128)(2,1)S(1)}, u32[]{:S(2)}, u32[]{:S(2)}) collective-permute-start(bf16[16,5120]{1,0:T(8,128)(2,1)S(1)} %collective-permute-done.85.refs_5_), channel_id=1, source_target_pairs={{0,4},{4,0},{8,12},{12,8},{16,20},{20,16},{24,28},{28,24},{1,5},{5... | collective-permute-start | bytes 491528 | tf_op jit(solution)/shard_map/ppermute | solution.py:58
  (220 other events, 3857.6 us)

commit v3 on v2

v3 whole, which is shorter than its diff:
```python
import functools
import math

import jax
import jax.numpy as jnp
from jax import lax
from jax.experimental import pallas as pl
from jax.experimental.pallas import tpu as pltpu
from jax.sharding import PartitionSpec as P

HEADS = 16
HD = 64
BLOCK = 25
EPSILON = 1e-05
GROUP = 8
TAIL = 128
PAIR = 2 * HD
STEP = 512
LOG2E = 1.4426950408889634
LOW = jnp.bfloat16
WIDE = jnp.float32
VMEM = pl.BlockSpec(memory_space=pltpu.VMEM)
SMEM = pl.BlockSpec(memory_space=pltpu.SMEM)
ANY = pl.BlockSpec(memory_space=pl.ANY)
PLACE, INDEX, CORE, X, Y, OWNED, HERE, LISTS = range(8)


def params(mib=56):
    return pltpu.CompilerParams(vmem_limit_bytes=mib << 20)


def cost():
    return pl.CostEstimate(flops=10**11, bytes_accessed=10**9, transcendentals=0)


def shape(*dims, dtype=LOW):
    return jax.ShapeDtypeStruct(dims, dtype)


def dot(left, right, dims=((1,), (0,))):
    return lax.dot_general(left, right, (dims, ((), ())), preferred_element_type=WIDE)


def left_dot(left, right):
    return dot(left, right, ((0,), (0,)))


def right_dot(left, right):
    return dot(left, right, ((1,), (1,)))


def part_of(start, size):
    return pl.ds(pl.multiple_of(start, size), size)


def swap(value, mask):
    size = lax.axis_size("dp")
    return lax.ppermute(value, "dp", [(i, i ^ mask) for i in range(size)])


def turn(value, k):
    size = lax.axis_size("ctx")
    return lax.ppermute(value, "ctx", [(i, (i + k) % size) for i in range(size)])


def exchange(value):
    return lax.all_to_all(value, "ctx", 0, 0)


def after(value, *others):
    return lax.optimization_barrier((value, *others))[0]


def shard_gather(value, *early):
    n = lax.axis_size("ctx")
    value = after(value, *early) if early else value
    if n != 4:
        got = [turn(value, k) for k in range(1, n)]
        return got, got[0]
    place = lax.axis_index("ctx")
    far = lax.ppermute(value, "ctx", [(0, 2), (1, 3), (2, 0), (3, 1)])
    up = lax.ppermute(value, "ctx", [(0, 1), (1, 2), (2, 3)])
    down = lax.ppermute(value, "ctx", [(1, 0), (2, 1), (3, 2)])
    on = lax.ppermute(far, "ctx", [(2, 3), (1, 0)])
    return [jnp.where(place == 0, on, up), far, jnp.where(place == n - 1, on, down)], far


class Order:
    def __init__(self, ids):
        self.ids = ids

    def call(self, body, *args, **kwargs):
        outs = pl.pallas_call(body, **kwargs)(self.ids, *args)
        self.wait(outs[0] if isinstance(outs, (list, tuple)) else outs)
        return outs

    def wait(self, *values):
        self.ids = after(self.ids, *values)


def gather_near(one, two):
    return jnp.stack([one, swap(one, 2)]), jnp.stack([two, swap(two, 4)])


def gather_far(one, two):
    return jnp.stack([one, swap(one, 4)]), jnp.stack([two, swap(two, 2)])


def gather_cores(one, two):
    return one, two, swap(one, 1), swap(two, 1)


def piece_of(arrays, mask, half):
    x, y = (mask >> 1) & 1, (mask >> 2) & 1
    return arrays[2 * (mask & 1) + half].at[(x, y) if half else (y, x)]


def loads(ids, own, pieces, sems, held, rows, row, col):
    n, _, cols = held.shape
    copies = []
    at = 0
    for ref, width in own:
        copies.append(
            pltpu.make_async_copy(ref, held.at[0, :, pl.ds(at, width)], sems.at[len(copies)])
        )
        at += width
    for i in range(2 * GROUP):
        where = ((ids[INDEX] ^ (i // 2)) * 2 + i % 2) * rows
        piece = piece_of(pieces, i // 2, i % 2)
        copies.append(
            pltpu.make_async_copy(
                piece.at[:, pl.ds(row, rows), pl.ds(col, cols)],
                held.at[pl.ds(1, n - 1), part_of(where, rows), :],
                sems.at[len(copies)],
            )
        )
    return copies


def begin(copies):
    for copy in copies:
        copy.start()


def finish(copies):
    for copy in copies:
        copy.wait()


def shard_of(ids, k, n):
    return lax.rem(ids[PLACE] + n - k, n)


def project(n, ids, *refs):
    row_ref, wq, wk, wv = refs[:4]
    refs = refs[4:]
    pieces, (bias, out, compact, held, sems) = refs[:4], refs[4:]
    width = row_ref.shape[1]
    slots = row_ref.shape[0] // n
    cols = width // n
    rows = pieces[0].shape[3]
    copies = []
    for j, own in enumerate((wq, wk, wv)):
        copies.append(
            pltpu.make_async_copy(
                own.at[:, part_of(ids[PLACE] * cols, cols)],
                held.at[0, :, pl.ds(j * cols, cols)],
                sems.at[len(copies)],
            )
        )
        for i in range(2 * GROUP):
            where = ((ids[INDEX] ^ (i // 2)) * 2 + i % 2) * rows
            piece = piece_of(pieces, i // 2, i % 2)
            copies.append(
                pltpu.make_async_copy(
                    piece.at[:, :, part_of(j * width + ids[PLACE] * cols, cols)],
                    held.at[pl.ds(1, n - 1), part_of(where, rows), pl.ds(j * cols, cols)],
                    sems.at[len(copies)],
                )
            )
    begin(copies)
    for g in range(n):
        compact[part_of(ids[LISTS + g] * slots, slots), :] = row_ref[g * slots : (g + 1) * slots, :]
    finish(copies)

    def block(i, _):
        row = part_of(i * 256, 256)
        total = bias[...]
        for k in range(n):
            column = part_of(shard_of(ids, k, n) * cols, cols)
            total = total + dot(compact[row, column], held[k])
        out[row, :] = total.astype(LOW)
        return 0

    lax.fori_loop(0, out.shape[0] // 256, block, 0)


def attend(n, ids, bias_ref, q_ref, k_ref, v_ref, *refs):
    out_ref, lse_ref = refs
    tile = pl.program_id(0)
    slots = q_ref.shape[0]
    first = lax.broadcasted_iota(jnp.int32, (1, PAIR), 1) < HD

    def work(rows):
        query = q_ref[:rows, :]
        keys, values = k_ref[...], v_ref[...]
        mixed = []
        for h in range(2):
            mine = first if h == 0 else jnp.logical_not(first)
            scores = right_dot(jnp.where(mine, query, 0), keys)
            scores = scores * (LOG2E / math.sqrt(HD)) + bias_ref[...]
            high = jnp.max(scores, -1, keepdims=True)
            expo = jnp.exp2(scores - high)
            total = jnp.sum(expo, -1, keepdims=True)
            probs = (expo * (1.0 / total)).astype(LOW)
            mixed.append(dot(probs, values))
            lse = jnp.broadcast_to(high + jnp.log2(total), (rows, 128))
            lse_ref[h : h + 1, :rows] = lse.T[:1, :]
        out_ref[0, :rows, :] = jnp.where(first, mixed[0], mixed[1]).astype(LOW)
        if rows < slots:
            out_ref[0, rows:, :] = jnp.zeros((slots - rows, PAIR), LOW)

    @pl.when(tile < n - 1)
    def _():
        work(slots)

    @pl.when(tile == n - 1)
    def _():
        work(TAIL)
        lse_ref[:, TAIL:] = jnp.zeros((8, slots - TAIL), WIDE)


def attention(order, qkv, bias, pair, pairs, n, slots):
    span = qkv.shape[0]
    whole = lambda col: pl.BlockSpec((span, PAIR), lambda t, ids: (0, col))
    return order.call(
        functools.partial(attend, n),
        *(bias, qkv, qkv, qkv),
        grid_spec=pltpu.PrefetchScalarGridSpec(
            num_scalar_prefetch=1,
            grid=(n,),
            in_specs=[
                pl.BlockSpec((1, span), lambda t, ids: (0, 0)),
                pl.BlockSpec((slots, PAIR), lambda t, ids: (t, pair)),
                whole(pairs + pair),
                whole(2 * pairs + pair),
            ],
            out_specs=[
                pl.BlockSpec((1, slots, PAIR), lambda t, ids: (ids[LISTS + n + t], 0, 0)),
                pl.BlockSpec((8, slots), lambda t, ids: (0, t)),
            ],
        ),
        out_shape=[shape(n, slots, PAIR), shape(8, n * slots, dtype=WIDE)],
        compiler_params=params(),
        cost_estimate=cost(),
    )


def attend_back(n, ids, bias_ref, q_ref, k_ref, v_ref, *refs):
    grad_ref, lse_ref, out_ref, do_ref, dk_ref, dv_ref = refs
    tile = pl.program_id(0)
    slots = q_ref.shape[0]
    span = k_ref.shape[0]
    first = lax.broadcasted_iota(jnp.int32, (1, PAIR), 1) < HD
    scale = 1.0 / math.sqrt(HD)

    @pl.when(tile == 0)
    def _():
        dk_ref[...] = jnp.zeros_like(dk_ref)
        dv_ref[...] = jnp.zeros_like(dv_ref)
        for g in range(n):
            do_ref[part_of(ids[LISTS + g] * slots, slots), :] = grad_ref[g]

    def work(rows):
        keys, values = k_ref[...], v_ref[...]
        here = pl.ds(pl.multiple_of(tile * slots, slots), rows)
        parts = []
        for h in range(2):
            mine = first if h == 0 else jnp.logical_not(first)
            query = jnp.where(mine, q_ref[:rows, :], 0)
            grad = jnp.where(mine, do_ref[here, :], 0)
            scores = right_dot(keys, query) * (LOG2E * scale)
            bias = jnp.concatenate([bias_ref[...]] * (rows // 128), 1)
            probs = jnp.exp2(scores + bias - lse_ref[h : h + 1, :rows])
            grad_probs = right_dot(values, grad)
            center = jnp.sum(grad_probs * probs, 0, keepdims=True)
            grad_scores = (probs * (grad_probs - center)).astype(LOW)
            dk_ref[:span, :] += dot(grad_scores, query)
            dv_ref[:span, :] += dot(probs.astype(LOW), grad)
            parts.append(left_dot(grad_scores, keys))
        group = ids[LISTS + n + tile]
        out_ref[group, :rows, :PAIR] = (jnp.where(first, parts[0], parts[1]) * scale).astype(LOW)
        if rows < slots:
            out_ref[group, rows:, :PAIR] = jnp.zeros((slots - rows, PAIR), LOW)

    @pl.when(tile < n - 1)
    def _():
        work(slots)

    @pl.when(tile == n - 1)
    def _():
        work(TAIL)
        for g in range(n):
            here = part_of(ids[LISTS + g] * slots, slots)
            out_ref[g, :, PAIR : 2 * PAIR] = (dk_ref[here, :] * scale).astype(LOW)
            out_ref[g, :, 2 * PAIR :] = dv_ref[here, :].astype(LOW)


def attention_back(order, qkv, bias, grad, lse, pair, pairs, n, slots):
    span = qkv.shape[0]
    whole = lambda col: pl.BlockSpec((span, PAIR), lambda t, ids: (0, col))
    return order.call(
        functools.partial(attend_back, n),
        *(bias, qkv, qkv, qkv, grad, lse),
        grid_spec=pltpu.PrefetchScalarGridSpec(
            num_scalar_prefetch=1,
            grid=(n,),
            in_specs=[
                pl.BlockSpec((span, 128), lambda t, ids: (0, 0)),
                pl.BlockSpec((slots, PAIR), lambda t, ids: (t, pair)),
                whole(pairs + pair),
                whole(2 * pairs + pair),
                pl.BlockSpec((n, slots, PAIR), lambda t, ids: (0, 0, pair)),
                pl.BlockSpec((8, slots), lambda t, ids: (0, t)),
            ],
            out_specs=pl.BlockSpec((n, slots, 3 * PAIR), lambda t, ids: (0, 0, 0)),
            scratch_shapes=[
                pltpu.VMEM((n * slots, PAIR), LOW),
                pltpu.VMEM((n * slots, PAIR), WIDE),
                pltpu.VMEM((n * slots, PAIR), WIDE),
            ],
        ),
        out_shape=shape(n, slots, 3 * PAIR),
        compiler_params=params(),
        cost_estimate=cost(),
    )


def normal(values):
    center = values - jnp.mean(values, -1, keepdims=True)
    scale = lax.rsqrt(jnp.mean(center * center, -1, keepdims=True) + EPSILON)
    return center * scale, scale


def normal_back(grad, unit, scale):
    inner = jnp.mean(grad * unit, -1, keepdims=True)
    return (grad - jnp.mean(grad, -1, keepdims=True) - unit * inner) * scale


def wide(ref):
    return ref[...].astype(WIDE)


def forward(n, pairs, ids, *refs):
    parts, refs = refs[:pairs], refs[pairs:]
    start, cotangent, wo_own, wi_own, wu_own = refs[:5]
    bo, bi, bu, gain1, shift1, gain2, shift2 = refs[5:12]
    refs = refs[12:]
    side, tall, refs = refs[:4], refs[4:8], refs[8:]
    attn, first, normed_low, active, slope, out, grad_second, second_low, sums = refs[:9]
    wo, wi, wu, normed, second, sem_o, sem_i, sem_u = refs[9:]
    slots, width = start.shape
    cols = width // n
    hidden = active.shape[1]
    deep = hidden // n
    row_o, row_u = cols // (2 * GROUP), deep // (2 * GROUP)
    get_o = loads(ids, [(wo_own, width)], tall, sem_o, wo, row_o, 0, 0)
    get_i = loads(ids, [(wi_own, hidden)], side, sem_i, wi, row_o, 0, 3 * width)
    get_u = loads(ids, [(wu_own, width)], tall, sem_u, wu, row_u, row_o, 0)
    begin(get_o)
    begin(get_i)
    begin(get_u)
    for g in range(n):
        for p in range(pairs):
            attn[:, pl.ds(g * cols + p * PAIR, PAIR)] = parts[p][g]
    finish(get_o)

    def mix(j, _):
        column = part_of(j * STEP, STEP)
        total = start[:, column] + wide(bo.at[:, column])
        for k in range(n):
            left = attn[:, part_of(shard_of(ids, k, n) * cols, cols)]
            total = total + dot(left, wo[k, :, column])
        first[:, column] = total
        return 0

    lax.fori_loop(0, width // STEP, mix, 0)

    def norm(i, _):
        row = part_of(i * 128, 128)
        unit, _ = normal(first[row, :])
        value = unit * wide(gain1) + wide(shift1)
        normed[row, :] = value
        normed_low[row, :] = value.astype(LOW)
        return 0

    lax.fori_loop(0, slots // 128, norm, 0)
    finish(get_i)

    def expand(j, _):
        column = part_of(j * STEP, STEP)
        x = jnp.broadcast_to(wide(bi.at[:, column]), (slots, STEP))
        for k in range(n):
            left = normed_low[:, part_of(shard_of(ids, k, n) * cols, cols)]
            x = x + dot(left, wi[k, :, column])
        factor = math.sqrt(2 / math.pi)
        square = x * x
        t = jnp.tanh(factor * x * (1.0 + 0.044715 * square))
        half = 0.5 * (1.0 + t)
        active[:, column] = (x * half).astype(LOW)
        slope[:, column] = half + (0.5 * factor) * x * (1.0 - t * t) * (1.0 + 0.134145 * square)
        return 0

    lax.fori_loop(0, hidden // STEP, expand, 0)
    finish(get_u)

    def contract(j, _):
        column = part_of(j * STEP, STEP)
        total = normed[:, column] + wide(bu.at[:, column])
        for k in range(n):
            left = active[:, part_of(shard_of(ids, k, n) * deep, deep)]
            total = total + dot(left, wu[k, :, column])
        second[:, column] = total
        return 0

    lax.fori_loop(0, width // STEP, contract, 0)
    sums[...] = jnp.zeros_like(sums)

    def last(i, _):
        row = part_of(i * 128, 128)
        live = lax.broadcasted_iota(jnp.int32, (128, 1), 0) + i * 128 < ids[OWNED]
        live = live.astype(WIDE)
        unit, scale = normal(second[row, :])
        out[row, :] = ((unit * wide(gain2) + wide(shift2)) * live).astype(LOW)
        grad = cotangent[row, :].astype(WIDE) * live
        result = normal_back(grad * wide(gain2), unit, scale)
        grad_second[row, :] = result
        second_low[row, :] = result.astype(LOW)
        for j, item in enumerate((grad * unit, grad, result)):
            sums[j : j + 1, :] += jnp.sum(item, 0, keepdims=True)
        return 0

    lax.fori_loop(0, slots // 128, last, 0)


def backward_inner(n, ids, *refs):
    second_low, slope, wu_own = refs[:3]
    tall, (inner_low, bias_sum, wu, sem_u) = refs[3:7], refs[7:]
    hidden = slope.shape[1]
    deep, cols = hidden // n, second_low.shape[1] // n
    row_o, row_u = cols // (2 * GROUP), deep // (2 * GROUP)
    get_u = loads(ids, [(wu_own, second_low.shape[1])], tall, sem_u, wu, row_u, row_o, 0)
    begin(get_u)
    finish(get_u)

    def expand(j, _):
        for k in range(n):
            column = part_of(shard_of(ids, k, n) * deep + j * STEP, STEP)
            grad = right_dot(second_low[...], wu[k, part_of(j * STEP, STEP), :])
            value = (grad * slope[:, column]).astype(LOW)
            inner_low[:, column] = value
            bias_sum[:, column] = jnp.sum(value.astype(WIDE), 0, keepdims=True)
        return 0

    lax.fori_loop(0, deep // STEP, expand, 0)


def backward(n, ids, *refs):
    inner_low, bias_sum, grad_second, first, gain1, sums, wo_own, wi_own = refs[:8]
    side, tall, refs = refs[8:12], refs[12:16], refs[16:]
    grad_first, first_low = refs[:2]
    grad_attn, small = refs[2:4]
    wo, wi, grad_normed, more, sem_o, sem_i = refs[4:]
    slots, width = first.shape
    cols = width // n
    hidden = inner_low.shape[1]
    deep = hidden // n
    row_o = cols // (2 * GROUP)
    get_o = loads(ids, [(wo_own, width)], tall, sem_o, wo, row_o, 0, 0)
    get_i = loads(ids, [(wi_own, hidden)], side, sem_i, wi, row_o, 0, 3 * width)
    begin(get_i)
    begin(get_o)
    finish(get_i)
    for k in range(n):
        column = part_of(shard_of(ids, k, n) * cols, cols)
        grad_normed[:, column] = right_dot(inner_low[...], wi[k]) + grad_second[:, column]
    more[...] = jnp.zeros_like(more)

    def norm(i, _):
        row = part_of(i * 128, 128)
        unit, scale = normal(first[row, :])
        grad = grad_normed[row, :]
        result = normal_back(grad * wide(gain1), unit, scale)
        grad_first[row, :] = result
        first_low[row, :] = result.astype(LOW)
        for j, item in enumerate((result, grad * unit, grad)):
            more[j : j + 1, :] += jnp.sum(item, 0, keepdims=True)
        return 0

    lax.fori_loop(0, slots // 128, norm, 0)
    finish(get_o)
    for k in range(n):
        grad_attn[shard_of(ids, k, n)] = right_dot(first_low[...], wo[k]).astype(LOW)
    small[...] = jnp.zeros_like(small)
    for z in range(n):
        here = pl.ds(z * cols, cols)
        rows = [more[0:1, here]]
        rows += [bias_sum[:, pl.ds(z * deep + j * cols, cols)] for j in range(deep // cols)]
        rows += [sums[2:3, here], more[1:2, here], more[2:3, here], sums[0:1, here], sums[1:2, here]]
        for j, item in enumerate(rows):
            small[z, j : j + 1, :] = item


def finish_hidden(n, pairs, ids, *refs):
    parts, refs = refs[:pairs], refs[pairs:]
    grad_first, wq, wk, wv = refs[:4]
    side, (out, total, held, acts, sems) = refs[4:8], refs[8:]
    slots, width = out.shape
    cols = width // n
    copies = loads(
        ids, [(wq, width), (wk, width), (wv, width)], side, sems, held, cols // (2 * GROUP), 0, 0
    )
    begin(copies)
    for g in range(n):
        for p in range(pairs):
            for j in range(3):
                column = j * width + g * cols + p * PAIR
                acts[:, column : column + PAIR] = parts[p][g, :, j * PAIR : (j + 1) * PAIR]
    finish(copies)
    for k in range(n):
        column = part_of(shard_of(ids, k, n) * cols, cols)
        out[:, column] = right_dot(acts[...], held[k]) + grad_first[:, column]
    block = lax.broadcasted_iota(jnp.int32, (32, 1), 0) < ids[HERE]
    total[...] = jnp.sum(jnp.where(block, out[:32, :], 0.0), 0, keepdims=True)


def outer_product(spec, keep, ids, *refs):
    lefts, rights = [], []
    for count, _ in spec:
        lefts.append(refs[:count])
        rights.append(refs[count : 2 * count])
        refs = refs[2 * count :]
    at = 0
    for (count, cols), left, right in zip(spec, lefts, rights):
        step = min(cols, 1024)
        for col in range(0, cols, step):
            total = left_dot(left[0][...], right[0][:, col : col + step])
            for i in range(1, count):
                total = total + left_dot(left[i][...], right[i][:, col : col + step])
            here = slice(at + col, at + col + step)
            if not keep:
                refs[0][0, :, here] = total.astype(LOW)
                continue
            got, outs = refs[0], refs[1:]
            total = (total + got[0, :, here].astype(WIDE)).astype(LOW)
            split_halves(ids, total, [out.at[0, :, here] for out in outs], (X, Y))
        at += cols


def split_halves(ids, total, outs, bits):
    rows = total.shape[0] // 4
    parts = [total[i * rows : (i + 1) * rows] for i in range(4)]
    for half, bit in enumerate(bits):
        high = ids[bit] == 1
        low_part, high_part = parts[2 * half], parts[2 * half + 1]
        outs[2 * half][...] = jnp.where(high, low_part, high_part)
        outs[2 * half + 1][...] = jnp.where(high, high_part, low_part)


def gradient(order, spec, n, got=None):
    rows = spec[0][0][0][0].shape[1] // (2 * n)
    keep = got is not None
    in_specs, args, total, flops = [], [], 0, 0
    for pairs, cols in spec:
        for left, _ in pairs:
            block = lambda z, ids: (0, 2 * z + (ids[CORE] if keep else 1 - ids[CORE]))
            in_specs.append(pl.BlockSpec((left.shape[0], rows), block))
            args.append(left)
        for _, right in pairs:
            in_specs.append(pl.BlockSpec(right.shape, lambda z, ids: (0, 0)))
            args.append(right)
            flops += 2 * n * rows * right.shape[0] * cols
        total += cols
    if keep:
        in_specs.append(pl.BlockSpec((1, rows, total), lambda z, ids: (z, 0, 0)))
        args.append(got)
    out_rows, count = (rows // 4, 4) if keep else (rows, 1)
    return order.call(
        functools.partial(outer_product, [(len(pairs), cols) for pairs, cols in spec], keep),
        *args,
        grid_spec=pltpu.PrefetchScalarGridSpec(
            num_scalar_prefetch=1,
            grid=(n,),
            in_specs=in_specs,
            out_specs=[pl.BlockSpec((1, out_rows, total), lambda z, ids: (z, 0, 0))] * count,
        ),
        out_shape=[shape(n, out_rows, total)] * count,
        compiler_params=params(),
        cost_estimate=cost(),
    )


def fold_two(ids, keep_one, got_one, keep_two, got_two, *outs):
    rows = keep_one.shape[1] // 2
    for z in range(keep_one.shape[0]):
        one = (keep_one[z].astype(WIDE) + got_one[z].astype(WIDE)).astype(LOW)
        two = (keep_two[z].astype(WIDE) + got_two[z].astype(WIDE)).astype(LOW)
        for total, bit, (send, keep) in ((one, Y, outs[:2]), (two, X, outs[2:])):
            high = ids[bit] == 1
            send[z] = jnp.where(high, total[:rows], total[rows:])
            keep[z] = jnp.where(high, total[rows:], total[:rows])


def fold_three(ids, keep_one, got_one, keep_two, got_two, out):
    for z in range(out.shape[0]):
        out[z, 0] = (keep_one[z].astype(WIDE) + got_one[z].astype(WIDE)).astype(LOW)
        out[z, 1] = (keep_two[z].astype(WIDE) + got_two[z].astype(WIDE)).astype(LOW)


def fold_four(split, ids, terms, *outs):
    n, cols = terms.shape[0], terms.shape[3]
    for h, out in enumerate(outs):
        if split < cols:
            total = terms[0, h, :, split:].astype(WIDE)
            for z in range(1, n):
                total = total + terms[z, h, :, split:].astype(WIDE)
            out[:, n * split :] = total.astype(LOW)
        for z in range(n if split else 0):
            out[:, z * split : (z + 1) * split] = terms[z, h, :, :split]


def small_call(order, body, args, outs):
    return order.call(
        body,
        *args,
        in_specs=[SMEM] + [VMEM] * len(args),
        out_specs=[VMEM] * len(outs),
        out_shape=outs,
        compiler_params=params(),
        cost_estimate=cost(),
    )


def reduce_first(order, spec, n):
    (send,) = gradient(order, spec, n)
    return swap(send, 1)


def reduce_second(order, spec, n, got):
    send_one, keep_one, send_two, keep_two = gradient(order, spec, n, got)
    return keep_one, swap(send_one, 2), keep_two, swap(send_two, 4)


def reduce_third(order, n, held):
    rows, cols = held[0].shape[1:]
    outs = [shape(n, rows // 2, cols)] * 4
    send_one, keep_one, send_two, keep_two = small_call(order, fold_two, held, outs)
    return keep_one, swap(send_one, 4), keep_two, swap(send_two, 2)


def reduce_fourth(order, n, held):
    rows, cols = held[0].shape[1:]
    (out,) = small_call(order, fold_three, held, [shape(n, 2, rows, cols)])
    return exchange(out)


def reduce_fifth(order, held, split=0):
    n, _, rows, cols = held.shape
    outs = [shape(rows, cols + (n - 1) * split)] * 2
    one, two = small_call(order, functools.partial(fold_four, split), [held], outs)
    mask = GROUP
    while mask < lax.axis_size("dp"):
        one, two = [(v.astype(WIDE) + swap(v, mask).astype(WIDE)).astype(LOW) for v in (one, two)]
        mask *= 2
    return one, two


def place_grad(plan, ids, *refs):
    pieces, outs = refs[:4], refs[4:]
    rows = pieces[0].shape[2]
    for i in range(2 * GROUP):
        piece = piece_of(pieces, i // 2, i % 2)
        home = ids[INDEX] ^ (i // 2)
        core, x, y = home & 1, (home >> 1) & 1, (home >> 2) & 1
        block = core * 8 + (x * 2 + y if i % 2 == 0 else 4 + y * 2 + x)
        row = part_of(block * rows, rows)
        for out, moves in zip(outs, plan):
            for source, target, size in moves:
                out[row, target : target + size] = piece[:, source : source + size].astype(WIDE)


def reduce_last(order, pieces, plan, widths):
    rows = pieces[0].shape[2] * 2 * GROUP
    return small_call(
        order,
        functools.partial(place_grad, plan),
        pieces,
        [shape(rows, width, dtype=WIDE) for width in widths],
    )


def per_device(
    hidden_in,
    cotangent,
    context_len,
    block_device,
    timestep,
    query_weight,
    key_weight,
    value_weight,
    output_weight,
    inner_weight,
    outer_weight,
    query_bias,
    value_bias,
    output_bias,
    inner_bias,
    outer_bias,
    attn_gain,
    attn_shift,
    ffn_gain,
    ffn_shift,
    time_table,
):
    n = lax.axis_size("ctx")
    place = lax.axis_index("ctx")
    d = lax.axis_index("dp") % GROUP
    _, slots, width = hidden_in.shape
    hidden = inner_weight.shape[1]
    cols = width // n
    deep = hidden // n
    pairs = cols // PAIR
    span = (n - 1) * slots + TAIL
    holder = block_device[0]
    context = context_len[0]

    groups = [j + (j >= holder).astype(jnp.int32) for j in range(n - 1)] + [holder]
    position = lambda g: jnp.where(g == holder, n - 1, g - (g > holder).astype(jnp.int32))
    counts = [context // (n - 1) + (j < context % (n - 1)).astype(jnp.int32) for j in range(n - 1)]
    counts = jnp.stack(counts + [jnp.int32(BLOCK)])
    slot = jnp.arange(slots, dtype=jnp.int32)
    live = (slot[None, :] < counts[:, None]).reshape(n * slots)[:span]
    bias = jnp.where(live, 0.0, -1e30).astype(WIDE)
    bias_row, bias_col = bias[None, :], jnp.broadcast_to(bias[:, None], (span, 128))
    owned = lax.dynamic_index_in_dim(counts, position(place), keepdims=False)
    here = jnp.where(holder == place, BLOCK, 0)
    ids = [place, d, d & 1, (d >> 1) & 1, (d >> 2) & 1, owned, here]
    ids += [position(jnp.int32(g)) for g in range(n)] + groups
    order = Order(jnp.stack([jnp.asarray(v, jnp.int32) for v in ids]))
    embed = lax.dynamic_slice_in_dim(time_table, timestep[0], 1, 0).astype(WIDE)
    block = ((holder == place) & (slot < BLOCK)).astype(WIDE)[:, None]
    start = hidden_in[0].astype(WIDE) + block * embed
    start_low = start.astype(LOW)

    def piece(weight):
        part = weight.shape[0] // GROUP
        return lax.dynamic_slice_in_dim(weight, d * part, part, 0).reshape(2, part // 2, -1)

    side_piece = jnp.concatenate(
        [piece(w) for w in (query_weight, key_weight, value_weight, inner_weight)], 2
    )
    tall_piece = jnp.concatenate([piece(output_weight), piece(outer_weight)], 1)
    side, early = shard_gather(side_piece)
    tall, late = shard_gather(tall_piece, early)
    row_low = lax.all_gather(after(start_low, late), "ctx", tiled=True)
    side, tall = jnp.stack(side), jnp.stack(tall)
    side = gather_cores(*gather_far(*gather_near(side[:, 0], side[:, 1])))
    tall = gather_near(tall[:, 0], tall[:, 1])
    order.wait(*tall)
    tall = gather_far(*tall)
    own_bias = lambda v: lax.dynamic_slice_in_dim(v, place * cols, cols, 0).astype(WIDE)
    qkv_bias = jnp.concatenate([own_bias(query_bias), jnp.zeros((cols,), WIDE), own_bias(value_bias)])
    qkv = order.call(
        functools.partial(project, n),
        *(row_low, query_weight, key_weight, value_weight, *side, qkv_bias[None]),
        in_specs=[SMEM] + [VMEM] + [ANY] * 7 + [VMEM],
        out_specs=VMEM,
        out_shape=shape(span, 3 * cols),
        scratch_shapes=[
            pltpu.VMEM((n * slots, width), LOW),
            pltpu.VMEM((n, cols, 3 * cols), LOW),
            pltpu.SemaphoreType.DMA((3 + 6 * GROUP,)),
        ],
        compiler_params=params(),
        cost_estimate=cost(),
    )

    mixed, lses = [], []
    for pair in range(pairs):
        if pair == 1:
            order.wait(*tall)
            tall = gather_cores(*tall)
        mix, lse = attention(order, qkv, bias_row, pair, pairs, n, slots)
        lses.append(lse)
        mixed.append(exchange(mix))

    row = lambda v: v[None, :]
    held_o = pltpu.VMEM((n, cols, width), LOW)
    held_i = pltpu.VMEM((n, cols, hidden), LOW)
    held_u = pltpu.VMEM((n, deep, width), LOW)
    wide_one = pltpu.VMEM((slots, width), WIDE)
    sem = pltpu.SemaphoreType.DMA((1 + 2 * GROUP,))
    flops = 2 * slots * width * (width + 2 * hidden)
    attn, first, normed_low, active, slope, out, grad_second, second_low, sums = order.call(
        functools.partial(forward, n, pairs),
        *(*mixed, start, cotangent[0], output_weight, inner_weight, outer_weight),
        *(row(output_bias), row(inner_bias), row(outer_bias)),
        *(row(attn_gain), row(attn_shift), row(ffn_gain), row(ffn_shift), *side, *tall),
        in_specs=[SMEM] + [VMEM] * (pairs + 2) + [ANY] * 3 + [VMEM] * 7 + [ANY] * 8,
        out_specs=[VMEM] * 9,
        out_shape=[
            shape(slots, width),
            shape(slots, width, dtype=WIDE),
            shape(slots, width),
            shape(slots, hidden),
            shape(slots, hidden, dtype=WIDE),
            shape(slots, width),
            shape(slots, width, dtype=WIDE),
            shape(slots, width),
            shape(8, width, dtype=WIDE),
        ],
        scratch_shapes=[held_o, held_i, held_u, wide_one, wide_one, sem, sem, sem],
        compiler_params=params(),
        cost_estimate=cost(),
    )
    outer_spec = [([(active, second_low)], width)]
    outer_held = reduce_first(order, outer_spec, n)
    inner_low, bias_sum = order.call(
        functools.partial(backward_inner, n),
        *(second_low, slope, outer_weight, *tall),
        in_specs=[SMEM] + [VMEM] * 2 + [ANY] * 5,
        out_specs=[VMEM] * 2,
        out_shape=[shape(slots, hidden), shape(1, hidden, dtype=WIDE)],
        scratch_shapes=[held_u, sem],
        compiler_params=params(),
        cost_estimate=cost(),
    )
    outer_held = reduce_second(order, outer_spec, n, outer_held)
    inner_spec = [([(normed_low, inner_low)], hidden)]
    inner_held = reduce_first(order, inner_spec, n)
    grad_first, first_low, grad_attn, small = order.call(
        functools.partial(backward, n),
        *(inner_low, bias_sum, grad_second, first, row(attn_gain), sums),
        *(output_weight, inner_weight, *side, *tall),
        in_specs=[SMEM] + [VMEM] * 6 + [ANY] * 10,
        out_specs=[VMEM] * 4,
        out_shape=[
            shape(slots, width, dtype=WIDE),
            shape(slots, width),
            shape(n, slots, cols),
            shape(n, 16, cols, dtype=WIDE),
        ],
        scratch_shapes=[held_o, held_i, wide_one, pltpu.VMEM((8, width), WIDE), sem, sem],
        compiler_params=params(),
        cost_estimate=cost(),
    )
    grad_mixed = exchange(grad_attn)
    outer_held = reduce_third(order, n, outer_held)
    inner_held = reduce_second(order, inner_spec, n, inner_held)
    order.wait(grad_mixed)
    outer_held = reduce_fourth(order, n, outer_held)

    backs, received = [], []

    def head_pair(pair):
        back = attention_back(order, qkv, bias_col, grad_mixed, lses[pair], pair, pairs, n, slots)
        backs.append(back)
        received.append(exchange(back))

    head_pair(0)
    order.wait(outer_held)
    inner_held = reduce_third(order, n, inner_held)
    for pair in range(1, pairs):
        head_pair(pair)
        order.wait(received[-2], *inner_held)
    outer_pieces = gather_near(*reduce_fifth(order, outer_held))
    rest_spec = [([(row_low, back.reshape(n * slots, -1))], 3 * PAIR) for back in backs]
    rest_spec += [([(attn, first_low)], width)]
    rest_held = reduce_first(order, rest_spec, n)
    order.wait(*outer_pieces)
    rest_held = reduce_second(order, rest_spec, n, rest_held)
    order.wait(*received)
    inner_held = reduce_fourth(order, n, inner_held)
    grad_hidden, block_sum = order.call(
        functools.partial(finish_hidden, n, pairs),
        *(*received, grad_first, query_weight, key_weight, value_weight, *side),
        in_specs=[SMEM] + [VMEM] * (pairs + 1) + [ANY] * 7,
        out_specs=[VMEM] * 2,
        out_shape=[shape(slots, width, dtype=WIDE), shape(1, width, dtype=WIDE)],
        scratch_shapes=[
            pltpu.VMEM((n, cols, 3 * width), LOW),
            pltpu.VMEM((slots, 3 * width), LOW),
            pltpu.SemaphoreType.DMA((3 + 2 * GROUP,)),
        ],
        compiler_params=params(),
        cost_estimate=cost(),
    )
    rest_held = reduce_third(order, n, rest_held)
    order.wait(*rest_held)
    outer_pieces = gather_far(*outer_pieces)
    order.wait(*outer_pieces)
    outer_pieces = gather_cores(*outer_pieces)
    order.wait(inner_held)

    packed = jnp.concatenate([small, block_sum.reshape(1, n, cols).repeat(n, 0)], 1)
    total = jnp.sum(exchange(after(packed, inner_held)), 0)
    order.wait(total)
    used = small.shape[1]
    bias_sums = jnp.stack([jnp.sum(back.astype(WIDE), (0, 1)) for back in backs])
    vector = jnp.concatenate([total[used:], jnp.full((1, cols), timestep[0], WIDE)])[None]
    total = jnp.concatenate([total[:used], bias_sums.reshape(-1, cols)])
    mask = 1
    while mask < lax.axis_size("dp"):
        flat = jnp.concatenate([total, vector.reshape(-1, cols)])
        flat = swap(flat, mask)
        total = total + flat[: total.shape[0]]
        vector = jnp.concatenate([vector, flat[total.shape[0] :].reshape(vector.shape)])
        mask *= 2
    per = deep // cols
    sums = [total[0], total[1 : 1 + per].reshape(deep)] + [total[1 + per + i] for i in range(5)]
    bias_sums = total[used:].reshape(pairs, 3 * PAIR)
    query_sum = bias_sums[:, :PAIR].reshape(cols)
    value_sum = bias_sums[:, 2 * PAIR :].reshape(cols)
    share = time_table.shape[0] // n
    levels = (jnp.arange(share, dtype=jnp.int32) + place * share).astype(WIDE)
    onehot = (vector[:, n, :1] == levels[None, :]).astype(WIDE)
    time_table_grad = lax.dot_general(
        onehot,
        vector[:, :n].reshape(-1, width),
        (((0,), (0,)), ((), ())),
        precision=lax.Precision.HIGHEST,
        preferred_element_type=WIDE,
    )

    inner_pieces = gather_near(*reduce_fifth(order, inner_held))
    rest_held = reduce_fourth(order, n, rest_held)
    order.wait(*inner_pieces)
    inner_pieces = gather_far(*inner_pieces)
    (outer_grad,) = reduce_last(order, outer_pieces, [[(0, 0, width)]], [width])
    rest_pieces = gather_near(*reduce_fifth(order, rest_held, 3 * cols))
    order.wait(*inner_pieces)
    inner_pieces = gather_cores(*inner_pieces)
    order.wait(*rest_pieces)
    rest_pieces = gather_far(*rest_pieces)
    (inner_grad,) = reduce_last(order, inner_pieces, [[(0, 0, hidden)]], [hidden])
    rest_pieces = gather_cores(*rest_pieces)
    plan = [
        [
            (g * 3 * cols + p * 3 * PAIR + j * PAIR, g * cols + p * PAIR, PAIR)
            for g in range(n)
            for p in range(pairs)
        ]
        for j in range(3)
    ]
    plan += [[(n * 3 * cols, 0, width)]]
    *weight_grads, output_grad = reduce_last(order, rest_pieces, plan, [width] * 4)
    return (
        out[None],
        grad_hidden[None],
        *weight_grads,
        output_grad,
        inner_grad,
        outer_grad,
        query_sum,
        value_sum,
        *sums,
        time_table_grad,
    )


def solution(mesh):
    row, shard, same = P("dp", "ctx", None), P("ctx", None), P()
    return jax.shard_map(
        per_device,
        mesh=mesh,
        in_specs=(row, row, P("dp"), P("dp"), P("dp")) + (shard,) * 6 + (same,) * 10,
        out_specs=(row, row) + (shard,) * 6 + (P("ctx"),) * 9 + (shard,),
        check_vma=False,
    )
```

time: 676 us -> 539 us (0.80)
  waiting for transfers between devices: 248 us -> 158 us
  starting transfers between devices: 172 us -> 93.3 us
  other arithmetic: 7.9 us -> 31.2 us
  between operations: 4.71 us -> 17.3 us
    ppermute x39 -> x8, waiting for transfers between devices: 167 us -> 47.6 us  [the longest x2 26.4 us: shard_gather(): on = lax.ppermute(far, 'ctx', [(2, 3), (1, 0)])]
    ppermute x39 -> x8, starting transfers between devices: 108 us -> 19.2 us  [the longest x2 9.19 us: shard_gather(): up = lax.ppermute(value, 'ctx', [(0, 1), (1, 2), (2, 3)])]
    all_to_all x0 -> x9, waiting for transfers between devices: none -> 40.4 us  [exchange(): return lax.all_to_all(value, 'ctx', 0, 0)]
    all_to_all x0 -> x9, starting transfers between devices: none -> 35.4 us  [exchange(): return lax.all_to_all(value, 'ctx', 0, 0)]
    ppermute x97 -> x48, starting transfers between devices: 63.5 us -> 38.6 us  [swap(): return lax.ppermute(value, 'dp', [(i, i ^ mask) for i in range(size)])]
    another operation x3 -> x25, other arithmetic: 1.51 us -> 23.3 us  [the longest x20 22.9 us: gather_far(): return (jnp.stack([one, swap(one, 4)]), jnp.stack([two, swap(two, 2)]))]
    ppermute x97 -> x48, waiting for transfers between devices: 81 us -> 69.5 us  [swap(): return lax.ppermute(value, 'dp', [(i, i ^ mask) for i in range(size)])]
    pallas_call x26 -> x27, Pallas kernels: 205 us -> 201 us  [call(): outs = pl.pallas_call(body, **kwargs)(self.ids, *args)]
  transfers between devices with their start and end apart: 136 -> 66, of which waited for: 42 -> 28; matrix products, arithmetic and copies ran while one was open for 3% -> 9% of each run, Pallas kernels for 22% -> 28%
where the time goes in v3:
time: 539 us; the launch traced here: 530 us
  Pallas kernels  201 us (37%)
  waiting for transfers between devices  158 us (29%)
  starting transfers between devices  93.3 us (17%)
  other arithmetic  31.2 us (6%)
  local copies, waits for them, and re-layouts  28.5 us (5%)
  between operations  17.3 us (3%)
    pallas_call x27, Pallas kernels, call(): outs = pl.pallas_call(body, **kwargs)(self.ids, *args)  201 us
    ppermute x48, waiting for transfers between devices, swap(): return lax.ppermute(value, 'dp', [(i, i ^ mask) for i in range(size)])  69.5 us
    all_to_all x9, waiting for transfers between devices, exchange(): return lax.all_to_all(value, 'ctx', 0, 0)  40.4 us
    ppermute x48, starting transfers between devices, swap(): return lax.ppermute(value, 'dp', [(i, i ^ mask) for i in range(size)])  38.6 us
    all_to_all x9, starting transfers between devices, exchange(): return lax.all_to_all(value, 'ctx', 0, 0)  35.4 us
    ppermute x2, waiting for transfers between devices, shard_gather(): on = lax.ppermute(far, 'ctx', [(2, 3), (1, 0)])  26.4 us
    another operation x20, other arithmetic, gather_far(): return (jnp.stack([one, swap(one, 4)]), jnp.stack([two, swap(two, 2)]))  22.9 us
    ppermute x2, waiting for transfers between devices, shard_gather(): far = lax.ppermute(value, 'ctx', [(0, 2), (1, 3), (2, 0), (3, 1)])  16.4 us
  transfers between devices with their start and end apart: 66, of which 28 were waited for; matrix products, arithmetic and copies ran while one was open for 9% of the time, Pallas kernels for 28%

profile of v3, /device:TPU:0, one launch (start us, length us, event | category | flops | bytes accessed | tf_op | source)
XLA Modules:
  0.0 529.8 jit_solution(4805865183760733026)
XLA Ops:
  10.1 4.1 collective-permute-start
  14.2 3.5 collective-permute-start.8
  19.0 16.4 %collective-permute-done = bf16[2,16,7168]{2,1,0:T(8,128)(2,1)S(1)} collective-permute-done((bf16[2,16,7168]{2,1,0:T(8,128)(2,1)S(1)}, bf16[2,16,7168]{2,1,0:T(8,128)(2,1)S(1)}, u32[]{:S(2)}, u32[]{:S(2)}) %collective-permute-start) | collective-permute-done | bytes 458784 | tf_op jit(solution)/shard_map/ppermute | solution.py:81
  36.7 4.8 collective-permute-done.9
  41.5 8.3 %collective-permute-done.7 = bf16[2,16,7168]{2,1,0:T(8,128)(2,1)S(1)} collective-permute-done((bf16[2,16,7168]{2,1,0:T(8,128)(2,1)S(1)}, bf16[2,16,7168]{2,1,0:T(8,128)(2,1)S(1)}, u32[]{:S(2)}, u32[]{:S(2)}) %collective-permute-start.7) | collective-permute-done | bytes 458784 | tf_op jit(solution)/shard_map/ppermute | solution.py:84
  58.0 9.0 %collective-permute-done.10 = bf16[3,16,7168]{2,1,0:T(8,128)(2,1)S(1)} collective-permute-done((bf16[3,16,7168]{2,1,0:T(8,128)(2,1)S(1)}, bf16[3,16,7168]{2,1,0:T(8,128)(2,1)S(1)}, u32[]{:S(2)}, u32[]{:S(2)}) %collective-permute-start.10) | collective-permute-done | bytes 688160 | tf_op jit(solution)/shard_map/ppermute | solution.py:58
  67.9 2.4 fusion.17
  71.6 2.8 collective-permute-done.12
  78.0 5.7 %collective-permute-start.3 = (bf16[2,80,1024]{2,1,0:T(8,128)(2,1)}, bf16[2,80,1024]{2,1,0:T(8,128)(2,1)S(1)}, u32[]{:S(2)}, u32[]{:S(2)}) collective-permute-start(bf16[2,80,1024]{2,1,0:T(8,128)(2,1)} %copy-done.14), channel_id=1, source_target_pairs={{0,1},{1,2},{2,3},{4,5},{5,6},{6,7},{8,9},{9,10},{10,11},{12,13},{... | collective-permute-start | bytes 983048 | tf_op jit(solution)/shard_map/ppermute | solution.py:82
  86.3 15.8 %collective-permute-done.11 = bf16[2,3,16,7168]{3,2,1,0:T(8,128)(2,1)} collective-permute-done((bf16[2,3,16,7168]{3,2,1,0:T(8,128)(2,1)}, bf16[2,3,16,7168]{3,2,1,0:T(8,128)(2,1)}, u32[]{:S(2)}, u32[]{:S(2)}) %collective-permute-start.11) | collective-permute-done | bytes 1376288 | tf_op jit(solution)/shard_map/ppermute | solution.py:58
  102.2 3.1 pad_maximum_fusion.refs_4_.refs_14_.refs_8_.refs_6_
  105.3 3.1 pad_maximum_fusion.1.refs_5_.refs_15_.refs_9_.refs_7_
  108.9 18.1 %collective-permute-done.2 = bf16[2,80,1024]{2,1,0:T(8,128)(2,1)S(1)} collective-permute-done((bf16[2,80,1024]{2,1,0:T(8,128)(2,1)}, bf16[2,80,1024]{2,1,0:T(8,128)(2,1)S(1)}, u32[]{:S(2)}, u32[]{:S(2)}) %collective-permute-start.2) | collective-permute-done | bytes 327712 | tf_op jit(solution)/shard_map/ppermute | solution.py:84
  130.5 9.0 %collective-permute-done.5 = bf16[3,80,1024]{2,1,0:T(8,128)(2,1)S(1)} collective-permute-done((bf16[3,80,1024]{2,1,0:T(8,128)(2,1)S(1)}, bf16[3,80,1024]{2,1,0:T(8,128)(2,1)S(1)}, u32[]{:S(2)}, u32[]{:S(2)}) %collective-permute-start.5) | collective-permute-done | bytes 491552 | tf_op jit(solution)/shard_map/ppermute | solution.py:58
  147.9 5.9 %collective-permute-done.16 = bf16[2,3,80,1024]{3,2,1,0:T(8,128)(2,1)} collective-permute-done((bf16[2,3,80,1024]{3,2,1,0:T(8,128)(2,1)S(1)}, bf16[2,3,80,1024]{3,2,1,0:T(8,128)(2,1)}, u32[]{:S(2)}, u32[]{:S(2)}) %collective-permute-start.16) | collective-permute-done | bytes 983072 | tf_op jit(solution)/shard_map/ppermute | solution.py:58
  153.9 2.7 pad_maximum_fusion.2.refs_18_.refs_3_.refs_12_
  156.6 2.7 pad_maximum_fusion.3.refs_19_.refs_4_.refs_13_
  159.7 8.0 %shard_map.340.q_ref.k_ref.v_ref = bf16[1280,768]{1,0:T(8,128)(2,1)} custom-call(s32[15]{0:T(128)} %stack.277.ids, bf16[1536,1024]{1,0:T(8,128)(2,1)} %all-gather.2.cloned.1.call-done.refs_0_.refs_2_, bf16[256,1024]{1,0:T(8,128)(2,1)} %refs_3_.3, bf16[256,1024]{1,0:T(8,128)(2,1)} %refs_4_.3, bf16[256,1024]{1,0:T(8,128)(2,1)} %refs_5_.3, ...), custom_call_target="tpu_custom_call" | custom-call | flops 99999997952 | bytes 1000000000 | tf_op jit(solution)/shard_map/pallas_call | solution.py:93
  167.7 10.7 %shard_map.341 = (bf16[4,384,128]{2,1,0:T(8,128)(2,1)}, f32[8,1536]{1,0:T(8,128)}) custom-call(s32[15]{0:T(128)} %stack.277.ids, f32[1,1280]{1,0:T(1,128)} %broadcast_in_dim.66.bias_ref, bf16[1280,768]{1,0:T(8,128)(2,1)} %shard_map.340.q_ref.k_ref.v_ref, bf16[1280,768]{1,0:T(8,128)(2,1)} %shard_map.340.q_ref.k_ref.v_ref, ...), custom_call_target="tpu_custom_call" | custom-call | flops 99999997952 | bytes 1000000000 | tf_op jit(solution)/shard_map/pallas_call | solution.py:93
  178.4 3.9 all-to-all-start
  182.4 10.8 %shard_map.342 = (bf16[4,384,128]{2,1,0:T(8,128)(2,1)}, f32[8,1536]{1,0:T(8,128)}) custom-call(s32[15]{0:T(128)} %stack.277.ids, f32[1,1280]{1,0:T(1,128)} %broadcast_in_dim.66.bias_ref, bf16[1280,768]{1,0:T(8,128)(2,1)} %shard_map.340.q_ref.k_ref.v_ref, bf16[1280,768]{1,0:T(8,128)(2,1)} %shard_map.340.q_ref.k_ref.v_ref, ...), custom_call_target="tpu_custom_call" | custom-call | flops 99999997952 | bytes 1000000000 | tf_op jit(solution)/shard_map/pallas_call | solution.py:93
  194.4 3.9 all-to-all-start.1
  202.6 7.4 %all-to-all-done.1.refs_1_ = bf16[4,384,128]{2,1,0:T(8,128)(2,1)S(1)} async-done(((bf16[4,384,128]{2,1,0:T(8,128)(2,1)}), bf16[4,384,128]{2,1,0:T(8,128)(2,1)S(1)}, u32[]{:S(2)}, u32[]{:S(2)}) %all-to-all-start.1) | async-done | bytes 393248 | tf_op jit(solution)/shard_map/all_to_all | solution.py:67
  210.7 24.3 %shard_map.343 = (bf16[384,1024]{1,0:T(8,128)(2,1)}, f32[384,1024]{1,0:T(8,128)}, bf16[384,1024]{1,0:T(8,128)(2,1)}, bf16[384,4096]{1,0:T(8,128)(2,1)}, f32[384,...) custom-call(s32[15]{0:T(128)} %stack.277.ids, ...), custom_call_target="tpu_custom_call" | custom-call | flops 99999997952 | bytes 1000000000 | tf_op jit(solution)/shard_map/pallas_call | solution.py:93
  235.1 6.6 %shard_map.344 = bf16[4,512,1024]{2,1,0:T(8,128)(2,1)} custom-call(s32[15]{0:T(128)} %stack.277.ids, bf16[384,4096]{1,0:T(8,128)(2,1)} %get-tuple-element.128.refs_0_, bf16[384,1024]{1,0:T(8,128)(2,1)} %get-tuple-element.129.refs_1_.refs_0_), custom_call_target="tpu_custom_call" | custom-call | flops 99999997952 | bytes 1000000000 | tf_op jit(solution)/shard_map/pallas_call | solution.py:93
  241.6 12.0 %shard_map.345 = (bf16[384,4096]{1,0:T(8,128)(2,1)}, f32[1,4096]{1,0:T(1,128)}) custom-call(s32[15]{0:T(128)} %stack.277.ids, bf16[384,1024]{1,0:T(8,128)(2,1)} %get-tuple-element.129.refs_1_.refs_0_, f32[384,4096]{1,0:T(8,128)} %get-tuple-element.131.refs_1_, bf16[1024,1024]{1,0:T(8,128)(2,1)} %refs_2_.3, ...), custom_call_target="tpu_custom_call" | custom-call | flops 99999997952 | bytes 1000000000 | tf_op jit(solution)/shard_map/pallas_call | solution.py:93
  255.7 7.2 %shard_map.346 = (bf16[4,128,1024]{2,1,0:T(8,128)(2,1)}, bf16[4,128,1024]{2,1,0:T(8,128)(2,1)}, bf16[4,128,1024]{2,1,0:T(8,128)(2,1)}, bf16[4,128,1024]{2,1,0:T(8,128)(2,1)}) custom-call(s32[15]{0:T(128)} %stack.277.ids, bf16[384,4096]{1,0:T(8,128)(2,1)} %get-tuple-element.128.refs_0_, bf16[384,1024]{1,0:T(8,128)(2,1)} %get-tuple-element.129.refs_1_.refs_0_, ...), custom_call_target="tpu_custom_call" | custom-call | flops 99999997952 | bytes 1000000000 | tf_op jit(solution)/shard_map/pallas_call | solution.py:93
  263.5 7.2 %shard_map.347 = bf16[4,128,4096]{2,1,0:T(8,128)(2,1)} custom-call(s32[15]{0:T(128)} %stack.277.ids, bf16[384,1024]{1,0:T(8,128)(2,1)} %get-tuple-element.136.refs_0_, bf16[384,4096]{1,0:T(8,128)(2,1)} %get-tuple-element.132.refs_1_.refs_0_), custom_call_target="tpu_custom_call" | custom-call | flops 99999997952 | bytes 1000000000 | tf_op jit(solution)/shard_map/pallas_call | solution.py:93
  272.3 13.2 %shard_map.348 = (f32[384,1024]{1,0:T(8,128)}, bf16[384,1024]{1,0:T(8,128)(2,1)}, bf16[4,384,256]{2,1,0:T(8,128)(2,1)}, f32[4,16,256]{2,1,0:T(8,128)}) custom-call(s32[15]{0:T(128)} %stack.277.ids, bf16[384,4096]{1,0:T(8,128)(2,1)} %get-tuple-element.132.refs_1_.refs_0_, f32[1,4096]{1,0:T(1,128)} %get-tuple-element.138.refs_1_, ...), custom_call_target="tpu_custom_call" | custom-call | flops 99999997952 | bytes 1000000000 | tf_op jit(solution)/shard_map/pallas_call | solution.py:93
  285.5 4.4 all-to-all-start.2
  289.9 6.4 %collective-permute-done.22.got_two = bf16[4,128,1024]{2,1,0:T(8,128)(2,1)S(1)} collective-permute-done((bf16[4,128,1024]{2,1,0:T(8,128)(2,1)S(1)}, bf16[4,128,1024]{2,1,0:T(8,128)(2,1)S(1)}, u32[]{:S(2)}, u32[]{:S(2)}) %collective-permute-start.22) | collective-permute-done | bytes 1048608 | tf_op jit(solution)/shard_map/ppermute | solution.py:58
  297.2 3.9 shard_map.349
  303.3 7.9 %shard_map.350 = (bf16[4,32,4096]{2,1,0:T(8,128)(2,1)}, bf16[4,32,4096]{2,1,0:T(8,128)(2,1)}, bf16[4,32,4096]{2,1,0:T(8,128)(2,1)}, bf16[4,32,4096]{2,1,0:T(8,128)(2,1)}) custom-call(s32[15]{0:T(128)} %stack.277.ids, bf16[384,1024]{1,0:T(8,128)(2,1)} %get-tuple-element.136.refs_0_, bf16[384,4096]{1,0:T(8,128)(2,1)} %get-tuple-element.132.refs_1_.refs_0_, ...), custom_call_target="tpu_custom_call" | custom-call | flops 99999997952 | bytes 1000000000 | tf_op jit(solution)/shard_map/pallas_call | solution.py:93
  311.2 3.6 collective-permute-done.24.got_one
  316.7 2.8 shard_map.351
  319.5 3.6 all-to-all-start.3
  326.5 16.0 %shard_map.352 = bf16[4,384,384]{2,1,0:T(8,128)(2,1)} custom-call(s32[15]{0:T(128)} %stack.277.ids, f32[1280,128]{1,0:T(8,128)} %broadcast_in_dim.75.bias_ref, bf16[1280,768]{1,0:T(8,128)(2,1)} %shard_map.340.q_ref.k_ref.v_ref, bf16[1280,768]{1,0:T(8,128)(2,1)} %shard_map.340.q_ref.k_ref.v_ref, bf16[1280,768]{1,0:T(8,128)(2,1)} %shard_map.340.q_ref.k_ref.v_ref, ...), custom_call_target="tpu_custom_call" | custom-call | flops 99999997952 | bytes 1000000000 | tf_op jit(solution)/shard_map/pallas_call | solution.py:93
  342.5 5.1 all-to-all-done.3.terms
  347.6 4.5 all-to-all-start.4
  352.2 3.9 shard_map.353
  358.2 16.0 %shard_map.354 = bf16[4,384,384]{2,1,0:T(8,128)(2,1)} custom-call(s32[15]{0:T(128)} %stack.277.ids, f32[1280,128]{1,0:T(8,128)} %broadcast_in_dim.75.bias_ref, bf16[1280,768]{1,0:T(8,128)(2,1)} %shard_map.340.q_ref.k_ref.v_ref, bf16[1280,768]{1,0:T(8,128)(2,1)} %shard_map.340.q_ref.k_ref.v_ref, bf16[1280,768]{1,0:T(8,128)(2,1)} %shard_map.340.q_ref.k_ref.v_ref, ...), custom_call_target="tpu_custom_call" | custom-call | flops 99999997952 | bytes 1000000000 | tf_op jit(solution)/shard_map/pallas_call | solution.py:93
  374.3 5.9 %all-to-all-done.4.refs_0_ = bf16[4,384,384]{2,1,0:T(8,128)(2,1)} async-done(((bf16[4,384,384]{2,1,0:T(8,128)(2,1)}), bf16[4,384,384]{2,1,0:T(8,128)(2,1)}, u32[]{:S(2)}, u32[]{:S(2)}) %all-to-all-start.4) | async-done | bytes 1179680 | tf_op jit(solution)/shard_map/all_to_all | solution.py:67
  380.2 2.4 shard_map.355
  382.7 7.6 %shard_map.356 = bf16[4,128,1792]{2,1,0:T(8,128)(2,1)} custom-call(s32[15]{0:T(128)} %stack.277.ids, bf16[1536,1024]{1,0:T(8,128)(2,1)} %all-gather.2.cloned.1.call-done.refs_0_.refs_2_, bf16[1536,384]{1,0:T(8,128)(2,1)} %bitcast.158, bf16[1536,1024]{1,0:T(8,128)(2,1)} %all-gather.2.cloned.1.call-done.refs_0_.refs_2_, bf16[1536,384]{1,0:T(8,128)(2,1)} %bitcast.62.refs_3_, ...), custom_call_target="tpu_custom_call" | custom-call | flops 99999997952 | bytes 1000000000 | tf_op jit(solution)/shard_map/pallas_call | solution.py:93
  392.5 3.5 all-to-all-start.5
  400.4 2.1 collective-permute-done.31
  404.5 2.9 collective-permute-done.37
  408.2 7.8 %shard_map.357 = (bf16[4,32,1792]{2,1,0:T(8,128)(2,1)}, bf16[4,32,1792]{2,1,0:T(8,128)(2,1)}, bf16[4,32,1792]{2,1,0:T(8,128)(2,1)}, bf16[4,32,1792]{2,1,0:T(8,128)(2,1)}) custom-call(s32[15]{0:T(128)} %stack.277.ids, bf16[1536,1024]{1,0:T(8,128)(2,1)} %all-gather.2.cloned.1.call-done.refs_0_.refs_2_, bf16[1536,384]{1,0:T(8,128)(2,1)} %bitcast.159, ...), custom_call_target="tpu_custom_call" | custom-call | flops 99999997952 | bytes 1000000000 | tf_op jit(solution)/shard_map/pallas_call | solution.py:93
  417.2 8.0 %all-to-all-done.5.refs_1_ = bf16[4,384,384]{2,1,0:T(8,128)(2,1)S(1)} async-done(((bf16[4,384,384]{2,1,0:T(8,128)(2,1)}), bf16[4,384,384]{2,1,0:T(8,128)(2,1)S(1)}, u32[]{:S(2)}, u32[]{:S(2)}) %all-to-all-start.5) | async-done | bytes 1179680 | tf_op jit(solution)/shard_map/all_to_all | solution.py:67
  425.3 3.2 shard_map.358
  428.4 4.6 all-to-all-start.6
  434.4 8.9 %shard_map.359 = (f32[384,1024]{1,0:T(8,128)}, f32[1,1024]{1,0:T(1,128)}) custom-call(s32[15]{0:T(128)} %stack.277.ids, bf16[4,384,384]{2,1,0:T(8,128)(2,1)} %all-to-all-done.4.refs_0_, bf16[4,384,384]{2,1,0:T(8,128)(2,1)} %copy-done.1, f32[384,1024]{1,0:T(8,128)} %get-tuple-element.142.refs_2_, bf16[256,1024]{1,0:T(8,128)(2,1)} %refs_3_.3, ...), custom_call_target="tpu_custom_call" | custom-call | flops 99999997952 | bytes 1000000000 | tf_op jit(solution)/shard_map/pallas_call | solution.py:93
  446.0 2.6 shard_map.360
  451.1 7.6 %all-to-all-done.6.terms = bf16[4,2,16,4096]{3,2,1,0:T(8,128)(2,1)} async-done(((bf16[4,2,16,4096]{3,2,1,0:T(8,128)(2,1)}), bf16[4,2,16,4096]{3,2,1,0:T(8,128)(2,1)}, u32[]{:S(2)}, u32[]{:S(2)}) %all-to-all-start.6) | async-done | bytes 1048608 | tf_op jit(solution)/shard_map/all_to_all | solution.py:67
  458.7 3.3 all-to-all-start.7
  463.8 4.0 all-to-all-done.7
  474.8 2.2 shard_map.362
  477.0 3.6 all-to-all-start.8
  487.5 3.8 shard_map.363
  498.9 2.1 collective-permute-done.45
  505.7 3.6 collective-permute-done.49
  509.5 2.2 collective-permute-done.50
  513.5 3.8 shard_map.365
  518.9 3.8 shard_map.366
  (296 shorter events, 102.0 us)
Async XLA Ops:
  7.2 152.5 %all-gather.2.cloned.1.call-start = ((), (), s32[]{:S(2)}) async-start(), calls=%async_computation.9 | async-start | bytes 3932160 | tf_op jit(solution)/shard_map/all_gather | solution.py:765
  10.1 25.3 %collective-permute-start = (bf16[2,16,7168]{2,1,0:T(8,128)(2,1)S(1)}, bf16[2,16,7168]{2,1,0:T(8,128)(2,1)S(1)}, u32[]{:S(2)}, u32[]{:S(2)}) collective-permute-start(bf16[2,16,7168]{2,1,0:T(8,128)(2,1)S(1)} %pad_maximum_fusion.16), channel_id=1, source_target_pairs={{0,2},{1,3},{2,0},{3,1},{4,6},{5,7},{6,4},{7,5},{8,10},{9,11},{10,... | collective-permute-start | bytes 1376264 | tf_op jit(solution)/shard_map/ppermute | solution.py:81
  14.2 22.5 %collective-permute-start.8 = (bf16[2,16,7168]{2,1,0:T(8,128)(2,1)S(1)}, bf16[2,16,7168]{2,1,0:T(8,128)(2,1)S(1)}, u32[]{:S(2)}, u32[]{:S(2)}) collective-permute-start(bf16[2,16,7168]{2,1,0:T(8,128)(2,1)S(1)} %pad_maximum_fusion.16), channel_id=1, source_target_pairs={{0,1},{1,2},{2,3},{4,5},{5,6},{6,7},{8,9},{9,10},{10,11},{12,13},{... | collective-permute-start | bytes 1376264 | tf_op jit(solution)/shard_map/ppermute | solution.py:82
  17.7 23.8 %collective-permute-start.9 = (bf16[2,16,7168]{2,1,0:T(8,128)(2,1)S(1)}, bf16[2,16,7168]{2,1,0:T(8,128)(2,1)S(1)}, u32[]{:S(2)}, u32[]{:S(2)}) collective-permute-start(bf16[2,16,7168]{2,1,0:T(8,128)(2,1)S(1)} %pad_maximum_fusion.16), channel_id=1, source_target_pairs={{1,0},{2,1},{3,2},{5,4},{6,5},{7,6},{9,8},{10,9},{11,10},{13,12},{... | collective-permute-start | bytes 1376264 | tf_op jit(solution)/shard_map/ppermute | solution.py:83
  35.4 14.4 %collective-permute-start.7 = (bf16[2,16,7168]{2,1,0:T(8,128)(2,1)S(1)}, bf16[2,16,7168]{2,1,0:T(8,128)(2,1)S(1)}, u32[]{:S(2)}, u32[]{:S(2)}) collective-permute-start(bf16[2,16,7168]{2,1,0:T(8,128)(2,1)S(1)} %collective-permute-done), channel_id=1, source_target_pairs={{2,3},{1,0},{6,7},{5,4},{10,11},{9,8},{14,15},{13,12},{18,19},{17,... | collective-permute-start | bytes 1376264 | tf_op jit(solution)/shard_map/ppermute | solution.py:84
  51.1 15.9 %collective-permute-start.10 = (bf16[3,16,7168]{2,1,0:T(8,128)(2,1)S(1)}, bf16[3,16,7168]{2,1,0:T(8,128)(2,1)S(1)}, u32[]{:S(2)}, u32[]{:S(2)}) collective-permute-start(bf16[3,16,7168]{2,1,0:T(8,128)(2,1)S(1)} %get-tuple-element.217), channel_id=1, source_target_pairs={{0,8},{4,12},{8,0},{12,4},{16,24},{20,28},{24,16},{28,20},{1,9},{5... | collective-permute-start | bytes 2064392 | tf_op jit(solution)/shard_map/ppermute | solution.py:58
  55.8 21.5 %collective-permute-start.1 = (bf16[2,80,1024]{2,1,0:T(8,128)(2,1)S(1)}, bf16[2,80,1024]{2,1,0:T(8,128)(2,1)S(1)}, u32[]{:S(2)}, u32[]{:S(2)}) collective-permute-start(bf16[2,80,1024]{2,1,0:T(8,128)(2,1)S(1)} %pad_maximum_fusion.17), channel_id=1, source_target_pairs={{0,2},{1,3},{2,0},{3,1},{4,6},{5,7},{6,4},{7,5},{8,10},{9,11},{10,... | collective-permute-start | bytes 983048 | tf_op jit(solution)/shard_map/ppermute | solution.py:81
  56.5 17.9 %collective-permute-start.12 = (bf16[3,16,7168]{2,1,0:T(8,128)(2,1)}, bf16[3,16,7168]{2,1,0:T(8,128)(2,1)S(1)}, u32[]{:S(2)}, u32[]{:S(2)}) collective-permute-start(bf16[3,16,7168]{2,1,0:T(8,128)(2,1)} %get-tuple-element.218), channel_id=1, source_target_pairs={{0,16},{4,20},{8,24},{12,28},{16,0},{20,4},{24,8},{28,12},{1,17},{... | collective-permute-start | bytes 2064392 | tf_op jit(solution)/shard_map/ppermute | solution.py:58
  70.3 31.9 %collective-permute-start.11 = (bf16[2,3,16,7168]{3,2,1,0:T(8,128)(2,1)}, bf16[2,3,16,7168]{3,2,1,0:T(8,128)(2,1)}, u32[]{:S(2)}, u32[]{:S(2)}) collective-permute-start(bf16[2,3,16,7168]{3,2,1,0:T(8,128)(2,1)} %get-tuple-element.221), channel_id=1, source_target_pairs={{0,16},{4,20},{8,24},{12,28},{16,0},{20,4},{24,8},{28,12},{1,17},{... | collective-permute-start | bytes 4128776 | tf_op jit(solution)/shard_map/ppermute | solution.py:58
  75.6 29.6 %collective-permute-start.13 = (bf16[2,3,16,7168]{3,2,1,0:T(8,128)(2,1)}, bf16[2,3,16,7168]{3,2,1,0:T(8,128)(2,1)}, u32[]{:S(2)}, u32[]{:S(2)}) collective-permute-start(bf16[2,3,16,7168]{3,2,1,0:T(8,128)(2,1)} %get-tuple-element.215), channel_id=1, source_target_pairs={{0,8},{4,12},{8,0},{12,4},{16,24},{20,28},{24,16},{28,20},{1,9},{5... | collective-permute-start | bytes 4128776 | tf_op jit(solution)/shard_map/ppermute | solution.py:58
  78.0 30.9 %collective-permute-start.3 = (bf16[2,80,1024]{2,1,0:T(8,128)(2,1)}, bf16[2,80,1024]{2,1,0:T(8,128)(2,1)S(1)}, u32[]{:S(2)}, u32[]{:S(2)}) collective-permute-start(bf16[2,80,1024]{2,1,0:T(8,128)(2,1)} %copy-done.14), channel_id=1, source_target_pairs={{0,1},{1,2},{2,3},{4,5},{5,6},{6,7},{8,9},{9,10},{10,11},{12,13},{... | collective-permute-start | bytes 983048 | tf_op jit(solution)/shard_map/ppermute | solution.py:82
  83.7 25.2 %collective-permute-start.4 = (bf16[2,80,1024]{2,1,0:T(8,128)(2,1)}, bf16[2,80,1024]{2,1,0:T(8,128)(2,1)S(1)}, u32[]{:S(2)}, u32[]{:S(2)}) collective-permute-start(bf16[2,80,1024]{2,1,0:T(8,128)(2,1)} %copy-done.14), channel_id=1, source_target_pairs={{1,0},{2,1},{3,2},{5,4},{6,5},{7,6},{9,8},{10,9},{11,10},{13,12},{... | collective-permute-start | bytes 983048 | tf_op jit(solution)/shard_map/ppermute | solution.py:83
  85.0 42.0 %collective-permute-start.2 = (bf16[2,80,1024]{2,1,0:T(8,128)(2,1)}, bf16[2,80,1024]{2,1,0:T(8,128)(2,1)S(1)}, u32[]{:S(2)}, u32[]{:S(2)}) collective-permute-start(bf16[2,80,1024]{2,1,0:T(8,128)(2,1)} %copy-done.15), channel_id=1, source_target_pairs={{2,3},{1,0},{6,7},{5,4},{10,11},{9,8},{14,15},{13,12},{18,19},{17,... | collective-permute-start | bytes 983048 | tf_op jit(solution)/shard_map/ppermute | solution.py:84
  105.3 54.5 %collective-permute-start.14 = (bf16[2,2,3,16,7168]{4,3,2,1,0:T(8,128)(2,1)}, bf16[2,2,3,16,7168]{4,3,2,1,0:T(8,128)(2,1)}, u32[]{:S(2)}, u32[]{:S(2)}) collective-permute-start(bf16[2,2,3,16,7168]{4,3,2,1,0:T(8,128)(2,1)} %pad_maximum_fusion.refs_4_.refs_14_.refs_8_.refs_6_), channel_id=1, source_target_pairs={{0,4},{4,0},{8,12},{12,8},{16,20},{20,16},{24,28},{28,24},{1,5},{5... | collective-permute-start | bytes 8257544 | tf_op jit(solution)/shard_map/ppermute | solution.py:58
  108.4 51.3 %collective-permute-start.15 = (bf16[2,2,3,16,7168]{4,3,2,1,0:T(8,128)(2,1)}, bf16[2,2,3,16,7168]{4,3,2,1,0:T(8,128)(2,1)}, u32[]{:S(2)}, u32[]{:S(2)}) collective-permute-start(bf16[2,2,3,16,7168]{4,3,2,1,0:T(8,128)(2,1)} %pad_maximum_fusion.1.refs_5_.refs_15_.refs_9_.refs_7_), channel_id=1, source_target_pairs={{0,4},{4,0},{8,12},{12,8},{16,20},{20,16},{24,28},{28,24},{1,5},{5... | collective-permute-start | bytes 8257544 | tf_op jit(solution)/shard_map/ppermute | solution.py:58
  127.4 12.0 %collective-permute-start.5 = (bf16[3,80,1024]{2,1,0:T(8,128)(2,1)S(1)}, bf16[3,80,1024]{2,1,0:T(8,128)(2,1)S(1)}, u32[]{:S(2)}, u32[]{:S(2)}) collective-permute-start(bf16[3,80,1024]{2,1,0:T(8,128)(2,1)S(1)} %get-tuple-element.227), channel_id=1, source_target_pairs={{0,8},{4,12},{8,0},{12,4},{16,24},{20,28},{24,16},{28,20},{1,9},{5... | collective-permute-start | bytes 1474568 | tf_op jit(solution)/shard_map/ppermute | solution.py:58
  129.0 11.2 %collective-permute-start.6 = (bf16[3,80,1024]{2,1,0:T(8,128)(2,1)S(1)}, bf16[3,80,1024]{2,1,0:T(8,128)(2,1)S(1)}, u32[]{:S(2)}, u32[]{:S(2)}) collective-permute-start(bf16[3,80,1024]{2,1,0:T(8,128)(2,1)S(1)} %get-tuple-element.228), channel_id=1, source_target_pairs={{0,16},{4,20},{8,24},{12,28},{16,0},{20,4},{24,8},{28,12},{1,17},{... | collective-permute-start | bytes 1474568 | tf_op jit(solution)/shard_map/ppermute | solution.py:58
  139.6 14.3 %collective-permute-start.16 = (bf16[2,3,80,1024]{3,2,1,0:T(8,128)(2,1)S(1)}, bf16[2,3,80,1024]{3,2,1,0:T(8,128)(2,1)}, u32[]{:S(2)}, u32[]{:S(2)}) collective-permute-start(bf16[2,3,80,1024]{3,2,1,0:T(8,128)(2,1)S(1)} %get-tuple-element.225), channel_id=1, source_target_pairs={{0,16},{4,20},{8,24},{12,28},{16,0},{20,4},{24,8},{28,12},{1,17},{... | collective-permute-start | bytes 2949128 | tf_op jit(solution)/shard_map/ppermute | solution.py:58
  141.2 15.3 %collective-permute-start.17 = (bf16[2,3,80,1024]{3,2,1,0:T(8,128)(2,1)}, bf16[2,3,80,1024]{3,2,1,0:T(8,128)(2,1)}, u32[]{:S(2)}, u32[]{:S(2)}) collective-permute-start(bf16[2,3,80,1024]{3,2,1,0:T(8,128)(2,1)} %get-tuple-element.223), channel_id=1, source_target_pairs={{0,8},{4,12},{8,0},{12,4},{16,24},{20,28},{24,16},{28,20},{1,9},{5... | collective-permute-start | bytes 2949128 | tf_op jit(solution)/shard_map/ppermute | solution.py:58
  156.6 46.0 %collective-permute-start.18 = (bf16[2,2,3,80,1024]{4,3,2,1,0:T(8,128)(2,1)}, bf16[2,2,3,80,1024]{4,3,2,1,0:T(8,128)(2,1)}, u32[]{:S(2)}, u32[]{:S(2)}) collective-permute-start(bf16[2,2,3,80,1024]{4,3,2,1,0:T(8,128)(2,1)} %pad_maximum_fusion.2.refs_18_.refs_3_.refs_12_), channel_id=1, source_target_pairs={{0,4},{4,0},{8,12},{12,8},{16,20},{20,16},{24,28},{28,24},{1,5},{5... | collective-permute-start | bytes 5898248 | tf_op jit(solution)/shard_map/ppermute | solution.py:58
  159.2 43.4 %collective-permute-start.19 = (bf16[2,2,3,80,1024]{4,3,2,1,0:T(8,128)(2,1)}, bf16[2,2,3,80,1024]{4,3,2,1,0:T(8,128)(2,1)}, u32[]{:S(2)}, u32[]{:S(2)}) collective-permute-start(bf16[2,2,3,80,1024]{4,3,2,1,0:T(8,128)(2,1)} %pad_maximum_fusion.3.refs_19_.refs_4_.refs_13_), channel_id=1, source_target_pairs={{0,4},{4,0},{8,12},{12,8},{16,20},{20,16},{24,28},{28,24},{1,5},{5... | collective-permute-start | bytes 5898248 | tf_op jit(solution)/shard_map/ppermute | solution.py:58
  178.4 16.0 %all-to-all-start = ((bf16[4,384,128]{2,1,0:T(8,128)(2,1)}), bf16[4,384,128]{2,1,0:T(8,128)(2,1)S(1)}, u32[]{:S(2)}, u32[]{:S(2)}) async-start(bf16[4,384,128]{2,1,0:T(8,128)(2,1)} %get-tuple-element.120), calls=%async_computation | async-start | bytes 786432 | tf_op jit(solution)/shard_map/all_to_all | solution.py:67
  194.4 15.5 %all-to-all-start.1 = ((bf16[4,384,128]{2,1,0:T(8,128)(2,1)}), bf16[4,384,128]{2,1,0:T(8,128)(2,1)S(1)}, u32[]{:S(2)}, u32[]{:S(2)}) async-start(bf16[4,384,128]{2,1,0:T(8,128)(2,1)} %get-tuple-element.123), calls=%async_computation.1 | async-start | bytes 786432 | tf_op jit(solution)/shard_map/all_to_all | solution.py:67
  241.6 12.1 %collective-permute-start.20 = (bf16[4,512,1024]{2,1,0:T(8,128)(2,1)}, bf16[4,512,1024]{2,1,0:T(8,128)(2,1)S(1)}, u32[]{:S(2)}, u32[]{:S(2)}) collective-permute-start(bf16[4,512,1024]{2,1,0:T(8,128)(2,1)} %shard_map.344), channel_id=1, source_target_pairs={{0,4},{4,0},{8,12},{12,8},{16,20},{20,16},{24,28},{28,24},{1,5},{5... | collective-permute-start | bytes 12582920 | tf_op jit(solution)/shard_map/ppermute | solution.py:58
  262.9 27.0 %collective-permute-start.21 = (bf16[4,128,1024]{2,1,0:T(8,128)(2,1)}, bf16[4,128,1024]{2,1,0:T(8,128)(2,1)}, u32[]{:S(2)}, u32[]{:S(2)}) collective-permute-start(bf16[4,128,1024]{2,1,0:T(8,128)(2,1)} %get-tuple-element.134), channel_id=1, source_target_pairs={{0,8},{4,12},{8,0},{12,4},{16,24},{20,28},{24,16},{28,20},{1,9},{5... | collective-permute-start | bytes 3145736 | tf_op jit(solution)/shard_map/ppermute | solution.py:58
  270.7 32.6 %collective-permute-start.23 = (bf16[4,128,4096]{2,1,0:T(8,128)(2,1)}, bf16[4,128,4096]{2,1,0:T(8,128)(2,1)}, u32[]{:S(2)}, u32[]{:S(2)}) collective-permute-start(bf16[4,128,4096]{2,1,0:T(8,128)(2,1)} %shard_map.347), channel_id=1, source_target_pairs={{0,4},{4,0},{8,12},{12,8},{16,20},{20,16},{24,28},{28,24},{1,5},{5... | collective-permute-start | bytes 12582920 | tf_op jit(solution)/shard_map/ppermute | solution.py:58
  270.9 25.3 %collective-permute-start.22 = (bf16[4,128,1024]{2,1,0:T(8,128)(2,1)S(1)}, bf16[4,128,1024]{2,1,0:T(8,128)(2,1)S(1)}, u32[]{:S(2)}, u32[]{:S(2)}) collective-permute-start(bf16[4,128,1024]{2,1,0:T(8,128)(2,1)S(1)} %copy-done.38), channel_id=1, source_target_pairs={{0,16},{4,20},{8,24},{12,28},{16,0},{20,4},{24,8},{28,12},{1,17},{... | collective-permute-start | bytes 3145736 | tf_op jit(solution)/shard_map/ppermute | solution.py:58
  285.5 25.7 %all-to-all-start.2 = ((bf16[4,384,256]{2,1,0:T(8,128)(2,1)}), bf16[4,384,256]{2,1,0:T(8,128)(2,1)}, u32[]{:S(2)}, u32[]{:S(2)}) async-start(bf16[4,384,256]{2,1,0:T(8,128)(2,1)} %get-tuple-element.151), calls=%async_computation.2 | async-start | bytes 1572864 | tf_op jit(solution)/shard_map/all_to_all | solution.py:67
  301.2 13.6 %collective-permute-start.24 = (bf16[4,64,1024]{2,1,0:T(8,128)(2,1)}, bf16[4,64,1024]{2,1,0:T(8,128)(2,1)S(1)}, u32[]{:S(2)}, u32[]{:S(2)}) collective-permute-start(bf16[4,64,1024]{2,1,0:T(8,128)(2,1)} %get-tuple-element.147), channel_id=1, source_target_pairs={{0,16},{4,20},{8,24},{12,28},{16,0},{20,4},{24,8},{28,12},{1,17},{... | collective-permute-start | bytes 1572872 | tf_op jit(solution)/shard_map/ppermute | solution.py:58
  302.5 13.3 %collective-permute-start.25 = (bf16[4,64,1024]{2,1,0:T(8,128)(2,1)}, bf16[4,64,1024]{2,1,0:T(8,128)(2,1)S(1)}, u32[]{:S(2)}, u32[]{:S(2)}) collective-permute-start(bf16[4,64,1024]{2,1,0:T(8,128)(2,1)} %get-tuple-element.155), channel_id=1, source_target_pairs={{0,8},{4,12},{8,0},{12,4},{16,24},{20,28},{24,16},{28,20},{1,9},{5... | collective-permute-start | bytes 1572872 | tf_op jit(solution)/shard_map/ppermute | solution.py:58
  319.5 28.2 %all-to-all-start.3 = ((bf16[4,2,64,1024]{3,2,1,0:T(8,128)(2,1)}), bf16[4,2,64,1024]{3,2,1,0:T(8,128)(2,1)S(1)}, u32[]{:S(2)}, u32[]{:S(2)}) async-start(bf16[4,2,64,1024]{3,2,1,0:T(8,128)(2,1)} %shard_map.351), calls=%async_computation.3 | async-start | bytes 2097152 | tf_op jit(solution)/shard_map/all_to_all | solution.py:67
  323.1 29.0 %collective-permute-start.26 = (bf16[4,32,4096]{2,1,0:T(8,128)(2,1)S(1)}, bf16[4,32,4096]{2,1,0:T(8,128)(2,1)}, u32[]{:S(2)}, u32[]{:S(2)}) collective-permute-start(bf16[4,32,4096]{2,1,0:T(8,128)(2,1)S(1)} %copy-done.37), channel_id=1, source_target_pairs={{0,8},{4,12},{8,0},{12,4},{16,24},{20,28},{24,16},{28,20},{1,9},{5... | collective-permute-start | bytes 3145736 | tf_op jit(solution)/shard_map/ppermute | solution.py:58
  324.0 28.2 %collective-permute-start.27 = (bf16[4,32,4096]{2,1,0:T(8,128)(2,1)S(1)}, bf16[4,32,4096]{2,1,0:T(8,128)(2,1)}, u32[]{:S(2)}, u32[]{:S(2)}) collective-permute-start(bf16[4,32,4096]{2,1,0:T(8,128)(2,1)S(1)} %copy-done.36), channel_id=1, source_target_pairs={{0,16},{4,20},{8,24},{12,28},{16,0},{20,4},{24,8},{28,12},{1,17},{... | collective-permute-start | bytes 3145736 | tf_op jit(solution)/shard_map/ppermute | solution.py:58
  347.6 32.6 %all-to-all-start.4 = ((bf16[4,384,384]{2,1,0:T(8,128)(2,1)}), bf16[4,384,384]{2,1,0:T(8,128)(2,1)}, u32[]{:S(2)}, u32[]{:S(2)}) async-start(bf16[4,384,384]{2,1,0:T(8,128)(2,1)} %shard_map.352), calls=%async_computation.4 | async-start | bytes 2359296 | tf_op jit(solution)/shard_map/all_to_all | solution.py:67
  356.1 24.2 %collective-permute-start.28 = (bf16[4,16,4096]{2,1,0:T(8,128)(2,1)}, bf16[4,16,4096]{2,1,0:T(8,128)(2,1)S(1)}, u32[]{:S(2)}, u32[]{:S(2)}) collective-permute-start(bf16[4,16,4096]{2,1,0:T(8,128)(2,1)} %get-tuple-element.163), channel_id=1, source_target_pairs={{0,16},{4,20},{8,24},{12,28},{16,0},{20,4},{24,8},{28,12},{1,17},{... | collective-permute-start | bytes 1572872 | tf_op jit(solution)/shard_map/ppermute | solution.py:58
  356.8 23.4 %collective-permute-start.29 = (bf16[4,16,4096]{2,1,0:T(8,128)(2,1)}, bf16[4,16,4096]{2,1,0:T(8,128)(2,1)S(1)}, u32[]{:S(2)}, u32[]{:S(2)}) collective-permute-start(bf16[4,16,4096]{2,1,0:T(8,128)(2,1)} %get-tuple-element.169), channel_id=1, source_target_pairs={{0,8},{4,12},{8,0},{12,4},{16,24},{20,28},{24,16},{28,20},{1,9},{5... | collective-permute-start | bytes 1572872 | tf_op jit(solution)/shard_map/ppermute | solution.py:58
  390.3 17.9 %collective-permute-start.32 = (bf16[4,128,1792]{2,1,0:T(8,128)(2,1)}, bf16[4,128,1792]{2,1,0:T(8,128)(2,1)}, u32[]{:S(2)}, u32[]{:S(2)}) collective-permute-start(bf16[4,128,1792]{2,1,0:T(8,128)(2,1)} %shard_map.356), channel_id=1, source_target_pairs={{0,4},{4,0},{8,12},{12,8},{16,20},{20,16},{24,28},{28,24},{1,5},{5... | collective-permute-start | bytes 5505032 | tf_op jit(solution)/shard_map/ppermute | solution.py:58
  391.4 6.1 %collective-permute-start.30 = (bf16[64,1024]{1,0:T(8,128)(2,1)S(1)}, bf16[64,1024]{1,0:T(8,128)(2,1)S(1)}, u32[]{:S(2)}, u32[]{:S(2)}) collective-permute-start(bf16[64,1024]{1,0:T(8,128)(2,1)S(1)} %copy-done.21), channel_id=1, source_target_pairs={{0,8},{4,12},{8,0},{12,4},{16,24},{20,28},{24,16},{28,20},{1,9},{5... | collective-permute-start | bytes 393224 | tf_op jit(solution)/shard_map/ppermute | solution.py:58
  392.5 32.7 %all-to-all-start.5 = ((bf16[4,384,384]{2,1,0:T(8,128)(2,1)}), bf16[4,384,384]{2,1,0:T(8,128)(2,1)S(1)}, u32[]{:S(2)}, u32[]{:S(2)}) async-start(bf16[4,384,384]{2,1,0:T(8,128)(2,1)} %shard_map.354), calls=%async_computation.5 | async-start | bytes 2359296 | tf_op jit(solution)/shard_map/all_to_all | solution.py:67
  396.1 6.4 %collective-permute-start.31 = (bf16[64,1024]{1,0:T(8,128)(2,1)S(1)}, bf16[64,1024]{1,0:T(8,128)(2,1)S(1)}, u32[]{:S(2)}, u32[]{:S(2)}) collective-permute-start(bf16[64,1024]{1,0:T(8,128)(2,1)S(1)} %copy-done.19), channel_id=1, source_target_pairs={{0,16},{4,20},{8,24},{12,28},{16,0},{20,4},{24,8},{28,12},{1,17},{... | collective-permute-start | bytes 393224 | tf_op jit(solution)/shard_map/ppermute | solution.py:58
  397.5 9.9 %collective-permute-start.37 = (bf16[2,64,1024]{2,1,0:T(8,128)(2,1)S(1)}, bf16[2,64,1024]{2,1,0:T(8,128)(2,1)S(1)}, u32[]{:S(2)}, u32[]{:S(2)}) collective-permute-start(bf16[2,64,1024]{2,1,0:T(8,128)(2,1)S(1)} %get-tuple-element.247), channel_id=1, source_target_pairs={{0,16},{4,20},{8,24},{12,28},{16,0},{20,4},{24,8},{28,12},{1,17},{... | collective-permute-start | bytes 786440 | tf_op jit(solution)/shard_map/ppermute | solution.py:58
  403.3 58.7 %collective-permute-start.38 = (bf16[2,64,1024]{2,1,0:T(8,128)(2,1)}, bf16[2,64,1024]{2,1,0:T(8,128)(2,1)}, u32[]{:S(2)}, u32[]{:S(2)}) collective-permute-start(bf16[2,64,1024]{2,1,0:T(8,128)(2,1)} %get-tuple-element.245), channel_id=1, source_target_pairs={{0,8},{4,12},{8,0},{12,4},{16,24},{20,28},{24,16},{28,20},{1,9},{5... | collective-permute-start | bytes 786440 | tf_op jit(solution)/shard_map/ppermute | solution.py:58
  408.2 79.2 %collective-permute-start.41 = (bf16[2,2,64,1024]{3,2,1,0:T(8,128)(2,1)}, bf16[2,2,64,1024]{3,2,1,0:T(8,128)(2,1)}, u32[]{:S(2)}, u32[]{:S(2)}) collective-permute-start(bf16[2,2,64,1024]{3,2,1,0:T(8,128)(2,1)} %pad_maximum_fusion.10.refs_0_), channel_id=1, source_target_pairs={{0,4},{4,0},{8,12},{12,8},{16,20},{20,16},{24,28},{28,24},{1,5},{5... | collective-permute-start | bytes 1572872 | tf_op jit(solution)/shard_map/ppermute | solution.py:58
  416.0 29.2 %collective-permute-start.33 = (bf16[4,32,1792]{2,1,0:T(8,128)(2,1)}, bf16[4,32,1792]{2,1,0:T(8,128)(2,1)}, u32[]{:S(2)}, u32[]{:S(2)}) collective-permute-start(bf16[4,32,1792]{2,1,0:T(8,128)(2,1)} %get-tuple-element.177), channel_id=1, source_target_pairs={{0,8},{4,12},{8,0},{12,4},{16,24},{20,28},{24,16},{28,20},{1,9},{5... | collective-permute-start | bytes 1376264 | tf_op jit(solution)/shard_map/ppermute | solution.py:58
  428.4 30.3 %all-to-all-start.6 = ((bf16[4,2,16,4096]{3,2,1,0:T(8,128)(2,1)}), bf16[4,2,16,4096]{3,2,1,0:T(8,128)(2,1)}, u32[]{:S(2)}, u32[]{:S(2)}) async-start(bf16[4,2,16,4096]{3,2,1,0:T(8,128)(2,1)} %shard_map.358), calls=%async_computation.6 | async-start | bytes 2097152 | tf_op jit(solution)/shard_map/all_to_all | solution.py:67
  433.1 12.1 %collective-permute-start.34 = (bf16[4,32,1792]{2,1,0:T(8,128)(2,1)S(1)}, bf16[4,32,1792]{2,1,0:T(8,128)(2,1)S(1)}, u32[]{:S(2)}, u32[]{:S(2)}) collective-permute-start(bf16[4,32,1792]{2,1,0:T(8,128)(2,1)S(1)} %copy-done.48), channel_id=1, source_target_pairs={{0,16},{4,20},{8,24},{12,28},{16,0},{20,4},{24,8},{28,12},{1,17},{... | collective-permute-start | bytes 1376264 | tf_op jit(solution)/shard_map/ppermute | solution.py:58
  448.6 15.2 %collective-permute-start.35 = (bf16[4,16,1792]{2,1,0:T(8,128)(2,1)}, bf16[4,16,1792]{2,1,0:T(8,128)(2,1)S(1)}, u32[]{:S(2)}, u32[]{:S(2)}) collective-permute-start(bf16[4,16,1792]{2,1,0:T(8,128)(2,1)} %get-tuple-element.186), channel_id=1, source_target_pairs={{0,16},{4,20},{8,24},{12,28},{16,0},{20,4},{24,8},{28,12},{1,17},{... | collective-permute-start | bytes 688136 | tf_op jit(solution)/shard_map/ppermute | solution.py:58
  449.6 14.2 %collective-permute-start.36 = (bf16[4,16,1792]{2,1,0:T(8,128)(2,1)}, bf16[4,16,1792]{2,1,0:T(8,128)(2,1)S(1)}, u32[]{:S(2)}, u32[]{:S(2)}) collective-permute-start(bf16[4,16,1792]{2,1,0:T(8,128)(2,1)} %get-tuple-element.190), channel_id=1, source_target_pairs={{0,8},{4,12},{8,0},{12,4},{16,24},{20,28},{24,16},{28,20},{1,9},{5... | collective-permute-start | bytes 688136 | tf_op jit(solution)/shard_map/ppermute | solution.py:58
  458.7 9.1 %all-to-all-start.7 = ((f32[4,20,256]{2,1,0:T(8,128)}), f32[4,20,256]{2,1,0:T(8,128)S(1)}, u32[]{:S(2)}, u32[]{:S(2)}) async-start(f32[4,20,256]{2,1,0:T(8,128)} %pad_maximum_fusion.24), calls=%async_computation.7 | async-start | bytes 196608 | tf_op jit(solution)/shard_map/all_to_all | solution.py:67
  463.8 23.6 %collective-permute-start.42 = (bf16[2,2,64,1024]{3,2,1,0:T(8,128)(2,1)}, bf16[2,2,64,1024]{3,2,1,0:T(8,128)(2,1)}, u32[]{:S(2)}, u32[]{:S(2)}) collective-permute-start(bf16[2,2,64,1024]{3,2,1,0:T(8,128)(2,1)} %pad_maximum_fusion.11.refs_1_), channel_id=1, source_target_pairs={{0,4},{4,0},{8,12},{12,8},{16,20},{20,16},{24,28},{28,24},{1,5},{5... | collective-permute-start | bytes 1572872 | tf_op jit(solution)/shard_map/ppermute | solution.py:58
  472.4 12.2 %collective-permute-start.39 = (bf16[16,4096]{1,0:T(8,128)(2,1)}, bf16[16,4096]{1,0:T(8,128)(2,1)S(1)}, u32[]{:S(2)}, u32[]{:S(2)}) collective-permute-start(bf16[16,4096]{1,0:T(8,128)(2,1)} %get-tuple-element.198), channel_id=1, source_target_pairs={{0,8},{4,12},{8,0},{12,4},{16,24},{20,28},{24,16},{28,20},{1,9},{5... | collective-permute-start | bytes 393224 | tf_op jit(solution)/shard_map/ppermute | solution.py:58
  473.4 7.9 %collective-permute-start.55 = (f32[39,256]{1,0:T(8,128)S(1)}, f32[39,256]{1,0:T(8,128)S(1)}, u32[]{:S(2)}, u32[]{:S(2)}) collective-permute-start(f32[39,256]{1,0:T(8,128)S(1)} %pad_maximum_fusion.25), channel_id=1, source_target_pairs={{0,16},{4,20},{8,24},{12,28},{16,0},{20,4},{24,8},{28,12},{1,17},{... | collective-permute-start | bytes 119816 | tf_op jit(solution)/shard_map/ppermute | solution.py:58
  477.0 16.4 %all-to-all-start.8 = ((bf16[4,2,16,1792]{3,2,1,0:T(8,128)(2,1)}), bf16[4,2,16,1792]{3,2,1,0:T(8,128)(2,1)S(1)}, u32[]{:S(2)}, u32[]{:S(2)}) async-start(bf16[4,2,16,1792]{3,2,1,0:T(8,128)(2,1)} %shard_map.362), calls=%async_computation.8 | async-start | bytes 917504 | tf_op jit(solution)/shard_map/all_to_all | solution.py:67
  480.6 5.5 %collective-permute-start.40 = (bf16[16,4096]{1,0:T(8,128)(2,1)S(1)}, bf16[16,4096]{1,0:T(8,128)(2,1)S(1)}, u32[]{:S(2)}, u32[]{:S(2)}) collective-permute-start(bf16[16,4096]{1,0:T(8,128)(2,1)S(1)} %copy-done.17), channel_id=1, source_target_pairs={{0,16},{4,20},{8,24},{12,28},{16,0},{20,4},{24,8},{28,12},{1,17},{... | collective-permute-start | bytes 393224 | tf_op jit(solution)/shard_map/ppermute | solution.py:58
  484.7 7.3 %collective-permute-start.43 = (bf16[2,16,4096]{2,1,0:T(8,128)(2,1)S(1)}, bf16[2,16,4096]{2,1,0:T(8,128)(2,1)S(1)}, u32[]{:S(2)}, u32[]{:S(2)}) collective-permute-start(bf16[2,16,4096]{2,1,0:T(8,128)(2,1)S(1)} %get-tuple-element.243), channel_id=1, source_target_pairs={{0,16},{4,20},{8,24},{12,28},{16,0},{20,4},{24,8},{28,12},{1,17},{... | collective-permute-start | bytes 786440 | tf_op jit(solution)/shard_map/ppermute | solution.py:58
  486.9 9.6 %collective-permute-start.44 = (bf16[2,16,4096]{2,1,0:T(8,128)(2,1)}, bf16[2,16,4096]{2,1,0:T(8,128)(2,1)}, u32[]{:S(2)}, u32[]{:S(2)}) collective-permute-start(bf16[2,16,4096]{2,1,0:T(8,128)(2,1)} %get-tuple-element.241), channel_id=1, source_target_pairs={{0,8},{4,12},{8,0},{12,4},{16,24},{20,28},{24,16},{28,20},{1,9},{5... | collective-permute-start | bytes 786440 | tf_op jit(solution)/shard_map/ppermute | solution.py:58
  492.1 19.8 %collective-permute-start.47 = (bf16[2,2,16,4096]{3,2,1,0:T(8,128)(2,1)S(1)}, bf16[2,2,16,4096]{3,2,1,0:T(8,128)(2,1)S(1)}, u32[]{:S(2)}, u32[]{:S(2)}) collective-permute-start(bf16[2,2,16,4096]{3,2,1,0:T(8,128)(2,1)S(1)} %pad_maximum_fusion.12.refs_0_), channel_id=1, source_target_pairs={{0,4},{4,0},{8,12},{12,8},{16,20},{20,16},{24,28},{28,24},{1,5},{5... | collective-permute-start | bytes 1572872 | tf_op jit(solution)/shard_map/ppermute | solution.py:58
  495.9 5.2 collective-permute-start.45
  497.5 14.4 %collective-permute-start.48 = (bf16[2,2,16,4096]{3,2,1,0:T(8,128)(2,1)S(1)}, bf16[2,2,16,4096]{3,2,1,0:T(8,128)(2,1)S(1)}, u32[]{:S(2)}, u32[]{:S(2)}) collective-permute-start(bf16[2,2,16,4096]{3,2,1,0:T(8,128)(2,1)S(1)} %pad_maximum_fusion.13.refs_1_), channel_id=1, source_target_pairs={{0,4},{4,0},{8,12},{12,8},{16,20},{20,16},{24,28},{28,24},{1,5},{5... | collective-permute-start | bytes 1572872 | tf_op jit(solution)/shard_map/ppermute | solution.py:58
  497.6 6.6 %collective-permute-start.46 = (bf16[16,4096]{1,0:T(8,128)(2,1)}, bf16[16,4096]{1,0:T(8,128)(2,1)S(1)}, u32[]{:S(2)}, u32[]{:S(2)}) collective-permute-start(bf16[16,4096]{1,0:T(8,128)(2,1)} %get-tuple-element.207), channel_id=1, source_target_pairs={{0,16},{4,20},{8,24},{12,28},{16,0},{20,4},{24,8},{28,12},{1,17},{... | collective-permute-start | bytes 393224 | tf_op jit(solution)/shard_map/ppermute | solution.py:58
  502.0 7.3 %collective-permute-start.49 = (bf16[2,16,4096]{2,1,0:T(8,128)(2,1)S(1)}, bf16[2,16,4096]{2,1,0:T(8,128)(2,1)S(1)}, u32[]{:S(2)}, u32[]{:S(2)}) collective-permute-start(bf16[2,16,4096]{2,1,0:T(8,128)(2,1)S(1)} %get-tuple-element.239), channel_id=1, source_target_pairs={{0,16},{4,20},{8,24},{12,28},{16,0},{20,4},{24,8},{28,12},{1,17},{... | collective-permute-start | bytes 786440 | tf_op jit(solution)/shard_map/ppermute | solution.py:58
  504.2 7.5 %collective-permute-start.50 = (bf16[2,16,4096]{2,1,0:T(8,128)(2,1)S(1)}, bf16[2,16,4096]{2,1,0:T(8,128)(2,1)S(1)}, u32[]{:S(2)}, u32[]{:S(2)}) collective-permute-start(bf16[2,16,4096]{2,1,0:T(8,128)(2,1)S(1)} %get-tuple-element.237), channel_id=1, source_target_pairs={{0,8},{4,12},{8,0},{12,4},{16,24},{20,28},{24,16},{28,20},{1,9},{5... | collective-permute-start | bytes 786440 | tf_op jit(solution)/shard_map/ppermute | solution.py:58
  509.4 7.9 %collective-permute-start.51 = (bf16[2,2,16,4096]{3,2,1,0:T(8,128)(2,1)S(1)}, bf16[2,2,16,4096]{3,2,1,0:T(8,128)(2,1)S(1)}, u32[]{:S(2)}, u32[]{:S(2)}) collective-permute-start(bf16[2,2,16,4096]{3,2,1,0:T(8,128)(2,1)S(1)} %pad_maximum_fusion.14.refs_0_), channel_id=1, source_target_pairs={{0,4},{4,0},{8,12},{12,8},{16,20},{20,16},{24,28},{28,24},{1,5},{5... | collective-permute-start | bytes 1572872 | tf_op jit(solution)/shard_map/ppermute | solution.py:58
  511.8 5.6 %collective-permute-start.52 = (bf16[2,2,16,4096]{3,2,1,0:T(8,128)(2,1)S(1)}, bf16[2,2,16,4096]{3,2,1,0:T(8,128)(2,1)S(1)}, u32[]{:S(2)}, u32[]{:S(2)}) collective-permute-start(bf16[2,2,16,4096]{3,2,1,0:T(8,128)(2,1)S(1)} %pad_maximum_fusion.15.refs_1_), channel_id=1, source_target_pairs={{0,4},{4,0},{8,12},{12,8},{16,20},{20,16},{24,28},{28,24},{1,5},{5... | collective-permute-start | bytes 1572872 | tf_op jit(solution)/shard_map/ppermute | solution.py:58
  (54 other events, 419.0 us)
Sparse Core Ops, SparseCore 0:
  78.2 69.6 all-gather.1

commit v4 on v3

--- a/solution.py
+++ b/solution.py
@@ -16,6 +16,7 @@
 TAIL = 128
 PAIR = 2 * HD
 STEP = 512
+FACTOR = 16
 LOG2E = 1.4426950408889634
 LOW = jnp.bfloat16
 WIDE = jnp.float32
@@ -29,8 +30,9 @@
     return pltpu.CompilerParams(vmem_limit_bytes=mib << 20)
 
 
-def cost():
-    return pl.CostEstimate(flops=10**11, bytes_accessed=10**9, transcendentals=0)
+def cost(us):
+    us = us * FACTOR
+    return pl.CostEstimate(flops=int(us * 1e9), bytes_accessed=int(us * 3e6), transcendentals=0)
 
 
 def shape(*dims, dtype=LOW):
@@ -58,31 +60,38 @@
     return lax.ppermute(value, "dp", [(i, i ^ mask) for i in range(size)])
 
 
-def turn(value, k):
-    size = lax.axis_size("ctx")
-    return lax.ppermute(value, "ctx", [(i, (i + k) % size) for i in range(size)])
-
-
-def exchange(value):
-    return lax.all_to_all(value, "ctx", 0, 0)
+def along(value, *pairs):
+    return lax.ppermute(value, "ctx", pairs)
+
+
+def exchange(value, axis="ctx"):
+    return lax.all_to_all(value, axis, 0, 0)
 
 
 def after(value, *others):
     return lax.optimization_barrier((value, *others))[0]
 
 
-def shard_gather(value, *early):
-    n = lax.axis_size("ctx")
-    value = after(value, *early) if early else value
-    if n != 4:
-        got = [turn(value, k) for k in range(1, n)]
-        return got, got[0]
+def two_off(value):
+    return along(value, (0, 2), (1, 3), (2, 0), (3, 1))
+
+
+def one_off(value):
+    return along(value, (0, 1), (1, 2), (2, 3)), along(value, (1, 0), (2, 1), (3, 2))
+
+
+def sent_on(far):
+    return along(far, (2, 3), (1, 0))
+
+
+def by_distance(far, up, down, on):
     place = lax.axis_index("ctx")
-    far = lax.ppermute(value, "ctx", [(0, 2), (1, 3), (2, 0), (3, 1)])
-    up = lax.ppermute(value, "ctx", [(0, 1), (1, 2), (2, 3)])
-    down = lax.ppermute(value, "ctx", [(1, 0), (2, 1), (3, 2)])
-    on = lax.ppermute(far, "ctx", [(2, 3), (1, 0)])
-    return [jnp.where(place == 0, on, up), far, jnp.where(place == n - 1, on, down)], far
+    return jnp.stack([jnp.where(place == 0, on, up), far, jnp.where(place == 3, on, down)])
+
+
+def copy_numbers(ids, out):
+    for i in range(ids.shape[0]):
+        out[i] = ids[i]
 
 
 class Order:
@@ -96,6 +105,20 @@
 
     def wait(self, *values):
         self.ids = after(self.ids, *values)
+
+    def tick(self, *values):
+        self.wait(*values)
+        self.call(
+            copy_numbers,
+            in_specs=[SMEM],
+            out_specs=SMEM,
+            out_shape=jax.ShapeDtypeStruct(self.ids.shape, jnp.int32),
+            cost_estimate=cost(0),
+        )
+
+    def release(self, *values):
+        outs = lax.optimization_barrier((*values, self.ids))[:-1]
+        return outs if len(outs) > 1 else outs[0]
 
 
 def gather_near(one, two):
@@ -252,7 +275,7 @@
         ),
         out_shape=[shape(n, slots, PAIR), shape(8, n * slots, dtype=WIDE)],
         compiler_params=params(),
-        cost_estimate=cost(),
+        cost_estimate=cost(11),
     )
 
 
@@ -332,7 +355,7 @@
         ),
         out_shape=shape(n, slots, 3 * PAIR),
         compiler_params=params(),
-        cost_estimate=cost(),
+        cost_estimate=cost(16),
     )
 
 
@@ -347,18 +370,15 @@
     return (grad - jnp.mean(grad, -1, keepdims=True) - unit * inner) * scale
 
 
-def wide(ref):
-    return ref[...].astype(WIDE)
-
-
 def forward(n, pairs, ids, *refs):
     parts, refs = refs[:pairs], refs[pairs:]
     start, cotangent, wo_own, wi_own, wu_own = refs[:5]
-    bo, bi, bu, gain1, shift1, gain2, shift2 = refs[5:12]
-    refs = refs[12:]
+    vectors, bi = refs[5:7]
+    bo, bu, gain1, shift1, gain2, shift2 = [vectors.at[i : i + 1] for i in range(6)]
+    refs = refs[7:]
     side, tall, refs = refs[:4], refs[4:8], refs[8:]
     attn, first, normed_low, active, slope, out, grad_second, second_low, sums = refs[:9]
-    wo, wi, wu, normed, second, sem_o, sem_i, sem_u = refs[9:]
+    wo, wi, wu, normed, second, ordered, sem_o, sem_i, sem_u = refs[9:]
     slots, width = start.shape
     cols = width // n
     hidden = active.shape[1]
@@ -373,15 +393,18 @@
     for g in range(n):
         for p in range(pairs):
             attn[:, pl.ds(g * cols + p * PAIR, PAIR)] = parts[p][g]
+
+    def put_in_order(ref):
+        for k in range(n):
+            ordered[:, k * cols : (k + 1) * cols] = ref[:, part_of(shard_of(ids, k, n) * cols, cols)]
+
+    put_in_order(attn)
     finish(get_o)
 
     def mix(j, _):
         column = part_of(j * STEP, STEP)
-        total = start[:, column] + wide(bo.at[:, column])
-        for k in range(n):
-            left = attn[:, part_of(shard_of(ids, k, n) * cols, cols)]
-            total = total + dot(left, wo[k, :, column])
-        first[:, column] = total
+        total = dot(ordered[...], wo[:, :, column].reshape(width, STEP))
+        first[:, column] = total + start[:, column] + bo[:, column]
         return 0
 
     lax.fori_loop(0, width // STEP, mix, 0)
@@ -389,26 +412,25 @@
     def norm(i, _):
         row = part_of(i * 128, 128)
         unit, _ = normal(first[row, :])
-        value = unit * wide(gain1) + wide(shift1)
+        value = unit * gain1[...] + shift1[...]
         normed[row, :] = value
         normed_low[row, :] = value.astype(LOW)
         return 0
 
     lax.fori_loop(0, slots // 128, norm, 0)
+    put_in_order(normed_low)
     finish(get_i)
 
     def expand(j, _):
         column = part_of(j * STEP, STEP)
-        x = jnp.broadcast_to(wide(bi.at[:, column]), (slots, STEP))
-        for k in range(n):
-            left = normed_low[:, part_of(shard_of(ids, k, n) * cols, cols)]
-            x = x + dot(left, wi[k, :, column])
+        x = dot(ordered[...], wi[:, :, column].reshape(width, STEP)) + bi[:, column]
         factor = math.sqrt(2 / math.pi)
         square = x * x
         t = jnp.tanh(factor * x * (1.0 + 0.044715 * square))
         half = 0.5 * (1.0 + t)
         active[:, column] = (x * half).astype(LOW)
-        slope[:, column] = half + (0.5 * factor) * x * (1.0 - t * t) * (1.0 + 0.134145 * square)
+        steep = half + (0.5 * factor) * x * (1.0 - t * t) * (1.0 + 0.134145 * square)
+        slope[:, column] = steep.astype(LOW)
         return 0
 
     lax.fori_loop(0, hidden // STEP, expand, 0)
@@ -416,7 +438,7 @@
 
     def contract(j, _):
         column = part_of(j * STEP, STEP)
-        total = normed[:, column] + wide(bu.at[:, column])
+        total = normed[:, column] + bu[:, column]
         for k in range(n):
             left = active[:, part_of(shard_of(ids, k, n) * deep, deep)]
             total = total + dot(left, wu[k, :, column])
@@ -431,9 +453,9 @@
         live = lax.broadcasted_iota(jnp.int32, (128, 1), 0) + i * 128 < ids[OWNED]
         live = live.astype(WIDE)
         unit, scale = normal(second[row, :])
-        out[row, :] = ((unit * wide(gain2) + wide(shift2)) * live).astype(LOW)
+        out[row, :] = ((unit * gain2[...] + shift2[...]) * live).astype(LOW)
         grad = cotangent[row, :].astype(WIDE) * live
-        result = normal_back(grad * wide(gain2), unit, scale)
+        result = normal_back(grad * gain2[...], unit, scale)
         grad_second[row, :] = result
         second_low[row, :] = result.astype(LOW)
         for j, item in enumerate((grad * unit, grad, result)):
@@ -457,7 +479,7 @@
         for k in range(n):
             column = part_of(shard_of(ids, k, n) * deep + j * STEP, STEP)
             grad = right_dot(second_low[...], wu[k, part_of(j * STEP, STEP), :])
-            value = (grad * slope[:, column]).astype(LOW)
+            value = (grad * slope[:, column].astype(WIDE)).astype(LOW)
             inner_low[:, column] = value
             bias_sum[:, column] = jnp.sum(value.astype(WIDE), 0, keepdims=True)
         return 0
@@ -466,7 +488,7 @@
 
 
 def backward(n, ids, *refs):
-    inner_low, bias_sum, grad_second, first, gain1, sums, wo_own, wi_own = refs[:8]
+    inner_low, bias_sum, grad_second, first, vectors, sums, wo_own, wi_own = refs[:8]
     side, tall, refs = refs[8:12], refs[12:16], refs[16:]
     grad_first, first_low = refs[:2]
     grad_attn, small = refs[2:4]
@@ -490,7 +512,7 @@
         row = part_of(i * 128, 128)
         unit, scale = normal(first[row, :])
         grad = grad_normed[row, :]
-        result = normal_back(grad * wide(gain1), unit, scale)
+        result = normal_back(grad * vectors[2:3], unit, scale)
         grad_first[row, :] = result
         first_low[row, :] = result.astype(LOW)
         for j, item in enumerate((result, grad * unit, grad)):
@@ -596,7 +618,7 @@
         ),
         out_shape=[shape(n, out_rows, total)] * count,
         compiler_params=params(),
-        cost_estimate=cost(),
+        cost_estimate=cost(0),
     )
 
 
@@ -617,16 +639,18 @@
         out[z, 1] = (keep_two[z].astype(WIDE) + got_two[z].astype(WIDE)).astype(LOW)
 
 
-def fold_four(split, ids, terms, *outs):
-    n, cols = terms.shape[0], terms.shape[3]
-    for h, out in enumerate(outs):
-        if split < cols:
-            total = terms[0, h, :, split:].astype(WIDE)
-            for z in range(1, n):
-                total = total + terms[z, h, :, split:].astype(WIDE)
-            out[:, n * split :] = total.astype(LOW)
-        for z in range(n if split else 0):
-            out[:, z * split : (z + 1) * split] = terms[z, h, :, :split]
+def fold_four(splits, ids, *refs):
+    parts, outs = refs[: len(splits)], refs[len(splits) :]
+    for i, (split, terms) in enumerate(zip(splits, parts)):
+        n, cols = terms.shape[0], terms.shape[3]
+        for h, out in enumerate(outs):
+            if split < cols:
+                total = terms[0, h, :, split:].astype(WIDE)
+                for z in range(1, n):
+                    total = total + terms[z, h, :, split:].astype(WIDE)
+                out[i, :, n * split :] = total.astype(LOW)
+            for z in range(n if split else 0):
+                out[i, :, z * split : (z + 1) * split] = terms[z, h, :, :split]
 
 
 def small_call(order, body, args, outs):
@@ -637,7 +661,7 @@
         out_specs=[VMEM] * len(outs),
         out_shape=outs,
         compiler_params=params(),
-        cost_estimate=cost(),
+        cost_estimate=cost(0),
     )
 
 
@@ -658,16 +682,16 @@
     return keep_one, swap(send_one, 4), keep_two, swap(send_two, 2)
 
 
-def reduce_fourth(order, n, held):
+def reduce_fourth(order, n, held, send=True):
     rows, cols = held[0].shape[1:]
     (out,) = small_call(order, fold_three, held, [shape(n, 2, rows, cols)])
-    return exchange(out)
-
-
-def reduce_fifth(order, held, split=0):
-    n, _, rows, cols = held.shape
-    outs = [shape(rows, cols + (n - 1) * split)] * 2
-    one, two = small_call(order, functools.partial(fold_four, split), [held], outs)
+    return exchange(out) if send else out
+
+
+def reduce_fifth(order, held, splits):
+    n, _, rows, cols = held[0].shape
+    outs = [shape(len(held), rows, cols + (n - 1) * splits[0])] * 2
+    one, two = small_call(order, functools.partial(fold_four, splits), held, outs)
     mask = GROUP
     while mask < lax.axis_size("dp"):
         one, two = [(v.astype(WIDE) + swap(v, mask).astype(WIDE)).astype(LOW) for v in (one, two)]
@@ -677,7 +701,7 @@
 
 def place_grad(plan, ids, *refs):
     pieces, outs = refs[:4], refs[4:]
-    rows = pieces[0].shape[2]
+    rows = pieces[0].shape[3]
     for i in range(2 * GROUP):
         piece = piece_of(pieces, i // 2, i % 2)
         home = ids[INDEX] ^ (i // 2)
@@ -685,12 +709,13 @@
         block = core * 8 + (x * 2 + y if i % 2 == 0 else 4 + y * 2 + x)
         row = part_of(block * rows, rows)
         for out, moves in zip(outs, plan):
-            for source, target, size in moves:
-                out[row, target : target + size] = piece[:, source : source + size].astype(WIDE)
+            for layer, source, target, size in moves:
+                value = piece[layer, :, source : source + size]
+                out[row, target : target + size] = value.astype(WIDE)
 
 
 def reduce_last(order, pieces, plan, widths):
-    rows = pieces[0].shape[2] * 2 * GROUP
+    rows = pieces[0].shape[3] * 2 * GROUP
     return small_call(
         order,
         functools.partial(place_grad, plan),
@@ -760,19 +785,40 @@
         [piece(w) for w in (query_weight, key_weight, value_weight, inner_weight)], 2
     )
     tall_piece = jnp.concatenate([piece(output_weight), piece(outer_weight)], 1)
-    side, early = shard_gather(side_piece)
-    tall, late = shard_gather(tall_piece, early)
-    row_low = lax.all_gather(after(start_low, late), "ctx", tiled=True)
-    side, tall = jnp.stack(side), jnp.stack(tall)
-    side = gather_cores(*gather_far(*gather_near(side[:, 0], side[:, 1])))
+    one, two = one_off(side_piece)
+    far = two_off(side_piece)
+    order.tick(far)
+    on = sent_on(order.release(far))
+    tall_far = two_off(order.release(tall_piece))
+    order.tick(one, two, on)
+    side = by_distance(far, one, two, on)
+    side = gather_near(side[:, 0], side[:, 1])
+    one, two = one_off(order.release(tall_piece))
+    order.tick(tall_far, *side)
+    on = sent_on(order.release(tall_far))
+    side = gather_far(*side)
+    order.tick(one, two, on)
+    row_low = exchange(jnp.broadcast_to(order.release(start_low), (n, slots, width)))
+    row_low = row_low.reshape(n * slots, width)
+    tall = by_distance(tall_far, one, two, on)
     tall = gather_near(tall[:, 0], tall[:, 1])
-    order.wait(*tall)
+    order.tick(*side)
+    side = gather_cores(*side)
+    order.tick(*tall)
     tall = gather_far(*tall)
+    vectors = (output_bias, outer_bias, attn_gain, attn_shift, ffn_gain, ffn_shift)
+    vectors = jnp.stack([v.astype(WIDE) for v in vectors])
+    inner_row = inner_bias.astype(WIDE)[None]
     own_bias = lambda v: lax.dynamic_slice_in_dim(v, place * cols, cols, 0).astype(WIDE)
     qkv_bias = jnp.concatenate([own_bias(query_bias), jnp.zeros((cols,), WIDE), own_bias(value_bias)])
+    qkv_bias = qkv_bias[None]
+    vectors, inner_row, qkv_bias, bias_row, bias_col, start = lax.optimization_barrier(
+        (vectors, inner_row, qkv_bias, bias_row, bias_col, start)
+    )
+    order.wait(vectors, inner_row, qkv_bias, bias_row, bias_col, start)
     qkv = order.call(
         functools.partial(project, n),
-        *(row_low, query_weight, key_weight, value_weight, *side, qkv_bias[None]),
+        *(row_low, query_weight, key_weight, value_weight, *side, qkv_bias),
         in_specs=[SMEM] + [VMEM] + [ANY] * 7 + [VMEM],
         out_specs=VMEM,
         out_shape=shape(span, 3 * cols),
@@ -782,7 +828,7 @@
             pltpu.SemaphoreType.DMA((3 + 6 * GROUP,)),
         ],
         compiler_params=params(),
-        cost_estimate=cost(),
+        cost_estimate=cost(8),
     )
 
     mixed, lses = [], []
@@ -792,9 +838,11 @@
             tall = gather_cores(*tall)
         mix, lse = attention(order, qkv, bias_row, pair, pairs, n, slots)
         lses.append(lse)
+        if mixed:
+            order.tick(mixed[-1])
+            mix = order.release(mix)
         mixed.append(exchange(mix))
 
-    row = lambda v: v[None, :]
     held_o = pltpu.VMEM((n, cols, width), LOW)
     held_i = pltpu.VMEM((n, cols, hidden), LOW)
     held_u = pltpu.VMEM((n, deep, width), LOW)
@@ -804,24 +852,27 @@
     attn, first, normed_low, active, slope, out, grad_second, second_low, sums = order.call(
         functools.partial(forward, n, pairs),
         *(*mixed, start, cotangent[0], output_weight, inner_weight, outer_weight),
-        *(row(output_bias), row(inner_bias), row(outer_bias)),
-        *(row(attn_gain), row(attn_shift), row(ffn_gain), row(ffn_shift), *side, *tall),
-        in_specs=[SMEM] + [VMEM] * (pairs + 2) + [ANY] * 3 + [VMEM] * 7 + [ANY] * 8,
+        *(vectors, inner_row, *side, *tall),
+        in_specs=[SMEM] + [VMEM] * (pairs + 2) + [ANY] * 3 + [VMEM] * 2 + [ANY] * 8,
         out_specs=[VMEM] * 9,
         out_shape=[
             shape(slots, width),
             shape(slots, width, dtype=WIDE),
             shape(slots, width),
             shape(slots, hidden),
-            shape(slots, hidden, dtype=WIDE),
+            shape(slots, hidden),
             shape(slots, width),
             shape(slots, width, dtype=WIDE),
             shape(slots, width),
             shape(8, width, dtype=WIDE),
         ],
-        scratch_shapes=[held_o, held_i, held_u, wide_one, wide_one, sem, sem, sem],
+        scratch_shapes=[
+            *(held_o, held_i, held_u, wide_one, wide_one),
+            pltpu.VMEM((slots, width), LOW),
+            *(sem, sem, sem),
+        ],
         compiler_params=params(),
-        cost_estimate=cost(),
+        cost_estimate=cost(24),
     )
     outer_spec = [([(active, second_low)], width)]
     outer_held = reduce_first(order, outer_spec, n)
@@ -833,14 +884,14 @@
         out_shape=[shape(slots, hidden), shape(1, hidden, dtype=WIDE)],
         scratch_shapes=[held_u, sem],
         compiler_params=params(),
-        cost_estimate=cost(),
+        cost_estimate=cost(12),
     )
     outer_held = reduce_second(order, outer_spec, n, outer_held)
     inner_spec = [([(normed_low, inner_low)], hidden)]
     inner_held = reduce_first(order, inner_spec, n)
     grad_first, first_low, grad_attn, small = order.call(
         functools.partial(backward, n),
-        *(inner_low, bias_sum, grad_second, first, row(attn_gain), sums),
+        *(inner_low, bias_sum, grad_second, first, vectors, sums),
         *(output_weight, inner_weight, *side, *tall),
         in_specs=[SMEM] + [VMEM] * 6 + [ANY] * 10,
         out_specs=[VMEM] * 4,
@@ -852,7 +903,7 @@
         ],
         scratch_shapes=[held_o, held_i, wide_one, pltpu.VMEM((8, width), WIDE), sem, sem],
         compiler_params=params(),
-        cost_estimate=cost(),
+        cost_estimate=cost(13),
     )
     grad_mixed = exchange(grad_attn)
     outer_held = reduce_third(order, n, outer_held)
@@ -861,26 +912,29 @@
     outer_held = reduce_fourth(order, n, outer_held)
 
     backs, received = [], []
-
-    def head_pair(pair):
-        back = attention_back(order, qkv, bias_col, grad_mixed, lses[pair], pair, pairs, n, slots)
-        backs.append(back)
-        received.append(exchange(back))
-
-    head_pair(0)
-    order.wait(outer_held)
-    inner_held = reduce_third(order, n, inner_held)
-    for pair in range(1, pairs):
-        head_pair(pair)
-        order.wait(received[-2], *inner_held)
-    outer_pieces = gather_near(*reduce_fifth(order, outer_held))
+    for pair in range(pairs):
+        if pair:
+            received.append(exchange(backs[-1]))
+            order.wait(outer_held)
+            outer_pieces = gather_near(*reduce_fifth(order, [outer_held], [0]))
+            inner_held = reduce_third(order, n, inner_held)
+        backs.append(
+            attention_back(order, qkv, bias_col, grad_mixed, lses[pair], pair, pairs, n, slots)
+        )
+    order.wait(*received, *inner_held, *outer_pieces)
+    received.append(exchange(backs[-1]))
+    outer_pieces = gather_far(*order.release(*outer_pieces))
     rest_spec = [([(row_low, back.reshape(n * slots, -1))], 3 * PAIR) for back in backs]
     rest_spec += [([(attn, first_low)], width)]
     rest_held = reduce_first(order, rest_spec, n)
+    inner_held = reduce_fourth(order, n, inner_held, False)
     order.wait(*outer_pieces)
+    outer_pieces = gather_cores(*order.release(*outer_pieces))
     rest_held = reduce_second(order, rest_spec, n, rest_held)
-    order.wait(*received)
-    inner_held = reduce_fourth(order, n, inner_held)
+    order.tick(received[-1])
+    inner_held = exchange(order.release(inner_held))
+    (outer_grad,) = reduce_last(order, outer_pieces, [[(0, 0, 0, width)]], [width])
+    rest_held = reduce_third(order, n, rest_held)
     grad_hidden, block_sum = order.call(
         functools.partial(finish_hidden, n, pairs),
         *(*received, grad_first, query_weight, key_weight, value_weight, *side),
@@ -893,29 +947,30 @@
             pltpu.SemaphoreType.DMA((3 + 2 * GROUP,)),
         ],
         compiler_params=params(),
-        cost_estimate=cost(),
-    )
-    rest_held = reduce_third(order, n, rest_held)
+        cost_estimate=cost(9),
+    )
     order.wait(*rest_held)
-    outer_pieces = gather_far(*outer_pieces)
-    order.wait(*outer_pieces)
-    outer_pieces = gather_cores(*outer_pieces)
-    order.wait(inner_held)
+    rest_held = reduce_fourth(order, n, rest_held, False)
+    order.tick(inner_held)
+    rest_held = exchange(order.release(rest_held))
+    inner_pieces = gather_near(*reduce_fifth(order, [inner_held], [0]))
+    order.tick(rest_held, *inner_pieces)
+    inner_pieces = gather_far(*order.release(*inner_pieces))
+    pieces = gather_near(*reduce_fifth(order, [rest_held], [3 * cols]))
 
     packed = jnp.concatenate([small, block_sum.reshape(1, n, cols).repeat(n, 0)], 1)
-    total = jnp.sum(exchange(after(packed, inner_held)), 0)
-    order.wait(total)
+    total = jnp.sum(exchange(order.release(packed)), 0)
     used = small.shape[1]
     bias_sums = jnp.stack([jnp.sum(back.astype(WIDE), (0, 1)) for back in backs])
-    vector = jnp.concatenate([total[used:], jnp.full((1, cols), timestep[0], WIDE)])[None]
-    total = jnp.concatenate([total[:used], bias_sums.reshape(-1, cols)])
-    mask = 1
-    while mask < lax.axis_size("dp"):
-        flat = jnp.concatenate([total, vector.reshape(-1, cols)])
-        flat = swap(flat, mask)
-        total = total + flat[: total.shape[0]]
-        vector = jnp.concatenate([vector, flat[total.shape[0] :].reshape(vector.shape)])
-        mask *= 2
+    level = jnp.full((1, cols), timestep[0], WIDE)
+    total = jnp.concatenate([total, level, bias_sums.reshape(-1, cols)])
+    order.tick(*inner_pieces, total)
+    inner_pieces = gather_cores(*order.release(*inner_pieces))
+    rows = lax.axis_size("dp")
+    total = exchange(jnp.broadcast_to(order.release(total), (rows, *total.shape)), "dp")
+    vector = total[:, used : used + n + 1]
+    total = jnp.sum(total, 0)
+    total = jnp.concatenate([total[:used], total[used + n + 1 :]])
     per = deep // cols
     sums = [total[0], total[1 : 1 + per].reshape(deep)] + [total[1 + per + i] for i in range(5)]
     bias_sums = total[used:].reshape(pairs, 3 * PAIR)
@@ -932,28 +987,21 @@
         preferred_element_type=WIDE,
     )
 
-    inner_pieces = gather_near(*reduce_fifth(order, inner_held))
-    rest_held = reduce_fourth(order, n, rest_held)
-    order.wait(*inner_pieces)
-    inner_pieces = gather_far(*inner_pieces)
-    (outer_grad,) = reduce_last(order, outer_pieces, [[(0, 0, width)]], [width])
-    rest_pieces = gather_near(*reduce_fifth(order, rest_held, 3 * cols))
-    order.wait(*inner_pieces)
-    inner_pieces = gather_cores(*inner_pieces)
-    order.wait(*rest_pieces)
-    rest_pieces = gather_far(*rest_pieces)
-    (inner_grad,) = reduce_last(order, inner_pieces, [[(0, 0, hidden)]], [hidden])
-    rest_pieces = gather_cores(*rest_pieces)
+    order.wait(*pieces)
+    pieces = gather_far(*order.release(*pieces))
+    (inner_grad,) = reduce_last(order, inner_pieces, [[(0, 0, 0, hidden)]], [hidden])
+    order.wait(*pieces)
+    pieces = gather_cores(*order.release(*pieces))
     plan = [
         [
-            (g * 3 * cols + p * 3 * PAIR + j * PAIR, g * cols + p * PAIR, PAIR)
+            (0, g * 3 * cols + p * 3 * PAIR + j * PAIR, g * cols + p * PAIR, PAIR)
             for g in range(n)
             for p in range(pairs)
         ]
         for j in range(3)
     ]
-    plan += [[(n * 3 * cols, 0, width)]]
-    *weight_grads, output_grad = reduce_last(order, rest_pieces, plan, [width] * 4)
+    plan += [[(0, n * 3 * cols, 0, width)]]
+    *weight_grads, output_grad = reduce_last(order, pieces, plan, [width] * 4)
     return (
         out[None],
         grad_hidden[None],

time: 539 us -> 528 us (0.980)
  between operations: 17.3 us -> 3.92 us
  starting transfers between devices: 93.3 us -> 99.5 us
    ppermute x8, waiting for transfers between devices: 47.6 us -> 31.1 us  [along(): return lax.ppermute(value, 'ctx', pairs)]
    ppermute x48 -> x45, waiting for transfers between devices: 69.5 us -> 79.5 us  [swap(): return lax.ppermute(value, 'dp', [(i, i ^ mask) for i in range(size)])]
    all_to_all x9 -> x11, starting transfers between devices: 35.4 us -> 44.3 us  [exchange(): return lax.all_to_all(value, axis, 0, 0)]
    all_to_all x9 -> x11, waiting for transfers between devices: 40.4 us -> 47.7 us  [exchange(): return lax.all_to_all(value, axis, 0, 0)]
    another operation x20 -> x14, other arithmetic: 22.9 us -> 19.2 us  [gather_far(): return (jnp.stack([one, swap(one, 4)]), jnp.stack([two, swap(two, 2)]))]
    ppermute x48 -> x45, starting transfers between devices: 38.6 us -> 37.4 us  [swap(): return lax.ppermute(value, 'dp', [(i, i ^ mask) for i in range(size)])]
    unnamed x107 -> x98, local copies, waits for them, and re-layouts: 12.2 us -> 13.4 us
  transfers between devices with their start and end apart: 66 -> 64, of which waited for: 28 -> 28; matrix products, arithmetic and copies ran while one was open for 9% -> 8% of each run, Pallas kernels for 28% -> 27%
where the time goes in v4:
time: 528 us; the launch traced here: 519 us
  Pallas kernels  198 us (38%)
  waiting for transfers between devices  158 us (30%)
  starting transfers between devices  99.5 us (19%)
  other arithmetic  30.6 us (6%)
  local copies, waits for them, and re-layouts  27.3 us (5%)
    pallas_call x27, Pallas kernels, call(): outs = pl.pallas_call(body, **kwargs)(self.ids, *args)  198 us
    ppermute x45, waiting for transfers between devices, swap(): return lax.ppermute(value, 'dp', [(i, i ^ mask) for i in range(size)])  79.5 us
    all_to_all x11, waiting for transfers between devices, exchange(): return lax.all_to_all(value, axis, 0, 0)  47.7 us
    all_to_all x11, starting transfers between devices, exchange(): return lax.all_to_all(value, axis, 0, 0)  44.3 us
    ppermute x45, starting transfers between devices, swap(): return lax.ppermute(value, 'dp', [(i, i ^ mask) for i in range(size)])  37.4 us
    ppermute x8, waiting for transfers between devices, along(): return lax.ppermute(value, 'ctx', pairs)  31.1 us
    another operation x14, other arithmetic, gather_far(): return (jnp.stack([one, swap(one, 4)]), jnp.stack([two, swap(two, 2)]))  19.2 us
    ppermute x8, starting transfers between devices, along(): return lax.ppermute(value, 'ctx', pairs)  17.9 us
  transfers between devices with their start and end apart: 64, of which 28 were waited for; matrix products, arithmetic and copies ran while one was open for 8% of the time, Pallas kernels for 27%

profile of v4, /device:TPU:0, one launch (start us, length us, event | category | flops | bytes accessed | tf_op | source)
XLA Modules:
  0.0 518.5 jit_solution(14466286408933701738)
XLA Ops:
  3.5 4.1 collective-permute-start
  7.6 3.5 collective-permute-start.1
  15.8 13.0 %collective-permute-done = bf16[2,16,7168]{2,1,0:T(8,128)(2,1)S(1)} collective-permute-done((bf16[2,16,7168]{2,1,0:T(8,128)(2,1)S(1)}, bf16[2,16,7168]{2,1,0:T(8,128)(2,1)S(1)}, u32[]{:S(2)}, u32[]{:S(2)}) %collective-permute-start) | collective-permute-done | bytes 458784 | tf_op jit(solution)/shard_map/ppermute | solution.py:64
  30.1 4.8 collective-permute-done.2
  34.9 8.3 %collective-permute-done.3 = bf16[2,16,7168]{2,1,0:T(8,128)(2,1)S(1)} collective-permute-done((bf16[2,16,7168]{2,1,0:T(8,128)(2,1)S(1)}, bf16[2,16,7168]{2,1,0:T(8,128)(2,1)S(1)}, u32[]{:S(2)}, u32[]{:S(2)}) %collective-permute-start.3) | collective-permute-done | bytes 458784 | tf_op jit(solution)/shard_map/ppermute | solution.py:64
  48.5 4.4 collective-permute-start.7
  55.8 3.9 collective-permute-done.6
  62.8 9.8 %collective-permute-done.5 = bf16[3,16,7168]{2,1,0:T(8,128)(2,1)S(1)} collective-permute-done((bf16[3,16,7168]{2,1,0:T(8,128)(2,1)S(1)}, bf16[3,16,7168]{2,1,0:T(8,128)(2,1)S(1)}, u32[]{:S(2)}, u32[]{:S(2)}) %collective-permute-start.5) | collective-permute-done | bytes 688160 | tf_op jit(solution)/shard_map/ppermute | solution.py:60
  78.4 5.0 collective-permute-done.9
  83.3 2.1 broadcast_in_dim.57
  85.4 3.7 all-to-all-start
  89.1 10.3 %collective-permute-done.11 = bf16[2,3,16,7168]{3,2,1,0:T(8,128)(2,1)} collective-permute-done((bf16[2,3,16,7168]{3,2,1,0:T(8,128)(2,1)}, bf16[2,3,16,7168]{3,2,1,0:T(8,128)(2,1)}, u32[]{:S(2)}, u32[]{:S(2)}) %collective-permute-start.11) | collective-permute-done | bytes 1376288 | tf_op jit(solution)/shard_map/ppermute | solution.py:60
  99.4 3.6 pad_maximum_fusion.1.refs_5_.refs_10_.refs_9_.refs_7_
  103.1 3.2 pad_maximum_fusion.refs_4_.refs_9_.refs_8_.refs_6_
  109.7 11.6 %collective-permute-done.13 = bf16[3,80,1024]{2,1,0:T(8,128)(2,1)S(1)} collective-permute-done((bf16[3,80,1024]{2,1,0:T(8,128)(2,1)S(1)}, bf16[3,80,1024]{2,1,0:T(8,128)(2,1)S(1)}, u32[]{:S(2)}, u32[]{:S(2)}) %collective-permute-start.13) | collective-permute-done | bytes 491552 | tf_op jit(solution)/shard_map/ppermute | solution.py:60
  130.8 15.7 %collective-permute-done.17 = bf16[2,3,80,1024]{3,2,1,0:T(8,128)(2,1)} collective-permute-done((bf16[2,3,80,1024]{3,2,1,0:T(8,128)(2,1)}, bf16[2,3,80,1024]{3,2,1,0:T(8,128)(2,1)}, u32[]{:S(2)}, u32[]{:S(2)}) %collective-permute-start.17) | collective-permute-done | bytes 983072 | tf_op jit(solution)/shard_map/ppermute | solution.py:60
  146.5 3.2 pad_maximum_fusion.3.refs_14_.refs_4_.refs_13_
  149.7 2.6 pad_maximum_fusion.2.refs_13_.refs_3_.refs_12_
  155.6 8.0 %shard_map.340.q_ref.k_ref.v_ref = bf16[1280,768]{1,0:T(8,128)(2,1)} custom-call(s32[15]{0:T(128)} %stack.307.ids, bf16[1536,1024]{1,0:T(8,128)(2,1)} %bitcast.162, bf16[256,1024]{1,0:T(8,128)(2,1)} %refs_3_.3, bf16[256,1024]{1,0:T(8,128)(2,1)} %refs_4_.3, bf16[256,1024]{1,0:T(8,128)(2,1)} %refs_5_.3, ...), custom_call_target="tpu_custom_call" | custom-call | flops 128000000000 | bytes 384000000 | tf_op jit(solution)/shard_map/pallas_call | solution.py:102
  163.5 10.7 %shard_map.341 = (bf16[4,384,128]{2,1,0:T(8,128)(2,1)}, f32[8,1536]{1,0:T(8,128)}) custom-call(s32[15]{0:T(128)} %stack.307.ids, f32[1,1280]{1,0:T(1,128)} %broadcast_in_dim.55.bias_ref, bf16[1280,768]{1,0:T(8,128)(2,1)} %shard_map.340.q_ref.k_ref.v_ref, bf16[1280,768]{1,0:T(8,128)(2,1)} %shard_map.340.q_ref.k_ref.v_ref, ...), custom_call_target="tpu_custom_call" | custom-call | flops 176000008192 | bytes 528000000 | tf_op jit(solution)/shard_map/pallas_call | solution.py:102
  174.3 4.6 all-to-all-start.1
  178.9 10.7 %shard_map.342 = (bf16[4,384,128]{2,1,0:T(8,128)(2,1)}, f32[8,1536]{1,0:T(8,128)}) custom-call(s32[15]{0:T(128)} %stack.307.ids, f32[1,1280]{1,0:T(1,128)} %broadcast_in_dim.55.bias_ref, bf16[1280,768]{1,0:T(8,128)(2,1)} %shard_map.340.q_ref.k_ref.v_ref, bf16[1280,768]{1,0:T(8,128)(2,1)} %shard_map.340.q_ref.k_ref.v_ref, ...), custom_call_target="tpu_custom_call" | custom-call | flops 176000008192 | bytes 528000000 | tf_op jit(solution)/shard_map/pallas_call | solution.py:102
  190.1 4.6 all-to-all-start.2
  194.7 10.6 %all-to-all-done.2.refs_1_ = bf16[4,384,128]{2,1,0:T(8,128)(2,1)S(1)} async-done(((bf16[4,384,128]{2,1,0:T(8,128)(2,1)}), bf16[4,384,128]{2,1,0:T(8,128)(2,1)S(1)}, u32[]{:S(2)}, u32[]{:S(2)}) %all-to-all-start.2) | async-done | bytes 393248 | tf_op jit(solution)/shard_map/all_to_all | solution.py:68
  206.0 23.5 %shard_map.343 = (bf16[384,1024]{1,0:T(8,128)(2,1)}, f32[384,1024]{1,0:T(8,128)}, bf16[384,1024]{1,0:T(8,128)(2,1)}, bf16[384,4096]{1,0:T(8,128)(2,1)}, bf16[384...) custom-call(s32[15]{0:T(128)} %stack.307.ids, ...), custom_call_target="tpu_custom_call" | custom-call | flops 384000000000 | bytes 1152000000 | tf_op jit(solution)/shard_map/pallas_call | solution.py:102
  229.5 6.6 %shard_map.344 = bf16[4,512,1024]{2,1,0:T(8,128)(2,1)} custom-call(s32[15]{0:T(128)} %stack.307.ids, bf16[384,4096]{1,0:T(8,128)(2,1)} %get-tuple-element.176.refs_0_, bf16[384,1024]{1,0:T(8,128)(2,1)} %get-tuple-element.177.refs_1_.refs_0_), custom_call_target="tpu_custom_call" | custom-call | tf_op jit(solution)/shard_map/pallas_call | solution.py:102
  236.0 11.3 %shard_map.345 = (bf16[384,4096]{1,0:T(8,128)(2,1)}, f32[1,4096]{1,0:T(1,128)}) custom-call(s32[15]{0:T(128)} %stack.307.ids, bf16[384,1024]{1,0:T(8,128)(2,1)} %get-tuple-element.177.refs_1_.refs_0_, bf16[384,4096]{1,0:T(8,128)(2,1)} %get-tuple-element.179.refs_1_, bf16[1024,1024]{1,0:T(8,128)(2,1)} %refs_2_.3, ...), custom_call_target="tpu_custom_call" | custom-call | flops 192000000000 | bytes 576000000 | tf_op jit(solution)/shard_map/pallas_call | solution.py:102
  247.4 7.2 %shard_map.346 = (bf16[4,128,1024]{2,1,0:T(8,128)(2,1)}, bf16[4,128,1024]{2,1,0:T(8,128)(2,1)}, bf16[4,128,1024]{2,1,0:T(8,128)(2,1)}, bf16[4,128,1024]{2,1,0:T(8,128)(2,1)}) custom-call(s32[15]{0:T(128)} %stack.307.ids, bf16[384,4096]{1,0:T(8,128)(2,1)} %get-tuple-element.176.refs_0_, bf16[384,1024]{1,0:T(8,128)(2,1)} %get-tuple-element.177.refs_1_.refs_0_, ...), custom_call_target="tpu_custom_call" | custom-call | tf_op jit(solution)/shard_map/pallas_call | solution.py:102
  256.1 7.1 %shard_map.347 = bf16[4,128,4096]{2,1,0:T(8,128)(2,1)} custom-call(s32[15]{0:T(128)} %stack.307.ids, bf16[384,1024]{1,0:T(8,128)(2,1)} %get-tuple-element.184.refs_0_, bf16[384,4096]{1,0:T(8,128)(2,1)} %get-tuple-element.180.refs_1_.refs_0_), custom_call_target="tpu_custom_call" | custom-call | tf_op jit(solution)/shard_map/pallas_call | solution.py:102
  263.9 13.3 %shard_map.348 = (f32[384,1024]{1,0:T(8,128)}, bf16[384,1024]{1,0:T(8,128)(2,1)}, bf16[4,384,256]{2,1,0:T(8,128)(2,1)}, f32[4,16,256]{2,1,0:T(8,128)}) custom-call(s32[15]{0:T(128)} %stack.307.ids, bf16[384,4096]{1,0:T(8,128)(2,1)} %get-tuple-element.180.refs_1_.refs_0_, f32[1,4096]{1,0:T(1,128)} %get-tuple-element.186.refs_1_, ...), custom_call_target="tpu_custom_call" | custom-call | flops 207999991808 | bytes 624000000 | tf_op jit(solution)/shard_map/pallas_call | solution.py:102
  277.2 3.7 all-to-all-start.3
  280.9 8.2 %collective-permute-done.22.got_two = bf16[4,128,1024]{2,1,0:T(8,128)(2,1)} collective-permute-done((bf16[4,128,1024]{2,1,0:T(8,128)(2,1)}, bf16[4,128,1024]{2,1,0:T(8,128)(2,1)}, u32[]{:S(2)}, u32[]{:S(2)}) %collective-permute-start.22) | collective-permute-done | bytes 1048608 | tf_op jit(solution)/shard_map/ppermute | solution.py:60
  289.1 3.9 shard_map.349
  294.0 7.9 %shard_map.350 = (bf16[4,32,4096]{2,1,0:T(8,128)(2,1)}, bf16[4,32,4096]{2,1,0:T(8,128)(2,1)}, bf16[4,32,4096]{2,1,0:T(8,128)(2,1)}, bf16[4,32,4096]{2,1,0:T(8,128)(2,1)}) custom-call(s32[15]{0:T(128)} %stack.307.ids, bf16[384,1024]{1,0:T(8,128)(2,1)} %get-tuple-element.184.refs_0_, bf16[384,4096]{1,0:T(8,128)(2,1)} %get-tuple-element.180.refs_1_.refs_0_, ...), custom_call_target="tpu_custom_call" | custom-call | tf_op jit(solution)/shard_map/pallas_call | solution.py:102
  301.9 4.5 collective-permute-done.24.got_one
  307.5 2.7 shard_map.351
  310.2 4.2 all-to-all-start.4
  316.6 16.0 %shard_map.352 = bf16[4,384,384]{2,1,0:T(8,128)(2,1)} custom-call(s32[15]{0:T(128)} %stack.307.ids, f32[1280,128]{1,0:T(8,128)} %broadcast_in_dim.56.bias_ref, bf16[1280,768]{1,0:T(8,128)(2,1)} %shard_map.340.q_ref.k_ref.v_ref, bf16[1280,768]{1,0:T(8,128)(2,1)} %shard_map.340.q_ref.k_ref.v_ref, bf16[1280,768]{1,0:T(8,128)(2,1)} %shard_map.340.q_ref.k_ref.v_ref, ...), custom_call_target="tpu_custom_call" | custom-call | flops 256000000000 | bytes 768000000 | tf_op jit(solution)/shard_map/pallas_call | solution.py:102
  332.7 6.5 %all-to-all-done.4.refs_0_ = bf16[4,2,64,1024]{3,2,1,0:T(8,128)(2,1)} async-done(((bf16[4,2,64,1024]{3,2,1,0:T(8,128)(2,1)}), bf16[4,2,64,1024]{3,2,1,0:T(8,128)(2,1)}, u32[]{:S(2)}, u32[]{:S(2)}) %all-to-all-start.4) | async-done | bytes 1048608 | tf_op jit(solution)/shard_map/all_to_all | solution.py:68
  339.2 4.5 all-to-all-start.5
  343.7 2.0 shard_map.353
  346.3 3.9 shard_map.354
  353.7 16.2 %shard_map.355 = bf16[4,384,384]{2,1,0:T(8,128)(2,1)} custom-call(s32[15]{0:T(128)} %stack.307.ids, f32[1280,128]{1,0:T(8,128)} %broadcast_in_dim.56.bias_ref, bf16[1280,768]{1,0:T(8,128)(2,1)} %shard_map.340.q_ref.k_ref.v_ref, bf16[1280,768]{1,0:T(8,128)(2,1)} %shard_map.340.q_ref.k_ref.v_ref, bf16[1280,768]{1,0:T(8,128)(2,1)} %shard_map.340.q_ref.k_ref.v_ref, ...), custom_call_target="tpu_custom_call" | custom-call | flops 256000000000 | bytes 768000000 | tf_op jit(solution)/shard_map/pallas_call | solution.py:102
  371.8 7.5 %shard_map.356 = bf16[4,128,1792]{2,1,0:T(8,128)(2,1)} custom-call(s32[15]{0:T(128)} %stack.307.ids, bf16[1536,1024]{1,0:T(8,128)(2,1)} %bitcast.163, bf16[1536,384]{1,0:T(8,128)(2,1)} %bitcast.167, bf16[1536,1024]{1,0:T(8,128)(2,1)} %bitcast.164, bf16[1536,384]{1,0:T(8,128)(2,1)} %bitcast.68.refs_3_, bf16[384,1024]{1,0:T(8,128)(2,1)} %get-tuple-element.174.refs_4_, ...), custom_call_target="tpu_custom_call" | custom-call | tf_op jit(solution)/shard_map/pallas_call | solution.py:102
  379.3 5.1 all-to-all-start.6
  386.3 2.7 shard_map.357
  389.0 3.8 collective-permute-done.33
  395.0 7.8 %shard_map.358 = (bf16[4,32,1792]{2,1,0:T(8,128)(2,1)}, bf16[4,32,1792]{2,1,0:T(8,128)(2,1)}, bf16[4,32,1792]{2,1,0:T(8,128)(2,1)}, bf16[4,32,1792]{2,1,0:T(8,128)(2,1)}) custom-call(s32[15]{0:T(128)} %stack.307.ids, bf16[1536,1024]{1,0:T(8,128)(2,1)} %bitcast.165, bf16[1536,384]{1,0:T(8,128)(2,1)} %bitcast.168, bf16[1536,1024]{1,0:T(8,128)(2,1)} %bitcast.166, ...), custom_call_target="tpu_custom_call" | custom-call | tf_op jit(solution)/shard_map/pallas_call | solution.py:102
  406.7 7.0 %all-to-all-done.6.refs_1_ = bf16[4,384,384]{2,1,0:T(8,128)(2,1)} async-done(((bf16[4,384,384]{2,1,0:T(8,128)(2,1)}), bf16[4,384,384]{2,1,0:T(8,128)(2,1)}, u32[]{:S(2)}, u32[]{:S(2)}) %all-to-all-start.6) | async-done | bytes 1179680 | tf_op jit(solution)/shard_map/all_to_all | solution.py:68
  414.5 3.8 shard_map.359
  418.3 3.8 all-to-all-start.7
  422.8 2.5 shard_map.360
  427.3 8.9 %shard_map.361 = (f32[384,1024]{1,0:T(8,128)}, f32[1,1024]{1,0:T(1,128)}) custom-call(s32[15]{0:T(128)} %stack.307.ids, bf16[4,384,384]{2,1,0:T(8,128)(2,1)} %all-to-all-done.5.refs_0_, bf16[4,384,384]{2,1,0:T(8,128)(2,1)} %all-to-all-done.6.refs_1_, f32[384,1024]{1,0:T(8,128)} %get-tuple-element.190.refs_2_, bf16[256,1024]{1,0:T(8,128)(2,1)} %refs_3_.3, ...), custom_call_target="tpu_custom_call" | custom-call | flops 143999991808 | bytes 432000000 | tf_op jit(solution)/shard_map/pallas_call | solution.py:102
  437.0 2.2 shard_map.362
  439.1 8.5 %all-to-all-done.7.refs_0_ = bf16[4,2,16,4096]{3,2,1,0:T(8,128)(2,1)S(1)} async-done(((bf16[4,2,16,4096]{3,2,1,0:T(8,128)(2,1)}), bf16[4,2,16,4096]{3,2,1,0:T(8,128)(2,1)S(1)}, u32[]{:S(2)}, u32[]{:S(2)}) %all-to-all-start.7) | async-done | bytes 1048608 | tf_op jit(solution)/shard_map/all_to_all | solution.py:68
  454.6 3.5 all-to-all-start.8
  459.2 10.8 %all-to-all-done.8.refs_0_ = bf16[4,2,16,1792]{3,2,1,0:T(8,128)(2,1)S(1)} async-done(((bf16[4,2,16,1792]{3,2,1,0:T(8,128)(2,1)}), bf16[4,2,16,1792]{3,2,1,0:T(8,128)(2,1)S(1)}, u32[]{:S(2)}, u32[]{:S(2)}) %all-to-all-start.8) | async-done | bytes 458784 | tf_op jit(solution)/shard_map/all_to_all | solution.py:68
  472.6 3.3 all-to-all-start.9
  481.8 6.7 %collective-permute-done.46 = bf16[1,16,4096]{2,1,0:T(8,128)(2,1)S(1)} collective-permute-done((bf16[1,16,4096]{2,1,0:T(8,128)(2,1)}, bf16[1,16,4096]{2,1,0:T(8,128)(2,1)S(1)}, u32[]{:S(2)}, u32[]{:S(2)}) %collective-permute-start.46) | collective-permute-done | bytes 131104 | tf_op jit(solution)/shard_map/ppermute | solution.py:60
  490.4 3.4 all-to-all-start.10
  497.8 2.6 all-to-all-done.10
  501.7 3.0 collective-permute-done.50
  506.6 3.8 shard_map.365
  514.5 3.8 shard_map.366
  (269 shorter events, 95.1 us)
Async XLA Ops:
  3.5 25.3 %collective-permute-start = (bf16[2,16,7168]{2,1,0:T(8,128)(2,1)S(1)}, bf16[2,16,7168]{2,1,0:T(8,128)(2,1)S(1)}, u32[]{:S(2)}, u32[]{:S(2)}) collective-permute-start(bf16[2,16,7168]{2,1,0:T(8,128)(2,1)S(1)} %pad_maximum_fusion.16), channel_id=1, source_target_pairs={{0,2},{1,3},{2,0},{3,1},{4,6},{5,7},{6,4},{7,5},{8,10},{9,11},{10,... | collective-permute-start | bytes 1376264 | tf_op jit(solution)/shard_map/ppermute | solution.py:64
  7.6 22.5 %collective-permute-start.1 = (bf16[2,16,7168]{2,1,0:T(8,128)(2,1)S(1)}, bf16[2,16,7168]{2,1,0:T(8,128)(2,1)S(1)}, u32[]{:S(2)}, u32[]{:S(2)}) collective-permute-start(bf16[2,16,7168]{2,1,0:T(8,128)(2,1)S(1)} %pad_maximum_fusion.16), channel_id=1, source_target_pairs={{0,1},{1,2},{2,3},{4,5},{5,6},{6,7},{8,9},{9,10},{10,11},{12,13},{... | collective-permute-start | bytes 1376264 | tf_op jit(solution)/shard_map/ppermute | solution.py:64
  11.1 23.8 %collective-permute-start.2 = (bf16[2,16,7168]{2,1,0:T(8,128)(2,1)S(1)}, bf16[2,16,7168]{2,1,0:T(8,128)(2,1)S(1)}, u32[]{:S(2)}, u32[]{:S(2)}) collective-permute-start(bf16[2,16,7168]{2,1,0:T(8,128)(2,1)S(1)} %pad_maximum_fusion.16), channel_id=1, source_target_pairs={{1,0},{2,1},{3,2},{5,4},{6,5},{7,6},{9,8},{10,9},{11,10},{13,12},{... | collective-permute-start | bytes 1376264 | tf_op jit(solution)/shard_map/ppermute | solution.py:64
  28.8 14.4 %collective-permute-start.3 = (bf16[2,16,7168]{2,1,0:T(8,128)(2,1)S(1)}, bf16[2,16,7168]{2,1,0:T(8,128)(2,1)S(1)}, u32[]{:S(2)}, u32[]{:S(2)}) collective-permute-start(bf16[2,16,7168]{2,1,0:T(8,128)(2,1)S(1)} %collective-permute-done), channel_id=1, source_target_pairs={{2,3},{1,0},{6,7},{5,4},{10,11},{9,8},{14,15},{13,12},{18,19},{17,... | collective-permute-start | bytes 1376264 | tf_op jit(solution)/shard_map/ppermute | solution.py:64
  43.7 16.0 %collective-permute-start.6 = (bf16[3,16,7168]{2,1,0:T(8,128)(2,1)S(1)}, bf16[3,16,7168]{2,1,0:T(8,128)(2,1)S(1)}, u32[]{:S(2)}, u32[]{:S(2)}) collective-permute-start(bf16[3,16,7168]{2,1,0:T(8,128)(2,1)S(1)} %get-tuple-element.282), channel_id=1, source_target_pairs={{0,16},{4,20},{8,24},{12,28},{16,0},{20,4},{24,8},{28,12},{1,17},{... | collective-permute-start | bytes 2064392 | tf_op jit(solution)/shard_map/ppermute | solution.py:60
  47.8 26.6 %collective-permute-start.4 = (bf16[2,80,1024]{2,1,0:T(8,128)(2,1)S(1)}, bf16[2,80,1024]{2,1,0:T(8,128)(2,1)S(1)}, u32[]{:S(2)}, u32[]{:S(2)}) collective-permute-start(bf16[2,80,1024]{2,1,0:T(8,128)(2,1)S(1)} %pad_maximum_fusion.17), channel_id=1, source_target_pairs={{0,2},{1,3},{2,0},{3,1},{4,6},{5,7},{6,4},{7,5},{8,10},{9,11},{10,... | collective-permute-start | bytes 983048 | tf_op jit(solution)/shard_map/ppermute | solution.py:64
  48.5 29.1 %collective-permute-start.7 = (bf16[2,80,1024]{2,1,0:T(8,128)(2,1)S(1)}, bf16[2,80,1024]{2,1,0:T(8,128)(2,1)S(1)}, u32[]{:S(2)}, u32[]{:S(2)}) collective-permute-start(bf16[2,80,1024]{2,1,0:T(8,128)(2,1)S(1)} %pad_maximum_fusion.17), channel_id=1, source_target_pairs={{0,1},{1,2},{2,3},{4,5},{5,6},{6,7},{8,9},{9,10},{10,11},{12,13},{... | collective-permute-start | bytes 983048 | tf_op jit(solution)/shard_map/ppermute | solution.py:64
  52.9 24.7 %collective-permute-start.8 = (bf16[2,80,1024]{2,1,0:T(8,128)(2,1)S(1)}, bf16[2,80,1024]{2,1,0:T(8,128)(2,1)S(1)}, u32[]{:S(2)}, u32[]{:S(2)}) collective-permute-start(bf16[2,80,1024]{2,1,0:T(8,128)(2,1)S(1)} %pad_maximum_fusion.17), channel_id=1, source_target_pairs={{1,0},{2,1},{3,2},{5,4},{6,5},{7,6},{9,8},{10,9},{11,10},{13,12},{... | collective-permute-start | bytes 983048 | tf_op jit(solution)/shard_map/ppermute | solution.py:64
  54.2 18.4 %collective-permute-start.5 = (bf16[3,16,7168]{2,1,0:T(8,128)(2,1)S(1)}, bf16[3,16,7168]{2,1,0:T(8,128)(2,1)S(1)}, u32[]{:S(2)}, u32[]{:S(2)}) collective-permute-start(bf16[3,16,7168]{2,1,0:T(8,128)(2,1)S(1)} %get-tuple-element.281), channel_id=1, source_target_pairs={{0,8},{4,12},{8,0},{12,4},{16,24},{20,28},{24,16},{28,20},{1,9},{5... | collective-permute-start | bytes 2064392 | tf_op jit(solution)/shard_map/ppermute | solution.py:60
  61.5 37.9 %collective-permute-start.11 = (bf16[2,3,16,7168]{3,2,1,0:T(8,128)(2,1)}, bf16[2,3,16,7168]{3,2,1,0:T(8,128)(2,1)}, u32[]{:S(2)}, u32[]{:S(2)}) collective-permute-start(bf16[2,3,16,7168]{3,2,1,0:T(8,128)(2,1)} %get-tuple-element.277), channel_id=1, source_target_pairs={{0,8},{4,12},{8,0},{12,4},{16,24},{20,28},{24,16},{28,20},{1,9},{5... | collective-permute-start | bytes 4128776 | tf_op jit(solution)/shard_map/ppermute | solution.py:60
  74.4 9.0 %collective-permute-start.9 = (bf16[2,80,1024]{2,1,0:T(8,128)(2,1)S(1)}, bf16[2,80,1024]{2,1,0:T(8,128)(2,1)S(1)}, u32[]{:S(2)}, u32[]{:S(2)}) collective-permute-start(bf16[2,80,1024]{2,1,0:T(8,128)(2,1)S(1)} %collective-permute-done.4), channel_id=1, source_target_pairs={{2,3},{1,0},{6,7},{5,4},{10,11},{9,8},{14,15},{13,12},{18,19},{17,... | collective-permute-start | bytes 983048 | tf_op jit(solution)/shard_map/ppermute | solution.py:64
  75.7 27.4 %collective-permute-start.10 = (bf16[2,3,16,7168]{3,2,1,0:T(8,128)(2,1)}, bf16[2,3,16,7168]{3,2,1,0:T(8,128)(2,1)}, u32[]{:S(2)}, u32[]{:S(2)}) collective-permute-start(bf16[2,3,16,7168]{3,2,1,0:T(8,128)(2,1)} %get-tuple-element.279), channel_id=1, source_target_pairs={{0,16},{4,20},{8,24},{12,28},{16,0},{20,4},{24,8},{28,12},{1,17},{... | collective-permute-start | bytes 4128776 | tf_op jit(solution)/shard_map/ppermute | solution.py:60
  85.4 68.5 %all-to-all-start = ((bf16[4,384,1024]{2,1,0:T(8,128)(2,1)}), bf16[4,384,1024]{2,1,0:T(8,128)(2,1)S(1)}, u32[]{:S(2)}, u32[]{:S(2)}) async-start(bf16[4,384,1024]{2,1,0:T(8,128)(2,1)} %broadcast_in_dim.57), calls=%async_computation | async-start | bytes 6291456 | tf_op jit(solution)/shard_map/all_to_all | solution.py:68
  103.1 49.8 %collective-permute-start.15 = (bf16[2,2,3,16,7168]{4,3,2,1,0:T(8,128)(2,1)}, bf16[2,2,3,16,7168]{4,3,2,1,0:T(8,128)(2,1)}, u32[]{:S(2)}, u32[]{:S(2)}) collective-permute-start(bf16[2,2,3,16,7168]{4,3,2,1,0:T(8,128)(2,1)} %pad_maximum_fusion.1.refs_5_.refs_10_.refs_9_.refs_7_), channel_id=1, source_target_pairs={{0,4},{4,0},{8,12},{12,8},{16,20},{20,16},{24,28},{28,24},{1,5},{5... | collective-permute-start | bytes 8257544 | tf_op jit(solution)/shard_map/ppermute | solution.py:60
  106.3 46.5 %collective-permute-start.14 = (bf16[2,2,3,16,7168]{4,3,2,1,0:T(8,128)(2,1)}, bf16[2,2,3,16,7168]{4,3,2,1,0:T(8,128)(2,1)}, u32[]{:S(2)}, u32[]{:S(2)}) collective-permute-start(bf16[2,2,3,16,7168]{4,3,2,1,0:T(8,128)(2,1)} %pad_maximum_fusion.refs_4_.refs_9_.refs_8_.refs_6_), channel_id=1, source_target_pairs={{0,4},{4,0},{8,12},{12,8},{16,20},{20,16},{24,28},{28,24},{1,5},{5... | collective-permute-start | bytes 8257544 | tf_op jit(solution)/shard_map/ppermute | solution.py:60
  107.7 13.7 %collective-permute-start.13 = (bf16[3,80,1024]{2,1,0:T(8,128)(2,1)S(1)}, bf16[3,80,1024]{2,1,0:T(8,128)(2,1)S(1)}, u32[]{:S(2)}, u32[]{:S(2)}) collective-permute-start(bf16[3,80,1024]{2,1,0:T(8,128)(2,1)S(1)} %get-tuple-element.290), channel_id=1, source_target_pairs={{0,16},{4,20},{8,24},{12,28},{16,0},{20,4},{24,8},{28,12},{1,17},{... | collective-permute-start | bytes 1474568 | tf_op jit(solution)/shard_map/ppermute | solution.py:60
  108.2 16.1 %collective-permute-start.12 = (bf16[3,80,1024]{2,1,0:T(8,128)(2,1)S(1)}, bf16[3,80,1024]{2,1,0:T(8,128)(2,1)S(1)}, u32[]{:S(2)}, u32[]{:S(2)}) collective-permute-start(bf16[3,80,1024]{2,1,0:T(8,128)(2,1)S(1)} %get-tuple-element.289), channel_id=1, source_target_pairs={{0,8},{4,12},{8,0},{12,4},{16,24},{20,28},{24,16},{28,20},{1,9},{5... | collective-permute-start | bytes 1474568 | tf_op jit(solution)/shard_map/ppermute | solution.py:60
  122.8 23.8 %collective-permute-start.17 = (bf16[2,3,80,1024]{3,2,1,0:T(8,128)(2,1)}, bf16[2,3,80,1024]{3,2,1,0:T(8,128)(2,1)}, u32[]{:S(2)}, u32[]{:S(2)}) collective-permute-start(bf16[2,3,80,1024]{3,2,1,0:T(8,128)(2,1)} %get-tuple-element.285), channel_id=1, source_target_pairs={{0,8},{4,12},{8,0},{12,4},{16,24},{20,28},{24,16},{28,20},{1,9},{5... | collective-permute-start | bytes 2949128 | tf_op jit(solution)/shard_map/ppermute | solution.py:60
  125.7 24.0 %collective-permute-start.16 = (bf16[2,3,80,1024]{3,2,1,0:T(8,128)(2,1)}, bf16[2,3,80,1024]{3,2,1,0:T(8,128)(2,1)}, u32[]{:S(2)}, u32[]{:S(2)}) collective-permute-start(bf16[2,3,80,1024]{3,2,1,0:T(8,128)(2,1)} %get-tuple-element.287), channel_id=1, source_target_pairs={{0,16},{4,20},{8,24},{12,28},{16,0},{20,4},{24,8},{28,12},{1,17},{... | collective-permute-start | bytes 2949128 | tf_op jit(solution)/shard_map/ppermute | solution.py:60
  149.7 44.9 %collective-permute-start.19 = (bf16[2,2,3,80,1024]{4,3,2,1,0:T(8,128)(2,1)}, bf16[2,2,3,80,1024]{4,3,2,1,0:T(8,128)(2,1)}, u32[]{:S(2)}, u32[]{:S(2)}) collective-permute-start(bf16[2,2,3,80,1024]{4,3,2,1,0:T(8,128)(2,1)} %pad_maximum_fusion.3.refs_14_.refs_4_.refs_13_), channel_id=1, source_target_pairs={{0,4},{4,0},{8,12},{12,8},{16,20},{20,16},{24,28},{28,24},{1,5},{5... | collective-permute-start | bytes 5898248 | tf_op jit(solution)/shard_map/ppermute | solution.py:60
  152.3 42.3 %collective-permute-start.18 = (bf16[2,2,3,80,1024]{4,3,2,1,0:T(8,128)(2,1)}, bf16[2,2,3,80,1024]{4,3,2,1,0:T(8,128)(2,1)}, u32[]{:S(2)}, u32[]{:S(2)}) collective-permute-start(bf16[2,2,3,80,1024]{4,3,2,1,0:T(8,128)(2,1)} %pad_maximum_fusion.2.refs_13_.refs_3_.refs_12_), channel_id=1, source_target_pairs={{0,4},{4,0},{8,12},{12,8},{16,20},{20,16},{24,28},{28,24},{1,5},{5... | collective-permute-start | bytes 5898248 | tf_op jit(solution)/shard_map/ppermute | solution.py:60
  174.3 15.8 %all-to-all-start.1 = ((bf16[4,384,128]{2,1,0:T(8,128)(2,1)}), bf16[4,384,128]{2,1,0:T(8,128)(2,1)}, u32[]{:S(2)}, u32[]{:S(2)}) async-start(bf16[4,384,128]{2,1,0:T(8,128)(2,1)} %get-tuple-element.166), calls=%async_computation.1 | async-start | bytes 786432 | tf_op jit(solution)/shard_map/all_to_all | solution.py:68
  190.1 15.2 %all-to-all-start.2 = ((bf16[4,384,128]{2,1,0:T(8,128)(2,1)}), bf16[4,384,128]{2,1,0:T(8,128)(2,1)S(1)}, u32[]{:S(2)}, u32[]{:S(2)}) async-start(bf16[4,384,128]{2,1,0:T(8,128)(2,1)} %get-tuple-element.172), calls=%async_computation.2 | async-start | bytes 786432 | tf_op jit(solution)/shard_map/all_to_all | solution.py:68
  236.0 11.3 %collective-permute-start.20 = (bf16[4,512,1024]{2,1,0:T(8,128)(2,1)}, bf16[4,512,1024]{2,1,0:T(8,128)(2,1)}, u32[]{:S(2)}, u32[]{:S(2)}) collective-permute-start(bf16[4,512,1024]{2,1,0:T(8,128)(2,1)} %shard_map.344), channel_id=1, source_target_pairs={{0,4},{4,0},{8,12},{12,8},{16,20},{20,16},{24,28},{28,24},{1,5},{5... | collective-permute-start | bytes 12582920 | tf_op jit(solution)/shard_map/ppermute | solution.py:60
  254.6 26.3 %collective-permute-start.21 = (bf16[4,128,1024]{2,1,0:T(8,128)(2,1)}, bf16[4,128,1024]{2,1,0:T(8,128)(2,1)}, u32[]{:S(2)}, u32[]{:S(2)}) collective-permute-start(bf16[4,128,1024]{2,1,0:T(8,128)(2,1)} %get-tuple-element.182), channel_id=1, source_target_pairs={{0,8},{4,12},{8,0},{12,4},{16,24},{20,28},{24,16},{28,20},{1,9},{5... | collective-permute-start | bytes 3145736 | tf_op jit(solution)/shard_map/ppermute | solution.py:60
  263.2 30.8 %collective-permute-start.23 = (bf16[4,128,4096]{2,1,0:T(8,128)(2,1)}, bf16[4,128,4096]{2,1,0:T(8,128)(2,1)}, u32[]{:S(2)}, u32[]{:S(2)}) collective-permute-start(bf16[4,128,4096]{2,1,0:T(8,128)(2,1)} %shard_map.347), channel_id=1, source_target_pairs={{0,4},{4,0},{8,12},{12,8},{16,20},{20,16},{24,28},{28,24},{1,5},{5... | collective-permute-start | bytes 12582920 | tf_op jit(solution)/shard_map/ppermute | solution.py:60
  263.4 25.7 %collective-permute-start.22 = (bf16[4,128,1024]{2,1,0:T(8,128)(2,1)}, bf16[4,128,1024]{2,1,0:T(8,128)(2,1)}, u32[]{:S(2)}, u32[]{:S(2)}) collective-permute-start(bf16[4,128,1024]{2,1,0:T(8,128)(2,1)} %get-tuple-element.194), channel_id=1, source_target_pairs={{0,16},{4,20},{8,24},{12,28},{16,0},{20,4},{24,8},{28,12},{1,17},{... | collective-permute-start | bytes 3145736 | tf_op jit(solution)/shard_map/ppermute | solution.py:60
  277.2 24.7 %all-to-all-start.3 = ((bf16[4,384,256]{2,1,0:T(8,128)(2,1)}), bf16[4,384,256]{2,1,0:T(8,128)(2,1)S(1)}, u32[]{:S(2)}, u32[]{:S(2)}) async-start(bf16[4,384,256]{2,1,0:T(8,128)(2,1)} %get-tuple-element.199), calls=%async_computation.3 | async-start | bytes 1572864 | tf_op jit(solution)/shard_map/all_to_all | solution.py:68
  292.9 13.5 %collective-permute-start.24 = (bf16[4,64,1024]{2,1,0:T(8,128)(2,1)}, bf16[4,64,1024]{2,1,0:T(8,128)(2,1)S(1)}, u32[]{:S(2)}, u32[]{:S(2)}) collective-permute-start(bf16[4,64,1024]{2,1,0:T(8,128)(2,1)} %get-tuple-element.195), channel_id=1, source_target_pairs={{0,16},{4,20},{8,24},{12,28},{16,0},{20,4},{24,8},{28,12},{1,17},{... | collective-permute-start | bytes 1572872 | tf_op jit(solution)/shard_map/ppermute | solution.py:60
  293.5 13.2 %collective-permute-start.25 = (bf16[4,64,1024]{2,1,0:T(8,128)(2,1)}, bf16[4,64,1024]{2,1,0:T(8,128)(2,1)S(1)}, u32[]{:S(2)}, u32[]{:S(2)}) collective-permute-start(bf16[4,64,1024]{2,1,0:T(8,128)(2,1)} %get-tuple-element.203), channel_id=1, source_target_pairs={{0,8},{4,12},{8,0},{12,4},{16,24},{20,28},{24,16},{28,20},{1,9},{5... | collective-permute-start | bytes 1572872 | tf_op jit(solution)/shard_map/ppermute | solution.py:60
  310.2 29.0 %all-to-all-start.4 = ((bf16[4,2,64,1024]{3,2,1,0:T(8,128)(2,1)}), bf16[4,2,64,1024]{3,2,1,0:T(8,128)(2,1)}, u32[]{:S(2)}, u32[]{:S(2)}) async-start(bf16[4,2,64,1024]{3,2,1,0:T(8,128)(2,1)} %shard_map.351), calls=%async_computation.4 | async-start | bytes 2097152 | tf_op jit(solution)/shard_map/all_to_all | solution.py:68
  314.5 31.9 %collective-permute-start.26 = (bf16[4,32,4096]{2,1,0:T(8,128)(2,1)}, bf16[4,32,4096]{2,1,0:T(8,128)(2,1)}, u32[]{:S(2)}, u32[]{:S(2)}) collective-permute-start(bf16[4,32,4096]{2,1,0:T(8,128)(2,1)} %get-tuple-element.197), channel_id=1, source_target_pairs={{0,8},{4,12},{8,0},{12,4},{16,24},{20,28},{24,16},{28,20},{1,9},{5... | collective-permute-start | bytes 3145736 | tf_op jit(solution)/shard_map/ppermute | solution.py:60
  315.1 31.2 %collective-permute-start.27 = (bf16[4,32,4096]{2,1,0:T(8,128)(2,1)}, bf16[4,32,4096]{2,1,0:T(8,128)(2,1)}, u32[]{:S(2)}, u32[]{:S(2)}) collective-permute-start(bf16[4,32,4096]{2,1,0:T(8,128)(2,1)} %get-tuple-element.212), channel_id=1, source_target_pairs={{0,16},{4,20},{8,24},{12,28},{16,0},{20,4},{24,8},{28,12},{1,17},{... | collective-permute-start | bytes 3145736 | tf_op jit(solution)/shard_map/ppermute | solution.py:60
  339.2 32.6 %all-to-all-start.5 = ((bf16[4,384,384]{2,1,0:T(8,128)(2,1)}), bf16[4,384,384]{2,1,0:T(8,128)(2,1)}, u32[]{:S(2)}, u32[]{:S(2)}) async-start(bf16[4,384,384]{2,1,0:T(8,128)(2,1)} %shard_map.352), calls=%async_computation.5 | async-start | bytes 2359296 | tf_op jit(solution)/shard_map/all_to_all | solution.py:68
  345.7 25.1 %collective-permute-start.30 = (bf16[1,64,1024]{2,1,0:T(8,128)(2,1)}, bf16[1,64,1024]{2,1,0:T(8,128)(2,1)}, u32[]{:S(2)}, u32[]{:S(2)}) collective-permute-start(bf16[1,64,1024]{2,1,0:T(8,128)(2,1)} %get-tuple-element.208), channel_id=1, source_target_pairs={{0,8},{4,12},{8,0},{12,4},{16,24},{20,28},{24,16},{28,20},{1,9},{5... | collective-permute-start | bytes 393224 | tf_op jit(solution)/shard_map/ppermute | solution.py:60
  350.2 21.6 %collective-permute-start.28 = (bf16[4,16,4096]{2,1,0:T(8,128)(2,1)}, bf16[4,16,4096]{2,1,0:T(8,128)(2,1)}, u32[]{:S(2)}, u32[]{:S(2)}) collective-permute-start(bf16[4,16,4096]{2,1,0:T(8,128)(2,1)} %get-tuple-element.213), channel_id=1, source_target_pairs={{0,16},{4,20},{8,24},{12,28},{16,0},{20,4},{24,8},{28,12},{1,17},{... | collective-permute-start | bytes 1572872 | tf_op jit(solution)/shard_map/ppermute | solution.py:60
  351.5 18.3 %collective-permute-start.31 = (bf16[1,64,1024]{2,1,0:T(8,128)(2,1)}, bf16[1,64,1024]{2,1,0:T(8,128)(2,1)}, u32[]{:S(2)}, u32[]{:S(2)}) collective-permute-start(bf16[1,64,1024]{2,1,0:T(8,128)(2,1)} %get-tuple-element.220), channel_id=1, source_target_pairs={{0,16},{4,20},{8,24},{12,28},{16,0},{20,4},{24,8},{28,12},{1,17},{... | collective-permute-start | bytes 393224 | tf_op jit(solution)/shard_map/ppermute | solution.py:60
  352.2 19.6 %collective-permute-start.29 = (bf16[4,16,4096]{2,1,0:T(8,128)(2,1)}, bf16[4,16,4096]{2,1,0:T(8,128)(2,1)}, u32[]{:S(2)}, u32[]{:S(2)}) collective-permute-start(bf16[4,16,4096]{2,1,0:T(8,128)(2,1)} %get-tuple-element.219), channel_id=1, source_target_pairs={{0,8},{4,12},{8,0},{12,4},{16,24},{20,28},{24,16},{28,20},{1,9},{5... | collective-permute-start | bytes 1572872 | tf_op jit(solution)/shard_map/ppermute | solution.py:60
  379.3 14.5 %collective-permute-start.34 = (bf16[4,128,1792]{2,1,0:T(8,128)(2,1)}, bf16[4,128,1792]{2,1,0:T(8,128)(2,1)S(1)}, u32[]{:S(2)}, u32[]{:S(2)}) collective-permute-start(bf16[4,128,1792]{2,1,0:T(8,128)(2,1)} %shard_map.356), channel_id=1, source_target_pairs={{0,4},{4,0},{8,12},{12,8},{16,20},{20,16},{24,28},{28,24},{1,5},{5... | collective-permute-start | bytes 5505032 | tf_op jit(solution)/shard_map/ppermute | solution.py:60
  379.3 34.4 %all-to-all-start.6 = ((bf16[4,384,384]{2,1,0:T(8,128)(2,1)}), bf16[4,384,384]{2,1,0:T(8,128)(2,1)}, u32[]{:S(2)}, u32[]{:S(2)}) async-start(bf16[4,384,384]{2,1,0:T(8,128)(2,1)} %shard_map.355), calls=%async_computation.6 | async-start | bytes 2359296 | tf_op jit(solution)/shard_map/all_to_all | solution.py:68
  384.4 8.4 %collective-permute-start.33 = (bf16[2,1,64,1024]{3,2,0,1:T(8,128)(2,1)S(1)}, bf16[2,1,64,1024]{3,2,0,1:T(8,128)(2,1)S(1)}, u32[]{:S(2)}, u32[]{:S(2)}) collective-permute-start(bf16[2,1,64,1024]{3,2,0,1:T(8,128)(2,1)S(1)} %pad_maximum_fusion.19), channel_id=1, source_target_pairs={{0,8},{4,12},{8,0},{12,4},{16,24},{20,28},{24,16},{28,20},{1,9},{5... | collective-permute-start | bytes 786440 | tf_op jit(solution)/shard_map/ppermute | solution.py:60
  385.0 8.2 %collective-permute-start.32 = (bf16[2,1,64,1024]{3,2,0,1:T(8,128)(2,1)S(1)}, bf16[2,1,64,1024]{3,2,0,1:T(8,128)(2,1)S(1)}, u32[]{:S(2)}, u32[]{:S(2)}) collective-permute-start(bf16[2,1,64,1024]{3,2,0,1:T(8,128)(2,1)S(1)} %pad_maximum_fusion.18), channel_id=1, source_target_pairs={{0,16},{4,20},{8,24},{12,28},{16,0},{20,4},{24,8},{28,12},{1,17},{... | collective-permute-start | bytes 786440 | tf_op jit(solution)/shard_map/ppermute | solution.py:60
  393.2 20.5 %collective-permute-start.35 = (bf16[2,2,1,64,1024]{4,3,2,1,0:T(8,128)(2,1)S(1)}, bf16[2,2,1,64,1024]{4,3,2,1,0:T(8,128)(2,1)S(1)}, u32[]{:S(2)}, u32[]{:S(2)}) collective-permute-start(bf16[2,2,1,64,1024]{4,3,2,1,0:T(8,128)(2,1)S(1)} %pad_maximum_fusion.10.refs_0_), channel_id=1, source_target_pairs={{0,4},{4,0},{8,12},{12,8},{16,20},{20,16},{24,28},{28,24},{1,5},{5... | collective-permute-start | bytes 1572872 | tf_op jit(solution)/shard_map/ppermute | solution.py:60
  393.3 20.4 %collective-permute-start.36 = (bf16[2,2,1,64,1024]{4,3,2,1,0:T(8,128)(2,1)S(1)}, bf16[2,2,1,64,1024]{4,3,2,1,0:T(8,128)(2,1)}, u32[]{:S(2)}, u32[]{:S(2)}) collective-permute-start(bf16[2,2,1,64,1024]{4,3,2,1,0:T(8,128)(2,1)S(1)} %pad_maximum_fusion.11.refs_1_), channel_id=1, source_target_pairs={{0,4},{4,0},{8,12},{12,8},{16,20},{20,16},{24,28},{28,24},{1,5},{5... | collective-permute-start | bytes 1572872 | tf_op jit(solution)/shard_map/ppermute | solution.py:60
  402.8 19.3 %collective-permute-start.37 = (bf16[4,32,1792]{2,1,0:T(8,128)(2,1)}, bf16[4,32,1792]{2,1,0:T(8,128)(2,1)S(1)}, u32[]{:S(2)}, u32[]{:S(2)}) collective-permute-start(bf16[4,32,1792]{2,1,0:T(8,128)(2,1)} %get-tuple-element.228), channel_id=1, source_target_pairs={{0,8},{4,12},{8,0},{12,4},{16,24},{20,28},{24,16},{28,20},{1,9},{5... | collective-permute-start | bytes 1376264 | tf_op jit(solution)/shard_map/ppermute | solution.py:60
  404.3 17.8 %collective-permute-start.38 = (bf16[4,32,1792]{2,1,0:T(8,128)(2,1)}, bf16[4,32,1792]{2,1,0:T(8,128)(2,1)}, u32[]{:S(2)}, u32[]{:S(2)}) collective-permute-start(bf16[4,32,1792]{2,1,0:T(8,128)(2,1)} %get-tuple-element.236), channel_id=1, source_target_pairs={{0,16},{4,20},{8,24},{12,28},{16,0},{20,4},{24,8},{28,12},{1,17},{... | collective-permute-start | bytes 1376264 | tf_op jit(solution)/shard_map/ppermute | solution.py:60
  418.3 29.3 %all-to-all-start.7 = ((bf16[4,2,16,4096]{3,2,1,0:T(8,128)(2,1)}), bf16[4,2,16,4096]{3,2,1,0:T(8,128)(2,1)S(1)}, u32[]{:S(2)}, u32[]{:S(2)}) async-start(bf16[4,2,16,4096]{3,2,1,0:T(8,128)(2,1)} %shard_map.357), calls=%async_computation.7 | async-start | bytes 2097152 | tf_op jit(solution)/shard_map/all_to_all | solution.py:68
  425.4 10.8 %collective-permute-start.39 = (bf16[4,16,1792]{2,1,0:T(8,128)(2,1)}, bf16[4,16,1792]{2,1,0:T(8,128)(2,1)S(1)}, u32[]{:S(2)}, u32[]{:S(2)}) collective-permute-start(bf16[4,16,1792]{2,1,0:T(8,128)(2,1)} %get-tuple-element.237), channel_id=1, source_target_pairs={{0,16},{4,20},{8,24},{12,28},{16,0},{20,4},{24,8},{28,12},{1,17},{... | collective-permute-start | bytes 688136 | tf_op jit(solution)/shard_map/ppermute | solution.py:60
  426.7 9.5 %collective-permute-start.40 = (bf16[4,16,1792]{2,1,0:T(8,128)(2,1)}, bf16[4,16,1792]{2,1,0:T(8,128)(2,1)S(1)}, u32[]{:S(2)}, u32[]{:S(2)}) collective-permute-start(bf16[4,16,1792]{2,1,0:T(8,128)(2,1)} %get-tuple-element.243), channel_id=1, source_target_pairs={{0,8},{4,12},{8,0},{12,4},{16,24},{20,28},{24,16},{28,20},{1,9},{5... | collective-permute-start | bytes 688136 | tf_op jit(solution)/shard_map/ppermute | solution.py:60
  450.6 7.5 %collective-permute-start.42 = (bf16[1,16,4096]{2,1,0:T(8,128)(2,1)}, bf16[1,16,4096]{2,1,0:T(8,128)(2,1)S(1)}, u32[]{:S(2)}, u32[]{:S(2)}) collective-permute-start(bf16[1,16,4096]{2,1,0:T(8,128)(2,1)} %get-tuple-element.251), channel_id=1, source_target_pairs={{0,16},{4,20},{8,24},{12,28},{16,0},{20,4},{24,8},{28,12},{1,17},{... | collective-permute-start | bytes 393224 | tf_op jit(solution)/shard_map/ppermute | solution.py:60
  454.0 5.2 collective-permute-start.41
  454.6 15.5 %all-to-all-start.8 = ((bf16[4,2,16,1792]{3,2,1,0:T(8,128)(2,1)}), bf16[4,2,16,1792]{3,2,1,0:T(8,128)(2,1)S(1)}, u32[]{:S(2)}, u32[]{:S(2)}) async-start(bf16[4,2,16,1792]{3,2,1,0:T(8,128)(2,1)} %shard_map.362), calls=%async_computation.8 | async-start | bytes 917504 | tf_op jit(solution)/shard_map/all_to_all | solution.py:68
  472.6 9.1 %all-to-all-start.9 = ((f32[4,20,256]{2,1,0:T(8,128)}), f32[4,20,256]{2,1,0:T(8,128)S(1)}, u32[]{:S(2)}, u32[]{:S(2)}) async-start(f32[4,20,256]{2,1,0:T(8,128)} %pad_maximum_fusion.24), calls=%async_computation.9 | async-start | bytes 196608 | tf_op jit(solution)/shard_map/all_to_all | solution.py:68
  477.4 16.4 %collective-permute-start.45 = (bf16[1,16,4096]{2,1,0:T(8,128)(2,1)}, bf16[1,16,4096]{2,1,0:T(8,128)(2,1)S(1)}, u32[]{:S(2)}, u32[]{:S(2)}) collective-permute-start(bf16[1,16,4096]{2,1,0:T(8,128)(2,1)} %get-tuple-element.253), channel_id=1, source_target_pairs={{0,8},{4,12},{8,0},{12,4},{16,24},{20,28},{24,16},{28,20},{1,9},{5... | collective-permute-start | bytes 393224 | tf_op jit(solution)/shard_map/ppermute | solution.py:60
  478.9 10.5 %collective-permute-start.44 = (bf16[2,1,16,4096]{3,2,0,1:T(8,128)(2,1)S(1)}, bf16[2,1,16,4096]{3,2,0,1:T(8,128)(2,1)S(1)}, u32[]{:S(2)}, u32[]{:S(2)}) collective-permute-start(bf16[2,1,16,4096]{3,2,0,1:T(8,128)(2,1)S(1)} %pad_maximum_fusion.21), channel_id=1, source_target_pairs={{0,8},{4,12},{8,0},{12,4},{16,24},{20,28},{24,16},{28,20},{1,9},{5... | collective-permute-start | bytes 786440 | tf_op jit(solution)/shard_map/ppermute | solution.py:60
  479.5 10.0 %collective-permute-start.43 = (bf16[2,1,16,4096]{3,2,0,1:T(8,128)(2,1)S(1)}, bf16[2,1,16,4096]{3,2,0,1:T(8,128)(2,1)S(1)}, u32[]{:S(2)}, u32[]{:S(2)}) collective-permute-start(bf16[2,1,16,4096]{3,2,0,1:T(8,128)(2,1)S(1)} %pad_maximum_fusion.20), channel_id=1, source_target_pairs={{0,16},{4,20},{8,24},{12,28},{16,0},{20,4},{24,8},{28,12},{1,17},{... | collective-permute-start | bytes 786440 | tf_op jit(solution)/shard_map/ppermute | solution.py:60
  480.3 8.2 %collective-permute-start.46 = (bf16[1,16,4096]{2,1,0:T(8,128)(2,1)}, bf16[1,16,4096]{2,1,0:T(8,128)(2,1)S(1)}, u32[]{:S(2)}, u32[]{:S(2)}) collective-permute-start(bf16[1,16,4096]{2,1,0:T(8,128)(2,1)} %get-tuple-element.261), channel_id=1, source_target_pairs={{0,16},{4,20},{8,24},{12,28},{16,0},{20,4},{24,8},{28,12},{1,17},{... | collective-permute-start | bytes 393224 | tf_op jit(solution)/shard_map/ppermute | solution.py:60
  490.4 10.0 %all-to-all-start.10 = ((f32[8,24,256]{2,1,0:T(8,128)}), f32[8,24,256]{2,1,0:T(8,128)S(1)}, u32[]{:S(2)}, u32[]{:S(2)}) async-start(f32[8,24,256]{2,1,0:T(8,128)} %broadcast_in_dim.61), calls=%async_computation.10 | async-start | bytes 393216 | tf_op jit(solution)/shard_map/all_to_all | solution.py:68
  493.9 10.8 %collective-permute-start.50 = (bf16[2,1,16,4096]{3,2,0,1:T(8,128)(2,1)S(1)}, bf16[2,1,16,4096]{3,2,0,1:T(8,128)(2,1)S(1)}, u32[]{:S(2)}, u32[]{:S(2)}) collective-permute-start(bf16[2,1,16,4096]{3,2,0,1:T(8,128)(2,1)S(1)} %pad_maximum_fusion.23), channel_id=1, source_target_pairs={{0,8},{4,12},{8,0},{12,4},{16,24},{20,28},{24,16},{28,20},{1,9},{5... | collective-permute-start | bytes 786440 | tf_op jit(solution)/shard_map/ppermute | solution.py:60
  495.8 9.0 %collective-permute-start.49 = (bf16[2,1,16,4096]{3,2,0,1:T(8,128)(2,1)S(1)}, bf16[2,1,16,4096]{3,2,0,1:T(8,128)(2,1)S(1)}, u32[]{:S(2)}, u32[]{:S(2)}) collective-permute-start(bf16[2,1,16,4096]{3,2,0,1:T(8,128)(2,1)S(1)} %pad_maximum_fusion.22), channel_id=1, source_target_pairs={{0,16},{4,20},{8,24},{12,28},{16,0},{20,4},{24,8},{28,12},{1,17},{... | collective-permute-start | bytes 786440 | tf_op jit(solution)/shard_map/ppermute | solution.py:60
  497.3 7.6 %collective-permute-start.47 = (bf16[2,2,1,16,4096]{4,3,2,1,0:T(8,128)(2,1)S(1)}, bf16[2,2,1,16,4096]{4,3,2,1,0:T(8,128)(2,1)S(1)}, u32[]{:S(2)}, u32[]{:S(2)}) collective-permute-start(bf16[2,2,1,16,4096]{4,3,2,1,0:T(8,128)(2,1)S(1)} %pad_maximum_fusion.12.refs_0_), channel_id=1, source_target_pairs={{0,4},{4,0},{8,12},{12,8},{16,20},{20,16},{24,28},{28,24},{1,5},{5... | collective-permute-start | bytes 1572872 | tf_op jit(solution)/shard_map/ppermute | solution.py:60
  497.3 7.6 %collective-permute-start.48 = (bf16[2,2,1,16,4096]{4,3,2,1,0:T(8,128)(2,1)S(1)}, bf16[2,2,1,16,4096]{4,3,2,1,0:T(8,128)(2,1)S(1)}, u32[]{:S(2)}, u32[]{:S(2)}) collective-permute-start(bf16[2,2,1,16,4096]{4,3,2,1,0:T(8,128)(2,1)S(1)} %pad_maximum_fusion.13.refs_1_), channel_id=1, source_target_pairs={{0,4},{4,0},{8,12},{12,8},{16,20},{20,16},{24,28},{28,24},{1,5},{5... | collective-permute-start | bytes 1572872 | tf_op jit(solution)/shard_map/ppermute | solution.py:60
  510.4 2.5 collective-permute-start.51
  510.4 2.7 collective-permute-start.52
  (47 other events, 290.0 us)

commit v5 on v4

--- a/solution.py
+++ b/solution.py
@@ -14,6 +14,7 @@
 EPSILON = 1e-05
 GROUP = 8
 TAIL = 128
+FEW = 32
 PAIR = 2 * HD
 STEP = 512
 FACTOR = 16
@@ -283,7 +284,7 @@
     grad_ref, lse_ref, out_ref, do_ref, dk_ref, dv_ref = refs
     tile = pl.program_id(0)
     slots = q_ref.shape[0]
-    span = k_ref.shape[0]
+    span = k_ref.shape[0] - TAIL + FEW
     first = lax.broadcasted_iota(jnp.int32, (1, PAIR), 1) < HD
     scale = 1.0 / math.sqrt(HD)
 
@@ -295,7 +296,7 @@
             do_ref[part_of(ids[LISTS + g] * slots, slots), :] = grad_ref[g]
 
     def work(rows):
-        keys, values = k_ref[...], v_ref[...]
+        keys, values = k_ref[:span, :], v_ref[:span, :]
         here = pl.ds(pl.multiple_of(tile * slots, slots), rows)
         parts = []
         for h in range(2):
@@ -303,7 +304,7 @@
             query = jnp.where(mine, q_ref[:rows, :], 0)
             grad = jnp.where(mine, do_ref[here, :], 0)
             scores = right_dot(keys, query) * (LOG2E * scale)
-            bias = jnp.concatenate([bias_ref[...]] * (rows // 128), 1)
+            bias = jnp.concatenate([bias_ref[:span, :]] * (rows // 128), 1)
             probs = jnp.exp2(scores + bias - lse_ref[h : h + 1, :rows])
             grad_probs = right_dot(values, grad)
             center = jnp.sum(grad_probs * probs, 0, keepdims=True)
@@ -952,25 +953,27 @@
     order.wait(*rest_held)
     rest_held = reduce_fourth(order, n, rest_held, False)
     order.tick(inner_held)
+
+    packed = jnp.concatenate([small, block_sum.reshape(1, n, cols).repeat(n, 0)], 1)
+    total = jnp.sum(exchange(order.release(packed)), 0)
+    inner_pieces = gather_near(*reduce_fifth(order, [inner_held], [0]))
+    order.tick(total)
     rest_held = exchange(order.release(rest_held))
-    inner_pieces = gather_near(*reduce_fifth(order, [inner_held], [0]))
-    order.tick(rest_held, *inner_pieces)
+    used = small.shape[1]
+    bias_sums = jnp.stack([jnp.sum(back.astype(WIDE), (0, 1)) for back in backs])
+    vector = jnp.concatenate([total[used:], jnp.full((1, cols), timestep[0], WIDE)])[None]
+    total = jnp.concatenate([total[:used], bias_sums.reshape(-1, cols)])
+    mask = 1
+    while mask < lax.axis_size("dp"):
+        flat = swap(jnp.concatenate([total, vector.reshape(-1, cols)]), mask)
+        total = total + flat[: total.shape[0]]
+        vector = jnp.concatenate([vector, flat[total.shape[0] :].reshape(vector.shape)])
+        mask *= 2
+    order.tick(rest_held, total, vector, *inner_pieces)
     inner_pieces = gather_far(*order.release(*inner_pieces))
     pieces = gather_near(*reduce_fifth(order, [rest_held], [3 * cols]))
-
-    packed = jnp.concatenate([small, block_sum.reshape(1, n, cols).repeat(n, 0)], 1)
-    total = jnp.sum(exchange(order.release(packed)), 0)
-    used = small.shape[1]
-    bias_sums = jnp.stack([jnp.sum(back.astype(WIDE), (0, 1)) for back in backs])
-    level = jnp.full((1, cols), timestep[0], WIDE)
-    total = jnp.concatenate([total, level, bias_sums.reshape(-1, cols)])
-    order.tick(*inner_pieces, total)
+    order.tick(*inner_pieces)
     inner_pieces = gather_cores(*order.release(*inner_pieces))
-    rows = lax.axis_size("dp")
-    total = exchange(jnp.broadcast_to(order.release(total), (rows, *total.shape)), "dp")
-    vector = total[:, used : used + n + 1]
-    total = jnp.sum(total, 0)
-    total = jnp.concatenate([total[:used], total[used + n + 1 :]])
     per = deep // cols
     sums = [total[0], total[1 : 1 + per].reshape(deep)] + [total[1 + per + i] for i in range(5)]
     bias_sums = total[used:].reshape(pairs, 3 * PAIR)

time: 528 us -> 521 us (0.987)
    all_to_all x11 -> x10, waiting for transfers between devices: 47.7 us -> 40.1 us  [exchange(): return lax.all_to_all(value, axis, 0, 0)]
    unnamed x98 -> x88, local copies, waits for them, and re-layouts: 13.4 us -> 9.68 us
    ppermute x45 -> x48, waiting for transfers between devices: 79.5 us -> 83.1 us  [swap(): return lax.ppermute(value, 'dp', [(i, i ^ mask) for i in range(size)])]
    all_to_all x11 -> x10, starting transfers between devices: 44.3 us -> 42.2 us  [exchange(): return lax.all_to_all(value, axis, 0, 0)]
    ppermute x45 -> x48, starting transfers between devices: 37.4 us -> 38.9 us  [swap(): return lax.ppermute(value, 'dp', [(i, i ^ mask) for i in range(size)])]
  transfers between devices with their start and end apart: 64 -> 66, of which waited for: 28 -> 30; matrix products, arithmetic and copies ran while one was open for 8% -> 9% of each run, Pallas kernels for 27% -> 27%
where the time goes in v5:
time: 521 us; the launch traced here: 512 us
  Pallas kernels  197 us (38%)
  waiting for transfers between devices  154 us (30%)
  starting transfers between devices  98.9 us (19%)
  other arithmetic  33.2 us (6%)
  local copies, waits for them, and re-layouts  23.3 us (4%)
    pallas_call x27, Pallas kernels, call(): outs = pl.pallas_call(body, **kwargs)(self.ids, *args)  197 us
    ppermute x48, waiting for transfers between devices, swap(): return lax.ppermute(value, 'dp', [(i, i ^ mask) for i in range(size)])  83.1 us
    all_to_all x10, starting transfers between devices, exchange(): return lax.all_to_all(value, axis, 0, 0)  42.2 us
    all_to_all x10, waiting for transfers between devices, exchange(): return lax.all_to_all(value, axis, 0, 0)  40.1 us
    ppermute x48, starting transfers between devices, swap(): return lax.ppermute(value, 'dp', [(i, i ^ mask) for i in range(size)])  38.9 us
    ppermute x8, waiting for transfers between devices, along(): return lax.ppermute(value, 'ctx', pairs)  31.1 us
    another operation x14, other arithmetic, gather_far(): return (jnp.stack([one, swap(one, 4)]), jnp.stack([two, swap(two, 2)]))  19.2 us
    ppermute x8, starting transfers between devices, along(): return lax.ppermute(value, 'ctx', pairs)  17.9 us
  transfers between devices with their start and end apart: 66, of which 30 were waited for; matrix products, arithmetic and copies ran while one was open for 9% of the time, Pallas kernels for 27%

profile of v5, /device:TPU:0, one launch (start us, length us, event | category | flops | bytes accessed | tf_op | source)
XLA Modules:
  0.0 511.6 jit_solution(12076627363761568809)
XLA Ops:
  3.5 4.1 collective-permute-start
  7.6 3.5 collective-permute-start.1
  15.7 13.1 %collective-permute-done = bf16[2,16,7168]{2,1,0:T(8,128)(2,1)S(1)} collective-permute-done((bf16[2,16,7168]{2,1,0:T(8,128)(2,1)S(1)}, bf16[2,16,7168]{2,1,0:T(8,128)(2,1)S(1)}, u32[]{:S(2)}, u32[]{:S(2)}) %collective-permute-start) | collective-permute-done | bytes 458784 | tf_op jit(solution)/shard_map/ppermute | solution.py:65
  30.1 4.8 collective-permute-done.2
  34.9 8.3 %collective-permute-done.3 = bf16[2,16,7168]{2,1,0:T(8,128)(2,1)S(1)} collective-permute-done((bf16[2,16,7168]{2,1,0:T(8,128)(2,1)S(1)}, bf16[2,16,7168]{2,1,0:T(8,128)(2,1)S(1)}, u32[]{:S(2)}, u32[]{:S(2)}) %collective-permute-start.3) | collective-permute-done | bytes 458784 | tf_op jit(solution)/shard_map/ppermute | solution.py:65
  48.5 4.4 collective-permute-start.7
  55.8 3.9 collective-permute-done.6
  62.8 9.8 %collective-permute-done.5 = bf16[3,16,7168]{2,1,0:T(8,128)(2,1)S(1)} collective-permute-done((bf16[3,16,7168]{2,1,0:T(8,128)(2,1)S(1)}, bf16[3,16,7168]{2,1,0:T(8,128)(2,1)S(1)}, u32[]{:S(2)}, u32[]{:S(2)}) %collective-permute-start.5) | collective-permute-done | bytes 688160 | tf_op jit(solution)/shard_map/ppermute | solution.py:61
  78.4 5.0 collective-permute-done.9
  83.3 2.1 broadcast_in_dim.57
  85.4 3.7 all-to-all-start
  89.1 10.3 %collective-permute-done.11 = bf16[2,3,16,7168]{3,2,1,0:T(8,128)(2,1)} collective-permute-done((bf16[2,3,16,7168]{3,2,1,0:T(8,128)(2,1)}, bf16[2,3,16,7168]{3,2,1,0:T(8,128)(2,1)}, u32[]{:S(2)}, u32[]{:S(2)}) %collective-permute-start.11) | collective-permute-done | bytes 1376288 | tf_op jit(solution)/shard_map/ppermute | solution.py:61
  99.4 3.6 pad_maximum_fusion.1.refs_5_.refs_10_.refs_9_.refs_7_
  103.1 3.2 pad_maximum_fusion.refs_4_.refs_9_.refs_8_.refs_6_
  109.7 11.6 %collective-permute-done.13 = bf16[3,80,1024]{2,1,0:T(8,128)(2,1)S(1)} collective-permute-done((bf16[3,80,1024]{2,1,0:T(8,128)(2,1)S(1)}, bf16[3,80,1024]{2,1,0:T(8,128)(2,1)S(1)}, u32[]{:S(2)}, u32[]{:S(2)}) %collective-permute-start.13) | collective-permute-done | bytes 491552 | tf_op jit(solution)/shard_map/ppermute | solution.py:61
  130.8 15.7 %collective-permute-done.17 = bf16[2,3,80,1024]{3,2,1,0:T(8,128)(2,1)} collective-permute-done((bf16[2,3,80,1024]{3,2,1,0:T(8,128)(2,1)}, bf16[2,3,80,1024]{3,2,1,0:T(8,128)(2,1)}, u32[]{:S(2)}, u32[]{:S(2)}) %collective-permute-start.17) | collective-permute-done | bytes 983072 | tf_op jit(solution)/shard_map/ppermute | solution.py:61
  146.5 3.2 pad_maximum_fusion.3.refs_14_.refs_4_.refs_13_
  149.7 2.6 pad_maximum_fusion.2.refs_13_.refs_3_.refs_12_
  155.6 7.9 %shard_map.340.q_ref.k_ref.v_ref = bf16[1280,768]{1,0:T(8,128)(2,1)} custom-call(s32[15]{0:T(128)} %stack.307.ids, bf16[1536,1024]{1,0:T(8,128)(2,1)} %bitcast.166, bf16[256,1024]{1,0:T(8,128)(2,1)} %refs_3_.3, bf16[256,1024]{1,0:T(8,128)(2,1)} %refs_4_.3, bf16[256,1024]{1,0:T(8,128)(2,1)} %refs_5_.3, ...), custom_call_target="tpu_custom_call" | custom-call | flops 128000000000 | bytes 384000000 | tf_op jit(solution)/shard_map/pallas_call | solution.py:103
  163.5 10.7 %shard_map.341 = (bf16[4,384,128]{2,1,0:T(8,128)(2,1)}, f32[8,1536]{1,0:T(8,128)}) custom-call(s32[15]{0:T(128)} %stack.307.ids, f32[1,1280]{1,0:T(1,128)} %broadcast_in_dim.55.bias_ref, bf16[1280,768]{1,0:T(8,128)(2,1)} %shard_map.340.q_ref.k_ref.v_ref, bf16[1280,768]{1,0:T(8,128)(2,1)} %shard_map.340.q_ref.k_ref.v_ref, ...), custom_call_target="tpu_custom_call" | custom-call | flops 176000008192 | bytes 528000000 | tf_op jit(solution)/shard_map/pallas_call | solution.py:103
  174.2 4.6 all-to-all-start.1
  178.8 10.7 %shard_map.342 = (bf16[4,384,128]{2,1,0:T(8,128)(2,1)}, f32[8,1536]{1,0:T(8,128)}) custom-call(s32[15]{0:T(128)} %stack.307.ids, f32[1,1280]{1,0:T(1,128)} %broadcast_in_dim.55.bias_ref, bf16[1280,768]{1,0:T(8,128)(2,1)} %shard_map.340.q_ref.k_ref.v_ref, bf16[1280,768]{1,0:T(8,128)(2,1)} %shard_map.340.q_ref.k_ref.v_ref, ...), custom_call_target="tpu_custom_call" | custom-call | flops 176000008192 | bytes 528000000 | tf_op jit(solution)/shard_map/pallas_call | solution.py:103
  190.1 4.6 all-to-all-start.2
  194.6 10.6 %all-to-all-done.2.refs_1_ = bf16[4,384,128]{2,1,0:T(8,128)(2,1)S(1)} async-done(((bf16[4,384,128]{2,1,0:T(8,128)(2,1)}), bf16[4,384,128]{2,1,0:T(8,128)(2,1)S(1)}, u32[]{:S(2)}, u32[]{:S(2)}) %all-to-all-start.2) | async-done | bytes 393248 | tf_op jit(solution)/shard_map/all_to_all | solution.py:69
  206.0 23.4 %shard_map.343 = (bf16[384,1024]{1,0:T(8,128)(2,1)}, f32[384,1024]{1,0:T(8,128)}, bf16[384,1024]{1,0:T(8,128)(2,1)}, bf16[384,4096]{1,0:T(8,128)(2,1)}, bf16[384...) custom-call(s32[15]{0:T(128)} %stack.307.ids, ...), custom_call_target="tpu_custom_call" | custom-call | flops 384000000000 | bytes 1152000000 | tf_op jit(solution)/shard_map/pallas_call | solution.py:103
  229.4 6.6 %shard_map.344 = bf16[4,512,1024]{2,1,0:T(8,128)(2,1)} custom-call(s32[15]{0:T(128)} %stack.307.ids, bf16[384,4096]{1,0:T(8,128)(2,1)} %get-tuple-element.176.refs_0_, bf16[384,1024]{1,0:T(8,128)(2,1)} %get-tuple-element.177.refs_1_.refs_0_), custom_call_target="tpu_custom_call" | custom-call | tf_op jit(solution)/shard_map/pallas_call | solution.py:103
  236.0 11.3 %shard_map.345 = (bf16[384,4096]{1,0:T(8,128)(2,1)}, f32[1,4096]{1,0:T(1,128)}) custom-call(s32[15]{0:T(128)} %stack.307.ids, bf16[384,1024]{1,0:T(8,128)(2,1)} %get-tuple-element.177.refs_1_.refs_0_, bf16[384,4096]{1,0:T(8,128)(2,1)} %get-tuple-element.179.refs_1_, bf16[1024,1024]{1,0:T(8,128)(2,1)} %refs_2_.3, ...), custom_call_target="tpu_custom_call" | custom-call | flops 192000000000 | bytes 576000000 | tf_op jit(solution)/shard_map/pallas_call | solution.py:103
  247.3 7.3 %shard_map.346 = (bf16[4,128,1024]{2,1,0:T(8,128)(2,1)}, bf16[4,128,1024]{2,1,0:T(8,128)(2,1)}, bf16[4,128,1024]{2,1,0:T(8,128)(2,1)}, bf16[4,128,1024]{2,1,0:T(8,128)(2,1)}) custom-call(s32[15]{0:T(128)} %stack.307.ids, bf16[384,4096]{1,0:T(8,128)(2,1)} %get-tuple-element.176.refs_0_, bf16[384,1024]{1,0:T(8,128)(2,1)} %get-tuple-element.177.refs_1_.refs_0_, ...), custom_call_target="tpu_custom_call" | custom-call | tf_op jit(solution)/shard_map/pallas_call | solution.py:103
  256.1 7.1 %shard_map.347 = bf16[4,128,4096]{2,1,0:T(8,128)(2,1)} custom-call(s32[15]{0:T(128)} %stack.307.ids, bf16[384,1024]{1,0:T(8,128)(2,1)} %get-tuple-element.184.refs_0_, bf16[384,4096]{1,0:T(8,128)(2,1)} %get-tuple-element.180.refs_1_.refs_0_), custom_call_target="tpu_custom_call" | custom-call | tf_op jit(solution)/shard_map/pallas_call | solution.py:103
  263.9 13.2 %shard_map.348 = (f32[384,1024]{1,0:T(8,128)}, bf16[384,1024]{1,0:T(8,128)(2,1)}, bf16[4,384,256]{2,1,0:T(8,128)(2,1)}, f32[4,16,256]{2,1,0:T(8,128)}) custom-call(s32[15]{0:T(128)} %stack.307.ids, bf16[384,4096]{1,0:T(8,128)(2,1)} %get-tuple-element.180.refs_1_.refs_0_, f32[1,4096]{1,0:T(1,128)} %get-tuple-element.186.refs_1_, ...), custom_call_target="tpu_custom_call" | custom-call | flops 207999991808 | bytes 624000000 | tf_op jit(solution)/shard_map/pallas_call | solution.py:103
  277.1 3.7 all-to-all-start.3
  280.8 8.2 %collective-permute-done.22.got_two = bf16[4,128,1024]{2,1,0:T(8,128)(2,1)} collective-permute-done((bf16[4,128,1024]{2,1,0:T(8,128)(2,1)}, bf16[4,128,1024]{2,1,0:T(8,128)(2,1)}, u32[]{:S(2)}, u32[]{:S(2)}) %collective-permute-start.22) | collective-permute-done | bytes 1048608 | tf_op jit(solution)/shard_map/ppermute | solution.py:61
  289.0 3.9 shard_map.349
  293.9 7.9 %shard_map.350 = (bf16[4,32,4096]{2,1,0:T(8,128)(2,1)}, bf16[4,32,4096]{2,1,0:T(8,128)(2,1)}, bf16[4,32,4096]{2,1,0:T(8,128)(2,1)}, bf16[4,32,4096]{2,1,0:T(8,128)(2,1)}) custom-call(s32[15]{0:T(128)} %stack.307.ids, bf16[384,1024]{1,0:T(8,128)(2,1)} %get-tuple-element.184.refs_0_, bf16[384,4096]{1,0:T(8,128)(2,1)} %get-tuple-element.180.refs_1_.refs_0_, ...), custom_call_target="tpu_custom_call" | custom-call | tf_op jit(solution)/shard_map/pallas_call | solution.py:103
  301.9 4.5 collective-permute-done.24.got_one
  307.5 2.7 shard_map.351
  310.2 4.3 all-to-all-start.4
  316.6 15.3 %shard_map.352 = bf16[4,384,384]{2,1,0:T(8,128)(2,1)} custom-call(s32[15]{0:T(128)} %stack.307.ids, f32[1280,128]{1,0:T(8,128)} %broadcast_in_dim.56.bias_ref, bf16[1280,768]{1,0:T(8,128)(2,1)} %shard_map.340.q_ref.k_ref.v_ref, bf16[1280,768]{1,0:T(8,128)(2,1)} %shard_map.340.q_ref.k_ref.v_ref, bf16[1280,768]{1,0:T(8,128)(2,1)} %shard_map.340.q_ref.k_ref.v_ref, ...), custom_call_target="tpu_custom_call" | custom-call | flops 256000000000 | bytes 768000000 | tf_op jit(solution)/shard_map/pallas_call | solution.py:103
  331.9 7.3 %all-to-all-done.4.refs_0_ = bf16[4,2,64,1024]{3,2,1,0:T(8,128)(2,1)} async-done(((bf16[4,2,64,1024]{3,2,1,0:T(8,128)(2,1)}), bf16[4,2,64,1024]{3,2,1,0:T(8,128)(2,1)}, u32[]{:S(2)}, u32[]{:S(2)}) %all-to-all-start.4) | async-done | bytes 1048608 | tf_op jit(solution)/shard_map/all_to_all | solution.py:69
  339.2 4.5 all-to-all-start.5
  346.3 3.9 shard_map.354
  353.7 15.5 %shard_map.355 = bf16[4,384,384]{2,1,0:T(8,128)(2,1)} custom-call(s32[15]{0:T(128)} %stack.307.ids, f32[1280,128]{1,0:T(8,128)} %broadcast_in_dim.56.bias_ref, bf16[1280,768]{1,0:T(8,128)(2,1)} %shard_map.340.q_ref.k_ref.v_ref, bf16[1280,768]{1,0:T(8,128)(2,1)} %shard_map.340.q_ref.k_ref.v_ref, bf16[1280,768]{1,0:T(8,128)(2,1)} %shard_map.340.q_ref.k_ref.v_ref, ...), custom_call_target="tpu_custom_call" | custom-call | flops 256000000000 | bytes 768000000 | tf_op jit(solution)/shard_map/pallas_call | solution.py:103
  371.8 7.5 %shard_map.356 = bf16[4,128,1792]{2,1,0:T(8,128)(2,1)} custom-call(s32[15]{0:T(128)} %stack.307.ids, bf16[1536,1024]{1,0:T(8,128)(2,1)} %bitcast.167, bf16[1536,384]{1,0:T(8,128)(2,1)} %bitcast.171, bf16[1536,1024]{1,0:T(8,128)(2,1)} %bitcast.168, bf16[1536,384]{1,0:T(8,128)(2,1)} %bitcast.68.refs_3_, bf16[384,1024]{1,0:T(8,128)(2,1)} %get-tuple-element.174.refs_4_, ...), custom_call_target="tpu_custom_call" | custom-call | tf_op jit(solution)/shard_map/pallas_call | solution.py:103
  379.3 4.4 all-to-all-start.6
  385.5 2.7 shard_map.357
  388.3 3.9 collective-permute-done.33
  393.0 7.8 %shard_map.358 = (bf16[4,32,1792]{2,1,0:T(8,128)(2,1)}, bf16[4,32,1792]{2,1,0:T(8,128)(2,1)}, bf16[4,32,1792]{2,1,0:T(8,128)(2,1)}, bf16[4,32,1792]{2,1,0:T(8,128)(2,1)}) custom-call(s32[15]{0:T(128)} %stack.307.ids, bf16[1536,1024]{1,0:T(8,128)(2,1)} %bitcast.169, bf16[1536,384]{1,0:T(8,128)(2,1)} %bitcast.172, bf16[1536,1024]{1,0:T(8,128)(2,1)} %bitcast.170, ...), custom_call_target="tpu_custom_call" | custom-call | tf_op jit(solution)/shard_map/pallas_call | solution.py:103
  405.7 7.2 %all-to-all-done.6.refs_1_ = bf16[4,384,384]{2,1,0:T(8,128)(2,1)S(1)} async-done(((bf16[4,384,384]{2,1,0:T(8,128)(2,1)}), bf16[4,384,384]{2,1,0:T(8,128)(2,1)S(1)}, u32[]{:S(2)}, u32[]{:S(2)}) %all-to-all-start.6) | async-done | bytes 1179680 | tf_op jit(solution)/shard_map/all_to_all | solution.py:69
  412.9 4.2 shard_map.359
  417.2 4.5 all-to-all-start.7
  421.7 2.5 shard_map.360
  426.1 8.9 %shard_map.361 = (f32[384,1024]{1,0:T(8,128)}, f32[1,1024]{1,0:T(1,128)}) custom-call(s32[15]{0:T(128)} %stack.307.ids, bf16[4,384,384]{2,1,0:T(8,128)(2,1)} %all-to-all-done.5.refs_0_, bf16[4,384,384]{2,1,0:T(8,128)(2,1)} %copy-done.11, f32[384,1024]{1,0:T(8,128)} %get-tuple-element.190.refs_2_, bf16[256,1024]{1,0:T(8,128)(2,1)} %refs_3_.3, ...), custom_call_target="tpu_custom_call" | custom-call | flops 143999991808 | bytes 432000000 | tf_op jit(solution)/shard_map/pallas_call | solution.py:103
  438.3 2.2 shard_map.362
  440.5 6.8 %all-to-all-done.7.refs_0_ = bf16[4,2,16,4096]{3,2,1,0:T(8,128)(2,1)} async-done(((bf16[4,2,16,4096]{3,2,1,0:T(8,128)(2,1)}), bf16[4,2,16,4096]{3,2,1,0:T(8,128)(2,1)}, u32[]{:S(2)}, u32[]{:S(2)}) %all-to-all-start.7) | async-done | bytes 1048608 | tf_op jit(solution)/shard_map/all_to_all | solution.py:69
  447.3 3.3 all-to-all-start.8
  456.6 4.7 all-to-all-start.9
  466.2 3.3 collective-permute-done.43
  469.5 5.5 %all-to-all-done.9.refs_0_ = bf16[4,2,16,1792]{3,2,1,0:T(8,128)(2,1)S(1)} async-done(((bf16[4,2,16,1792]{3,2,1,0:T(8,128)(2,1)}), bf16[4,2,16,1792]{3,2,1,0:T(8,128)(2,1)S(1)}, u32[]{:S(2)}, u32[]{:S(2)}) %all-to-all-start.9) | async-done | bytes 458784 | tf_op jit(solution)/shard_map/all_to_all | solution.py:69
  481.6 2.4 collective-permute-done.49
  485.9 2.7 collective-permute-done.47
  493.3 2.2 collective-permute-done.53
  495.5 2.4 collective-permute-done.52
  499.6 3.8 shard_map.365
  507.6 3.8 shard_map.366
  (279 shorter events, 98.3 us)
Async XLA Ops:
  3.5 25.3 %collective-permute-start = (bf16[2,16,7168]{2,1,0:T(8,128)(2,1)S(1)}, bf16[2,16,7168]{2,1,0:T(8,128)(2,1)S(1)}, u32[]{:S(2)}, u32[]{:S(2)}) collective-permute-start(bf16[2,16,7168]{2,1,0:T(8,128)(2,1)S(1)} %pad_maximum_fusion.16), channel_id=1, source_target_pairs={{0,2},{1,3},{2,0},{3,1},{4,6},{5,7},{6,4},{7,5},{8,10},{9,11},{10,... | collective-permute-start | bytes 1376264 | tf_op jit(solution)/shard_map/ppermute | solution.py:65
  7.6 22.5 %collective-permute-start.1 = (bf16[2,16,7168]{2,1,0:T(8,128)(2,1)S(1)}, bf16[2,16,7168]{2,1,0:T(8,128)(2,1)S(1)}, u32[]{:S(2)}, u32[]{:S(2)}) collective-permute-start(bf16[2,16,7168]{2,1,0:T(8,128)(2,1)S(1)} %pad_maximum_fusion.16), channel_id=1, source_target_pairs={{0,1},{1,2},{2,3},{4,5},{5,6},{6,7},{8,9},{9,10},{10,11},{12,13},{... | collective-permute-start | bytes 1376264 | tf_op jit(solution)/shard_map/ppermute | solution.py:65
  11.1 23.8 %collective-permute-start.2 = (bf16[2,16,7168]{2,1,0:T(8,128)(2,1)S(1)}, bf16[2,16,7168]{2,1,0:T(8,128)(2,1)S(1)}, u32[]{:S(2)}, u32[]{:S(2)}) collective-permute-start(bf16[2,16,7168]{2,1,0:T(8,128)(2,1)S(1)} %pad_maximum_fusion.16), channel_id=1, source_target_pairs={{1,0},{2,1},{3,2},{5,4},{6,5},{7,6},{9,8},{10,9},{11,10},{13,12},{... | collective-permute-start | bytes 1376264 | tf_op jit(solution)/shard_map/ppermute | solution.py:65
  28.8 14.4 %collective-permute-start.3 = (bf16[2,16,7168]{2,1,0:T(8,128)(2,1)S(1)}, bf16[2,16,7168]{2,1,0:T(8,128)(2,1)S(1)}, u32[]{:S(2)}, u32[]{:S(2)}) collective-permute-start(bf16[2,16,7168]{2,1,0:T(8,128)(2,1)S(1)} %collective-permute-done), channel_id=1, source_target_pairs={{2,3},{1,0},{6,7},{5,4},{10,11},{9,8},{14,15},{13,12},{18,19},{17,... | collective-permute-start | bytes 1376264 | tf_op jit(solution)/shard_map/ppermute | solution.py:65
  43.7 16.0 %collective-permute-start.6 = (bf16[3,16,7168]{2,1,0:T(8,128)(2,1)S(1)}, bf16[3,16,7168]{2,1,0:T(8,128)(2,1)S(1)}, u32[]{:S(2)}, u32[]{:S(2)}) collective-permute-start(bf16[3,16,7168]{2,1,0:T(8,128)(2,1)S(1)} %get-tuple-element.282), channel_id=1, source_target_pairs={{0,16},{4,20},{8,24},{12,28},{16,0},{20,4},{24,8},{28,12},{1,17},{... | collective-permute-start | bytes 2064392 | tf_op jit(solution)/shard_map/ppermute | solution.py:61
  47.8 26.6 %collective-permute-start.4 = (bf16[2,80,1024]{2,1,0:T(8,128)(2,1)S(1)}, bf16[2,80,1024]{2,1,0:T(8,128)(2,1)S(1)}, u32[]{:S(2)}, u32[]{:S(2)}) collective-permute-start(bf16[2,80,1024]{2,1,0:T(8,128)(2,1)S(1)} %pad_maximum_fusion.17), channel_id=1, source_target_pairs={{0,2},{1,3},{2,0},{3,1},{4,6},{5,7},{6,4},{7,5},{8,10},{9,11},{10,... | collective-permute-start | bytes 983048 | tf_op jit(solution)/shard_map/ppermute | solution.py:65
  48.5 29.1 %collective-permute-start.7 = (bf16[2,80,1024]{2,1,0:T(8,128)(2,1)S(1)}, bf16[2,80,1024]{2,1,0:T(8,128)(2,1)S(1)}, u32[]{:S(2)}, u32[]{:S(2)}) collective-permute-start(bf16[2,80,1024]{2,1,0:T(8,128)(2,1)S(1)} %pad_maximum_fusion.17), channel_id=1, source_target_pairs={{0,1},{1,2},{2,3},{4,5},{5,6},{6,7},{8,9},{9,10},{10,11},{12,13},{... | collective-permute-start | bytes 983048 | tf_op jit(solution)/shard_map/ppermute | solution.py:65
  52.9 24.7 %collective-permute-start.8 = (bf16[2,80,1024]{2,1,0:T(8,128)(2,1)S(1)}, bf16[2,80,1024]{2,1,0:T(8,128)(2,1)S(1)}, u32[]{:S(2)}, u32[]{:S(2)}) collective-permute-start(bf16[2,80,1024]{2,1,0:T(8,128)(2,1)S(1)} %pad_maximum_fusion.17), channel_id=1, source_target_pairs={{1,0},{2,1},{3,2},{5,4},{6,5},{7,6},{9,8},{10,9},{11,10},{13,12},{... | collective-permute-start | bytes 983048 | tf_op jit(solution)/shard_map/ppermute | solution.py:65
  54.2 18.4 %collective-permute-start.5 = (bf16[3,16,7168]{2,1,0:T(8,128)(2,1)S(1)}, bf16[3,16,7168]{2,1,0:T(8,128)(2,1)S(1)}, u32[]{:S(2)}, u32[]{:S(2)}) collective-permute-start(bf16[3,16,7168]{2,1,0:T(8,128)(2,1)S(1)} %get-tuple-element.281), channel_id=1, source_target_pairs={{0,8},{4,12},{8,0},{12,4},{16,24},{20,28},{24,16},{28,20},{1,9},{5... | collective-permute-start | bytes 2064392 | tf_op jit(solution)/shard_map/ppermute | solution.py:61
  61.5 38.0 %collective-permute-start.11 = (bf16[2,3,16,7168]{3,2,1,0:T(8,128)(2,1)}, bf16[2,3,16,7168]{3,2,1,0:T(8,128)(2,1)}, u32[]{:S(2)}, u32[]{:S(2)}) collective-permute-start(bf16[2,3,16,7168]{3,2,1,0:T(8,128)(2,1)} %get-tuple-element.277), channel_id=1, source_target_pairs={{0,8},{4,12},{8,0},{12,4},{16,24},{20,28},{24,16},{28,20},{1,9},{5... | collective-permute-start | bytes 4128776 | tf_op jit(solution)/shard_map/ppermute | solution.py:61
  74.4 9.0 %collective-permute-start.9 = (bf16[2,80,1024]{2,1,0:T(8,128)(2,1)S(1)}, bf16[2,80,1024]{2,1,0:T(8,128)(2,1)S(1)}, u32[]{:S(2)}, u32[]{:S(2)}) collective-permute-start(bf16[2,80,1024]{2,1,0:T(8,128)(2,1)S(1)} %collective-permute-done.4), channel_id=1, source_target_pairs={{2,3},{1,0},{6,7},{5,4},{10,11},{9,8},{14,15},{13,12},{18,19},{17,... | collective-permute-start | bytes 983048 | tf_op jit(solution)/shard_map/ppermute | solution.py:65
  75.7 27.4 %collective-permute-start.10 = (bf16[2,3,16,7168]{3,2,1,0:T(8,128)(2,1)}, bf16[2,3,16,7168]{3,2,1,0:T(8,128)(2,1)}, u32[]{:S(2)}, u32[]{:S(2)}) collective-permute-start(bf16[2,3,16,7168]{3,2,1,0:T(8,128)(2,1)} %get-tuple-element.279), channel_id=1, source_target_pairs={{0,16},{4,20},{8,24},{12,28},{16,0},{20,4},{24,8},{28,12},{1,17},{... | collective-permute-start | bytes 4128776 | tf_op jit(solution)/shard_map/ppermute | solution.py:61
  85.4 68.5 %all-to-all-start = ((bf16[4,384,1024]{2,1,0:T(8,128)(2,1)}), bf16[4,384,1024]{2,1,0:T(8,128)(2,1)S(1)}, u32[]{:S(2)}, u32[]{:S(2)}) async-start(bf16[4,384,1024]{2,1,0:T(8,128)(2,1)} %broadcast_in_dim.57), calls=%async_computation | async-start | bytes 6291456 | tf_op jit(solution)/shard_map/all_to_all | solution.py:69
  103.1 49.8 %collective-permute-start.15 = (bf16[2,2,3,16,7168]{4,3,2,1,0:T(8,128)(2,1)}, bf16[2,2,3,16,7168]{4,3,2,1,0:T(8,128)(2,1)}, u32[]{:S(2)}, u32[]{:S(2)}) collective-permute-start(bf16[2,2,3,16,7168]{4,3,2,1,0:T(8,128)(2,1)} %pad_maximum_fusion.1.refs_5_.refs_10_.refs_9_.refs_7_), channel_id=1, source_target_pairs={{0,4},{4,0},{8,12},{12,8},{16,20},{20,16},{24,28},{28,24},{1,5},{5... | collective-permute-start | bytes 8257544 | tf_op jit(solution)/shard_map/ppermute | solution.py:61
  106.3 46.5 %collective-permute-start.14 = (bf16[2,2,3,16,7168]{4,3,2,1,0:T(8,128)(2,1)}, bf16[2,2,3,16,7168]{4,3,2,1,0:T(8,128)(2,1)}, u32[]{:S(2)}, u32[]{:S(2)}) collective-permute-start(bf16[2,2,3,16,7168]{4,3,2,1,0:T(8,128)(2,1)} %pad_maximum_fusion.refs_4_.refs_9_.refs_8_.refs_6_), channel_id=1, source_target_pairs={{0,4},{4,0},{8,12},{12,8},{16,20},{20,16},{24,28},{28,24},{1,5},{5... | collective-permute-start | bytes 8257544 | tf_op jit(solution)/shard_map/ppermute | solution.py:61
  107.7 13.7 %collective-permute-start.13 = (bf16[3,80,1024]{2,1,0:T(8,128)(2,1)S(1)}, bf16[3,80,1024]{2,1,0:T(8,128)(2,1)S(1)}, u32[]{:S(2)}, u32[]{:S(2)}) collective-permute-start(bf16[3,80,1024]{2,1,0:T(8,128)(2,1)S(1)} %get-tuple-element.290), channel_id=1, source_target_pairs={{0,16},{4,20},{8,24},{12,28},{16,0},{20,4},{24,8},{28,12},{1,17},{... | collective-permute-start | bytes 1474568 | tf_op jit(solution)/shard_map/ppermute | solution.py:61
  108.2 16.1 %collective-permute-start.12 = (bf16[3,80,1024]{2,1,0:T(8,128)(2,1)S(1)}, bf16[3,80,1024]{2,1,0:T(8,128)(2,1)S(1)}, u32[]{:S(2)}, u32[]{:S(2)}) collective-permute-start(bf16[3,80,1024]{2,1,0:T(8,128)(2,1)S(1)} %get-tuple-element.289), channel_id=1, source_target_pairs={{0,8},{4,12},{8,0},{12,4},{16,24},{20,28},{24,16},{28,20},{1,9},{5... | collective-permute-start | bytes 1474568 | tf_op jit(solution)/shard_map/ppermute | solution.py:61
  122.8 23.8 %collective-permute-start.17 = (bf16[2,3,80,1024]{3,2,1,0:T(8,128)(2,1)}, bf16[2,3,80,1024]{3,2,1,0:T(8,128)(2,1)}, u32[]{:S(2)}, u32[]{:S(2)}) collective-permute-start(bf16[2,3,80,1024]{3,2,1,0:T(8,128)(2,1)} %get-tuple-element.285), channel_id=1, source_target_pairs={{0,8},{4,12},{8,0},{12,4},{16,24},{20,28},{24,16},{28,20},{1,9},{5... | collective-permute-start | bytes 2949128 | tf_op jit(solution)/shard_map/ppermute | solution.py:61
  125.7 24.0 %collective-permute-start.16 = (bf16[2,3,80,1024]{3,2,1,0:T(8,128)(2,1)}, bf16[2,3,80,1024]{3,2,1,0:T(8,128)(2,1)}, u32[]{:S(2)}, u32[]{:S(2)}) collective-permute-start(bf16[2,3,80,1024]{3,2,1,0:T(8,128)(2,1)} %get-tuple-element.287), channel_id=1, source_target_pairs={{0,16},{4,20},{8,24},{12,28},{16,0},{20,4},{24,8},{28,12},{1,17},{... | collective-permute-start | bytes 2949128 | tf_op jit(solution)/shard_map/ppermute | solution.py:61
  149.7 44.9 %collective-permute-start.19 = (bf16[2,2,3,80,1024]{4,3,2,1,0:T(8,128)(2,1)}, bf16[2,2,3,80,1024]{4,3,2,1,0:T(8,128)(2,1)}, u32[]{:S(2)}, u32[]{:S(2)}) collective-permute-start(bf16[2,2,3,80,1024]{4,3,2,1,0:T(8,128)(2,1)} %pad_maximum_fusion.3.refs_14_.refs_4_.refs_13_), channel_id=1, source_target_pairs={{0,4},{4,0},{8,12},{12,8},{16,20},{20,16},{24,28},{28,24},{1,5},{5... | collective-permute-start | bytes 5898248 | tf_op jit(solution)/shard_map/ppermute | solution.py:61
  152.3 42.3 %collective-permute-start.18 = (bf16[2,2,3,80,1024]{4,3,2,1,0:T(8,128)(2,1)}, bf16[2,2,3,80,1024]{4,3,2,1,0:T(8,128)(2,1)}, u32[]{:S(2)}, u32[]{:S(2)}) collective-permute-start(bf16[2,2,3,80,1024]{4,3,2,1,0:T(8,128)(2,1)} %pad_maximum_fusion.2.refs_13_.refs_3_.refs_12_), channel_id=1, source_target_pairs={{0,4},{4,0},{8,12},{12,8},{16,20},{20,16},{24,28},{28,24},{1,5},{5... | collective-permute-start | bytes 5898248 | tf_op jit(solution)/shard_map/ppermute | solution.py:61
  174.2 15.8 %all-to-all-start.1 = ((bf16[4,384,128]{2,1,0:T(8,128)(2,1)}), bf16[4,384,128]{2,1,0:T(8,128)(2,1)}, u32[]{:S(2)}, u32[]{:S(2)}) async-start(bf16[4,384,128]{2,1,0:T(8,128)(2,1)} %get-tuple-element.166), calls=%async_computation.1 | async-start | bytes 786432 | tf_op jit(solution)/shard_map/all_to_all | solution.py:69
  190.1 15.2 %all-to-all-start.2 = ((bf16[4,384,128]{2,1,0:T(8,128)(2,1)}), bf16[4,384,128]{2,1,0:T(8,128)(2,1)S(1)}, u32[]{:S(2)}, u32[]{:S(2)}) async-start(bf16[4,384,128]{2,1,0:T(8,128)(2,1)} %get-tuple-element.172), calls=%async_computation.2 | async-start | bytes 786432 | tf_op jit(solution)/shard_map/all_to_all | solution.py:69
  236.0 11.3 %collective-permute-start.20 = (bf16[4,512,1024]{2,1,0:T(8,128)(2,1)}, bf16[4,512,1024]{2,1,0:T(8,128)(2,1)}, u32[]{:S(2)}, u32[]{:S(2)}) collective-permute-start(bf16[4,512,1024]{2,1,0:T(8,128)(2,1)} %shard_map.344), channel_id=1, source_target_pairs={{0,4},{4,0},{8,12},{12,8},{16,20},{20,16},{24,28},{28,24},{1,5},{5... | collective-permute-start | bytes 12582920 | tf_op jit(solution)/shard_map/ppermute | solution.py:61
  254.6 26.2 %collective-permute-start.21 = (bf16[4,128,1024]{2,1,0:T(8,128)(2,1)}, bf16[4,128,1024]{2,1,0:T(8,128)(2,1)}, u32[]{:S(2)}, u32[]{:S(2)}) collective-permute-start(bf16[4,128,1024]{2,1,0:T(8,128)(2,1)} %get-tuple-element.182), channel_id=1, source_target_pairs={{0,8},{4,12},{8,0},{12,4},{16,24},{20,28},{24,16},{28,20},{1,9},{5... | collective-permute-start | bytes 3145736 | tf_op jit(solution)/shard_map/ppermute | solution.py:61
  263.1 30.8 %collective-permute-start.23 = (bf16[4,128,4096]{2,1,0:T(8,128)(2,1)}, bf16[4,128,4096]{2,1,0:T(8,128)(2,1)}, u32[]{:S(2)}, u32[]{:S(2)}) collective-permute-start(bf16[4,128,4096]{2,1,0:T(8,128)(2,1)} %shard_map.347), channel_id=1, source_target_pairs={{0,4},{4,0},{8,12},{12,8},{16,20},{20,16},{24,28},{28,24},{1,5},{5... | collective-permute-start | bytes 12582920 | tf_op jit(solution)/shard_map/ppermute | solution.py:61
  263.3 25.7 %collective-permute-start.22 = (bf16[4,128,1024]{2,1,0:T(8,128)(2,1)}, bf16[4,128,1024]{2,1,0:T(8,128)(2,1)}, u32[]{:S(2)}, u32[]{:S(2)}) collective-permute-start(bf16[4,128,1024]{2,1,0:T(8,128)(2,1)} %get-tuple-element.194), channel_id=1, source_target_pairs={{0,16},{4,20},{8,24},{12,28},{16,0},{20,4},{24,8},{28,12},{1,17},{... | collective-permute-start | bytes 3145736 | tf_op jit(solution)/shard_map/ppermute | solution.py:61
  277.1 24.8 %all-to-all-start.3 = ((bf16[4,384,256]{2,1,0:T(8,128)(2,1)}), bf16[4,384,256]{2,1,0:T(8,128)(2,1)S(1)}, u32[]{:S(2)}, u32[]{:S(2)}) async-start(bf16[4,384,256]{2,1,0:T(8,128)(2,1)} %get-tuple-element.199), calls=%async_computation.3 | async-start | bytes 1572864 | tf_op jit(solution)/shard_map/all_to_all | solution.py:69
  292.9 13.5 %collective-permute-start.24 = (bf16[4,64,1024]{2,1,0:T(8,128)(2,1)}, bf16[4,64,1024]{2,1,0:T(8,128)(2,1)S(1)}, u32[]{:S(2)}, u32[]{:S(2)}) collective-permute-start(bf16[4,64,1024]{2,1,0:T(8,128)(2,1)} %get-tuple-element.195), channel_id=1, source_target_pairs={{0,16},{4,20},{8,24},{12,28},{16,0},{20,4},{24,8},{28,12},{1,17},{... | collective-permute-start | bytes 1572872 | tf_op jit(solution)/shard_map/ppermute | solution.py:61
  293.4 13.3 %collective-permute-start.25 = (bf16[4,64,1024]{2,1,0:T(8,128)(2,1)}, bf16[4,64,1024]{2,1,0:T(8,128)(2,1)S(1)}, u32[]{:S(2)}, u32[]{:S(2)}) collective-permute-start(bf16[4,64,1024]{2,1,0:T(8,128)(2,1)} %get-tuple-element.203), channel_id=1, source_target_pairs={{0,8},{4,12},{8,0},{12,4},{16,24},{20,28},{24,16},{28,20},{1,9},{5... | collective-permute-start | bytes 1572872 | tf_op jit(solution)/shard_map/ppermute | solution.py:61
  310.2 29.0 %all-to-all-start.4 = ((bf16[4,2,64,1024]{3,2,1,0:T(8,128)(2,1)}), bf16[4,2,64,1024]{3,2,1,0:T(8,128)(2,1)}, u32[]{:S(2)}, u32[]{:S(2)}) async-start(bf16[4,2,64,1024]{3,2,1,0:T(8,128)(2,1)} %shard_map.351), calls=%async_computation.4 | async-start | bytes 2097152 | tf_op jit(solution)/shard_map/all_to_all | solution.py:69
  314.5 31.8 %collective-permute-start.26 = (bf16[4,32,4096]{2,1,0:T(8,128)(2,1)}, bf16[4,32,4096]{2,1,0:T(8,128)(2,1)}, u32[]{:S(2)}, u32[]{:S(2)}) collective-permute-start(bf16[4,32,4096]{2,1,0:T(8,128)(2,1)} %get-tuple-element.197), channel_id=1, source_target_pairs={{0,8},{4,12},{8,0},{12,4},{16,24},{20,28},{24,16},{28,20},{1,9},{5... | collective-permute-start | bytes 3145736 | tf_op jit(solution)/shard_map/ppermute | solution.py:61
  315.1 31.2 %collective-permute-start.27 = (bf16[4,32,4096]{2,1,0:T(8,128)(2,1)}, bf16[4,32,4096]{2,1,0:T(8,128)(2,1)}, u32[]{:S(2)}, u32[]{:S(2)}) collective-permute-start(bf16[4,32,4096]{2,1,0:T(8,128)(2,1)} %get-tuple-element.212), channel_id=1, source_target_pairs={{0,16},{4,20},{8,24},{12,28},{16,0},{20,4},{24,8},{28,12},{1,17},{... | collective-permute-start | bytes 3145736 | tf_op jit(solution)/shard_map/ppermute | solution.py:61
  339.2 32.6 %all-to-all-start.5 = ((bf16[4,384,384]{2,1,0:T(8,128)(2,1)}), bf16[4,384,384]{2,1,0:T(8,128)(2,1)}, u32[]{:S(2)}, u32[]{:S(2)}) async-start(bf16[4,384,384]{2,1,0:T(8,128)(2,1)} %shard_map.352), calls=%async_computation.5 | async-start | bytes 2359296 | tf_op jit(solution)/shard_map/all_to_all | solution.py:69
  345.7 24.5 %collective-permute-start.30 = (bf16[1,64,1024]{2,1,0:T(8,128)(2,1)}, bf16[1,64,1024]{2,1,0:T(8,128)(2,1)}, u32[]{:S(2)}, u32[]{:S(2)}) collective-permute-start(bf16[1,64,1024]{2,1,0:T(8,128)(2,1)} %get-tuple-element.208), channel_id=1, source_target_pairs={{0,8},{4,12},{8,0},{12,4},{16,24},{20,28},{24,16},{28,20},{1,9},{5... | collective-permute-start | bytes 393224 | tf_op jit(solution)/shard_map/ppermute | solution.py:61
  350.1 21.6 %collective-permute-start.28 = (bf16[4,16,4096]{2,1,0:T(8,128)(2,1)}, bf16[4,16,4096]{2,1,0:T(8,128)(2,1)}, u32[]{:S(2)}, u32[]{:S(2)}) collective-permute-start(bf16[4,16,4096]{2,1,0:T(8,128)(2,1)} %get-tuple-element.213), channel_id=1, source_target_pairs={{0,16},{4,20},{8,24},{12,28},{16,0},{20,4},{24,8},{28,12},{1,17},{... | collective-permute-start | bytes 1572872 | tf_op jit(solution)/shard_map/ppermute | solution.py:61
  351.4 17.7 %collective-permute-start.31 = (bf16[1,64,1024]{2,1,0:T(8,128)(2,1)}, bf16[1,64,1024]{2,1,0:T(8,128)(2,1)}, u32[]{:S(2)}, u32[]{:S(2)}) collective-permute-start(bf16[1,64,1024]{2,1,0:T(8,128)(2,1)} %get-tuple-element.220), channel_id=1, source_target_pairs={{0,16},{4,20},{8,24},{12,28},{16,0},{20,4},{24,8},{28,12},{1,17},{... | collective-permute-start | bytes 393224 | tf_op jit(solution)/shard_map/ppermute | solution.py:61
  352.2 19.6 %collective-permute-start.29 = (bf16[4,16,4096]{2,1,0:T(8,128)(2,1)}, bf16[4,16,4096]{2,1,0:T(8,128)(2,1)}, u32[]{:S(2)}, u32[]{:S(2)}) collective-permute-start(bf16[4,16,4096]{2,1,0:T(8,128)(2,1)} %get-tuple-element.219), channel_id=1, source_target_pairs={{0,8},{4,12},{8,0},{12,4},{16,24},{20,28},{24,16},{28,20},{1,9},{5... | collective-permute-start | bytes 1572872 | tf_op jit(solution)/shard_map/ppermute | solution.py:61
  379.3 13.8 %collective-permute-start.34 = (bf16[4,128,1792]{2,1,0:T(8,128)(2,1)}, bf16[4,128,1792]{2,1,0:T(8,128)(2,1)}, u32[]{:S(2)}, u32[]{:S(2)}) collective-permute-start(bf16[4,128,1792]{2,1,0:T(8,128)(2,1)} %shard_map.356), channel_id=1, source_target_pairs={{0,4},{4,0},{8,12},{12,8},{16,20},{20,16},{24,28},{28,24},{1,5},{5... | collective-permute-start | bytes 5505032 | tf_op jit(solution)/shard_map/ppermute | solution.py:61
  379.3 33.6 %all-to-all-start.6 = ((bf16[4,384,384]{2,1,0:T(8,128)(2,1)}), bf16[4,384,384]{2,1,0:T(8,128)(2,1)S(1)}, u32[]{:S(2)}, u32[]{:S(2)}) async-start(bf16[4,384,384]{2,1,0:T(8,128)(2,1)} %shard_map.355), calls=%async_computation.6 | async-start | bytes 2359296 | tf_op jit(solution)/shard_map/all_to_all | solution.py:69
  383.7 8.4 %collective-permute-start.33 = (bf16[2,1,64,1024]{3,2,0,1:T(8,128)(2,1)S(1)}, bf16[2,1,64,1024]{3,2,0,1:T(8,128)(2,1)S(1)}, u32[]{:S(2)}, u32[]{:S(2)}) collective-permute-start(bf16[2,1,64,1024]{3,2,0,1:T(8,128)(2,1)S(1)} %pad_maximum_fusion.19), channel_id=1, source_target_pairs={{0,8},{4,12},{8,0},{12,4},{16,24},{20,28},{24,16},{28,20},{1,9},{5... | collective-permute-start | bytes 786440 | tf_op jit(solution)/shard_map/ppermute | solution.py:61
  384.2 8.2 %collective-permute-start.32 = (bf16[2,1,64,1024]{3,2,0,1:T(8,128)(2,1)S(1)}, bf16[2,1,64,1024]{3,2,0,1:T(8,128)(2,1)S(1)}, u32[]{:S(2)}, u32[]{:S(2)}) collective-permute-start(bf16[2,1,64,1024]{3,2,0,1:T(8,128)(2,1)S(1)} %pad_maximum_fusion.18), channel_id=1, source_target_pairs={{0,16},{4,20},{8,24},{12,28},{16,0},{20,4},{24,8},{28,12},{1,17},{... | collective-permute-start | bytes 786440 | tf_op jit(solution)/shard_map/ppermute | solution.py:61
  392.5 20.5 %collective-permute-start.35 = (bf16[2,2,1,64,1024]{4,3,2,1,0:T(8,128)(2,1)S(1)}, bf16[2,2,1,64,1024]{4,3,2,1,0:T(8,128)(2,1)}, u32[]{:S(2)}, u32[]{:S(2)}) collective-permute-start(bf16[2,2,1,64,1024]{4,3,2,1,0:T(8,128)(2,1)S(1)} %pad_maximum_fusion.10.refs_0_), channel_id=1, source_target_pairs={{0,4},{4,0},{8,12},{12,8},{16,20},{20,16},{24,28},{28,24},{1,5},{5... | collective-permute-start | bytes 1572872 | tf_op jit(solution)/shard_map/ppermute | solution.py:61
  392.5 20.4 %collective-permute-start.36 = (bf16[2,2,1,64,1024]{4,3,2,1,0:T(8,128)(2,1)S(1)}, bf16[2,2,1,64,1024]{4,3,2,1,0:T(8,128)(2,1)}, u32[]{:S(2)}, u32[]{:S(2)}) collective-permute-start(bf16[2,2,1,64,1024]{4,3,2,1,0:T(8,128)(2,1)S(1)} %pad_maximum_fusion.11.refs_1_), channel_id=1, source_target_pairs={{0,4},{4,0},{8,12},{12,8},{16,20},{20,16},{24,28},{28,24},{1,5},{5... | collective-permute-start | bytes 1572872 | tf_op jit(solution)/shard_map/ppermute | solution.py:61
  400.8 20.9 %collective-permute-start.37 = (bf16[4,32,1792]{2,1,0:T(8,128)(2,1)}, bf16[4,32,1792]{2,1,0:T(8,128)(2,1)}, u32[]{:S(2)}, u32[]{:S(2)}) collective-permute-start(bf16[4,32,1792]{2,1,0:T(8,128)(2,1)} %get-tuple-element.228), channel_id=1, source_target_pairs={{0,8},{4,12},{8,0},{12,4},{16,24},{20,28},{24,16},{28,20},{1,9},{5... | collective-permute-start | bytes 1376264 | tf_op jit(solution)/shard_map/ppermute | solution.py:61
  402.4 19.3 %collective-permute-start.38 = (bf16[4,32,1792]{2,1,0:T(8,128)(2,1)}, bf16[4,32,1792]{2,1,0:T(8,128)(2,1)}, u32[]{:S(2)}, u32[]{:S(2)}) collective-permute-start(bf16[4,32,1792]{2,1,0:T(8,128)(2,1)} %get-tuple-element.236), channel_id=1, source_target_pairs={{0,16},{4,20},{8,24},{12,28},{16,0},{20,4},{24,8},{28,12},{1,17},{... | collective-permute-start | bytes 1376264 | tf_op jit(solution)/shard_map/ppermute | solution.py:61
  417.2 30.2 %all-to-all-start.7 = ((bf16[4,2,16,4096]{3,2,1,0:T(8,128)(2,1)}), bf16[4,2,16,4096]{3,2,1,0:T(8,128)(2,1)}, u32[]{:S(2)}, u32[]{:S(2)}) async-start(bf16[4,2,16,4096]{3,2,1,0:T(8,128)(2,1)} %shard_map.357), calls=%async_computation.7 | async-start | bytes 2097152 | tf_op jit(solution)/shard_map/all_to_all | solution.py:69
  424.2 13.3 %collective-permute-start.39 = (bf16[4,16,1792]{2,1,0:T(8,128)(2,1)}, bf16[4,16,1792]{2,1,0:T(8,128)(2,1)S(1)}, u32[]{:S(2)}, u32[]{:S(2)}) collective-permute-start(bf16[4,16,1792]{2,1,0:T(8,128)(2,1)} %get-tuple-element.237), channel_id=1, source_target_pairs={{0,16},{4,20},{8,24},{12,28},{16,0},{20,4},{24,8},{28,12},{1,17},{... | collective-permute-start | bytes 688136 | tf_op jit(solution)/shard_map/ppermute | solution.py:61
  425.5 12.0 %collective-permute-start.40 = (bf16[4,16,1792]{2,1,0:T(8,128)(2,1)}, bf16[4,16,1792]{2,1,0:T(8,128)(2,1)S(1)}, u32[]{:S(2)}, u32[]{:S(2)}) collective-permute-start(bf16[4,16,1792]{2,1,0:T(8,128)(2,1)} %get-tuple-element.243), channel_id=1, source_target_pairs={{0,8},{4,12},{8,0},{12,4},{16,24},{20,28},{24,16},{28,20},{1,9},{5... | collective-permute-start | bytes 688136 | tf_op jit(solution)/shard_map/ppermute | solution.py:61
  447.3 9.1 %all-to-all-start.8 = ((f32[4,20,256]{2,1,0:T(8,128)}), f32[4,20,256]{2,1,0:T(8,128)S(1)}, u32[]{:S(2)}, u32[]{:S(2)}) async-start(f32[4,20,256]{2,1,0:T(8,128)} %pad_maximum_fusion.24), calls=%async_computation.8 | async-start | bytes 196608 | tf_op jit(solution)/shard_map/all_to_all | solution.py:69
  454.2 12.0 %collective-permute-start.44 = (bf16[1,16,4096]{2,1,0:T(8,128)(2,1)}, bf16[1,16,4096]{2,1,0:T(8,128)(2,1)S(1)}, u32[]{:S(2)}, u32[]{:S(2)}) collective-permute-start(bf16[1,16,4096]{2,1,0:T(8,128)(2,1)} %get-tuple-element.248), channel_id=1, source_target_pairs={{0,8},{4,12},{8,0},{12,4},{16,24},{20,28},{24,16},{28,20},{1,9},{5... | collective-permute-start | bytes 393224 | tf_op jit(solution)/shard_map/ppermute | solution.py:61
  454.7 8.2 %collective-permute-start.45 = (bf16[1,16,4096]{2,1,0:T(8,128)(2,1)}, bf16[1,16,4096]{2,1,0:T(8,128)(2,1)S(1)}, u32[]{:S(2)}, u32[]{:S(2)}) collective-permute-start(bf16[1,16,4096]{2,1,0:T(8,128)(2,1)} %get-tuple-element.255), channel_id=1, source_target_pairs={{0,16},{4,20},{8,24},{12,28},{16,0},{20,4},{24,8},{28,12},{1,17},{... | collective-permute-start | bytes 393224 | tf_op jit(solution)/shard_map/ppermute | solution.py:61
  456.5 4.7 collective-permute-start.41
  456.6 18.4 %all-to-all-start.9 = ((bf16[4,2,16,1792]{3,2,1,0:T(8,128)(2,1)}), bf16[4,2,16,1792]{3,2,1,0:T(8,128)(2,1)S(1)}, u32[]{:S(2)}, u32[]{:S(2)}) async-start(bf16[4,2,16,1792]{3,2,1,0:T(8,128)(2,1)} %shard_map.362), calls=%async_computation.9 | async-start | bytes 917504 | tf_op jit(solution)/shard_map/all_to_all | solution.py:69
  461.3 4.0 collective-permute-start.42
  465.4 4.1 collective-permute-start.43
  477.5 6.5 %collective-permute-start.49 = (bf16[1,16,4096]{2,1,0:T(8,128)(2,1)}, bf16[1,16,4096]{2,1,0:T(8,128)(2,1)S(1)}, u32[]{:S(2)}, u32[]{:S(2)}) collective-permute-start(bf16[1,16,4096]{2,1,0:T(8,128)(2,1)} %get-tuple-element.262), channel_id=1, source_target_pairs={{0,16},{4,20},{8,24},{12,28},{16,0},{20,4},{24,8},{28,12},{1,17},{... | collective-permute-start | bytes 393224 | tf_op jit(solution)/shard_map/ppermute | solution.py:61
  478.2 6.7 %collective-permute-start.48 = (bf16[1,16,4096]{2,1,0:T(8,128)(2,1)}, bf16[1,16,4096]{2,1,0:T(8,128)(2,1)S(1)}, u32[]{:S(2)}, u32[]{:S(2)}) collective-permute-start(bf16[1,16,4096]{2,1,0:T(8,128)(2,1)} %get-tuple-element.257), channel_id=1, source_target_pairs={{0,8},{4,12},{8,0},{12,4},{16,24},{20,28},{24,16},{28,20},{1,9},{5... | collective-permute-start | bytes 393224 | tf_op jit(solution)/shard_map/ppermute | solution.py:61
  479.7 8.8 %collective-permute-start.47 = (bf16[2,1,16,4096]{3,2,0,1:T(8,128)(2,1)S(1)}, bf16[2,1,16,4096]{3,2,0,1:T(8,128)(2,1)S(1)}, u32[]{:S(2)}, u32[]{:S(2)}) collective-permute-start(bf16[2,1,16,4096]{3,2,0,1:T(8,128)(2,1)S(1)} %pad_maximum_fusion.21), channel_id=1, source_target_pairs={{0,8},{4,12},{8,0},{12,4},{16,24},{20,28},{24,16},{28,20},{1,9},{5... | collective-permute-start | bytes 786440 | tf_op jit(solution)/shard_map/ppermute | solution.py:61
  480.2 8.4 %collective-permute-start.46 = (bf16[2,1,16,4096]{3,2,0,1:T(8,128)(2,1)S(1)}, bf16[2,1,16,4096]{3,2,0,1:T(8,128)(2,1)S(1)}, u32[]{:S(2)}, u32[]{:S(2)}) collective-permute-start(bf16[2,1,16,4096]{3,2,0,1:T(8,128)(2,1)S(1)} %pad_maximum_fusion.20), channel_id=1, source_target_pairs={{0,16},{4,20},{8,24},{12,28},{16,0},{20,4},{24,8},{28,12},{1,17},{... | collective-permute-start | bytes 786440 | tf_op jit(solution)/shard_map/ppermute | solution.py:61
  488.7 6.8 %collective-permute-start.53 = (bf16[2,1,16,4096]{3,2,0,1:T(8,128)(2,1)S(1)}, bf16[2,1,16,4096]{3,2,0,1:T(8,128)(2,1)S(1)}, u32[]{:S(2)}, u32[]{:S(2)}) collective-permute-start(bf16[2,1,16,4096]{3,2,0,1:T(8,128)(2,1)S(1)} %pad_maximum_fusion.23), channel_id=1, source_target_pairs={{0,8},{4,12},{8,0},{12,4},{16,24},{20,28},{24,16},{28,20},{1,9},{5... | collective-permute-start | bytes 786440 | tf_op jit(solution)/shard_map/ppermute | solution.py:61
  491.5 6.4 %collective-permute-start.52 = (bf16[2,1,16,4096]{3,2,0,1:T(8,128)(2,1)S(1)}, bf16[2,1,16,4096]{3,2,0,1:T(8,128)(2,1)S(1)}, u32[]{:S(2)}, u32[]{:S(2)}) collective-permute-start(bf16[2,1,16,4096]{3,2,0,1:T(8,128)(2,1)S(1)} %pad_maximum_fusion.22), channel_id=1, source_target_pairs={{0,16},{4,20},{8,24},{12,28},{16,0},{20,4},{24,8},{28,12},{1,17},{... | collective-permute-start | bytes 786440 | tf_op jit(solution)/shard_map/ppermute | solution.py:61
  492.8 5.2 %collective-permute-start.50 = (bf16[2,2,1,16,4096]{4,3,2,1,0:T(8,128)(2,1)S(1)}, bf16[2,2,1,16,4096]{4,3,2,1,0:T(8,128)(2,1)S(1)}, u32[]{:S(2)}, u32[]{:S(2)}) collective-permute-start(bf16[2,2,1,16,4096]{4,3,2,1,0:T(8,128)(2,1)S(1)} %pad_maximum_fusion.12.refs_0_), channel_id=1, source_target_pairs={{0,4},{4,0},{8,12},{12,8},{16,20},{20,16},{24,28},{28,24},{1,5},{5... | collective-permute-start | bytes 1572872 | tf_op jit(solution)/shard_map/ppermute | solution.py:61
  492.8 5.2 %collective-permute-start.51 = (bf16[2,2,1,16,4096]{4,3,2,1,0:T(8,128)(2,1)S(1)}, bf16[2,2,1,16,4096]{4,3,2,1,0:T(8,128)(2,1)S(1)}, u32[]{:S(2)}, u32[]{:S(2)}) collective-permute-start(bf16[2,2,1,16,4096]{4,3,2,1,0:T(8,128)(2,1)S(1)} %pad_maximum_fusion.13.refs_1_), channel_id=1, source_target_pairs={{0,4},{4,0},{8,12},{12,8},{16,20},{20,16},{24,28},{28,24},{1,5},{5... | collective-permute-start | bytes 1572872 | tf_op jit(solution)/shard_map/ppermute | solution.py:61
  (44 other events, 244.3 us)

commit v6 on v5

--- a/solution.py
+++ b/solution.py
@@ -788,7 +788,8 @@
     tall_piece = jnp.concatenate([piece(output_weight), piece(outer_weight)], 1)
     one, two = one_off(side_piece)
     far = two_off(side_piece)
-    order.tick(far)
+    copies = jnp.broadcast_to(start_low, (n, slots, width))
+    order.tick(far, copies)
     on = sent_on(order.release(far))
     tall_far = two_off(order.release(tall_piece))
     order.tick(one, two, on)
@@ -799,7 +800,7 @@
     on = sent_on(order.release(tall_far))
     side = gather_far(*side)
     order.tick(one, two, on)
-    row_low = exchange(jnp.broadcast_to(order.release(start_low), (n, slots, width)))
+    row_low = exchange(order.release(copies))
     row_low = row_low.reshape(n * slots, width)
     tall = by_distance(tall_far, one, two, on)
     tall = gather_near(tall[:, 0], tall[:, 1])

time: 521 us -> 522 us (level)
  transfers between devices with their start and end apart: 66 -> 66, of which waited for: 30 -> 29; matrix products, arithmetic and copies ran while one was open for 9% -> 9% of each run, Pallas kernels for 27% -> 27%
where the time goes in v6:
time: 522 us; the launch traced here: 512 us
  Pallas kernels  197 us (38%)
  waiting for transfers between devices  154 us (30%)
  starting transfers between devices  98.9 us (19%)
  other arithmetic  33.2 us (6%)
  local copies, waits for them, and re-layouts  24.1 us (5%)
    pallas_call x27, Pallas kernels, call(): outs = pl.pallas_call(body, **kwargs)(self.ids, *args)  197 us
    ppermute x48, waiting for transfers between devices, swap(): return lax.ppermute(value, 'dp', [(i, i ^ mask) for i in range(size)])  85.8 us
    all_to_all x10, starting transfers between devices, exchange(): return lax.all_to_all(value, axis, 0, 0)  41.2 us
    all_to_all x10, waiting for transfers between devices, exchange(): return lax.all_to_all(value, axis, 0, 0)  41 us
    ppermute x48, starting transfers between devices, swap(): return lax.ppermute(value, 'dp', [(i, i ^ mask) for i in range(size)])  37.9 us
    ppermute x8, waiting for transfers between devices, along(): return lax.ppermute(value, 'ctx', pairs)  27.5 us
    ppermute x8, starting transfers between devices, along(): return lax.ppermute(value, 'ctx', pairs)  19.8 us
    another operation x14, other arithmetic, gather_far(): return (jnp.stack([one, swap(one, 4)]), jnp.stack([two, swap(two, 2)]))  19.2 us
  transfers between devices with their start and end apart: 66, of which 29 were waited for; matrix products, arithmetic and copies ran while one was open for 9% of the time, Pallas kernels for 27%

profile of v6, /device:TPU:0, one launch (start us, length us, event | category | flops | bytes accessed | tf_op | source)
XLA Modules:
  0.0 512.3 jit_solution(1450798789062325847)
XLA Ops:
  3.6 4.1 collective-permute-start
  7.7 3.5 collective-permute-start.1
  18.5 10.4 %collective-permute-done = bf16[2,16,7168]{2,1,0:T(8,128)(2,1)S(1)} collective-permute-done((bf16[2,16,7168]{2,1,0:T(8,128)(2,1)S(1)}, bf16[2,16,7168]{2,1,0:T(8,128)(2,1)S(1)}, u32[]{:S(2)}, u32[]{:S(2)}) %collective-permute-start) | collective-permute-done | bytes 458784 | tf_op jit(solution)/shard_map/ppermute | solution.py:65
  28.9 2.1 broadcast_in_dim.49
  33.4 10.3 %collective-permute-done.3 = bf16[2,16,7168]{2,1,0:T(8,128)(2,1)S(1)} collective-permute-done((bf16[2,16,7168]{2,1,0:T(8,128)(2,1)S(1)}, bf16[2,16,7168]{2,1,0:T(8,128)(2,1)S(1)}, u32[]{:S(2)}, u32[]{:S(2)}) %collective-permute-start.3) | collective-permute-done | bytes 458784 | tf_op jit(solution)/shard_map/ppermute | solution.py:65
  46.6 2.7 collective-permute-start.4
  49.3 4.4 collective-permute-start.7
  56.5 2.7 collective-permute-done.6
  61.6 11.8 %collective-permute-done.5 = bf16[3,16,7168]{2,1,0:T(8,128)(2,1)S(1)} collective-permute-done((bf16[3,16,7168]{2,1,0:T(8,128)(2,1)S(1)}, bf16[3,16,7168]{2,1,0:T(8,128)(2,1)S(1)}, u32[]{:S(2)}, u32[]{:S(2)}) %collective-permute-start.5) | collective-permute-done | bytes 688160 | tf_op jit(solution)/shard_map/ppermute | solution.py:61
  78.4 5.6 %collective-permute-done.9 = bf16[2,80,1024]{2,1,0:T(8,128)(2,1)S(1)} collective-permute-done((bf16[2,80,1024]{2,1,0:T(8,128)(2,1)S(1)}, bf16[2,80,1024]{2,1,0:T(8,128)(2,1)S(1)}, u32[]{:S(2)}, u32[]{:S(2)}) %collective-permute-start.9) | collective-permute-done | bytes 327712 | tf_op jit(solution)/shard_map/ppermute | solution.py:65
  84.1 3.7 all-to-all-start
  87.8 12.4 %collective-permute-done.11 = bf16[2,3,16,7168]{3,2,1,0:T(8,128)(2,1)} collective-permute-done((bf16[2,3,16,7168]{3,2,1,0:T(8,128)(2,1)}, bf16[2,3,16,7168]{3,2,1,0:T(8,128)(2,1)}, u32[]{:S(2)}, u32[]{:S(2)}) %collective-permute-start.11) | collective-permute-done | bytes 1376288 | tf_op jit(solution)/shard_map/ppermute | solution.py:61
  100.2 3.6 pad_maximum_fusion.1.refs_5_.refs_10_.refs_9_.refs_7_
  103.9 3.2 pad_maximum_fusion.refs_4_.refs_9_.refs_8_.refs_6_
  110.5 11.6 %collective-permute-done.13 = bf16[3,80,1024]{2,1,0:T(8,128)(2,1)S(1)} collective-permute-done((bf16[3,80,1024]{2,1,0:T(8,128)(2,1)S(1)}, bf16[3,80,1024]{2,1,0:T(8,128)(2,1)S(1)}, u32[]{:S(2)}, u32[]{:S(2)}) %collective-permute-start.13) | collective-permute-done | bytes 491552 | tf_op jit(solution)/shard_map/ppermute | solution.py:61
  131.5 15.7 %collective-permute-done.17 = bf16[2,3,80,1024]{3,2,1,0:T(8,128)(2,1)} collective-permute-done((bf16[2,3,80,1024]{3,2,1,0:T(8,128)(2,1)}, bf16[2,3,80,1024]{3,2,1,0:T(8,128)(2,1)}, u32[]{:S(2)}, u32[]{:S(2)}) %collective-permute-start.17) | collective-permute-done | bytes 983072 | tf_op jit(solution)/shard_map/ppermute | solution.py:61
  147.3 3.2 pad_maximum_fusion.3.refs_14_.refs_4_.refs_13_
  150.5 2.6 pad_maximum_fusion.2.refs_13_.refs_3_.refs_12_
  155.3 7.9 %shard_map.340.q_ref.k_ref.v_ref = bf16[1280,768]{1,0:T(8,128)(2,1)} custom-call(s32[15]{0:T(128)} %stack.307.ids, bf16[1536,1024]{1,0:T(8,128)(2,1)} %bitcast.166, bf16[256,1024]{1,0:T(8,128)(2,1)} %refs_3_.3, bf16[256,1024]{1,0:T(8,128)(2,1)} %refs_4_.3, bf16[256,1024]{1,0:T(8,128)(2,1)} %refs_5_.3, ...), custom_call_target="tpu_custom_call" | custom-call | flops 128000000000 | bytes 384000000 | tf_op jit(solution)/shard_map/pallas_call | solution.py:103
  163.2 10.7 %shard_map.341 = (bf16[4,384,128]{2,1,0:T(8,128)(2,1)}, f32[8,1536]{1,0:T(8,128)}) custom-call(s32[15]{0:T(128)} %stack.307.ids, f32[1,1280]{1,0:T(1,128)} %broadcast_in_dim.56.bias_ref, bf16[1280,768]{1,0:T(8,128)(2,1)} %shard_map.340.q_ref.k_ref.v_ref, bf16[1280,768]{1,0:T(8,128)(2,1)} %shard_map.340.q_ref.k_ref.v_ref, ...), custom_call_target="tpu_custom_call" | custom-call | flops 176000008192 | bytes 528000000 | tf_op jit(solution)/shard_map/pallas_call | solution.py:103
  173.9 4.6 all-to-all-start.1
  178.5 10.7 %shard_map.342 = (bf16[4,384,128]{2,1,0:T(8,128)(2,1)}, f32[8,1536]{1,0:T(8,128)}) custom-call(s32[15]{0:T(128)} %stack.307.ids, f32[1,1280]{1,0:T(1,128)} %broadcast_in_dim.56.bias_ref, bf16[1280,768]{1,0:T(8,128)(2,1)} %shard_map.340.q_ref.k_ref.v_ref, bf16[1280,768]{1,0:T(8,128)(2,1)} %shard_map.340.q_ref.k_ref.v_ref, ...), custom_call_target="tpu_custom_call" | custom-call | flops 176000008192 | bytes 528000000 | tf_op jit(solution)/shard_map/pallas_call | solution.py:103
  190.7 3.6 all-to-all-start.2
  194.3 11.6 %all-to-all-done.2.refs_1_ = bf16[4,384,128]{2,1,0:T(8,128)(2,1)S(1)} async-done(((bf16[4,384,128]{2,1,0:T(8,128)(2,1)}), bf16[4,384,128]{2,1,0:T(8,128)(2,1)S(1)}, u32[]{:S(2)}, u32[]{:S(2)}) %all-to-all-start.2) | async-done | bytes 393248 | tf_op jit(solution)/shard_map/all_to_all | solution.py:69
  206.6 23.4 %shard_map.343 = (bf16[384,1024]{1,0:T(8,128)(2,1)}, f32[384,1024]{1,0:T(8,128)}, bf16[384,1024]{1,0:T(8,128)(2,1)}, bf16[384,4096]{1,0:T(8,128)(2,1)}, bf16[384...) custom-call(s32[15]{0:T(128)} %stack.307.ids, ...), custom_call_target="tpu_custom_call" | custom-call | flops 384000000000 | bytes 1152000000 | tf_op jit(solution)/shard_map/pallas_call | solution.py:103
  230.1 6.6 %shard_map.344 = bf16[4,512,1024]{2,1,0:T(8,128)(2,1)} custom-call(s32[15]{0:T(128)} %stack.307.ids, bf16[384,4096]{1,0:T(8,128)(2,1)} %get-tuple-element.176.refs_0_, bf16[384,1024]{1,0:T(8,128)(2,1)} %get-tuple-element.177.refs_1_.refs_0_), custom_call_target="tpu_custom_call" | custom-call | tf_op jit(solution)/shard_map/pallas_call | solution.py:103
  236.6 11.3 %shard_map.345 = (bf16[384,4096]{1,0:T(8,128)(2,1)}, f32[1,4096]{1,0:T(1,128)}) custom-call(s32[15]{0:T(128)} %stack.307.ids, bf16[384,1024]{1,0:T(8,128)(2,1)} %get-tuple-element.177.refs_1_.refs_0_, bf16[384,4096]{1,0:T(8,128)(2,1)} %get-tuple-element.179.refs_1_, bf16[1024,1024]{1,0:T(8,128)(2,1)} %refs_2_.3, ...), custom_call_target="tpu_custom_call" | custom-call | flops 192000000000 | bytes 576000000 | tf_op jit(solution)/shard_map/pallas_call | solution.py:103
  248.0 7.3 %shard_map.346 = (bf16[4,128,1024]{2,1,0:T(8,128)(2,1)}, bf16[4,128,1024]{2,1,0:T(8,128)(2,1)}, bf16[4,128,1024]{2,1,0:T(8,128)(2,1)}, bf16[4,128,1024]{2,1,0:T(8,128)(2,1)}) custom-call(s32[15]{0:T(128)} %stack.307.ids, bf16[384,4096]{1,0:T(8,128)(2,1)} %get-tuple-element.176.refs_0_, bf16[384,1024]{1,0:T(8,128)(2,1)} %get-tuple-element.177.refs_1_.refs_0_, ...), custom_call_target="tpu_custom_call" | custom-call | tf_op jit(solution)/shard_map/pallas_call | solution.py:103
  256.7 7.1 %shard_map.347 = bf16[4,128,4096]{2,1,0:T(8,128)(2,1)} custom-call(s32[15]{0:T(128)} %stack.307.ids, bf16[384,1024]{1,0:T(8,128)(2,1)} %get-tuple-element.184.refs_0_, bf16[384,4096]{1,0:T(8,128)(2,1)} %get-tuple-element.180.refs_1_.refs_0_), custom_call_target="tpu_custom_call" | custom-call | tf_op jit(solution)/shard_map/pallas_call | solution.py:103
  264.5 13.2 %shard_map.348 = (f32[384,1024]{1,0:T(8,128)}, bf16[384,1024]{1,0:T(8,128)(2,1)}, bf16[4,384,256]{2,1,0:T(8,128)(2,1)}, f32[4,16,256]{2,1,0:T(8,128)}) custom-call(s32[15]{0:T(128)} %stack.307.ids, bf16[384,4096]{1,0:T(8,128)(2,1)} %get-tuple-element.180.refs_1_.refs_0_, f32[1,4096]{1,0:T(1,128)} %get-tuple-element.186.refs_1_, ...), custom_call_target="tpu_custom_call" | custom-call | flops 207999991808 | bytes 624000000 | tf_op jit(solution)/shard_map/pallas_call | solution.py:103
  277.8 3.7 all-to-all-start.3
  281.5 8.2 %collective-permute-done.22.got_two = bf16[4,128,1024]{2,1,0:T(8,128)(2,1)} collective-permute-done((bf16[4,128,1024]{2,1,0:T(8,128)(2,1)}, bf16[4,128,1024]{2,1,0:T(8,128)(2,1)}, u32[]{:S(2)}, u32[]{:S(2)}) %collective-permute-start.22) | collective-permute-done | bytes 1048608 | tf_op jit(solution)/shard_map/ppermute | solution.py:61
  289.7 3.9 shard_map.349
  294.6 7.9 %shard_map.350 = (bf16[4,32,4096]{2,1,0:T(8,128)(2,1)}, bf16[4,32,4096]{2,1,0:T(8,128)(2,1)}, bf16[4,32,4096]{2,1,0:T(8,128)(2,1)}, bf16[4,32,4096]{2,1,0:T(8,128)(2,1)}) custom-call(s32[15]{0:T(128)} %stack.307.ids, bf16[384,1024]{1,0:T(8,128)(2,1)} %get-tuple-element.184.refs_0_, bf16[384,4096]{1,0:T(8,128)(2,1)} %get-tuple-element.180.refs_1_.refs_0_, ...), custom_call_target="tpu_custom_call" | custom-call | tf_op jit(solution)/shard_map/pallas_call | solution.py:103
  302.6 4.5 collective-permute-done.24.got_one
  308.1 2.7 shard_map.351
  310.9 4.3 all-to-all-start.4
  317.2 15.3 %shard_map.352 = bf16[4,384,384]{2,1,0:T(8,128)(2,1)} custom-call(s32[15]{0:T(128)} %stack.307.ids, f32[1280,128]{1,0:T(8,128)} %broadcast_in_dim.57.bias_ref, bf16[1280,768]{1,0:T(8,128)(2,1)} %shard_map.340.q_ref.k_ref.v_ref, bf16[1280,768]{1,0:T(8,128)(2,1)} %shard_map.340.q_ref.k_ref.v_ref, bf16[1280,768]{1,0:T(8,128)(2,1)} %shard_map.340.q_ref.k_ref.v_ref, ...), custom_call_target="tpu_custom_call" | custom-call | flops 256000000000 | bytes 768000000 | tf_op jit(solution)/shard_map/pallas_call | solution.py:103
  332.5 7.3 %all-to-all-done.4.refs_0_ = bf16[4,2,64,1024]{3,2,1,0:T(8,128)(2,1)} async-done(((bf16[4,2,64,1024]{3,2,1,0:T(8,128)(2,1)}), bf16[4,2,64,1024]{3,2,1,0:T(8,128)(2,1)}, u32[]{:S(2)}, u32[]{:S(2)}) %all-to-all-start.4) | async-done | bytes 1048608 | tf_op jit(solution)/shard_map/all_to_all | solution.py:69
  339.9 4.5 all-to-all-start.5
  346.9 3.9 shard_map.354
  354.3 15.5 %shard_map.355 = bf16[4,384,384]{2,1,0:T(8,128)(2,1)} custom-call(s32[15]{0:T(128)} %stack.307.ids, f32[1280,128]{1,0:T(8,128)} %broadcast_in_dim.57.bias_ref, bf16[1280,768]{1,0:T(8,128)(2,1)} %shard_map.340.q_ref.k_ref.v_ref, bf16[1280,768]{1,0:T(8,128)(2,1)} %shard_map.340.q_ref.k_ref.v_ref, bf16[1280,768]{1,0:T(8,128)(2,1)} %shard_map.340.q_ref.k_ref.v_ref, ...), custom_call_target="tpu_custom_call" | custom-call | flops 256000000000 | bytes 768000000 | tf_op jit(solution)/shard_map/pallas_call | solution.py:103
  372.4 7.5 %shard_map.356 = bf16[4,128,1792]{2,1,0:T(8,128)(2,1)} custom-call(s32[15]{0:T(128)} %stack.307.ids, bf16[1536,1024]{1,0:T(8,128)(2,1)} %bitcast.167, bf16[1536,384]{1,0:T(8,128)(2,1)} %bitcast.171, bf16[1536,1024]{1,0:T(8,128)(2,1)} %bitcast.168, bf16[1536,384]{1,0:T(8,128)(2,1)} %bitcast.68.refs_3_, bf16[384,1024]{1,0:T(8,128)(2,1)} %get-tuple-element.174.refs_4_, ...), custom_call_target="tpu_custom_call" | custom-call | tf_op jit(solution)/shard_map/pallas_call | solution.py:103
  379.9 4.4 all-to-all-start.6
  386.2 2.7 shard_map.357
  388.9 3.9 collective-permute-done.33
  393.7 7.8 %shard_map.358 = (bf16[4,32,1792]{2,1,0:T(8,128)(2,1)}, bf16[4,32,1792]{2,1,0:T(8,128)(2,1)}, bf16[4,32,1792]{2,1,0:T(8,128)(2,1)}, bf16[4,32,1792]{2,1,0:T(8,128)(2,1)}) custom-call(s32[15]{0:T(128)} %stack.307.ids, bf16[1536,1024]{1,0:T(8,128)(2,1)} %bitcast.169, bf16[1536,384]{1,0:T(8,128)(2,1)} %bitcast.172, bf16[1536,1024]{1,0:T(8,128)(2,1)} %bitcast.170, ...), custom_call_target="tpu_custom_call" | custom-call | tf_op jit(solution)/shard_map/pallas_call | solution.py:103
  406.3 7.2 %all-to-all-done.6.refs_1_ = bf16[4,384,384]{2,1,0:T(8,128)(2,1)S(1)} async-done(((bf16[4,384,384]{2,1,0:T(8,128)(2,1)}), bf16[4,384,384]{2,1,0:T(8,128)(2,1)S(1)}, u32[]{:S(2)}, u32[]{:S(2)}) %all-to-all-start.6) | async-done | bytes 1179680 | tf_op jit(solution)/shard_map/all_to_all | solution.py:69
  413.6 4.2 shard_map.359
  417.8 4.5 all-to-all-start.7
  422.4 2.5 shard_map.360
  426.7 8.9 %shard_map.361 = (f32[384,1024]{1,0:T(8,128)}, f32[1,1024]{1,0:T(1,128)}) custom-call(s32[15]{0:T(128)} %stack.307.ids, bf16[4,384,384]{2,1,0:T(8,128)(2,1)} %all-to-all-done.5.refs_0_, bf16[4,384,384]{2,1,0:T(8,128)(2,1)} %copy-done.11, f32[384,1024]{1,0:T(8,128)} %get-tuple-element.190.refs_2_, bf16[256,1024]{1,0:T(8,128)(2,1)} %refs_3_.3, ...), custom_call_target="tpu_custom_call" | custom-call | flops 143999991808 | bytes 432000000 | tf_op jit(solution)/shard_map/pallas_call | solution.py:103
  438.9 2.2 shard_map.362
  441.1 6.8 %all-to-all-done.7.refs_0_ = bf16[4,2,16,4096]{3,2,1,0:T(8,128)(2,1)} async-done(((bf16[4,2,16,4096]{3,2,1,0:T(8,128)(2,1)}), bf16[4,2,16,4096]{3,2,1,0:T(8,128)(2,1)}, u32[]{:S(2)}, u32[]{:S(2)}) %all-to-all-start.7) | async-done | bytes 1048608 | tf_op jit(solution)/shard_map/all_to_all | solution.py:69
  448.0 3.3 all-to-all-start.8
  457.2 4.7 all-to-all-start.9
  466.9 3.3 collective-permute-done.43
  470.2 5.5 %all-to-all-done.9.refs_0_ = bf16[4,2,16,1792]{3,2,1,0:T(8,128)(2,1)S(1)} async-done(((bf16[4,2,16,1792]{3,2,1,0:T(8,128)(2,1)}), bf16[4,2,16,1792]{3,2,1,0:T(8,128)(2,1)S(1)}, u32[]{:S(2)}, u32[]{:S(2)}) %all-to-all-start.9) | async-done | bytes 458784 | tf_op jit(solution)/shard_map/all_to_all | solution.py:69
  482.2 2.4 collective-permute-done.49
  486.5 2.7 collective-permute-done.47
  493.9 2.2 collective-permute-done.53
  496.2 2.4 collective-permute-done.52
  500.3 3.8 shard_map.365
  508.2 3.8 shard_map.366
  (279 shorter events, 98.5 us)
Async XLA Ops:
  3.6 25.3 %collective-permute-start = (bf16[2,16,7168]{2,1,0:T(8,128)(2,1)S(1)}, bf16[2,16,7168]{2,1,0:T(8,128)(2,1)S(1)}, u32[]{:S(2)}, u32[]{:S(2)}) collective-permute-start(bf16[2,16,7168]{2,1,0:T(8,128)(2,1)S(1)} %pad_maximum_fusion.16), channel_id=1, source_target_pairs={{0,2},{1,3},{2,0},{3,1},{4,6},{5,7},{6,4},{7,5},{8,10},{9,11},{10,... | collective-permute-start | bytes 1376264 | tf_op jit(solution)/shard_map/ppermute | solution.py:65
  7.7 24.6 %collective-permute-start.1 = (bf16[2,16,7168]{2,1,0:T(8,128)(2,1)S(1)}, bf16[2,16,7168]{2,1,0:T(8,128)(2,1)S(1)}, u32[]{:S(2)}, u32[]{:S(2)}) collective-permute-start(bf16[2,16,7168]{2,1,0:T(8,128)(2,1)S(1)} %pad_maximum_fusion.16), channel_id=1, source_target_pairs={{0,1},{1,2},{2,3},{4,5},{5,6},{6,7},{8,9},{9,10},{10,11},{12,13},{... | collective-permute-start | bytes 1376264 | tf_op jit(solution)/shard_map/ppermute | solution.py:65
  11.2 22.3 %collective-permute-start.2 = (bf16[2,16,7168]{2,1,0:T(8,128)(2,1)S(1)}, bf16[2,16,7168]{2,1,0:T(8,128)(2,1)S(1)}, u32[]{:S(2)}, u32[]{:S(2)}) collective-permute-start(bf16[2,16,7168]{2,1,0:T(8,128)(2,1)S(1)} %pad_maximum_fusion.16), channel_id=1, source_target_pairs={{1,0},{2,1},{3,2},{5,4},{6,5},{7,6},{9,8},{10,9},{11,10},{13,12},{... | collective-permute-start | bytes 1376264 | tf_op jit(solution)/shard_map/ppermute | solution.py:65
  30.9 12.8 %collective-permute-start.3 = (bf16[2,16,7168]{2,1,0:T(8,128)(2,1)S(1)}, bf16[2,16,7168]{2,1,0:T(8,128)(2,1)S(1)}, u32[]{:S(2)}, u32[]{:S(2)}) collective-permute-start(bf16[2,16,7168]{2,1,0:T(8,128)(2,1)S(1)} %collective-permute-done), channel_id=1, source_target_pairs={{2,3},{1,0},{6,7},{5,4},{10,11},{9,8},{14,15},{13,12},{18,19},{17,... | collective-permute-start | bytes 1376264 | tf_op jit(solution)/shard_map/ppermute | solution.py:65
  44.3 14.9 %collective-permute-start.6 = (bf16[3,16,7168]{2,1,0:T(8,128)(2,1)S(1)}, bf16[3,16,7168]{2,1,0:T(8,128)(2,1)S(1)}, u32[]{:S(2)}, u32[]{:S(2)}) collective-permute-start(bf16[3,16,7168]{2,1,0:T(8,128)(2,1)S(1)} %get-tuple-element.282), channel_id=1, source_target_pairs={{0,16},{4,20},{8,24},{12,28},{16,0},{20,4},{24,8},{28,12},{1,17},{... | collective-permute-start | bytes 2064392 | tf_op jit(solution)/shard_map/ppermute | solution.py:61
  46.6 28.5 %collective-permute-start.4 = (bf16[2,80,1024]{2,1,0:T(8,128)(2,1)S(1)}, bf16[2,80,1024]{2,1,0:T(8,128)(2,1)S(1)}, u32[]{:S(2)}, u32[]{:S(2)}) collective-permute-start(bf16[2,80,1024]{2,1,0:T(8,128)(2,1)S(1)} %pad_maximum_fusion.17), channel_id=1, source_target_pairs={{0,2},{1,3},{2,0},{3,1},{4,6},{5,7},{6,4},{7,5},{8,10},{9,11},{10,... | collective-permute-start | bytes 983048 | tf_op jit(solution)/shard_map/ppermute | solution.py:65
  49.3 27.7 %collective-permute-start.7 = (bf16[2,80,1024]{2,1,0:T(8,128)(2,1)S(1)}, bf16[2,80,1024]{2,1,0:T(8,128)(2,1)S(1)}, u32[]{:S(2)}, u32[]{:S(2)}) collective-permute-start(bf16[2,80,1024]{2,1,0:T(8,128)(2,1)S(1)} %pad_maximum_fusion.17), channel_id=1, source_target_pairs={{0,1},{1,2},{2,3},{4,5},{5,6},{6,7},{8,9},{9,10},{10,11},{12,13},{... | collective-permute-start | bytes 983048 | tf_op jit(solution)/shard_map/ppermute | solution.py:65
  53.7 23.3 %collective-permute-start.8 = (bf16[2,80,1024]{2,1,0:T(8,128)(2,1)S(1)}, bf16[2,80,1024]{2,1,0:T(8,128)(2,1)S(1)}, u32[]{:S(2)}, u32[]{:S(2)}) collective-permute-start(bf16[2,80,1024]{2,1,0:T(8,128)(2,1)S(1)} %pad_maximum_fusion.17), channel_id=1, source_target_pairs={{1,0},{2,1},{3,2},{5,4},{6,5},{7,6},{9,8},{10,9},{11,10},{13,12},{... | collective-permute-start | bytes 983048 | tf_op jit(solution)/shard_map/ppermute | solution.py:65
  55.0 18.4 %collective-permute-start.5 = (bf16[3,16,7168]{2,1,0:T(8,128)(2,1)S(1)}, bf16[3,16,7168]{2,1,0:T(8,128)(2,1)S(1)}, u32[]{:S(2)}, u32[]{:S(2)}) collective-permute-start(bf16[3,16,7168]{2,1,0:T(8,128)(2,1)S(1)} %get-tuple-element.281), channel_id=1, source_target_pairs={{0,8},{4,12},{8,0},{12,4},{16,24},{20,28},{24,16},{28,20},{1,9},{5... | collective-permute-start | bytes 2064392 | tf_op jit(solution)/shard_map/ppermute | solution.py:61
  61.0 39.2 %collective-permute-start.11 = (bf16[2,3,16,7168]{3,2,1,0:T(8,128)(2,1)}, bf16[2,3,16,7168]{3,2,1,0:T(8,128)(2,1)}, u32[]{:S(2)}, u32[]{:S(2)}) collective-permute-start(bf16[2,3,16,7168]{3,2,1,0:T(8,128)(2,1)} %get-tuple-element.277), channel_id=1, source_target_pairs={{0,8},{4,12},{8,0},{12,4},{16,24},{20,28},{24,16},{28,20},{1,9},{5... | collective-permute-start | bytes 4128776 | tf_op jit(solution)/shard_map/ppermute | solution.py:61
  75.1 9.0 %collective-permute-start.9 = (bf16[2,80,1024]{2,1,0:T(8,128)(2,1)S(1)}, bf16[2,80,1024]{2,1,0:T(8,128)(2,1)S(1)}, u32[]{:S(2)}, u32[]{:S(2)}) collective-permute-start(bf16[2,80,1024]{2,1,0:T(8,128)(2,1)S(1)} %collective-permute-done.4), channel_id=1, source_target_pairs={{2,3},{1,0},{6,7},{5,4},{10,11},{9,8},{14,15},{13,12},{18,19},{17,... | collective-permute-start | bytes 983048 | tf_op jit(solution)/shard_map/ppermute | solution.py:65
  76.4 27.4 %collective-permute-start.10 = (bf16[2,3,16,7168]{3,2,1,0:T(8,128)(2,1)}, bf16[2,3,16,7168]{3,2,1,0:T(8,128)(2,1)}, u32[]{:S(2)}, u32[]{:S(2)}) collective-permute-start(bf16[2,3,16,7168]{3,2,1,0:T(8,128)(2,1)} %get-tuple-element.279), channel_id=1, source_target_pairs={{0,16},{4,20},{8,24},{12,28},{16,0},{20,4},{24,8},{28,12},{1,17},{... | collective-permute-start | bytes 4128776 | tf_op jit(solution)/shard_map/ppermute | solution.py:61
  84.1 69.5 %all-to-all-start = ((bf16[4,384,1024]{2,1,0:T(8,128)(2,1)}), bf16[4,384,1024]{2,1,0:T(8,128)(2,1)S(1)}, u32[]{:S(2)}, u32[]{:S(2)}) async-start(bf16[4,384,1024]{2,1,0:T(8,128)(2,1)} %broadcast_in_dim.49), calls=%async_computation | async-start | bytes 6291456 | tf_op jit(solution)/shard_map/all_to_all | solution.py:69
  103.8 49.8 %collective-permute-start.15 = (bf16[2,2,3,16,7168]{4,3,2,1,0:T(8,128)(2,1)}, bf16[2,2,3,16,7168]{4,3,2,1,0:T(8,128)(2,1)}, u32[]{:S(2)}, u32[]{:S(2)}) collective-permute-start(bf16[2,2,3,16,7168]{4,3,2,1,0:T(8,128)(2,1)} %pad_maximum_fusion.1.refs_5_.refs_10_.refs_9_.refs_7_), channel_id=1, source_target_pairs={{0,4},{4,0},{8,12},{12,8},{16,20},{20,16},{24,28},{28,24},{1,5},{5... | collective-permute-start | bytes 8257544 | tf_op jit(solution)/shard_map/ppermute | solution.py:61
  107.1 46.5 %collective-permute-start.14 = (bf16[2,2,3,16,7168]{4,3,2,1,0:T(8,128)(2,1)}, bf16[2,2,3,16,7168]{4,3,2,1,0:T(8,128)(2,1)}, u32[]{:S(2)}, u32[]{:S(2)}) collective-permute-start(bf16[2,2,3,16,7168]{4,3,2,1,0:T(8,128)(2,1)} %pad_maximum_fusion.refs_4_.refs_9_.refs_8_.refs_6_), channel_id=1, source_target_pairs={{0,4},{4,0},{8,12},{12,8},{16,20},{20,16},{24,28},{28,24},{1,5},{5... | collective-permute-start | bytes 8257544 | tf_op jit(solution)/shard_map/ppermute | solution.py:61
  108.4 13.7 %collective-permute-start.13 = (bf16[3,80,1024]{2,1,0:T(8,128)(2,1)S(1)}, bf16[3,80,1024]{2,1,0:T(8,128)(2,1)S(1)}, u32[]{:S(2)}, u32[]{:S(2)}) collective-permute-start(bf16[3,80,1024]{2,1,0:T(8,128)(2,1)S(1)} %get-tuple-element.290), channel_id=1, source_target_pairs={{0,16},{4,20},{8,24},{12,28},{16,0},{20,4},{24,8},{28,12},{1,17},{... | collective-permute-start | bytes 1474568 | tf_op jit(solution)/shard_map/ppermute | solution.py:61
  109.0 16.1 %collective-permute-start.12 = (bf16[3,80,1024]{2,1,0:T(8,128)(2,1)S(1)}, bf16[3,80,1024]{2,1,0:T(8,128)(2,1)S(1)}, u32[]{:S(2)}, u32[]{:S(2)}) collective-permute-start(bf16[3,80,1024]{2,1,0:T(8,128)(2,1)S(1)} %get-tuple-element.289), channel_id=1, source_target_pairs={{0,8},{4,12},{8,0},{12,4},{16,24},{20,28},{24,16},{28,20},{1,9},{5... | collective-permute-start | bytes 1474568 | tf_op jit(solution)/shard_map/ppermute | solution.py:61
  123.5 23.8 %collective-permute-start.17 = (bf16[2,3,80,1024]{3,2,1,0:T(8,128)(2,1)}, bf16[2,3,80,1024]{3,2,1,0:T(8,128)(2,1)}, u32[]{:S(2)}, u32[]{:S(2)}) collective-permute-start(bf16[2,3,80,1024]{3,2,1,0:T(8,128)(2,1)} %get-tuple-element.285), channel_id=1, source_target_pairs={{0,8},{4,12},{8,0},{12,4},{16,24},{20,28},{24,16},{28,20},{1,9},{5... | collective-permute-start | bytes 2949128 | tf_op jit(solution)/shard_map/ppermute | solution.py:61
  126.5 24.0 %collective-permute-start.16 = (bf16[2,3,80,1024]{3,2,1,0:T(8,128)(2,1)}, bf16[2,3,80,1024]{3,2,1,0:T(8,128)(2,1)}, u32[]{:S(2)}, u32[]{:S(2)}) collective-permute-start(bf16[2,3,80,1024]{3,2,1,0:T(8,128)(2,1)} %get-tuple-element.287), channel_id=1, source_target_pairs={{0,16},{4,20},{8,24},{12,28},{16,0},{20,4},{24,8},{28,12},{1,17},{... | collective-permute-start | bytes 2949128 | tf_op jit(solution)/shard_map/ppermute | solution.py:61
  150.4 43.9 %collective-permute-start.19 = (bf16[2,2,3,80,1024]{4,3,2,1,0:T(8,128)(2,1)}, bf16[2,2,3,80,1024]{4,3,2,1,0:T(8,128)(2,1)}, u32[]{:S(2)}, u32[]{:S(2)}) collective-permute-start(bf16[2,2,3,80,1024]{4,3,2,1,0:T(8,128)(2,1)} %pad_maximum_fusion.3.refs_14_.refs_4_.refs_13_), channel_id=1, source_target_pairs={{0,4},{4,0},{8,12},{12,8},{16,20},{20,16},{24,28},{28,24},{1,5},{5... | collective-permute-start | bytes 5898248 | tf_op jit(solution)/shard_map/ppermute | solution.py:61
  153.1 41.2 %collective-permute-start.18 = (bf16[2,2,3,80,1024]{4,3,2,1,0:T(8,128)(2,1)}, bf16[2,2,3,80,1024]{4,3,2,1,0:T(8,128)(2,1)}, u32[]{:S(2)}, u32[]{:S(2)}) collective-permute-start(bf16[2,2,3,80,1024]{4,3,2,1,0:T(8,128)(2,1)} %pad_maximum_fusion.2.refs_13_.refs_3_.refs_12_), channel_id=1, source_target_pairs={{0,4},{4,0},{8,12},{12,8},{16,20},{20,16},{24,28},{28,24},{1,5},{5... | collective-permute-start | bytes 5898248 | tf_op jit(solution)/shard_map/ppermute | solution.py:61
  173.9 16.8 %all-to-all-start.1 = ((bf16[4,384,128]{2,1,0:T(8,128)(2,1)}), bf16[4,384,128]{2,1,0:T(8,128)(2,1)}, u32[]{:S(2)}, u32[]{:S(2)}) async-start(bf16[4,384,128]{2,1,0:T(8,128)(2,1)} %get-tuple-element.166), calls=%async_computation.1 | async-start | bytes 786432 | tf_op jit(solution)/shard_map/all_to_all | solution.py:69
  190.7 15.2 %all-to-all-start.2 = ((bf16[4,384,128]{2,1,0:T(8,128)(2,1)}), bf16[4,384,128]{2,1,0:T(8,128)(2,1)S(1)}, u32[]{:S(2)}, u32[]{:S(2)}) async-start(bf16[4,384,128]{2,1,0:T(8,128)(2,1)} %get-tuple-element.172), calls=%async_computation.2 | async-start | bytes 786432 | tf_op jit(solution)/shard_map/all_to_all | solution.py:69
  236.6 11.3 %collective-permute-start.20 = (bf16[4,512,1024]{2,1,0:T(8,128)(2,1)}, bf16[4,512,1024]{2,1,0:T(8,128)(2,1)}, u32[]{:S(2)}, u32[]{:S(2)}) collective-permute-start(bf16[4,512,1024]{2,1,0:T(8,128)(2,1)} %shard_map.344), channel_id=1, source_target_pairs={{0,4},{4,0},{8,12},{12,8},{16,20},{20,16},{24,28},{28,24},{1,5},{5... | collective-permute-start | bytes 12582920 | tf_op jit(solution)/shard_map/ppermute | solution.py:61
  255.2 26.2 %collective-permute-start.21 = (bf16[4,128,1024]{2,1,0:T(8,128)(2,1)}, bf16[4,128,1024]{2,1,0:T(8,128)(2,1)}, u32[]{:S(2)}, u32[]{:S(2)}) collective-permute-start(bf16[4,128,1024]{2,1,0:T(8,128)(2,1)} %get-tuple-element.182), channel_id=1, source_target_pairs={{0,8},{4,12},{8,0},{12,4},{16,24},{20,28},{24,16},{28,20},{1,9},{5... | collective-permute-start | bytes 3145736 | tf_op jit(solution)/shard_map/ppermute | solution.py:61
  263.8 30.8 %collective-permute-start.23 = (bf16[4,128,4096]{2,1,0:T(8,128)(2,1)}, bf16[4,128,4096]{2,1,0:T(8,128)(2,1)}, u32[]{:S(2)}, u32[]{:S(2)}) collective-permute-start(bf16[4,128,4096]{2,1,0:T(8,128)(2,1)} %shard_map.347), channel_id=1, source_target_pairs={{0,4},{4,0},{8,12},{12,8},{16,20},{20,16},{24,28},{28,24},{1,5},{5... | collective-permute-start | bytes 12582920 | tf_op jit(solution)/shard_map/ppermute | solution.py:61
  264.0 25.7 %collective-permute-start.22 = (bf16[4,128,1024]{2,1,0:T(8,128)(2,1)}, bf16[4,128,1024]{2,1,0:T(8,128)(2,1)}, u32[]{:S(2)}, u32[]{:S(2)}) collective-permute-start(bf16[4,128,1024]{2,1,0:T(8,128)(2,1)} %get-tuple-element.194), channel_id=1, source_target_pairs={{0,16},{4,20},{8,24},{12,28},{16,0},{20,4},{24,8},{28,12},{1,17},{... | collective-permute-start | bytes 3145736 | tf_op jit(solution)/shard_map/ppermute | solution.py:61
  277.8 24.8 %all-to-all-start.3 = ((bf16[4,384,256]{2,1,0:T(8,128)(2,1)}), bf16[4,384,256]{2,1,0:T(8,128)(2,1)S(1)}, u32[]{:S(2)}, u32[]{:S(2)}) async-start(bf16[4,384,256]{2,1,0:T(8,128)(2,1)} %get-tuple-element.199), calls=%async_computation.3 | async-start | bytes 1572864 | tf_op jit(solution)/shard_map/all_to_all | solution.py:69
  293.6 13.5 %collective-permute-start.24 = (bf16[4,64,1024]{2,1,0:T(8,128)(2,1)}, bf16[4,64,1024]{2,1,0:T(8,128)(2,1)S(1)}, u32[]{:S(2)}, u32[]{:S(2)}) collective-permute-start(bf16[4,64,1024]{2,1,0:T(8,128)(2,1)} %get-tuple-element.195), channel_id=1, source_target_pairs={{0,16},{4,20},{8,24},{12,28},{16,0},{20,4},{24,8},{28,12},{1,17},{... | collective-permute-start | bytes 1572872 | tf_op jit(solution)/shard_map/ppermute | solution.py:61
  294.1 13.3 %collective-permute-start.25 = (bf16[4,64,1024]{2,1,0:T(8,128)(2,1)}, bf16[4,64,1024]{2,1,0:T(8,128)(2,1)S(1)}, u32[]{:S(2)}, u32[]{:S(2)}) collective-permute-start(bf16[4,64,1024]{2,1,0:T(8,128)(2,1)} %get-tuple-element.203), channel_id=1, source_target_pairs={{0,8},{4,12},{8,0},{12,4},{16,24},{20,28},{24,16},{28,20},{1,9},{5... | collective-permute-start | bytes 1572872 | tf_op jit(solution)/shard_map/ppermute | solution.py:61
  310.9 29.0 %all-to-all-start.4 = ((bf16[4,2,64,1024]{3,2,1,0:T(8,128)(2,1)}), bf16[4,2,64,1024]{3,2,1,0:T(8,128)(2,1)}, u32[]{:S(2)}, u32[]{:S(2)}) async-start(bf16[4,2,64,1024]{3,2,1,0:T(8,128)(2,1)} %shard_map.351), calls=%async_computation.4 | async-start | bytes 2097152 | tf_op jit(solution)/shard_map/all_to_all | solution.py:69
  315.1 31.8 %collective-permute-start.26 = (bf16[4,32,4096]{2,1,0:T(8,128)(2,1)}, bf16[4,32,4096]{2,1,0:T(8,128)(2,1)}, u32[]{:S(2)}, u32[]{:S(2)}) collective-permute-start(bf16[4,32,4096]{2,1,0:T(8,128)(2,1)} %get-tuple-element.197), channel_id=1, source_target_pairs={{0,8},{4,12},{8,0},{12,4},{16,24},{20,28},{24,16},{28,20},{1,9},{5... | collective-permute-start | bytes 3145736 | tf_op jit(solution)/shard_map/ppermute | solution.py:61
  315.7 31.2 %collective-permute-start.27 = (bf16[4,32,4096]{2,1,0:T(8,128)(2,1)}, bf16[4,32,4096]{2,1,0:T(8,128)(2,1)}, u32[]{:S(2)}, u32[]{:S(2)}) collective-permute-start(bf16[4,32,4096]{2,1,0:T(8,128)(2,1)} %get-tuple-element.212), channel_id=1, source_target_pairs={{0,16},{4,20},{8,24},{12,28},{16,0},{20,4},{24,8},{28,12},{1,17},{... | collective-permute-start | bytes 3145736 | tf_op jit(solution)/shard_map/ppermute | solution.py:61
  339.9 32.6 %all-to-all-start.5 = ((bf16[4,384,384]{2,1,0:T(8,128)(2,1)}), bf16[4,384,384]{2,1,0:T(8,128)(2,1)}, u32[]{:S(2)}, u32[]{:S(2)}) async-start(bf16[4,384,384]{2,1,0:T(8,128)(2,1)} %shard_map.352), calls=%async_computation.5 | async-start | bytes 2359296 | tf_op jit(solution)/shard_map/all_to_all | solution.py:69
  346.4 24.5 %collective-permute-start.30 = (bf16[1,64,1024]{2,1,0:T(8,128)(2,1)}, bf16[1,64,1024]{2,1,0:T(8,128)(2,1)}, u32[]{:S(2)}, u32[]{:S(2)}) collective-permute-start(bf16[1,64,1024]{2,1,0:T(8,128)(2,1)} %get-tuple-element.208), channel_id=1, source_target_pairs={{0,8},{4,12},{8,0},{12,4},{16,24},{20,28},{24,16},{28,20},{1,9},{5... | collective-permute-start | bytes 393224 | tf_op jit(solution)/shard_map/ppermute | solution.py:61
  350.8 21.6 %collective-permute-start.28 = (bf16[4,16,4096]{2,1,0:T(8,128)(2,1)}, bf16[4,16,4096]{2,1,0:T(8,128)(2,1)}, u32[]{:S(2)}, u32[]{:S(2)}) collective-permute-start(bf16[4,16,4096]{2,1,0:T(8,128)(2,1)} %get-tuple-element.213), channel_id=1, source_target_pairs={{0,16},{4,20},{8,24},{12,28},{16,0},{20,4},{24,8},{28,12},{1,17},{... | collective-permute-start | bytes 1572872 | tf_op jit(solution)/shard_map/ppermute | solution.py:61
  352.1 17.7 %collective-permute-start.31 = (bf16[1,64,1024]{2,1,0:T(8,128)(2,1)}, bf16[1,64,1024]{2,1,0:T(8,128)(2,1)}, u32[]{:S(2)}, u32[]{:S(2)}) collective-permute-start(bf16[1,64,1024]{2,1,0:T(8,128)(2,1)} %get-tuple-element.220), channel_id=1, source_target_pairs={{0,16},{4,20},{8,24},{12,28},{16,0},{20,4},{24,8},{28,12},{1,17},{... | collective-permute-start | bytes 393224 | tf_op jit(solution)/shard_map/ppermute | solution.py:61
  352.8 19.6 %collective-permute-start.29 = (bf16[4,16,4096]{2,1,0:T(8,128)(2,1)}, bf16[4,16,4096]{2,1,0:T(8,128)(2,1)}, u32[]{:S(2)}, u32[]{:S(2)}) collective-permute-start(bf16[4,16,4096]{2,1,0:T(8,128)(2,1)} %get-tuple-element.219), channel_id=1, source_target_pairs={{0,8},{4,12},{8,0},{12,4},{16,24},{20,28},{24,16},{28,20},{1,9},{5... | collective-permute-start | bytes 1572872 | tf_op jit(solution)/shard_map/ppermute | solution.py:61
  379.9 13.8 %collective-permute-start.34 = (bf16[4,128,1792]{2,1,0:T(8,128)(2,1)}, bf16[4,128,1792]{2,1,0:T(8,128)(2,1)}, u32[]{:S(2)}, u32[]{:S(2)}) collective-permute-start(bf16[4,128,1792]{2,1,0:T(8,128)(2,1)} %shard_map.356), channel_id=1, source_target_pairs={{0,4},{4,0},{8,12},{12,8},{16,20},{20,16},{24,28},{28,24},{1,5},{5... | collective-permute-start | bytes 5505032 | tf_op jit(solution)/shard_map/ppermute | solution.py:61
  379.9 33.6 %all-to-all-start.6 = ((bf16[4,384,384]{2,1,0:T(8,128)(2,1)}), bf16[4,384,384]{2,1,0:T(8,128)(2,1)S(1)}, u32[]{:S(2)}, u32[]{:S(2)}) async-start(bf16[4,384,384]{2,1,0:T(8,128)(2,1)} %shard_map.355), calls=%async_computation.6 | async-start | bytes 2359296 | tf_op jit(solution)/shard_map/all_to_all | solution.py:69
  384.4 8.4 %collective-permute-start.33 = (bf16[2,1,64,1024]{3,2,0,1:T(8,128)(2,1)S(1)}, bf16[2,1,64,1024]{3,2,0,1:T(8,128)(2,1)S(1)}, u32[]{:S(2)}, u32[]{:S(2)}) collective-permute-start(bf16[2,1,64,1024]{3,2,0,1:T(8,128)(2,1)S(1)} %pad_maximum_fusion.19), channel_id=1, source_target_pairs={{0,8},{4,12},{8,0},{12,4},{16,24},{20,28},{24,16},{28,20},{1,9},{5... | collective-permute-start | bytes 786440 | tf_op jit(solution)/shard_map/ppermute | solution.py:61
  384.9 8.2 %collective-permute-start.32 = (bf16[2,1,64,1024]{3,2,0,1:T(8,128)(2,1)S(1)}, bf16[2,1,64,1024]{3,2,0,1:T(8,128)(2,1)S(1)}, u32[]{:S(2)}, u32[]{:S(2)}) collective-permute-start(bf16[2,1,64,1024]{3,2,0,1:T(8,128)(2,1)S(1)} %pad_maximum_fusion.18), channel_id=1, source_target_pairs={{0,16},{4,20},{8,24},{12,28},{16,0},{20,4},{24,8},{28,12},{1,17},{... | collective-permute-start | bytes 786440 | tf_op jit(solution)/shard_map/ppermute | solution.py:61
  393.1 20.5 %collective-permute-start.35 = (bf16[2,2,1,64,1024]{4,3,2,1,0:T(8,128)(2,1)S(1)}, bf16[2,2,1,64,1024]{4,3,2,1,0:T(8,128)(2,1)}, u32[]{:S(2)}, u32[]{:S(2)}) collective-permute-start(bf16[2,2,1,64,1024]{4,3,2,1,0:T(8,128)(2,1)S(1)} %pad_maximum_fusion.10.refs_0_), channel_id=1, source_target_pairs={{0,4},{4,0},{8,12},{12,8},{16,20},{20,16},{24,28},{28,24},{1,5},{5... | collective-permute-start | bytes 1572872 | tf_op jit(solution)/shard_map/ppermute | solution.py:61
  393.2 20.4 %collective-permute-start.36 = (bf16[2,2,1,64,1024]{4,3,2,1,0:T(8,128)(2,1)S(1)}, bf16[2,2,1,64,1024]{4,3,2,1,0:T(8,128)(2,1)}, u32[]{:S(2)}, u32[]{:S(2)}) collective-permute-start(bf16[2,2,1,64,1024]{4,3,2,1,0:T(8,128)(2,1)S(1)} %pad_maximum_fusion.11.refs_1_), channel_id=1, source_target_pairs={{0,4},{4,0},{8,12},{12,8},{16,20},{20,16},{24,28},{28,24},{1,5},{5... | collective-permute-start | bytes 1572872 | tf_op jit(solution)/shard_map/ppermute | solution.py:61
  401.5 20.9 %collective-permute-start.37 = (bf16[4,32,1792]{2,1,0:T(8,128)(2,1)}, bf16[4,32,1792]{2,1,0:T(8,128)(2,1)}, u32[]{:S(2)}, u32[]{:S(2)}) collective-permute-start(bf16[4,32,1792]{2,1,0:T(8,128)(2,1)} %get-tuple-element.228), channel_id=1, source_target_pairs={{0,8},{4,12},{8,0},{12,4},{16,24},{20,28},{24,16},{28,20},{1,9},{5... | collective-permute-start | bytes 1376264 | tf_op jit(solution)/shard_map/ppermute | solution.py:61
  403.0 19.3 %collective-permute-start.38 = (bf16[4,32,1792]{2,1,0:T(8,128)(2,1)}, bf16[4,32,1792]{2,1,0:T(8,128)(2,1)}, u32[]{:S(2)}, u32[]{:S(2)}) collective-permute-start(bf16[4,32,1792]{2,1,0:T(8,128)(2,1)} %get-tuple-element.236), channel_id=1, source_target_pairs={{0,16},{4,20},{8,24},{12,28},{16,0},{20,4},{24,8},{28,12},{1,17},{... | collective-permute-start | bytes 1376264 | tf_op jit(solution)/shard_map/ppermute | solution.py:61
  417.8 30.2 %all-to-all-start.7 = ((bf16[4,2,16,4096]{3,2,1,0:T(8,128)(2,1)}), bf16[4,2,16,4096]{3,2,1,0:T(8,128)(2,1)}, u32[]{:S(2)}, u32[]{:S(2)}) async-start(bf16[4,2,16,4096]{3,2,1,0:T(8,128)(2,1)} %shard_map.357), calls=%async_computation.7 | async-start | bytes 2097152 | tf_op jit(solution)/shard_map/all_to_all | solution.py:69
  424.9 13.3 %collective-permute-start.39 = (bf16[4,16,1792]{2,1,0:T(8,128)(2,1)}, bf16[4,16,1792]{2,1,0:T(8,128)(2,1)S(1)}, u32[]{:S(2)}, u32[]{:S(2)}) collective-permute-start(bf16[4,16,1792]{2,1,0:T(8,128)(2,1)} %get-tuple-element.237), channel_id=1, source_target_pairs={{0,16},{4,20},{8,24},{12,28},{16,0},{20,4},{24,8},{28,12},{1,17},{... | collective-permute-start | bytes 688136 | tf_op jit(solution)/shard_map/ppermute | solution.py:61
  426.2 12.0 %collective-permute-start.40 = (bf16[4,16,1792]{2,1,0:T(8,128)(2,1)}, bf16[4,16,1792]{2,1,0:T(8,128)(2,1)S(1)}, u32[]{:S(2)}, u32[]{:S(2)}) collective-permute-start(bf16[4,16,1792]{2,1,0:T(8,128)(2,1)} %get-tuple-element.243), channel_id=1, source_target_pairs={{0,8},{4,12},{8,0},{12,4},{16,24},{20,28},{24,16},{28,20},{1,9},{5... | collective-permute-start | bytes 688136 | tf_op jit(solution)/shard_map/ppermute | solution.py:61
  448.0 9.1 %all-to-all-start.8 = ((f32[4,20,256]{2,1,0:T(8,128)}), f32[4,20,256]{2,1,0:T(8,128)S(1)}, u32[]{:S(2)}, u32[]{:S(2)}) async-start(f32[4,20,256]{2,1,0:T(8,128)} %pad_maximum_fusion.24), calls=%async_computation.8 | async-start | bytes 196608 | tf_op jit(solution)/shard_map/all_to_all | solution.py:69
  454.9 12.0 %collective-permute-start.44 = (bf16[1,16,4096]{2,1,0:T(8,128)(2,1)}, bf16[1,16,4096]{2,1,0:T(8,128)(2,1)S(1)}, u32[]{:S(2)}, u32[]{:S(2)}) collective-permute-start(bf16[1,16,4096]{2,1,0:T(8,128)(2,1)} %get-tuple-element.248), channel_id=1, source_target_pairs={{0,8},{4,12},{8,0},{12,4},{16,24},{20,28},{24,16},{28,20},{1,9},{5... | collective-permute-start | bytes 393224 | tf_op jit(solution)/shard_map/ppermute | solution.py:61
  455.4 8.2 %collective-permute-start.45 = (bf16[1,16,4096]{2,1,0:T(8,128)(2,1)}, bf16[1,16,4096]{2,1,0:T(8,128)(2,1)S(1)}, u32[]{:S(2)}, u32[]{:S(2)}) collective-permute-start(bf16[1,16,4096]{2,1,0:T(8,128)(2,1)} %get-tuple-element.255), channel_id=1, source_target_pairs={{0,16},{4,20},{8,24},{12,28},{16,0},{20,4},{24,8},{28,12},{1,17},{... | collective-permute-start | bytes 393224 | tf_op jit(solution)/shard_map/ppermute | solution.py:61
  457.2 4.7 collective-permute-start.41
  457.2 18.4 %all-to-all-start.9 = ((bf16[4,2,16,1792]{3,2,1,0:T(8,128)(2,1)}), bf16[4,2,16,1792]{3,2,1,0:T(8,128)(2,1)S(1)}, u32[]{:S(2)}, u32[]{:S(2)}) async-start(bf16[4,2,16,1792]{3,2,1,0:T(8,128)(2,1)} %shard_map.362), calls=%async_computation.9 | async-start | bytes 917504 | tf_op jit(solution)/shard_map/all_to_all | solution.py:69
  462.0 4.0 collective-permute-start.42
  466.0 4.1 collective-permute-start.43
  478.2 6.5 %collective-permute-start.49 = (bf16[1,16,4096]{2,1,0:T(8,128)(2,1)}, bf16[1,16,4096]{2,1,0:T(8,128)(2,1)S(1)}, u32[]{:S(2)}, u32[]{:S(2)}) collective-permute-start(bf16[1,16,4096]{2,1,0:T(8,128)(2,1)} %get-tuple-element.262), channel_id=1, source_target_pairs={{0,16},{4,20},{8,24},{12,28},{16,0},{20,4},{24,8},{28,12},{1,17},{... | collective-permute-start | bytes 393224 | tf_op jit(solution)/shard_map/ppermute | solution.py:61
  478.9 6.7 %collective-permute-start.48 = (bf16[1,16,4096]{2,1,0:T(8,128)(2,1)}, bf16[1,16,4096]{2,1,0:T(8,128)(2,1)S(1)}, u32[]{:S(2)}, u32[]{:S(2)}) collective-permute-start(bf16[1,16,4096]{2,1,0:T(8,128)(2,1)} %get-tuple-element.257), channel_id=1, source_target_pairs={{0,8},{4,12},{8,0},{12,4},{16,24},{20,28},{24,16},{28,20},{1,9},{5... | collective-permute-start | bytes 393224 | tf_op jit(solution)/shard_map/ppermute | solution.py:61
  480.4 8.8 %collective-permute-start.47 = (bf16[2,1,16,4096]{3,2,0,1:T(8,128)(2,1)S(1)}, bf16[2,1,16,4096]{3,2,0,1:T(8,128)(2,1)S(1)}, u32[]{:S(2)}, u32[]{:S(2)}) collective-permute-start(bf16[2,1,16,4096]{3,2,0,1:T(8,128)(2,1)S(1)} %pad_maximum_fusion.21), channel_id=1, source_target_pairs={{0,8},{4,12},{8,0},{12,4},{16,24},{20,28},{24,16},{28,20},{1,9},{5... | collective-permute-start | bytes 786440 | tf_op jit(solution)/shard_map/ppermute | solution.py:61
  480.9 8.4 %collective-permute-start.46 = (bf16[2,1,16,4096]{3,2,0,1:T(8,128)(2,1)S(1)}, bf16[2,1,16,4096]{3,2,0,1:T(8,128)(2,1)S(1)}, u32[]{:S(2)}, u32[]{:S(2)}) collective-permute-start(bf16[2,1,16,4096]{3,2,0,1:T(8,128)(2,1)S(1)} %pad_maximum_fusion.20), channel_id=1, source_target_pairs={{0,16},{4,20},{8,24},{12,28},{16,0},{20,4},{24,8},{28,12},{1,17},{... | collective-permute-start | bytes 786440 | tf_op jit(solution)/shard_map/ppermute | solution.py:61
  489.3 6.8 %collective-permute-start.53 = (bf16[2,1,16,4096]{3,2,0,1:T(8,128)(2,1)S(1)}, bf16[2,1,16,4096]{3,2,0,1:T(8,128)(2,1)S(1)}, u32[]{:S(2)}, u32[]{:S(2)}) collective-permute-start(bf16[2,1,16,4096]{3,2,0,1:T(8,128)(2,1)S(1)} %pad_maximum_fusion.23), channel_id=1, source_target_pairs={{0,8},{4,12},{8,0},{12,4},{16,24},{20,28},{24,16},{28,20},{1,9},{5... | collective-permute-start | bytes 786440 | tf_op jit(solution)/shard_map/ppermute | solution.py:61
  492.1 6.4 %collective-permute-start.52 = (bf16[2,1,16,4096]{3,2,0,1:T(8,128)(2,1)S(1)}, bf16[2,1,16,4096]{3,2,0,1:T(8,128)(2,1)S(1)}, u32[]{:S(2)}, u32[]{:S(2)}) collective-permute-start(bf16[2,1,16,4096]{3,2,0,1:T(8,128)(2,1)S(1)} %pad_maximum_fusion.22), channel_id=1, source_target_pairs={{0,16},{4,20},{8,24},{12,28},{16,0},{20,4},{24,8},{28,12},{1,17},{... | collective-permute-start | bytes 786440 | tf_op jit(solution)/shard_map/ppermute | solution.py:61
  493.4 5.2 %collective-permute-start.50 = (bf16[2,2,1,16,4096]{4,3,2,1,0:T(8,128)(2,1)S(1)}, bf16[2,2,1,16,4096]{4,3,2,1,0:T(8,128)(2,1)S(1)}, u32[]{:S(2)}, u32[]{:S(2)}) collective-permute-start(bf16[2,2,1,16,4096]{4,3,2,1,0:T(8,128)(2,1)S(1)} %pad_maximum_fusion.12.refs_0_), channel_id=1, source_target_pairs={{0,4},{4,0},{8,12},{12,8},{16,20},{20,16},{24,28},{28,24},{1,5},{5... | collective-permute-start | bytes 1572872 | tf_op jit(solution)/shard_map/ppermute | solution.py:61
  493.4 5.2 %collective-permute-start.51 = (bf16[2,2,1,16,4096]{4,3,2,1,0:T(8,128)(2,1)S(1)}, bf16[2,2,1,16,4096]{4,3,2,1,0:T(8,128)(2,1)S(1)}, u32[]{:S(2)}, u32[]{:S(2)}) collective-permute-start(bf16[2,2,1,16,4096]{4,3,2,1,0:T(8,128)(2,1)S(1)} %pad_maximum_fusion.13.refs_1_), channel_id=1, source_target_pairs={{0,4},{4,0},{8,12},{12,8},{16,20},{20,16},{24,28},{28,24},{1,5},{5... | collective-permute-start | bytes 1572872 | tf_op jit(solution)/shard_map/ppermute | solution.py:61
  (44 other events, 245.8 us)
